TPU v7x, 32 devices: a whole 2x2x4 slice. The times are simulated.
32 devices in a mesh: strata: 8 (over z, x), shard: 4 (over y, core).
Axes of the slice: x: 2, y: 2, z: 4, core: 2. Of those that a mesh axis runs over, the one named last changes fastest.
Arguments:
- user_factors: bfloat16 [32768, 512], P(('strata', 'shard')), may hold values from -1.1953125 to 1.1953125
- item_factors: float32 [4096, 512], P(('strata', 'shard')), may hold values from -1.2 to 1.2
- tile_blocks: int32 [8, 4, 3, 8, 2], P('strata', 'shard'), may hold values from 0 to 7, as said below
- tile_counts: int32 [8, 4, 3], P('strata', 'shard'), may hold values from 1 to 8, as said below
- ratings: bfloat16 [8, 4, 3, 8, 128, 128], P('strata', 'shard'), may hold values from -5 to 5
- mask_words: int32 [8, 4, 3, 8, 16, 128], P('strata', 'shard'), may hold values from 0 to 255
Outputs:
- users_out: bfloat16 [32768, 512], P(('strata', 'shard'))
- items_out: float32 [4096, 512], P(('strata', 'shard'))
Inputs may be any that keep to these rules, and one draw needn't show every extreme that they name: `tile_blocks`: entry 0 is a user block below 8, entry 1 an item block below 4; the 8 pairs of one stratum, shard and visit are distinct. `tile_counts`: some stratum, shard and visit has exactly 8 live slots in every draw.
All inputs are finite; a program needn't handle non-finite values.
Results may differ from a plain program's by a relative error of at most 0.0095.
Values may be sent and summed in bfloat16 or wider, within the bound.
No kernel may reach another device: no remote copies, remote signals or barrier semaphores. Data moves between devices by JAX's collectives and lax.ppermute only.
A program may use at most 64 MiB of HBM per device.

v0:
```python
import jax
import jax.numpy as jnp
from jax import lax
from jax.sharding import PartitionSpec as P

step_user = 0.05
step_item = 0.004
shrinkage = 0.05


def shifted(x, axis, by):
    peers = lax.axis_size(axis)
    return lax.ppermute(x, axis, [(i, (i + by) % peers) for i in range(peers)])


def unpack_mask(words):
    shifts = jnp.arange(8, dtype=jnp.int32)
    bits = jnp.bitwise_and(jnp.right_shift(words[:, :, None, :], shifts[None, None, :, None]), 1)
    return bits.reshape(words.shape[0], words.shape[1] * 8, words.shape[2]).astype(jnp.float32)


def device_terms(users, panel_low, blocks, count, rates, words):
    tile_side = rates.shape[-1]
    width = users.shape[1]
    user_count = users.shape[0] // tile_side
    item_count = panel_low.shape[0] // tile_side
    live = (jnp.arange(blocks.shape[0], dtype=jnp.int32) < count).astype(jnp.float32)
    weights = unpack_mask(words) * live[:, None, None]
    user_rows = jnp.take(users.reshape(user_count, tile_side, width), blocks[:, 0], axis=0)
    item_rows = jnp.take(panel_low.reshape(item_count, tile_side, width), blocks[:, 1], axis=0)
    predicted = jnp.einsum("kur,kir->kui", user_rows, item_rows, preferred_element_type=jnp.float32)
    error_tile = (weights * (rates.astype(jnp.float32) - predicted)).astype(jnp.bfloat16)
    user_terms = jnp.einsum(
        "kui,kir->kur", error_tile, item_rows, preferred_element_type=jnp.float32
    )
    item_terms = jnp.einsum(
        "kui,kur->kir", error_tile, user_rows, preferred_element_type=jnp.float32
    )
    user_hot = (blocks[:, 0][:, None] == jnp.arange(user_count, dtype=jnp.int32)[None, :]).astype(
        jnp.float32
    )
    item_hot = (blocks[:, 1][:, None] == jnp.arange(item_count, dtype=jnp.int32)[None, :]).astype(
        jnp.float32
    )
    grad_user = jnp.einsum(
        "kb,kur->bur", user_hot, user_terms, precision=lax.Precision.HIGHEST
    ).reshape(-1, width)
    grad_item = jnp.einsum(
        "kb,kir->bir", item_hot, item_terms, precision=lax.Precision.HIGHEST
    ).reshape(-1, width)
    return (grad_user, grad_item)


def shards(user_factors, item_factors, tile_blocks, tile_counts, ratings, mask_words):
    blocks_all = tile_blocks[0, 0]
    counts_all = tile_counts[0, 0]
    rates_all = ratings[0, 0]
    words_all = mask_words[0, 0]
    visits = counts_all.shape[0]
    users = user_factors
    panel = item_factors
    for visit in range(visits):
        panel_low = lax.all_gather(panel.astype(jnp.bfloat16), "shard", axis=0, tiled=True)
        grad_user, grad_item = device_terms(
            users,
            panel_low,
            blocks_all[visit],
            counts_all[visit],
            rates_all[visit],
            words_all[visit],
        )
        summed = lax.psum_scatter(
            grad_item.astype(jnp.bfloat16), "shard", scatter_dimension=0, tiled=True
        ).astype(jnp.float32)
        factor = users.astype(jnp.float32)
        users = (factor + step_user * (grad_user - shrinkage * factor)).astype(jnp.bfloat16)
        panel = panel + step_item * (summed - shrinkage * panel)
        if visit + 1 < visits:
            panel = shifted(panel.astype(jnp.bfloat16), "strata", 1).astype(panel.dtype)
    return (users, panel)


def solution(mesh):
    placed = (
        P(("strata", "shard"), None),
        P(("strata", "shard"), None),
        P("strata", "shard", None, None, None),
        P("strata", "shard", None),
        P("strata", "shard", None, None, None, None),
        P("strata", "shard", None, None, None, None),
    )
    return jax.shard_map(
        shards,
        mesh=mesh,
        in_specs=placed,
        out_specs=(P(("strata", "shard"), None), P(("strata", "shard"), None)),
        check_vma=False,
    )
```

profile of v0, /device:TPU:0, one launch (start us, length us, event | category | flops | bytes accessed | tf_op | source)
XLA Modules:
  0.0 144.2 jit_solution(1562608202516303314)
XLA Ops:
  7.2 0.8 slice_bitcast_fusion.3
  8.0 0.5 slice_bitcast_fusion.10
  8.5 0.6 compare_and_fusion.4
  9.1 1.4 fusion.83
  10.5 1.2 compare_convert_fusion.2
  11.7 0.6 shift_right_arithmetic.70
  12.3 1.0 convert_element_type.130
  13.3 1.5 %slice_bitcast_fusion = (s32[8,16,128]{2,1,0:T(8,128)S(1)}, s32[8,16,128]{2,1,0:T(8,128)}, s32[8,16,128]{2,1,0:T(8,128)S(1)}) fusion(s32[1,1,3,8,16,128]{5,4,3,2,1,0:T(8,128)} %param.15), kind=kLoop, calls=%fused_computation.79 | loop fusion | bytes 393216 | tf_op jit(solution)/shard_map/shift_right_arithmetic | solution.py:18
  14.8 8.6 %all_gather.9 = bf16[512,512]{1,0:T(8,128)(2,1)S(1)} all-gather(bf16[128,512]{1,0:T(8,128)(2,1)S(1)} %convert_element_type.130), channel_id=1, replica_groups=mesh['strata'=8,'shard'=4] {'shard'}, dimensions={0}, use_global_device_ids=true | all-gather | bytes 655360 | tf_op jit(solution)/shard_map/all_gather | solution.py:63
  23.5 0.6 gather_fusion.1
  24.1 0.6 gather_fusion
  24.7 1.5 %fusion.35 = bf16[8,128,128]{2,1,0:T(8,128)(2,1)S(1)} fusion(bf16[8,128,512]{2,1,0:T(8,128)(2,1)S(1)} %gather_fusion, pred[8]{0:T(512)(128)(4,1)} %get-tuple-element.32, bf16[8,128,512]{2,1,0:T(8,128)(2,1)S(1)} %gather_fusion.1, pred[8]{0:T(512)(128)(4,1)} %get-tuple-element.12, bf16[1,1,3,8,128,128]{5,4,3,2,1,0:T(8,128)(2,1)} %param.14, ...), kind=kOutput, calls=%fused_computation.44 | convolution fusion | flops 136314880 | bytes 2687536 | tf_op jit(solution)/shard_map/kur,kir->kui/dot_general | solution.py:31
  26.3 0.5 fusion.45
  26.9 2.2 %fusion.21 = bf16[4,128,512]{2,0,1:T(4,128)(2,1)S(1)} fusion(f32[8,128,512]{2,1,0:T(8,128)S(1)} %fusion.45, s32[8]{0:T(128)S(1)} %copy-done.6), kind=kOutput, calls=%fused_computation.33 | convolution fusion | flops 25428000 | bytes 2621472 | tf_op jit(solution)/shard_map/kb,kir->bir/dot_general | solution.py:48
  29.1 0.9 copy.9
  30.6 2.2 %fusion.19 = f32[8,128,512]{2,0,1:T(8,128)S(1)} fusion(f32[8,128,512]{2,1,0:T(8,128)S(1)} %fusion.46, s32[8]{0:T(128)S(1)} %get-tuple-element.31), kind=kOutput, calls=%fused_computation.31 | convolution fusion | flops 50331712 | bytes 4194336 | tf_op jit(solution)/shard_map/kb,kur->bur/dot_general | solution.py:45
  32.8 1.2 copy.8
  34.5 18.2 %reduce-scatter.4.cloned.1.call-done = bf16[128,512]{1,0:T(8,128)(2,1)} async-done(((bf16[512,512]{1,0:T(8,128)(2,1)}), bf16[128,512]{1,0:T(8,128)(2,1)}) %reduce-scatter.4.cloned.1.call-update) | async-done | bytes 131088 | tf_op jit(solution)/shard_map/reduce_scatter | solution.py:72
  52.7 1.0 add_convert_fusion
  53.7 1.5 %collective-permute-start = (bf16[128,512]{1,0:T(8,128)(2,1)S(1)}, bf16[128,512]{1,0:T(8,128)(2,1)S(1)}, u32[]{:S(2)}, u32[]{:S(2)}) collective-permute-start(bf16[128,512]{1,0:T(8,128)(2,1)S(1)} %add_convert_fusion), channel_id=1, source_target_pairs={{0,4},{4,8},{8,12},{12,16},{16,20},{20,24},{24,28},{28,0},{1,5},{5... | collective-permute-start | bytes 393224 | tf_op jit(solution)/shard_map/ppermute | solution.py:13
  55.2 1.6 %gather_fusion.2 = bf16[8,128,512]{2,1,0:T(8,128)(2,1)} fusion(bf16[8,128,512]{2,1,0:T(8,128)(2,1)S(1)} %bitcast.123, s32[1024]{0:T(1024)S(1)} %get-tuple-element.42), kind=kCustom, calls=%fused_computation.2.clone | custom fusion | bytes 2097184 | tf_op jit(solution)/shard_map/jit(_take)/gather | solution.py:29
  56.8 0.6 compare_convert_fusion.1
  57.4 4.3 %collective-permute-done = bf16[128,512]{1,0:T(8,128)(2,1)S(1)} collective-permute-done((bf16[128,512]{1,0:T(8,128)(2,1)S(1)}, bf16[128,512]{1,0:T(8,128)(2,1)S(1)}, u32[]{:S(2)}, u32[]{:S(2)}) %collective-permute-start) | collective-permute-done | bytes 131104 | tf_op jit(solution)/shard_map/ppermute | solution.py:13
  61.7 6.7 %all_gather.10 = bf16[512,512]{1,0:T(8,128)(2,1)S(1)} all-gather(bf16[128,512]{1,0:T(8,128)(2,1)S(1)} %collective-permute-done), channel_id=1, replica_groups=mesh['strata'=8,'shard'=4] {'shard'}, dimensions={0}, use_global_device_ids=true | all-gather | bytes 655360 | tf_op jit(solution)/shard_map/all_gather | solution.py:63
  68.3 0.6 gather_fusion.3
  69.0 1.9 %fusion.34 = bf16[8,128,128]{2,1,0:T(8,128)(2,1)S(1)} fusion(bf16[8,128,512]{2,1,0:T(8,128)(2,1)} %gather_fusion.2, pred[8]{0:T(512)(128)(4,1)S(1)} %get-tuple-element.28, bf16[8,128,512]{2,1,0:T(8,128)(2,1)S(1)} %gather_fusion.3, pred[8]{0:T(512)(128)(4,1)S(1)} %get-tuple-element.8, bf16[1,1,3,8,128,128]{5,4,3,2,1,0:T(8,128)(2,1)} %param.14, ...), kind=kOutput, calls=%fused_computation.43 | convolution fusion | flops 136314880 | bytes 2687536 | tf_op jit(solution)/shard_map/kur,kir->kui/dot_general | solution.py:31
  70.9 0.5 fusion.47
  71.4 2.2 %fusion.24 = bf16[4,128,512]{2,0,1:T(4,128)(2,1)S(1)} fusion(f32[8,128,512]{2,1,0:T(8,128)S(1)} %fusion.47, s32[8]{0:T(128)S(1)} %get-tuple-element.38), kind=kOutput, calls=%fused_computation.34 | convolution fusion | flops 25428000 | bytes 2621472 | tf_op jit(solution)/shard_map/kb,kir->bir/dot_general | solution.py:48
  73.6 0.9 copy.11
  74.6 0.6 compare_convert_fusion
  75.8 2.2 %fusion.15 = f32[8,128,512]{2,0,1:T(8,128)S(1)} fusion(f32[8,128,512]{2,1,0:T(8,128)S(1)} %fusion.48, s32[8]{0:T(128)S(1)} %get-tuple-element.37), kind=kOutput, calls=%fused_computation.27 | convolution fusion | flops 50331712 | bytes 4194336 | tf_op jit(solution)/shard_map/kb,kur->bur/dot_general | solution.py:45
  78.0 2.5 %copy.10 = f32[8,128,512]{2,1,0:T(8,128)} copy(f32[8,128,512]{2,0,1:T(8,128)S(1)} %fusion.15) | data formatting | bytes 4194304 | tf_op jit(solution)/shard_map/kb,kur->bur/dot_general | solution.py:45
  80.6 13.8 %reduce-scatter.6.cloned.1.call-done = bf16[128,512]{1,0:T(8,128)(2,1)} async-done(((bf16[512,512]{1,0:T(8,128)(2,1)}), bf16[128,512]{1,0:T(8,128)(2,1)}) %reduce-scatter.6.cloned.1.call-update) | async-done | bytes 131088 | tf_op jit(solution)/shard_map/reduce_scatter | solution.py:72
  94.3 1.0 fusion.53
  95.3 1.5 %collective-permute-start.1 = (bf16[128,512]{1,0:T(8,128)(2,1)S(1)}, bf16[128,512]{1,0:T(8,128)(2,1)S(1)}, u32[]{:S(2)}, u32[]{:S(2)}) collective-permute-start(bf16[128,512]{1,0:T(8,128)(2,1)S(1)} %fusion.53), channel_id=1, source_target_pairs={{0,4},{4,8},{8,12},{12,16},{16,20},{20,24},{24,28},{28,0},{1,5},{5... | collective-permute-start | bytes 393224 | tf_op jit(solution)/shard_map/ppermute | solution.py:13
  96.8 2.0 %fusion.5 = bf16[1024,512]{1,0:T(8,128)(2,1)S(1)} fusion(bf16[1024,512]{1,0:T(8,128)(2,1)S(1)} %fusion.2, f32[8,128,512]{2,1,0:T(8,128)} %copy.10), kind=kLoop, calls=%fused_computation.17 | loop fusion | flops 3145728 | bytes 4194304 | tf_op jit(solution)/shard_map/convert_element_type | solution.py:76
  98.8 1.6 %gather_fusion.4 = bf16[8,128,512]{2,1,0:T(8,128)(2,1)} fusion(bf16[8,128,512]{2,1,0:T(8,128)(2,1)S(1)} %bitcast.124, s32[1024]{0:T(1024)S(1)} %get-tuple-element.44), kind=kCustom, calls=%fused_computation.3.clone | custom fusion | bytes 2097184 | tf_op jit(solution)/shard_map/jit(_take)/gather | solution.py:29
  100.4 2.9 %collective-permute-done.1 = bf16[128,512]{1,0:T(8,128)(2,1)S(1)} collective-permute-done((bf16[128,512]{1,0:T(8,128)(2,1)S(1)}, bf16[128,512]{1,0:T(8,128)(2,1)S(1)}, u32[]{:S(2)}, u32[]{:S(2)}) %collective-permute-start.1) | collective-permute-done | bytes 131104 | tf_op jit(solution)/shard_map/ppermute | solution.py:13
  103.3 6.7 %all_gather.11 = bf16[512,512]{1,0:T(8,128)(2,1)S(1)} all-gather(bf16[128,512]{1,0:T(8,128)(2,1)S(1)} %collective-permute-done.1), channel_id=1, replica_groups=mesh['strata'=8,'shard'=4] {'shard'}, dimensions={0}, use_global_device_ids=true | all-gather | bytes 655360 | tf_op jit(solution)/shard_map/all_gather | solution.py:63
  110.0 0.6 gather_fusion.5
  110.6 1.9 %fusion.33 = bf16[8,128,128]{2,1,0:T(8,128)(2,1)S(1)} fusion(bf16[8,128,512]{2,1,0:T(8,128)(2,1)} %gather_fusion.4, pred[8]{0:T(512)(128)(4,1)S(1)} %get-tuple-element.24, bf16[8,128,512]{2,1,0:T(8,128)(2,1)S(1)} %gather_fusion.5, pred[8]{0:T(512)(128)(4,1)S(1)} %get-tuple-element.4, bf16[1,1,3,8,128,128]{5,4,3,2,1,0:T(8,128)(2,1)} %param.14, ...), kind=kOutput, calls=%fused_computation.42 | convolution fusion | flops 136314880 | bytes 2687536 | tf_op jit(solution)/shard_map/kur,kir->kui/dot_general | solution.py:31
  113.0 2.2 %fusion.27 = bf16[4,128,512]{2,0,1:T(4,128)(2,1)S(1)} fusion(f32[8,128,512]{2,1,0:T(8,128)S(1)} %fusion.49, s32[8]{0:T(128)S(1)} %get-tuple-element.22), kind=kOutput, calls=%fused_computation.35 | convolution fusion | flops 25428000 | bytes 2621472 | tf_op jit(solution)/shard_map/kb,kir->bir/dot_general | solution.py:48
  115.3 0.9 copy.13
  116.7 2.2 %fusion.11 = f32[8,128,512]{2,0,1:T(8,128)S(1)} fusion(f32[8,128,512]{2,1,0:T(8,128)S(1)} %fusion.50, s32[8]{0:T(128)S(1)} %get-tuple-element.23), kind=kOutput, calls=%fused_computation.23 | convolution fusion | flops 50331712 | bytes 4194336 | tf_op jit(solution)/shard_map/kb,kur->bur/dot_general | solution.py:45
  118.9 1.2 copy.12
  120.1 1.4 fusion.8
  121.6 14.4 %reduce-scatter.8.cloned.1.call-done = bf16[128,512]{1,0:T(8,128)(2,1)} async-done(((bf16[512,512]{1,0:T(8,128)(2,1)}), bf16[128,512]{1,0:T(8,128)(2,1)}) %reduce-scatter.8.cloned.1.call-update) | async-done | bytes 131088 | tf_op jit(solution)/shard_map/reduce_scatter | solution.py:72
  136.0 1.7 %convert_add_fusion.3 = f32[128,512]{1,0:T(8,128)} fusion(bf16[128,512]{1,0:T(8,128)(2,1)S(1)} %collective-permute-done.1, bf16[128,512]{1,0:T(8,128)(2,1)} %reduce-scatter.8.cloned.1.call-done), kind=kLoop, calls=%fused_computation.69 | loop fusion | flops 393216 | bytes 524288 | tf_op jit(solution)/shard_map/add | solution.py:77
  (34 shorter events, 2.7 us)
Async XLA Ops:
  7.2 16.9 %copy-start.2 = (bf16[1024,512]{1,0:T(8,128)(2,1)S(1)}, bf16[1024,512]{1,0:T(8,128)(2,1)}, u32[]{:S(2)}) copy-start(bf16[1024,512]{1,0:T(8,128)(2,1)} %param.10) | copy-start | bytes 3145732
  7.2 45.5 %reduce-scatter.4.cloned.1.call-start = ((), (), s32[]{:S(2)}) async-start(), calls=%async_computation.3 | async-start | bytes 655360 | tf_op jit(solution)/shard_map/reduce_scatter | solution.py:72
  24.7 1.5 %copy-start.5 = (pred[8]{0:T(512)(128)(4,1)S(1)}, pred[8]{0:T(512)(128)(4,1)}, u32[]{:S(2)}) copy-start(pred[8]{0:T(512)(128)(4,1)} %get-tuple-element.32) | copy-start | bytes 28
  26.3 0.6 copy-start.6
  26.9 3.2 %copy-start.4 = (pred[8]{0:T(512)(128)(4,1)S(1)}, pred[8]{0:T(512)(128)(4,1)}, u32[]{:S(2)}) copy-start(pred[8]{0:T(512)(128)(4,1)} %get-tuple-element.12) | copy-start | bytes 28
  30.0 64.3 %reduce-scatter.6.cloned.1.call-start = ((), (), s32[]{:S(2)}) async-start(), calls=%async_computation.4 | async-start | bytes 655360 | tf_op jit(solution)/shard_map/reduce_scatter | solution.py:72
  34.1 18.6 %copy-start.3 = (f32[128,512]{1,0:T(8,128)S(1)}, f32[128,512]{1,0:T(8,128)}, u32[]{:S(2)}) copy-start(f32[128,512]{1,0:T(8,128)} %param.11) | copy-start | bytes 786436
  53.7 8.0 %collective-permute-start = (bf16[128,512]{1,0:T(8,128)(2,1)S(1)}, bf16[128,512]{1,0:T(8,128)(2,1)S(1)}, u32[]{:S(2)}, u32[]{:S(2)}) collective-permute-start(bf16[128,512]{1,0:T(8,128)(2,1)S(1)} %add_convert_fusion), channel_id=1, source_target_pairs={{0,4},{4,8},{8,12},{12,16},{16,20},{20,24},{24,28},{28,0},{1,5},{5... | collective-permute-start | bytes 393224 | tf_op jit(solution)/shard_map/ppermute | solution.py:13
  55.2 13.8 %copy-start.7 = (s32[128]{0:T(128)S(1)}, s32[128]{0:T(128)}, u32[]{:S(2)}) copy-start(s32[128]{0:T(128)} %shift_right_arithmetic.70) | copy-start | bytes 1540
  69.0 1.9 %copy-start = (bf16[8,128,512]{2,1,0:T(8,128)(2,1)S(1)}, bf16[8,128,512]{2,1,0:T(8,128)(2,1)}, u32[]{:S(2)}) copy-start(bf16[8,128,512]{2,1,0:T(8,128)(2,1)} %gather_fusion.2) | copy-start | bytes 3145732
  74.5 61.4 %reduce-scatter.8.cloned.1.call-start = ((), (), s32[]{:S(2)}) async-start(), calls=%async_computation.5 | async-start | bytes 655360 | tf_op jit(solution)/shard_map/reduce_scatter | solution.py:72
  95.3 8.0 %collective-permute-start.1 = (bf16[128,512]{1,0:T(8,128)(2,1)S(1)}, bf16[128,512]{1,0:T(8,128)(2,1)S(1)}, u32[]{:S(2)}, u32[]{:S(2)}) collective-permute-start(bf16[128,512]{1,0:T(8,128)(2,1)S(1)} %fusion.53), channel_id=1, source_target_pairs={{0,4},{4,8},{8,12},{12,16},{16,20},{20,24},{24,28},{28,0},{1,5},{5... | collective-permute-start | bytes 393224 | tf_op jit(solution)/shard_map/ppermute | solution.py:13
  110.6 1.9 %copy-start.1 = (bf16[8,128,512]{2,1,0:T(8,128)(2,1)S(1)}, bf16[8,128,512]{2,1,0:T(8,128)(2,1)}, u32[]{:S(2)}) copy-start(bf16[8,128,512]{2,1,0:T(8,128)(2,1)} %gather_fusion.4) | copy-start | bytes 3145732
Sparse Core Ops, SparseCore 0:
  30.2 22.4 reduce-scatter.3
  74.7 19.5 reduce-scatter.5
  116.3 19.6 reduce-scatter.7
where the time goes:
time: 145 us; the launch traced here: 144 us
  waiting for transfers between devices  53.5 us (37%)
  blocking collectives  22 us (15%)
  matrix products  21.7 us (15%)
  local copies, waits for them, and re-layouts  18.3 us (13%)
  between operations  14.1 us (10%)
  other arithmetic  11.5 us (8%)
  starting transfers between devices  3.17 us (2%)
    reduce_scatter x3, waiting for transfers between devices, shards(): lax.psum_scatter(grad_item.astype(jnp.bfloat16), 'shard', scatter_dimensi...  46.3 us
    all_gather x3, blocking collectives, shards(): lax.all_gather(panel.astype(jnp.bfloat16), 'shard', axis=0, tiled=True)  22 us
    ppermute x2, waiting for transfers between devices, shifted(): return lax.ppermute(x, axis, [(i, (i + by) % peers) for i in range(peers)])  7.15 us
    dot_general x3, matrix products, device_terms(): jnp.einsum('kb,kir->bir', item_hot, item_terms, precision=lax.Precision.H...  6.7 us
    dot_general x3, matrix products, device_terms(): jnp.einsum('kb,kur->bur', user_hot, user_terms, precision=lax.Precision.H...  6.69 us
    dot_general x3, matrix products, device_terms(): jnp.einsum('kur,kir->kui', user_rows, item_rows, preferred_element_type=j...  5.29 us
    dot_general x3, local copies, waits for them, and re-layouts, device_terms(): jnp.einsum('kb,kur->bur', user_hot, user_terms, precision=lax.Precision.H...  4.99 us
    convert_element_type x3, other arithmetic, shards(): (factor + step_user * (grad_user - shrinkage * factor)).astype(jnp.bfloat16)  3.86 us
  transfers between devices with their start and end apart: 5, of which 5 were waited for; matrix products, arithmetic and copies ran while one was open for 15% of the time, Pallas kernels for 0%

commit v1 on v0

v1 whole, which is shorter than its diff:
```python
import functools

import jax
import jax.numpy as jnp
from jax import lax
from jax.experimental import pallas as pl
from jax.experimental.pallas import tpu as pltpu
from jax.sharding import PartitionSpec as P

step_user = 0.05
step_item = 0.004
shrinkage = 0.05

VM = pl.BlockSpec(memory_space=pltpu.VMEM)
SM = pl.BlockSpec(memory_space=pltpu.SMEM)
CORES = 2


def rows_at(index, size):
    return pl.ds(pl.multiple_of(index * size, size), size)


def observed(words):
    count, lanes = words.shape
    shift = lax.broadcasted_iota(jnp.int32, (8, lanes), 0)
    parts = [
        jnp.bitwise_and(jnp.right_shift(jnp.broadcast_to(words[i : i + 1], (8, lanes)), shift), 1)
        for i in range(count)
    ]
    return jnp.concatenate(parts, 0) != 0


def tiles_kernel(visit, chips, place, blocks, counts, users, rates, words, *rest):
    pieces, rest = rest[: CORES * chips], rest[CORES * chips :]
    errors, near, far, panel, total = rest
    side = rates.shape[-1]
    rows = pieces[0].shape[0]
    core, chip = place[0], place[1]
    for k in range(chips):
        origin = lax.rem(chip + chips - k, chips)
        panel[rows_at(CORES * origin + core, rows), :] = pieces[k][...]
        panel[rows_at(CORES * origin + 1 - core, rows), :] = pieces[chips + k][...]
    total[...] = jnp.zeros_like(total)

    def tile(k, carry):
        user = blocks[0, 0, visit, k, 0]
        item = blocks[0, 0, visit, k, 1]
        user_rows = users[rows_at(user, side), :]
        item_rows = panel[rows_at(item, side), :]
        predicted = lax.dot_general(
            user_rows, item_rows, (((1,), (1,)), ((), ())), preferred_element_type=jnp.float32
        )
        seen = observed(words[0, 0, visit, k])
        error = jnp.where(seen, rates[0, 0, visit, k].astype(jnp.float32) - predicted, 0.0)
        error = error.astype(jnp.bfloat16)
        errors[k] = error
        total[rows_at(item, side), :] += lax.dot_general(
            error, user_rows, (((0,), (0,)), ((), ())), preferred_element_type=jnp.float32
        )
        return carry

    lax.fori_loop(0, counts[0, 0, visit], tile, 0)
    for k in range(chips):
        owner = lax.rem(chip + k, chips)
        at = pl.ds(k * rows, rows)
        near[at, :] = total[rows_at(CORES * owner + core, rows), :]
        far[at, :] = total[rows_at(CORES * owner + 1 - core, rows), :].astype(far.dtype)


def users_kernel(visit, chips, place, blocks, counts, users, errors, *rest):
    pieces, (out, panel, total) = rest[: CORES * chips], rest[CORES * chips :]
    side = errors.shape[-1]
    rows = pieces[0].shape[0]
    core, chip = place[0], place[1]
    for k in range(chips):
        origin = lax.rem(chip + chips - k, chips)
        panel[rows_at(CORES * origin + core, rows), :] = pieces[k][...]
        panel[rows_at(CORES * origin + 1 - core, rows), :] = pieces[chips + k][...]
    total[...] = jnp.zeros_like(total)

    def tile(k, carry):
        user = blocks[0, 0, visit, k, 0]
        item = blocks[0, 0, visit, k, 1]
        total[rows_at(user, side), :] += jnp.dot(
            errors[k], panel[rows_at(item, side), :], preferred_element_type=jnp.float32
        )
        return carry

    lax.fori_loop(0, counts[0, 0, visit], tile, 0)
    factor = users[...].astype(jnp.float32)
    out[...] = (factor + step_user * (total[...] - shrinkage * factor)).astype(out.dtype)


def add_kernel(near, far, *outs):
    rows = outs[0].shape[0]
    for k, out in enumerate(outs):
        at = pl.ds(k * rows, rows)
        out[...] = (near[at, :] + far[at, :].astype(jnp.float32)).astype(out.dtype)


def tiles(visit, chips, place, blocks, counts, users, rates, words, pieces):
    slots, side = rates.shape[3], rates.shape[-1]
    rows, width = pieces[0].shape
    whole = CORES * chips * rows
    half = chips * rows
    return pl.pallas_call(
        functools.partial(tiles_kernel, visit, chips),
        name="tiles",
        out_shape=(
            pltpu.VMEM((slots, side, side), jnp.bfloat16),
            pltpu.VMEM((half, width), jnp.float32),
            pltpu.VMEM((half, width), jnp.bfloat16),
        ),
        in_specs=[SM] * 3 + [VM] * (3 + len(pieces)),
        out_specs=(VM,) * 3,
        scratch_shapes=[
            pltpu.VMEM((whole, width), jnp.bfloat16),
            pltpu.VMEM((whole, width), jnp.float32),
        ],
        cost_estimate=pl.CostEstimate(flops=4 * slots * side * side * width, bytes_accessed=8 << 20, transcendentals=0),
    )(place, blocks, counts, users, rates, words, *pieces)


def new_users(visit, last, chips, place, blocks, counts, users, errors, pieces):
    slots, side = errors.shape[0], errors.shape[-1]
    rows, width = pieces[0].shape
    whole = CORES * chips * rows
    return pl.pallas_call(
        functools.partial(users_kernel, visit, chips),
        name="users",
        out_shape=jax.ShapeDtypeStruct(users.shape, users.dtype)
        if last
        else pltpu.VMEM(users.shape, users.dtype),
        in_specs=[SM] * 3 + [VM] * (2 + len(pieces)),
        out_specs=VM,
        scratch_shapes=[
            pltpu.VMEM((whole, width), jnp.bfloat16),
            pltpu.VMEM(users.shape, jnp.float32),
        ],
        cost_estimate=pl.CostEstimate(flops=2 * slots * side * side * width, bytes_accessed=8 << 20, transcendentals=0),
    )(place, blocks, counts, users, errors, *pieces)


def added(chips, near, far):
    rows, width = near.shape[0] // chips, near.shape[1]
    return pl.pallas_call(
        add_kernel,
        name="add",
        out_shape=(pltpu.VMEM((rows, width), jnp.bfloat16),) * chips,
        in_specs=[VM] * 2,
        out_specs=(VM,) * chips,
        cost_estimate=pl.CostEstimate(flops=near.size, bytes_accessed=2 << 20, transcendentals=0),
    )(near, far)


def moved(x, by_strata, by_chip, flip, *, strata, peers):
    pairs = []
    for s in range(strata):
        for h in range(peers):
            chip, core = divmod(h, CORES)
            chip = (chip + by_chip) % (peers // CORES)
            core = 1 - core if flip else core
            pairs.append((s * peers + h, (s + by_strata) % strata * peers + chip * CORES + core))
    return lax.ppermute(x, ("strata", "shard"), pairs)


def shards(user_factors, item_factors, tile_blocks, tile_counts, ratings, mask_words):
    strata, peers = lax.axis_size("strata"), lax.axis_size("shard")
    chips = peers // CORES
    move = functools.partial(moved, strata=strata, peers=peers)
    visits = tile_counts.shape[-1]
    me = lax.axis_index("shard")
    place = jnp.stack([me % CORES, me // CORES]).astype(jnp.int32)
    users = user_factors
    panel = item_factors
    panel_low = panel.astype(jnp.bfloat16)
    for visit in range(visits):
        last = visit + 1 == visits
        mine = [panel_low] + [move(panel_low, 0, k, False) for k in range(1, chips)]
        pieces = mine + [move(x, 0, 0, True) for x in mine]
        if not last:
            panel_next = move(panel_low, 1, 0, False)
        errors, near, far = tiles(
            visit, chips, place, tile_blocks, tile_counts, users, ratings, mask_words, pieces
        )
        sums = added(chips, near, move(far, 0, 0, True))
        users = new_users(visit, last, chips, place, tile_blocks, tile_counts, users, errors, pieces)
        if last:
            parts = sums[:1] + tuple(move(sums[k], 0, k, False) for k in range(1, chips))
            old = panel
        else:
            parts = tuple(move(sums[k], 1, k, False) for k in range(chips))
            old = panel_next.astype(jnp.float32)
        summed = functools.reduce(jnp.add, [x.astype(jnp.float32) for x in parts])
        panel = old + step_item * (summed - shrinkage * old)
        panel_low = panel.astype(jnp.bfloat16)
    return (users, panel)


def solution(mesh):
    placed = (
        P(("strata", "shard"), None),
        P(("strata", "shard"), None),
        P("strata", "shard", None, None, None),
        P("strata", "shard", None),
        P("strata", "shard", None, None, None, None),
        P("strata", "shard", None, None, None, None),
    )
    return jax.shard_map(
        shards,
        mesh=mesh,
        in_specs=placed,
        out_specs=(P(("strata", "shard"), None), P(("strata", "shard"), None)),
        check_vma=False,
    )
```

time: 145 us -> 92.3 us (0.64)
  waiting for transfers between devices: 53.5 us -> 31.3 us
  blocking collectives: 22 us -> 0 us
  matrix products: 21.7 us -> 0 us
  Pallas kernels: 0 us -> 20.2 us
  starting transfers between devices: 3.17 us -> 23.1 us
  between operations: 14.1 us -> 0.84 us
  other arithmetic: 11.5 us -> 2.61 us
  local copies, waits for them, and re-layouts: 18.3 us -> 13.8 us
    reduce_scatter x3 -> x0, waiting for transfers between devices: 46.3 us -> none  [shards(): lax.psum_scatter(grad_item.astype(jnp.bfloat16), 'shard', scatter_dimensi...]
    ppermute x2 -> x19, waiting for transfers between devices: 7.15 us -> 31.3 us  [moved(): return lax.ppermute(x, ('strata', 'shard'), pairs)]
    all_gather x3 -> x0, blocking collectives: 22 us -> none  [shards(): lax.all_gather(panel.astype(jnp.bfloat16), 'shard', axis=0, tiled=True)]
    dot_general x15 -> x0, matrix products: 21.7 us -> none  [the longest x3 6.7 us: device_terms(): jnp.einsum('kb,kir->bir', item_hot, item_terms, precision=lax.Precision.H...]
    pallas_call x0 -> x9, Pallas kernels: none -> 20.2 us  [the longest x3 8.49 us: tiles(): pl.pallas_call(functools.partial(tiles_kernel, visit, chips), name='tiles...]
    ppermute x2 -> x19, starting transfers between devices: 3.05 us -> 23.1 us  [moved(): return lax.ppermute(x, ('strata', 'shard'), pairs)]
    unnamed x16 -> x51, local copies, waits for them, and re-layouts: 0.13 us -> 13.8 us
    convert_element_type x9 -> x3, other arithmetic: 9.18 us -> 1.12 us  [shards(): panel_low = panel.astype(jnp.bfloat16)]
  transfers between devices with their start and end apart: 5 -> 19, of which waited for: 5 -> 12; matrix products, arithmetic and copies ran while one was open for 15% -> 1% of each run, Pallas kernels for 0% -> 12%
where the time goes in v1:
time: 92.3 us; the launch traced here: 91.8 us
  waiting for transfers between devices  31.3 us (34%)
  starting transfers between devices  23.1 us (25%)
  Pallas kernels  20.2 us (22%)
  local copies, waits for them, and re-layouts  13.8 us (15%)
  other arithmetic  2.61 us (3%)
    ppermute x19, waiting for transfers between devices, moved(): return lax.ppermute(x, ('strata', 'shard'), pairs)  31.3 us
    ppermute x19, starting transfers between devices, moved(): return lax.ppermute(x, ('strata', 'shard'), pairs)  23.1 us
    unnamed x51, local copies, waits for them, and re-layouts  13.8 us
    pallas_call x3, Pallas kernels, tiles(): pl.pallas_call(functools.partial(tiles_kernel, visit, chips), name='tiles...  8.49 us
    pallas_call x3, Pallas kernels, new_users(): pl.pallas_call(functools.partial(users_kernel, visit, chips), name='users...  8.29 us
    pallas_call x3, Pallas kernels, added(): pl.pallas_call(add_kernel, name='add', out_shape=(pltpu.VMEM((rows, width...  3.46 us
  transfers between devices with their start and end apart: 19, of which 12 were waited for; matrix products, arithmetic and copies ran while one was open for 1% of the time, Pallas kernels for 12%

profile of v1, /device:TPU:0, one launch (start us, length us, event | category | flops | bytes accessed | tf_op | source)
XLA Modules:
  0.0 91.8 jit_solution(2651978092729798027)
XLA Ops:
  0.6 1.0 %convert_element_type.33.rest_0_ = bf16[128,512]{1,0:T(8,128)(2,1)S(1)} convert(f32[128,512]{1,0:T(8,128)} %param.7) | non-fusion elementwise | flops 65536 | bytes 393216 | tf_op jit(solution)/shard_map/convert_element_type | solution.py:176
  1.6 3.0 %collective-permute-start = (bf16[128,512]{1,0:T(8,128)(2,1)S(1)}, bf16[128,512]{1,0:T(8,128)(2,1)S(1)}, u32[]{:S(2)}, u32[]{:S(2)}) collective-permute-start(bf16[128,512]{1,0:T(8,128)(2,1)S(1)} %convert_element_type.33.rest_0_), channel_id=1, source_target_pairs={{0,2},{1,3},{2,0},{3,1},{4,6},{5,7},{6,4},{7,5},{8,10},{9,11},{10,... | collective-permute-start | bytes 393224 | tf_op jit(solution)/shard_map/ppermute | solution.py:164
  4.6 3.5 %collective-permute-done.rest_1_ = bf16[128,512]{1,0:T(8,128)(2,1)S(1)} collective-permute-done((bf16[128,512]{1,0:T(8,128)(2,1)S(1)}, bf16[128,512]{1,0:T(8,128)(2,1)S(1)}, u32[]{:S(2)}, u32[]{:S(2)}) %collective-permute-start) | collective-permute-done | bytes 131104 | tf_op jit(solution)/shard_map/ppermute | solution.py:164
  8.1 0.7 copy-done.24
  8.8 0.7 copy.13.blocks
  10.8 0.6 copy-done.14
  11.5 4.0 %tiles.3 = (bf16[8,128,128]{2,1,0:T(8,128)(2,1)S(1)}, f32[256,512]{1,0:T(8,128)S(1)}, bf16[256,512]{1,0:T(8,128)(2,1)S(1)}) custom-call(s32[2]{0:T(128)} %pad_add_fusion.place, s32[1,1,3,8,2]{4,3,2,1,0:T(8,128)} %copy.13.blocks, s32[1,1,3]{2,1,0:T(1,128)} %counts.11, bf16[1024,512]{1,0:T(8,128)(2,1)} %users.7, bf16[1,1,3,8,128,128]{5,4,3,2,1,0:T(8,128)(2,1)} %rates.5, ...), custom_call_target="tpu_custom_call" | custom-call | flops 268435456 | bytes 8388608 | tf_op jit(solution)/shard_map/tiles/pallas_call | solution.py:106
  15.5 0.8 copy-done.2
  16.3 0.7 copy-done.5
  17.0 3.0 %collective-permute-start.3 = (bf16[128,512]{1,0:T(8,128)(2,1)}, bf16[128,512]{1,0:T(8,128)(2,1)S(1)}, u32[]{:S(2)}, u32[]{:S(2)}) collective-permute-start(bf16[128,512]{1,0:T(8,128)(2,1)} %copy-done.8), channel_id=1, source_target_pairs={{0,4},{1,5},{2,6},{3,7},{4,8},{5,9},{6,10},{7,11},{8,12},{9,13},{1... | collective-permute-start | bytes 393224 | tf_op jit(solution)/shard_map/ppermute | solution.py:164
  20.0 0.7 copy-done.21
  20.7 1.2 %add.51 = (bf16[128,512]{1,0:T(8,128)(2,1)S(1)}, bf16[128,512]{1,0:T(8,128)(2,1)S(1)}) custom-call(f32[256,512]{1,0:T(8,128)} %copy-done.2, bf16[256,512]{1,0:T(8,128)(2,1)} %copy-done.21), custom_call_target="tpu_custom_call" | custom-call | flops 131072 | bytes 2097152 | tf_op jit(solution)/shard_map/add/pallas_call | solution.py:146
  21.9 2.1 %collective-permute-start.5 = (bf16[128,512]{1,0:T(8,128)(2,1)S(1)}, bf16[128,512]{1,0:T(8,128)(2,1)S(1)}, u32[]{:S(2)}, u32[]{:S(2)}) collective-permute-start(bf16[128,512]{1,0:T(8,128)(2,1)S(1)} %get-tuple-element.20), channel_id=1, source_target_pairs={{0,4},{1,5},{2,6},{3,7},{4,8},{5,9},{6,10},{7,11},{8,12},{9,13},{1... | collective-permute-start | bytes 393224 | tf_op jit(solution)/shard_map/ppermute | solution.py:164
  24.0 2.4 %collective-permute-start.6 = (bf16[128,512]{1,0:T(8,128)(2,1)S(1)}, bf16[128,512]{1,0:T(8,128)(2,1)S(1)}, u32[]{:S(2)}, u32[]{:S(2)}) collective-permute-start(bf16[128,512]{1,0:T(8,128)(2,1)S(1)} %get-tuple-element.21), channel_id=1, source_target_pairs={{0,6},{1,7},{2,4},{3,5},{4,10},{5,11},{6,8},{7,9},{8,14},{9,15},{1... | collective-permute-start | bytes 393224 | tf_op jit(solution)/shard_map/ppermute | solution.py:164
  26.5 4.4 %collective-permute-done.5 = bf16[128,512]{1,0:T(8,128)(2,1)S(1)} collective-permute-done((bf16[128,512]{1,0:T(8,128)(2,1)S(1)}, bf16[128,512]{1,0:T(8,128)(2,1)S(1)}, u32[]{:S(2)}, u32[]{:S(2)}) %collective-permute-start.5) | collective-permute-done | bytes 131104 | tf_op jit(solution)/shard_map/ppermute | solution.py:164
  30.9 2.6 %collective-permute-done.6 = bf16[128,512]{1,0:T(8,128)(2,1)S(1)} collective-permute-done((bf16[128,512]{1,0:T(8,128)(2,1)S(1)}, bf16[128,512]{1,0:T(8,128)(2,1)S(1)}, u32[]{:S(2)}, u32[]{:S(2)}) %collective-permute-start.6) | collective-permute-done | bytes 131104 | tf_op jit(solution)/shard_map/ppermute | solution.py:164
  33.7 1.0 %collective-permute-start.7 = (bf16[128,512]{1,0:T(8,128)(2,1)S(1)}, bf16[128,512]{1,0:T(8,128)(2,1)S(1)}, u32[]{:S(2)}, u32[]{:S(2)}) collective-permute-start(bf16[128,512]{1,0:T(8,128)(2,1)S(1)} %fusion.2.rest_0_), channel_id=1, source_target_pairs={{0,2},{1,3},{2,0},{3,1},{4,6},{5,7},{6,4},{7,5},{8,10},{9,11},{10,... | collective-permute-start | bytes 393224 | tf_op jit(solution)/shard_map/ppermute | solution.py:164
  34.7 4.0 %collective-permute-done.7.rest_1_ = bf16[128,512]{1,0:T(8,128)(2,1)S(1)} collective-permute-done((bf16[128,512]{1,0:T(8,128)(2,1)S(1)}, bf16[128,512]{1,0:T(8,128)(2,1)S(1)}, u32[]{:S(2)}, u32[]{:S(2)}) %collective-permute-start.7) | collective-permute-done | bytes 131104 | tf_op jit(solution)/shard_map/ppermute | solution.py:164
  38.7 2.9 %users.6 = bf16[1024,512]{1,0:T(8,128)(2,1)S(1)} custom-call(s32[2]{0:T(128)} %pad_add_fusion.place, s32[1,1,3,8,2]{4,3,2,1,0:T(8,128)} %copy.13.blocks, s32[1,1,3]{2,1,0:T(1,128)} %counts.11, bf16[1024,512]{1,0:T(8,128)(2,1)} %users.7, bf16[8,128,128]{2,1,0:T(8,128)(2,1)} %copy-done.5, bf16[128,512]{1,0:T(8,128)(2,1)} %copy-done.8, ...), custom_call_target="tpu_custom_call" | custom-call | flops 134217728 | bytes 8388608 | tf_op jit(solution)/shard_map/users/pallas_call | solution.py:128
  41.7 1.0 %copy-done = bf16[1024,512]{1,0:T(8,128)(2,1)} copy-done((bf16[1024,512]{1,0:T(8,128)(2,1)}, bf16[1024,512]{1,0:T(8,128)(2,1)S(1)}, u32[]{:S(2)}) %copy-start) | copy-done | bytes 1048600
  43.9 2.2 %tiles.4 = (bf16[8,128,128]{2,1,0:T(8,128)(2,1)S(1)}, f32[256,512]{1,0:T(8,128)S(1)}, bf16[256,512]{1,0:T(8,128)(2,1)S(1)}) custom-call(s32[2]{0:T(128)} %pad_add_fusion.place, s32[1,1,3,8,2]{4,3,2,1,0:T(8,128)} %copy.13.blocks, s32[1,1,3]{2,1,0:T(1,128)} %counts.11, bf16[1024,512]{1,0:T(8,128)(2,1)} %copy-done, bf16[1,1,3,8,128,128]{5,4,3,2,1,0:T(8,128)(2,1)} %rates.5, ...), custom_call_target="tpu_custom_call" | custom-call | flops 268435456 | bytes 8388608 | tf_op jit(solution)/shard_map/tiles/pallas_call | solution.py:106
  46.2 0.8 copy-done.3
  47.0 0.7 copy-done.6
  47.7 2.9 %collective-permute-start.11 = (bf16[256,512]{1,0:T(8,128)(2,1)S(1)}, bf16[256,512]{1,0:T(8,128)(2,1)S(1)}, u32[]{:S(2)}, u32[]{:S(2)}) collective-permute-start(bf16[256,512]{1,0:T(8,128)(2,1)S(1)} %get-tuple-element.24), channel_id=1, source_target_pairs={{0,1},{1,0},{2,3},{3,2},{4,5},{5,4},{6,7},{7,6},{8,9},{9,8},{10,11... | collective-permute-start | bytes 786440 | tf_op jit(solution)/shard_map/ppermute | solution.py:164
  50.6 1.2 %collective-permute-done.11.far = bf16[256,512]{1,0:T(8,128)(2,1)S(1)} collective-permute-done((bf16[256,512]{1,0:T(8,128)(2,1)S(1)}, bf16[256,512]{1,0:T(8,128)(2,1)S(1)}, u32[]{:S(2)}, u32[]{:S(2)}) %collective-permute-start.11) | collective-permute-done | bytes 262176 | tf_op jit(solution)/shard_map/ppermute | solution.py:164
  51.8 0.7 copy-done.22
  52.5 1.2 %add.52 = (bf16[128,512]{1,0:T(8,128)(2,1)S(1)}, bf16[128,512]{1,0:T(8,128)(2,1)S(1)}) custom-call(f32[256,512]{1,0:T(8,128)} %copy-done.3, bf16[256,512]{1,0:T(8,128)(2,1)} %copy-done.22), custom_call_target="tpu_custom_call" | custom-call | flops 131072 | bytes 2097152 | tf_op jit(solution)/shard_map/add/pallas_call | solution.py:146
  53.6 0.6 collective-permute-start.12
  54.3 2.2 %collective-permute-start.13 = (bf16[128,512]{1,0:T(8,128)(2,1)S(1)}, bf16[128,512]{1,0:T(8,128)(2,1)S(1)}, u32[]{:S(2)}, u32[]{:S(2)}) collective-permute-start(bf16[128,512]{1,0:T(8,128)(2,1)S(1)} %get-tuple-element.26), channel_id=1, source_target_pairs={{0,6},{1,7},{2,4},{3,5},{4,10},{5,11},{6,8},{7,9},{8,14},{9,15},{1... | collective-permute-start | bytes 393224 | tf_op jit(solution)/shard_map/ppermute | solution.py:164
  56.5 2.2 %collective-permute-done.10 = bf16[128,512]{1,0:T(8,128)(2,1)S(1)} collective-permute-done((bf16[128,512]{1,0:T(8,128)(2,1)S(1)}, bf16[128,512]{1,0:T(8,128)(2,1)S(1)}, u32[]{:S(2)}, u32[]{:S(2)}) %collective-permute-start.10) | collective-permute-done | bytes 131104 | tf_op jit(solution)/shard_map/ppermute | solution.py:164
  58.7 4.0 %collective-permute-done.12 = bf16[128,512]{1,0:T(8,128)(2,1)S(1)} collective-permute-done((bf16[128,512]{1,0:T(8,128)(2,1)S(1)}, bf16[128,512]{1,0:T(8,128)(2,1)S(1)}, u32[]{:S(2)}, u32[]{:S(2)}) %collective-permute-start.12) | collective-permute-done | bytes 131104 | tf_op jit(solution)/shard_map/ppermute | solution.py:164
  62.7 3.1 %collective-permute-done.13 = bf16[128,512]{1,0:T(8,128)(2,1)S(1)} collective-permute-done((bf16[128,512]{1,0:T(8,128)(2,1)S(1)}, bf16[128,512]{1,0:T(8,128)(2,1)S(1)}, u32[]{:S(2)}, u32[]{:S(2)}) %collective-permute-start.13) | collective-permute-done | bytes 131104 | tf_op jit(solution)/shard_map/ppermute | solution.py:164
  65.9 0.7 collective-permute-start.14
  66.6 4.3 %collective-permute-done.14.rest_1_ = bf16[128,512]{1,0:T(8,128)(2,1)S(1)} collective-permute-done((bf16[128,512]{1,0:T(8,128)(2,1)S(1)}, bf16[128,512]{1,0:T(8,128)(2,1)S(1)}, u32[]{:S(2)}, u32[]{:S(2)}) %collective-permute-start.14) | collective-permute-done | bytes 131104 | tf_op jit(solution)/shard_map/ppermute | solution.py:164
  70.9 2.2 %users.8 = bf16[1024,512]{1,0:T(8,128)(2,1)S(1)} custom-call(s32[2]{0:T(128)} %pad_add_fusion.place, s32[1,1,3,8,2]{4,3,2,1,0:T(8,128)} %copy.13.blocks, s32[1,1,3]{2,1,0:T(1,128)} %counts.11, bf16[1024,512]{1,0:T(8,128)(2,1)} %copy-done, bf16[8,128,128]{2,1,0:T(8,128)(2,1)} %copy-done.6, bf16[128,512]{1,0:T(8,128)(2,1)} %copy-done.9, ...), custom_call_target="tpu_custom_call" | custom-call | flops 134217728 | bytes 8388608 | tf_op jit(solution)/shard_map/users/pallas_call | solution.py:128
  73.2 1.0 %copy-done.1 = bf16[1024,512]{1,0:T(8,128)(2,1)} copy-done((bf16[1024,512]{1,0:T(8,128)(2,1)}, bf16[1024,512]{1,0:T(8,128)(2,1)S(1)}, u32[]{:S(2)}) %copy-start.1) | copy-done | bytes 1048600
  74.8 0.7 copy-done.20
  75.5 2.2 %tiles.5 = (bf16[8,128,128]{2,1,0:T(8,128)(2,1)S(1)}, f32[256,512]{1,0:T(8,128)S(1)}, bf16[256,512]{1,0:T(8,128)(2,1)S(1)}) custom-call(s32[2]{0:T(128)} %pad_add_fusion.place, s32[1,1,3,8,2]{4,3,2,1,0:T(8,128)} %copy.13.blocks, s32[1,1,3]{2,1,0:T(1,128)} %counts.11, bf16[1024,512]{1,0:T(8,128)(2,1)} %copy-done.1, bf16[1,1,3,8,128,128]{5,4,3,2,1,0:T(8,128)(2,1)} %rates.5, ...), custom_call_target="tpu_custom_call" | custom-call | flops 268435456 | bytes 8388608 | tf_op jit(solution)/shard_map/tiles/pallas_call | solution.py:106
  77.7 0.8 copy-done.4
  78.5 0.7 copy-done.7
  79.2 1.5 %collective-permute-start.17 = (bf16[256,512]{1,0:T(8,128)(2,1)S(1)}, bf16[256,512]{1,0:T(8,128)(2,1)S(1)}, u32[]{:S(2)}, u32[]{:S(2)}) collective-permute-start(bf16[256,512]{1,0:T(8,128)(2,1)S(1)} %get-tuple-element.29), channel_id=1, source_target_pairs={{0,1},{1,0},{2,3},{3,2},{4,5},{5,4},{6,7},{7,6},{8,9},{9,8},{10,11... | collective-permute-start | bytes 786440 | tf_op jit(solution)/shard_map/ppermute | solution.py:164
  80.7 1.2 %collective-permute-done.17.far = bf16[256,512]{1,0:T(8,128)(2,1)S(1)} collective-permute-done((bf16[256,512]{1,0:T(8,128)(2,1)S(1)}, bf16[256,512]{1,0:T(8,128)(2,1)S(1)}, u32[]{:S(2)}, u32[]{:S(2)}) %collective-permute-start.17) | collective-permute-done | bytes 262176 | tf_op jit(solution)/shard_map/ppermute | solution.py:164
  81.9 0.7 copy-done.23
  82.6 1.2 %add.53 = (bf16[128,512]{1,0:T(8,128)(2,1)S(1)}, bf16[128,512]{1,0:T(8,128)(2,1)S(1)}) custom-call(f32[256,512]{1,0:T(8,128)} %copy-done.4, bf16[256,512]{1,0:T(8,128)(2,1)} %copy-done.23), custom_call_target="tpu_custom_call" | custom-call | flops 131072 | bytes 2097152 | tf_op jit(solution)/shard_map/add/pallas_call | solution.py:146
  83.8 3.4 %collective-permute-start.18 = (bf16[128,512]{1,0:T(8,128)(2,1)S(1)}, bf16[128,512]{1,0:T(8,128)(2,1)S(1)}, u32[]{:S(2)}, u32[]{:S(2)}) collective-permute-start(bf16[128,512]{1,0:T(8,128)(2,1)S(1)} %get-tuple-element.31), channel_id=1, source_target_pairs={{0,2},{1,3},{2,0},{3,1},{4,6},{5,7},{6,4},{7,5},{8,10},{9,11},{10,... | collective-permute-start | bytes 393224 | tf_op jit(solution)/shard_map/ppermute | solution.py:164
  87.2 3.1 %users.9 = bf16[1024,512]{1,0:T(8,128)(2,1)} custom-call(s32[2]{0:T(128)} %pad_add_fusion.place, s32[1,1,3,8,2]{4,3,2,1,0:T(8,128)} %copy.13.blocks, s32[1,1,3]{2,1,0:T(1,128)} %counts.11, bf16[1024,512]{1,0:T(8,128)(2,1)} %copy-done.1, bf16[8,128,128]{2,1,0:T(8,128)(2,1)} %copy-done.7, bf16[128,512]{1,0:T(8,128)(2,1)} %copy-done.11, ...), custom_call_target="tpu_custom_call" | custom-call | flops 134217728 | bytes 8388608 | tf_op jit(solution)/shard_map/users/pallas_call | solution.py:128
  90.3 0.7 collective-permute-done.18
  91.0 0.8 multiply_add_fusion
  (55 shorter events, 3.6 us)
Async XLA Ops:
  1.6 8.6 %copy-start.8 = (bf16[128,512]{1,0:T(8,128)(2,1)}, bf16[128,512]{1,0:T(8,128)(2,1)S(1)}, u32[]{:S(2)}) copy-start(bf16[128,512]{1,0:T(8,128)(2,1)S(1)} %convert_element_type.33.rest_0_) | copy-start | bytes 393220
  1.6 6.5 %collective-permute-start = (bf16[128,512]{1,0:T(8,128)(2,1)S(1)}, bf16[128,512]{1,0:T(8,128)(2,1)S(1)}, u32[]{:S(2)}, u32[]{:S(2)}) collective-permute-start(bf16[128,512]{1,0:T(8,128)(2,1)S(1)} %convert_element_type.33.rest_0_), channel_id=1, source_target_pairs={{0,2},{1,3},{2,0},{3,1},{4,6},{5,7},{6,4},{7,5},{8,10},{9,11},{10,... | collective-permute-start | bytes 393224 | tf_op jit(solution)/shard_map/ppermute | solution.py:164
  4.6 5.5 %collective-permute-start.1 = (bf16[128,512]{1,0:T(8,128)(2,1)S(1)}, bf16[128,512]{1,0:T(8,128)(2,1)S(1)}, u32[]{:S(2)}, u32[]{:S(2)}) collective-permute-start(bf16[128,512]{1,0:T(8,128)(2,1)S(1)} %convert_element_type.33.rest_0_), channel_id=1, source_target_pairs={{0,1},{1,0},{2,3},{3,2},{4,5},{5,4},{6,7},{7,6},{8,9},{9,8},{10,11... | collective-permute-start | bytes 393224 | tf_op jit(solution)/shard_map/ppermute | solution.py:164
  8.1 2.0 %copy-start.12 = (bf16[128,512]{1,0:T(8,128)(2,1)}, bf16[128,512]{1,0:T(8,128)(2,1)S(1)}, u32[]{:S(2)}) copy-start(bf16[128,512]{1,0:T(8,128)(2,1)S(1)} %collective-permute-done.rest_1_) | copy-start | bytes 393220
  8.1 2.0 %collective-permute-start.2 = (bf16[128,512]{1,0:T(8,128)(2,1)S(1)}, bf16[128,512]{1,0:T(8,128)(2,1)S(1)}, u32[]{:S(2)}, u32[]{:S(2)}) collective-permute-start(bf16[128,512]{1,0:T(8,128)(2,1)S(1)} %collective-permute-done.rest_1_), channel_id=1, source_target_pairs={{0,1},{1,0},{2,3},{3,2},{4,5},{5,4},{6,7},{7,6},{8,9},{9,8},{10,11... | collective-permute-start | bytes 393224 | tf_op jit(solution)/shard_map/ppermute | solution.py:164
  8.1 0.7 copy-start.24
  10.2 0.7 copy-start.13
  10.8 0.6 copy-start.14
  15.5 0.8 copy-start.2
  16.3 0.7 copy-start.5
  17.0 3.0 %collective-permute-start.4 = (bf16[256,512]{1,0:T(8,128)(2,1)S(1)}, bf16[256,512]{1,0:T(8,128)(2,1)S(1)}, u32[]{:S(2)}, u32[]{:S(2)}) collective-permute-start(bf16[256,512]{1,0:T(8,128)(2,1)S(1)} %get-tuple-element.19), channel_id=1, source_target_pairs={{0,1},{1,0},{2,3},{3,2},{4,5},{5,4},{6,7},{7,6},{8,9},{9,8},{10,11... | collective-permute-start | bytes 786440 | tf_op jit(solution)/shard_map/ppermute | solution.py:164
  17.0 9.5 %collective-permute-start.3 = (bf16[128,512]{1,0:T(8,128)(2,1)}, bf16[128,512]{1,0:T(8,128)(2,1)S(1)}, u32[]{:S(2)}, u32[]{:S(2)}) collective-permute-start(bf16[128,512]{1,0:T(8,128)(2,1)} %copy-done.8), channel_id=1, source_target_pairs={{0,4},{1,5},{2,6},{3,7},{4,8},{5,9},{6,10},{7,11},{8,12},{9,13},{1... | collective-permute-start | bytes 393224 | tf_op jit(solution)/shard_map/ppermute | solution.py:164
  20.0 0.7 copy-start.21
  21.9 9.1 %collective-permute-start.5 = (bf16[128,512]{1,0:T(8,128)(2,1)S(1)}, bf16[128,512]{1,0:T(8,128)(2,1)S(1)}, u32[]{:S(2)}, u32[]{:S(2)}) collective-permute-start(bf16[128,512]{1,0:T(8,128)(2,1)S(1)} %get-tuple-element.20), channel_id=1, source_target_pairs={{0,4},{1,5},{2,6},{3,7},{4,8},{5,9},{6,10},{7,11},{8,12},{9,13},{1... | collective-permute-start | bytes 393224 | tf_op jit(solution)/shard_map/ppermute | solution.py:164
  24.0 9.6 %collective-permute-start.6 = (bf16[128,512]{1,0:T(8,128)(2,1)S(1)}, bf16[128,512]{1,0:T(8,128)(2,1)S(1)}, u32[]{:S(2)}, u32[]{:S(2)}) collective-permute-start(bf16[128,512]{1,0:T(8,128)(2,1)S(1)} %get-tuple-element.21), channel_id=1, source_target_pairs={{0,6},{1,7},{2,4},{3,5},{4,10},{5,11},{6,8},{7,9},{8,14},{9,15},{1... | collective-permute-start | bytes 393224 | tf_op jit(solution)/shard_map/ppermute | solution.py:164
  33.6 8.0 %copy-start.9 = (bf16[128,512]{1,0:T(8,128)(2,1)}, bf16[128,512]{1,0:T(8,128)(2,1)S(1)}, u32[]{:S(2)}) copy-start(bf16[128,512]{1,0:T(8,128)(2,1)S(1)} %fusion.2.rest_0_) | copy-start | bytes 393220
  33.7 5.0 %collective-permute-start.7 = (bf16[128,512]{1,0:T(8,128)(2,1)S(1)}, bf16[128,512]{1,0:T(8,128)(2,1)S(1)}, u32[]{:S(2)}, u32[]{:S(2)}) collective-permute-start(bf16[128,512]{1,0:T(8,128)(2,1)S(1)} %fusion.2.rest_0_), channel_id=1, source_target_pairs={{0,2},{1,3},{2,0},{3,1},{4,6},{5,7},{6,4},{7,5},{8,10},{9,11},{10,... | collective-permute-start | bytes 393224 | tf_op jit(solution)/shard_map/ppermute | solution.py:164
  34.7 8.0 %collective-permute-start.8 = (bf16[128,512]{1,0:T(8,128)(2,1)S(1)}, bf16[128,512]{1,0:T(8,128)(2,1)S(1)}, u32[]{:S(2)}, u32[]{:S(2)}) collective-permute-start(bf16[128,512]{1,0:T(8,128)(2,1)S(1)} %fusion.2.rest_0_), channel_id=1, source_target_pairs={{0,1},{1,0},{2,3},{3,2},{4,5},{5,4},{6,7},{7,6},{8,9},{9,8},{10,11... | collective-permute-start | bytes 393224 | tf_op jit(solution)/shard_map/ppermute | solution.py:164
  38.7 3.0 %copy-start.15 = (bf16[128,512]{1,0:T(8,128)(2,1)}, bf16[128,512]{1,0:T(8,128)(2,1)S(1)}, u32[]{:S(2)}) copy-start(bf16[128,512]{1,0:T(8,128)(2,1)S(1)} %collective-permute-done.7.rest_1_) | copy-start | bytes 393220
  38.7 3.9 %collective-permute-start.9 = (bf16[128,512]{1,0:T(8,128)(2,1)S(1)}, bf16[128,512]{1,0:T(8,128)(2,1)S(1)}, u32[]{:S(2)}, u32[]{:S(2)}) collective-permute-start(bf16[128,512]{1,0:T(8,128)(2,1)S(1)} %collective-permute-done.7.rest_1_), channel_id=1, source_target_pairs={{0,1},{1,0},{2,3},{3,2},{4,5},{5,4},{6,7},{7,6},{8,9},{9,8},{10,11... | collective-permute-start | bytes 393224 | tf_op jit(solution)/shard_map/ppermute | solution.py:164
  41.6 1.0 %copy-start = (bf16[1024,512]{1,0:T(8,128)(2,1)}, bf16[1024,512]{1,0:T(8,128)(2,1)S(1)}, u32[]{:S(2)}) copy-start(bf16[1024,512]{1,0:T(8,128)(2,1)S(1)} %users.6) | copy-start | bytes 3145732
  42.6 0.6 copy-start.16
  42.6 8.0 %copy-start.10 = (bf16[128,512]{1,0:T(8,128)(2,1)S(1)}, bf16[128,512]{1,0:T(8,128)(2,1)}, u32[]{:S(2)}) copy-start(bf16[128,512]{1,0:T(8,128)(2,1)} %copy-done.9) | copy-start | bytes 393220
  43.3 0.6 copy-start.17
  46.2 0.8 copy-start.3
  47.0 0.7 copy-start.6
  47.7 4.1 %collective-permute-start.11 = (bf16[256,512]{1,0:T(8,128)(2,1)S(1)}, bf16[256,512]{1,0:T(8,128)(2,1)S(1)}, u32[]{:S(2)}, u32[]{:S(2)}) collective-permute-start(bf16[256,512]{1,0:T(8,128)(2,1)S(1)} %get-tuple-element.24), channel_id=1, source_target_pairs={{0,1},{1,0},{2,3},{3,2},{4,5},{5,4},{6,7},{7,6},{8,9},{9,8},{10,11... | collective-permute-start | bytes 786440 | tf_op jit(solution)/shard_map/ppermute | solution.py:164
  50.6 8.1 %collective-permute-start.10 = (bf16[128,512]{1,0:T(8,128)(2,1)S(1)}, bf16[128,512]{1,0:T(8,128)(2,1)S(1)}, u32[]{:S(2)}, u32[]{:S(2)}) collective-permute-start(bf16[128,512]{1,0:T(8,128)(2,1)S(1)} %copy-done.10), channel_id=1, source_target_pairs={{0,4},{1,5},{2,6},{3,7},{4,8},{5,9},{6,10},{7,11},{8,12},{9,13},{1... | collective-permute-start | bytes 393224 | tf_op jit(solution)/shard_map/ppermute | solution.py:164
  51.8 0.7 copy-start.22
  53.6 9.1 %collective-permute-start.12 = (bf16[128,512]{1,0:T(8,128)(2,1)S(1)}, bf16[128,512]{1,0:T(8,128)(2,1)S(1)}, u32[]{:S(2)}, u32[]{:S(2)}) collective-permute-start(bf16[128,512]{1,0:T(8,128)(2,1)S(1)} %get-tuple-element.25), channel_id=1, source_target_pairs={{0,4},{1,5},{2,6},{3,7},{4,8},{5,9},{6,10},{7,11},{8,12},{9,13},{1... | collective-permute-start | bytes 393224 | tf_op jit(solution)/shard_map/ppermute | solution.py:164
  54.3 11.5 %collective-permute-start.13 = (bf16[128,512]{1,0:T(8,128)(2,1)S(1)}, bf16[128,512]{1,0:T(8,128)(2,1)S(1)}, u32[]{:S(2)}, u32[]{:S(2)}) collective-permute-start(bf16[128,512]{1,0:T(8,128)(2,1)S(1)} %get-tuple-element.26), channel_id=1, source_target_pairs={{0,6},{1,7},{2,4},{3,5},{4,10},{5,11},{6,8},{7,9},{8,14},{9,15},{1... | collective-permute-start | bytes 393224 | tf_op jit(solution)/shard_map/ppermute | solution.py:164
  65.9 7.3 %copy-start.11 = (bf16[128,512]{1,0:T(8,128)(2,1)}, bf16[128,512]{1,0:T(8,128)(2,1)S(1)}, u32[]{:S(2)}) copy-start(bf16[128,512]{1,0:T(8,128)(2,1)S(1)} %fusion.5.rest_0_) | copy-start | bytes 393220
  65.9 5.0 %collective-permute-start.14 = (bf16[128,512]{1,0:T(8,128)(2,1)S(1)}, bf16[128,512]{1,0:T(8,128)(2,1)S(1)}, u32[]{:S(2)}, u32[]{:S(2)}) collective-permute-start(bf16[128,512]{1,0:T(8,128)(2,1)S(1)} %fusion.5.rest_0_), channel_id=1, source_target_pairs={{0,2},{1,3},{2,0},{3,1},{4,6},{5,7},{6,4},{7,5},{8,10},{9,11},{10,... | collective-permute-start | bytes 393224 | tf_op jit(solution)/shard_map/ppermute | solution.py:164
  66.6 7.6 %collective-permute-start.15 = (bf16[128,512]{1,0:T(8,128)(2,1)S(1)}, bf16[128,512]{1,0:T(8,128)(2,1)S(1)}, u32[]{:S(2)}, u32[]{:S(2)}) collective-permute-start(bf16[128,512]{1,0:T(8,128)(2,1)S(1)} %fusion.5.rest_0_), channel_id=1, source_target_pairs={{0,1},{1,0},{2,3},{3,2},{4,5},{5,4},{6,7},{7,6},{8,9},{9,8},{10,11... | collective-permute-start | bytes 393224 | tf_op jit(solution)/shard_map/ppermute | solution.py:164
  70.9 2.2 %copy-start.18 = (bf16[128,512]{1,0:T(8,128)(2,1)}, bf16[128,512]{1,0:T(8,128)(2,1)S(1)}, u32[]{:S(2)}) copy-start(bf16[128,512]{1,0:T(8,128)(2,1)S(1)} %collective-permute-done.14.rest_1_) | copy-start | bytes 393220
  70.9 3.3 %collective-permute-start.16 = (bf16[128,512]{1,0:T(8,128)(2,1)S(1)}, bf16[128,512]{1,0:T(8,128)(2,1)S(1)}, u32[]{:S(2)}, u32[]{:S(2)}) collective-permute-start(bf16[128,512]{1,0:T(8,128)(2,1)S(1)} %collective-permute-done.14.rest_1_), channel_id=1, source_target_pairs={{0,1},{1,0},{2,3},{3,2},{4,5},{5,4},{6,7},{7,6},{8,9},{9,8},{10,11... | collective-permute-start | bytes 393224 | tf_op jit(solution)/shard_map/ppermute | solution.py:164
  73.2 1.0 %copy-start.1 = (bf16[1024,512]{1,0:T(8,128)(2,1)}, bf16[1024,512]{1,0:T(8,128)(2,1)S(1)}, u32[]{:S(2)}) copy-start(bf16[1024,512]{1,0:T(8,128)(2,1)S(1)} %users.8) | copy-start | bytes 3145732
  74.2 0.7 copy-start.19
  74.8 0.7 copy-start.20
  77.7 0.8 copy-start.4
  78.5 0.7 copy-start.7
  79.2 2.7 %collective-permute-start.17 = (bf16[256,512]{1,0:T(8,128)(2,1)S(1)}, bf16[256,512]{1,0:T(8,128)(2,1)S(1)}, u32[]{:S(2)}, u32[]{:S(2)}) collective-permute-start(bf16[256,512]{1,0:T(8,128)(2,1)S(1)} %get-tuple-element.29), channel_id=1, source_target_pairs={{0,1},{1,0},{2,3},{3,2},{4,5},{5,4},{6,7},{7,6},{8,9},{9,8},{10,11... | collective-permute-start | bytes 786440 | tf_op jit(solution)/shard_map/ppermute | solution.py:164
  81.9 0.7 copy-start.23
  83.8 7.2 %collective-permute-start.18 = (bf16[128,512]{1,0:T(8,128)(2,1)S(1)}, bf16[128,512]{1,0:T(8,128)(2,1)S(1)}, u32[]{:S(2)}, u32[]{:S(2)}) collective-permute-start(bf16[128,512]{1,0:T(8,128)(2,1)S(1)} %get-tuple-element.31), channel_id=1, source_target_pairs={{0,2},{1,3},{2,0},{3,1},{4,6},{5,7},{6,4},{7,5},{8,10},{9,11},{10,... | collective-permute-start | bytes 393224 | tf_op jit(solution)/shard_map/ppermute | solution.py:164

commit v2 on v0

v2 whole, which is shorter than its diff:
```python
import functools

import jax
import jax.numpy as jnp
from jax import lax
from jax.experimental import pallas as pl
from jax.experimental.pallas import tpu as pltpu
from jax.sharding import PartitionSpec as P

step_user = 0.05
step_item = 0.004
shrinkage = 0.05

VM = pl.BlockSpec(memory_space=pltpu.VMEM)
SM = pl.BlockSpec(memory_space=pltpu.SMEM)
HB = pl.BlockSpec(memory_space=pltpu.HBM)
CORES = 2
CHUNK = 512


def place_of(close, chip, core, rows):
    return pl.multiple_of((chip if close else CORES * chip + core) * rows, rows)


def multiply(a, b, across, over):
    return lax.dot_general(a, b, (((across,), (over,)), ((), ())), preferred_element_type=jnp.float32)


def observed(words):
    count, lanes = words.shape
    shift = lax.broadcasted_iota(jnp.int32, (8, lanes), 0)
    parts = [
        jnp.bitwise_and(jnp.right_shift(jnp.broadcast_to(words[i : i + 1], (8, lanes)), shift), 1)
        for i in range(count)
    ]
    return jnp.concatenate(parts, 0) != 0


def round_kernel(panel, out):
    out[...] = panel[...].astype(out.dtype)


def stage_kernel(*refs):
    count, sem = (len(refs) - 2) // 2, refs[-1]
    copies = [
        pltpu.make_async_copy(refs[1 + i], refs[1 + count + i], sem.at[i]) for i in range(count)
    ]
    for copy in copies:
        copy.start()
    for copy in copies:
        copy.wait()


def prepare_kernel(visit, rows, close, place, blocks, counts, rates, words, keep, send):
    side = rates.shape[-1]
    core = place[0]
    nothing = jnp.full((side, side), jnp.nan, keep.dtype)
    for at in range(0, keep.shape[0], side):
        for lane in range(0, keep.shape[1], side):
            keep[at : at + side, lane : lane + side] = nothing
            send[at : at + side, lane : lane + side] = nothing

    def tile(k, carry):
        users = pl.ds(pl.multiple_of(blocks[0, 0, visit, 0, k] * side, side), side)
        first = blocks[0, 0, visit, 1, k] * side
        seen = observed(words[0, 0, visit, k])
        known = jnp.where(seen, rates[0, 0, visit, k].astype(jnp.float32), jnp.nan)
        if close:
            piece = lax.div(first, rows)
            at = lax.div(piece, CORES) * rows + lax.rem(first, rows)
            at = pl.ds(pl.multiple_of(at, side), side)
            known = known.astype(keep.dtype)

            @pl.when(lax.rem(piece, CORES) == core)
            def _():
                keep[users, at] = known

            @pl.when(lax.rem(piece, CORES) != core)
            def _():
                send[users, at] = known
        else:
            at = pl.ds(pl.multiple_of(first, side), side)
            piece = lax.div(first + lax.broadcasted_iota(jnp.int32, known.shape, 1), rows)
            mine = lax.rem(piece, CORES) == core
            keep[users, at] = jnp.where(mine, known, jnp.nan).astype(keep.dtype)
            send[users, at] = jnp.where(mine, jnp.nan, known).astype(keep.dtype)
        return carry

    lax.fori_loop(0, counts[0, 0, visit], tile, 0)


def tiles_kernel(first, last, chips, close, place, *refs):
    arrived, refs = refs[:chips], refs[chips:]
    (users, peers, rates, peer_rates), refs = refs[:4], refs[4:]
    (low, errors, peer_errors), refs = refs[:3], refs[3:]
    outs, (panel, total) = refs[:-2], refs[-2:]
    core, chip = place[0], place[1]
    rows = panel.shape[0] // chips
    if first:
        for k in range(chips):
            origin = lax.rem(chip + chips - k, chips)
            at = pl.multiple_of(origin * rows, rows)
            panel[pl.ds(at, rows), :] = arrived[k][...].astype(jnp.float32)
    else:
        now = arrived[0][...].astype(jnp.float32)
        for other in arrived[1:]:
            now = now + step_item * other[...].astype(jnp.float32)
        panel[...] = now
    if close:
        low[...] = panel[...].astype(low.dtype)
    else:
        low[...] = jnp.zeros_like(low)
        for j in range(chips):
            low[pl.ds(place_of(close, j, core, rows), rows), :] = panel[
                j * rows : (j + 1) * rows, :
            ].astype(low.dtype)
    for who, known, error in ((users, rates, errors), (peers, peer_rates, peer_errors)):
        for at in range(0, who.shape[0], CHUNK):
            cut = slice(at, at + CHUNK)
            predicted = multiply(who[cut, :], low[...], 1, 1)
            rating = known[cut, :].astype(jnp.float32)
            error[cut, :] = jnp.where(rating == rating, rating - predicted, 0.0).astype(error.dtype)
    total[...] = multiply(errors[...], users[...], 0, 0)
    total[...] += multiply(peer_errors[...], peers[...], 0, 0)
    if last:
        for k in range(chips):
            owner = lax.rem(chip + k, chips)
            term = total[pl.ds(place_of(close, owner, core, rows), rows), :]
            if k == 0:
                old = panel[pl.ds(pl.multiple_of(owner * rows, rows), rows), :]
                term = old + step_item * (term - shrinkage * old)
            outs[k][...] = term.astype(outs[k].dtype)
    else:
        for j in range(chips):
            cut = slice(j * rows, (j + 1) * rows)
            term = total[pl.ds(place_of(close, j, core, rows), rows), :]
            old = panel[cut, :]
            outs[0][cut, :] = (old + step_item * (term - shrinkage * old)).astype(outs[0].dtype)
            outs[1][cut, :] = term.astype(outs[1].dtype)


def users_kernel(count, *refs):
    (low, other_low), refs = refs[:2], refs[2:]
    for i in range(count):
        users, errors, other_errors = refs[3 * i : 3 * i + 3]
        out = refs[3 * count + i]
        for at in range(0, users.shape[0], CHUNK):
            cut = slice(at, at + CHUNK)
            grad = multiply(errors[cut, :], low[...], 1, 0)
            grad = grad + multiply(other_errors[cut, :], other_low[...], 1, 0)
            factor = users[cut, :].astype(jnp.float32)
            out[cut, :] = (factor + step_user * (grad - shrinkage * factor)).astype(out.dtype)


def final_kernel(count, *refs):
    refs = refs[:count] + refs[count + 1 :]
    total = refs[0][...]
    for other in refs[1:count]:
        total = total + step_item * other[...].astype(jnp.float32)
    refs[count][...] = total


def kernel_call(body, name, ins, outs, flops, scratch=(), extra=()):
    return pl.pallas_call(
        body,
        name=name,
        out_shape=tuple(outs),
        in_specs=[SM if x.dtype == jnp.int32 and x.ndim != 6 else VM for x in ins] + [HB] * len(extra),
        out_specs=(VM,) * len(outs),
        scratch_shapes=list(scratch),
        compiler_params=pltpu.CompilerParams(vmem_limit_bytes=16 << 20),
        cost_estimate=pl.CostEstimate(flops=flops, bytes_accessed=1024, transcendentals=0),
    )(*ins, *[pltpu.with_memory_space_constraint(x, pltpu.HBM) for x in extra])


def moved(x, by_strata, by_chip, flip, *, strata, peers):
    pairs = []
    for s in range(strata):
        for h in range(peers):
            chip, core = divmod(h, CORES)
            chip = (chip + by_chip) % (peers // CORES)
            core = 1 - core if flip else core
            pairs.append((s * peers + h, (s + by_strata) % strata * peers + chip * CORES + core))
    return lax.ppermute(x, ("strata", "shard"), pairs)


def shards(user_factors, item_factors, tile_blocks, tile_counts, ratings, mask_words):
    low_type, full_type = jnp.bfloat16, jnp.float32
    strata, peers = lax.axis_size("strata"), lax.axis_size("shard")
    chips = peers // CORES
    move = functools.partial(moved, strata=strata, peers=peers)
    swap = lambda x: move(x, 0, 0, True)
    visits = tile_counts.shape[-1]
    side = ratings.shape[-1]
    rows, width = item_factors.shape
    count = user_factors.shape[0]
    close = rows % side == 0
    held = (chips if close else peers) * rows
    part = chips * rows
    me = lax.axis_index("shard")
    place = jnp.stack([lax.rem(me, CORES), lax.div(me, CORES)]).astype(jnp.int32)
    blocks = jnp.swapaxes(tile_blocks, 3, 4)

    def prepared(visit):
        keep, send = kernel_call(
            functools.partial(prepare_kernel, visit, rows, close),
            "prepare",
            [place, blocks, tile_counts, rates, words],
            [pltpu.VMEM((count, held), low_type)] * 2,
            1024,
        )
        return keep, swap(send)

    panel_low = item_factors.astype(low_type)
    users, rates, words = kernel_call(
        stage_kernel,
        "stage",
        [panel_low],
        [pltpu.VMEM(x.shape, x.dtype) for x in (user_factors, ratings, mask_words)],
        1024,
        [pltpu.SemaphoreType.DMA((3,))],
        [user_factors, ratings, mask_words],
    )
    arrived = [panel_low] + [move(panel_low, 0, k, False) for k in range(1, chips)]
    other_users = swap(users)
    for visit in range(visits):
        last = visit + 1 == visits
        known, other_known = prepared(visit)
        if last:
            sent = [pltpu.VMEM((rows, width), full_type)]
            sent += [pltpu.VMEM((rows, width), low_type)] * (chips - 1)
        else:
            sent = [pltpu.VMEM((part, width), low_type)] * 2
        low, errors, other_errors, *sent = kernel_call(
            functools.partial(tiles_kernel, visit == 0, last, chips, close),
            "tiles",
            [place, *arrived, users, other_users, known, other_known],
            [pltpu.VMEM((held, width), low_type)] + [pltpu.VMEM((count, held), low_type)] * 2 + sent,
            1024,
            [pltpu.VMEM((part, width), full_type), pltpu.VMEM((held, width), full_type)],
        )
        if last:
            arrived = sent[:1] + [move(sent[k], 0, k, False) for k in range(1, chips)]
        else:
            arrived = [move(sent[min(k, 1)], 1, k, False) for k in range(chips)]
        sets = [low, swap(low), users, errors, swap(other_errors)]
        if not last:
            sets += [other_users, other_errors, swap(errors)]
        kind = jax.ShapeDtypeStruct if last else pltpu.VMEM
        users, *other_users = kernel_call(
            functools.partial(users_kernel, 1 if last else 2),
            "users",
            sets,
            [kind((count, width), low_type)] * (1 if last else 2),
            1024,
        )
        if not last:
            other_users = other_users[0]
    (panel,) = kernel_call(
        functools.partial(final_kernel, chips),
        "final",
        arrived,
        [jax.ShapeDtypeStruct((rows, width), full_type)],
        1024,
        extra=[users],
    )
    return (users, panel)


def solution(mesh):
    placed = (
        P(("strata", "shard"), None),
        P(("strata", "shard"), None),
        P("strata", "shard", None, None, None),
        P("strata", "shard", None),
        P("strata", "shard", None, None, None, None),
        P("strata", "shard", None, None, None, None),
    )
    return jax.shard_map(
        shards,
        mesh=mesh,
        in_specs=placed,
        out_specs=(P(("strata", "shard"), None), P(("strata", "shard"), None)),
        check_vma=False,
    )
```

time: 145 us -> 61.5 us (0.42)
  blocking collectives: 22 us -> 0 us
  matrix products: 21.7 us -> 0 us
  waiting for transfers between devices: 53.5 us -> 31.8 us
  local copies, waits for them, and re-layouts: 18.3 us -> 0.69 us
  Pallas kernels: 0 us -> 15.3 us
  between operations: 14.1 us -> 0.79 us
  other arithmetic: 11.5 us -> 1.04 us
  starting transfers between devices: 3.17 us -> 11.7 us
    reduce_scatter x3 -> x0, waiting for transfers between devices: 46.3 us -> none  [shards(): lax.psum_scatter(grad_item.astype(jnp.bfloat16), 'shard', scatter_dimensi...]
    ppermute x2 -> x18, waiting for transfers between devices: 7.15 us -> 31.8 us  [moved(): return lax.ppermute(x, ('strata', 'shard'), pairs)]
    all_gather x3 -> x0, blocking collectives: 22 us -> none  [shards(): lax.all_gather(panel.astype(jnp.bfloat16), 'shard', axis=0, tiled=True)]
    dot_general x15 -> x0, matrix products: 21.7 us -> none  [the longest x3 6.7 us: device_terms(): jnp.einsum('kb,kir->bir', item_hot, item_terms, precision=lax.Precision.H...]
    pallas_call x0 -> x11, Pallas kernels: none -> 15.3 us  [kernel_call(): pl.pallas_call(body, name=name, out_shape=tuple(outs), in_specs=[SM if x....]
    ppermute x2 -> x18, starting transfers between devices: 3.05 us -> 11.7 us  [moved(): return lax.ppermute(x, ('strata', 'shard'), pairs)]
    convert_element_type x9 -> x1, other arithmetic: 9.18 us -> 0.97 us  [shards(): panel_low = item_factors.astype(low_type)]
    gather x6 -> x0, local copies, waits for them, and re-layouts: 5.61 us -> none  [the longest x3 3.78 us: device_terms(): jnp.take(users.reshape(user_count, tile_side, width), blocks[:, 0], axis=0)]
  transfers between devices with their start and end apart: 5 -> 18, of which waited for: 5 -> 8; matrix products, arithmetic and copies ran while one was open for 15% -> 0% of each run, Pallas kernels for 0% -> 15%
where the time goes in v2:
time: 61.5 us; the launch traced here: 61.3 us
  waiting for transfers between devices  31.8 us (52%)
  Pallas kernels  15.3 us (25%)
  starting transfers between devices  11.7 us (19%)
  other arithmetic  1.04 us (2%)
  between operations  0.79 us (1%)
  local copies, waits for them, and re-layouts  0.69 us (1%)
    ppermute x18, waiting for transfers between devices, moved(): return lax.ppermute(x, ('strata', 'shard'), pairs)  31.8 us
    pallas_call x11, Pallas kernels, kernel_call(): pl.pallas_call(body, name=name, out_shape=tuple(outs), in_specs=[SM if x....  15.3 us
    ppermute x18, starting transfers between devices, moved(): return lax.ppermute(x, ('strata', 'shard'), pairs)  11.7 us
  transfers between devices with their start and end apart: 18, of which 8 were waited for; matrix products, arithmetic and copies ran while one was open for 0% of the time, Pallas kernels for 15%

profile of v2, /device:TPU:0, one launch (start us, length us, event | category | flops | bytes accessed | tf_op | source)
XLA Modules:
  0.0 61.3 jit_solution(17224192270587812442)
XLA Ops:
  0.6 1.0 %convert_element_type.3.refs_0_ = bf16[128,512]{1,0:T(8,128)(2,1)S(1)} convert(f32[128,512]{1,0:T(8,128)} %param.7) | non-fusion elementwise | flops 65536 | bytes 393216 | tf_op jit(solution)/shard_map/convert_element_type | solution.py:214
  1.6 1.5 %stage.1 = (bf16[1024,512]{1,0:T(8,128)(2,1)S(1)}, bf16[1,1,3,8,128,128]{5,4,3,2,1,0:T(8,128)(2,1)S(1)}, s32[1,1,3,8,16,128]{5,4,3,2,1,0:T(8,128)S(1)}) custom-call(bf16[128,512]{1,0:T(8,128)(2,1)S(1)} %convert_element_type.3.refs_0_, bf16[1024,512]{1,0:T(8,128)(2,1)} %refs_1_.1, bf16[1,1,3,8,128,128]{5,4,3,2,1,0:T(8,128)(2,1)} %refs_2_.1, ...), custom_call_target="tpu_custom_call" | custom-call | flops 1024 | bytes 1024 | tf_op jit(solution)/shard_map/stage/pallas_call | solution.py:164
  3.1 0.5 collective-permute-start.1
  3.6 0.1 pad_add_fusion.place
  3.7 0.7 %copy-done = s32[1,1,3,8,2]{3,4,2,1,0:T(2,128)S(1)} copy-done((s32[1,1,3,8,2]{3,4,2,1,0:T(2,128)S(1)}, s32[1,1,3,8,2]{3,4,2,1,0:T(2,128)}, u32[]{:S(2)}) %copy-start) | copy-done | bytes 216
  4.4 0.8 %prepare.3 = (bf16[1024,256]{1,0:T(8,128)(2,1)S(1)}, bf16[1024,256]{1,0:T(8,128)(2,1)S(1)}) custom-call(s32[2]{0:T(128)S(1)} %pad_add_fusion.place, s32[1,1,3,2,8]{4,3,2,1,0:T(2,128)S(1)} %bitcast.3, s32[1,1,3]{2,1,0:T(1,128)S(1)} %copy-done.1, bf16[1,1,3,8,128,128]{5,4,3,2,1,0:T(8,128)(2,1)S(1)} %get-tuple-element.31.rates, ...), custom_call_target="tpu_custom_call" | custom-call | flops 1024 | bytes 1024 | tf_op jit(solution)/shard_map/prepare/pallas_call | solution.py:164
  5.3 0.1 collective-permute-start.2
  5.3 3.0 %collective-permute-start = (bf16[128,512]{1,0:T(8,128)(2,1)S(1)}, bf16[128,512]{1,0:T(8,128)(2,1)S(1)}, u32[]{:S(2)}, u32[]{:S(2)}) collective-permute-start(bf16[128,512]{1,0:T(8,128)(2,1)S(1)} %convert_element_type.3.refs_0_), channel_id=1, source_target_pairs={{0,2},{1,3},{2,0},{3,1},{4,6},{5,7},{6,4},{7,5},{8,10},{9,11},{10,... | collective-permute-start | bytes 393224 | tf_op jit(solution)/shard_map/ppermute | solution.py:184
  8.3 0.9 %prepare.4 = (bf16[1024,256]{1,0:T(8,128)(2,1)S(1)}, bf16[1024,256]{1,0:T(8,128)(2,1)S(1)}) custom-call(s32[2]{0:T(128)S(1)} %pad_add_fusion.place, s32[1,1,3,2,8]{4,3,2,1,0:T(2,128)S(1)} %bitcast.4, s32[1,1,3]{2,1,0:T(1,128)S(1)} %copy-done.1, bf16[1,1,3,8,128,128]{5,4,3,2,1,0:T(8,128)(2,1)S(1)} %get-tuple-element.31.rates, ...), custom_call_target="tpu_custom_call" | custom-call | flops 1024 | bytes 1024 | tf_op jit(solution)/shard_map/prepare/pallas_call | solution.py:164
  9.2 2.9 %collective-permute-done.refs_1_ = bf16[128,512]{1,0:T(8,128)(2,1)S(1)} collective-permute-done((bf16[128,512]{1,0:T(8,128)(2,1)S(1)}, bf16[128,512]{1,0:T(8,128)(2,1)S(1)}, u32[]{:S(2)}, u32[]{:S(2)}) %collective-permute-start) | collective-permute-done | bytes 131104 | tf_op jit(solution)/shard_map/ppermute | solution.py:184
  12.0 0.0 collective-permute-done.2.refs_5_
  12.0 0.0 collective-permute-done.1.refs_3_.refs_5_
  12.0 1.9 %tiles.3 = (bf16[256,512]{1,0:T(8,128)(2,1)S(1)}, bf16[1024,256]{1,0:T(8,128)(2,1)S(1)}, bf16[1024,256]{1,0:T(8,128)(2,1)S(1)}, bf16[256,512]{1,0:T(8,128)(2,1)S(1)}, bf16[256,512]{1,0:T(8,128)(2,1)S(1)}) custom-call(s32[2]{0:T(128)S(1)} %pad_add_fusion.place, bf16[128,512]{1,0:T(8,128)(2,1)S(1)} %convert_element_type.3.refs_0_, ...), custom_call_target="tpu_custom_call" | custom-call | flops 1024 | bytes 1024 | tf_op jit(solution)/shard_map/tiles/pallas_call | solution.py:164
  14.0 0.1 collective-permute-start.6
  14.1 0.5 collective-permute-start.5
  14.6 0.1 collective-permute-start.7
  14.6 0.4 collective-permute-start.8
  15.1 1.8 %collective-permute-start.3 = (bf16[256,512]{1,0:T(8,128)(2,1)S(1)}, bf16[256,512]{1,0:T(8,128)(2,1)S(1)}, u32[]{:S(2)}, u32[]{:S(2)}) collective-permute-start(bf16[256,512]{1,0:T(8,128)(2,1)S(1)} %get-tuple-element.35), channel_id=1, source_target_pairs={{0,4},{1,5},{2,6},{3,7},{4,8},{5,9},{6,10},{7,11},{8,12},{9,13},{1... | collective-permute-start | bytes 786440 | tf_op jit(solution)/shard_map/ppermute | solution.py:184
  16.9 0.0 collective-permute-done.5.refs_1_
  16.9 2.5 %collective-permute-start.4 = (bf16[256,512]{1,0:T(8,128)(2,1)S(1)}, bf16[256,512]{1,0:T(8,128)(2,1)S(1)}, u32[]{:S(2)}, u32[]{:S(2)}) collective-permute-start(bf16[256,512]{1,0:T(8,128)(2,1)S(1)} %get-tuple-element.36), channel_id=1, source_target_pairs={{0,6},{1,7},{2,4},{3,5},{4,10},{5,11},{6,8},{7,9},{8,14},{9,15},{1... | collective-permute-start | bytes 786440 | tf_op jit(solution)/shard_map/ppermute | solution.py:184
  19.4 0.9 %prepare.5 = (bf16[1024,256]{1,0:T(8,128)(2,1)S(1)}, bf16[1024,256]{1,0:T(8,128)(2,1)S(1)}) custom-call(s32[2]{0:T(128)S(1)} %pad_add_fusion.place, s32[1,1,3,2,8]{4,3,2,1,0:T(2,128)S(1)} %bitcast.5, s32[1,1,3]{2,1,0:T(1,128)S(1)} %copy-done.1, bf16[1,1,3,8,128,128]{5,4,3,2,1,0:T(8,128)(2,1)S(1)} %get-tuple-element.31.rates, ...), custom_call_target="tpu_custom_call" | custom-call | flops 1024 | bytes 1024 | tf_op jit(solution)/shard_map/prepare/pallas_call | solution.py:164
  20.3 0.0 collective-permute-done.6.refs_4_
  20.3 0.1 collective-permute-start.14
  20.4 0.0 collective-permute-done.7.refs_7_
  20.4 1.4 %users.3 = (bf16[1024,512]{1,0:T(8,128)(2,1)S(1)}, bf16[1024,512]{1,0:T(8,128)(2,1)S(1)}) custom-call(bf16[256,512]{1,0:T(8,128)(2,1)S(1)} %get-tuple-element.37.refs_0_, bf16[256,512]{1,0:T(8,128)(2,1)S(1)} %collective-permute-done.5.refs_1_, bf16[1024,512]{1,0:T(8,128)(2,1)S(1)} %get-tuple-element.30.refs_2_, ...), custom_call_target="tpu_custom_call" | custom-call | flops 1024 | bytes 1024 | tf_op jit(solution)/shard_map/users/pallas_call | solution.py:164
  21.8 0.0 collective-permute-done.8.refs_5_
  21.9 5.2 %collective-permute-done.3.refs_0_ = bf16[256,512]{1,0:T(8,128)(2,1)S(1)} collective-permute-done((bf16[256,512]{1,0:T(8,128)(2,1)S(1)}, bf16[256,512]{1,0:T(8,128)(2,1)S(1)}, u32[]{:S(2)}, u32[]{:S(2)}) %collective-permute-start.3) | collective-permute-done | bytes 262176 | tf_op jit(solution)/shard_map/ppermute | solution.py:184
  27.0 6.0 %collective-permute-done.4.refs_1_ = bf16[256,512]{1,0:T(8,128)(2,1)S(1)} collective-permute-done((bf16[256,512]{1,0:T(8,128)(2,1)S(1)}, bf16[256,512]{1,0:T(8,128)(2,1)S(1)}, u32[]{:S(2)}, u32[]{:S(2)}) %collective-permute-start.4) | collective-permute-done | bytes 262176 | tf_op jit(solution)/shard_map/ppermute | solution.py:184
  33.0 1.9 %tiles.4 = (bf16[256,512]{1,0:T(8,128)(2,1)S(1)}, bf16[1024,256]{1,0:T(8,128)(2,1)S(1)}, bf16[1024,256]{1,0:T(8,128)(2,1)S(1)}, bf16[256,512]{1,0:T(8,128)(2,1)S(1)}, bf16[256,512]{1,0:T(8,128)(2,1)S(1)}) custom-call(s32[2]{0:T(128)S(1)} %pad_add_fusion.place, bf16[256,512]{1,0:T(8,128)(2,1)S(1)} %collective-permute-done.3.refs_0_, ...), custom_call_target="tpu_custom_call" | custom-call | flops 1024 | bytes 1024 | tf_op jit(solution)/shard_map/tiles/pallas_call | solution.py:164
  35.0 0.1 collective-permute-start.12
  35.0 0.5 collective-permute-start.13
  35.5 0.1 collective-permute-start.11
  35.6 0.0 collective-permute-start.9
  35.6 2.4 %collective-permute-done.11.refs_1_ = bf16[256,512]{1,0:T(8,128)(2,1)S(1)} collective-permute-done((bf16[256,512]{1,0:T(8,128)(2,1)S(1)}, bf16[256,512]{1,0:T(8,128)(2,1)S(1)}, u32[]{:S(2)}, u32[]{:S(2)}) %collective-permute-start.11) | collective-permute-done | bytes 262176 | tf_op jit(solution)/shard_map/ppermute | solution.py:184
  38.1 0.0 collective-permute-done.13.refs_7_
  38.1 1.4 %users.4 = (bf16[1024,512]{1,0:T(8,128)(2,1)S(1)}, bf16[1024,512]{1,0:T(8,128)(2,1)S(1)}) custom-call(bf16[256,512]{1,0:T(8,128)(2,1)S(1)} %get-tuple-element.46.refs_0_, bf16[256,512]{1,0:T(8,128)(2,1)S(1)} %collective-permute-done.11.refs_1_, bf16[1024,512]{1,0:T(8,128)(2,1)S(1)} %get-tuple-element.40.refs_2_, ...), custom_call_target="tpu_custom_call" | custom-call | flops 1024 | bytes 1024 | tf_op jit(solution)/shard_map/users/pallas_call | solution.py:164
  39.5 0.0 collective-permute-done.14.refs_5_
  39.5 7.9 %collective-permute-done.9.refs_0_ = bf16[256,512]{1,0:T(8,128)(2,1)S(1)} collective-permute-done((bf16[256,512]{1,0:T(8,128)(2,1)S(1)}, bf16[256,512]{1,0:T(8,128)(2,1)S(1)}, u32[]{:S(2)}, u32[]{:S(2)}) %collective-permute-start.9) | collective-permute-done | bytes 262176 | tf_op jit(solution)/shard_map/ppermute | solution.py:184
  47.4 5.1 %collective-permute-done.10.refs_1_ = bf16[256,512]{1,0:T(8,128)(2,1)S(1)} collective-permute-done((bf16[256,512]{1,0:T(8,128)(2,1)S(1)}, bf16[256,512]{1,0:T(8,128)(2,1)S(1)}, u32[]{:S(2)}, u32[]{:S(2)}) %collective-permute-start.10) | collective-permute-done | bytes 262176 | tf_op jit(solution)/shard_map/ppermute | solution.py:184
  52.6 2.0 %tiles.5 = (bf16[256,512]{1,0:T(8,128)(2,1)S(1)}, bf16[1024,256]{1,0:T(8,128)(2,1)S(1)}, bf16[1024,256]{1,0:T(8,128)(2,1)S(1)}, f32[128,512]{1,0:T(8,128)S(1)}, bf16[128,512]{1,0:T(8,128)(2,1)S(1)}) custom-call(s32[2]{0:T(128)S(1)} %pad_add_fusion.place, bf16[256,512]{1,0:T(8,128)(2,1)S(1)} %collective-permute-done.9.refs_0_, ...), custom_call_target="tpu_custom_call" | custom-call | flops 1024 | bytes 1024 | tf_op jit(solution)/shard_map/tiles/pallas_call | solution.py:164
  54.5 0.1 collective-permute-start.16
  54.6 0.5 collective-permute-start.15
  55.1 1.5 %collective-permute-start.17 = (bf16[128,512]{1,0:T(8,128)(2,1)S(1)}, bf16[128,512]{1,0:T(8,128)(2,1)S(1)}, u32[]{:S(2)}, u32[]{:S(2)}) collective-permute-start(bf16[128,512]{1,0:T(8,128)(2,1)S(1)} %get-tuple-element.57), channel_id=1, source_target_pairs={{0,2},{1,3},{2,0},{3,1},{4,6},{5,7},{6,4},{7,5},{8,10},{9,11},{10,... | collective-permute-start | bytes 393224 | tf_op jit(solution)/shard_map/ppermute | solution.py:184
  56.6 0.3 collective-permute-done.15.refs_1_
  56.9 0.0 collective-permute-done.16.refs_4_
  56.9 1.8 %users.5.refs_2_ = bf16[1024,512]{1,0:T(8,128)(2,1)} custom-call(bf16[256,512]{1,0:T(8,128)(2,1)S(1)} %get-tuple-element.53.refs_0_, bf16[256,512]{1,0:T(8,128)(2,1)S(1)} %collective-permute-done.15.refs_1_, bf16[1024,512]{1,0:T(8,128)(2,1)S(1)} %get-tuple-element.49.refs_2_, bf16[1024,256]{1,0:T(8,128)(2,1)S(1)} %get-tuple-element.54.refs_3_, ...), custom_call_target="tpu_custom_call" | custom-call | flops 1024 | bytes 1024 | tf_op jit(solution)/shard_map/users/pallas_call | solution.py:164
  58.7 1.9 %collective-permute-done.17.refs_1_ = bf16[128,512]{1,0:T(8,128)(2,1)S(1)} collective-permute-done((bf16[128,512]{1,0:T(8,128)(2,1)S(1)}, bf16[128,512]{1,0:T(8,128)(2,1)S(1)}, u32[]{:S(2)}, u32[]{:S(2)}) %collective-permute-start.17) | collective-permute-done | bytes 131104 | tf_op jit(solution)/shard_map/ppermute | solution.py:184
  60.6 0.7 %final.1 = f32[128,512]{1,0:T(8,128)} custom-call(f32[128,512]{1,0:T(8,128)S(1)} %get-tuple-element.56.refs_0_, bf16[128,512]{1,0:T(8,128)(2,1)S(1)} %collective-permute-done.17.refs_1_, bf16[1024,512]{1,0:T(8,128)(2,1)} %users.5.refs_2_), custom_call_target="tpu_custom_call" | custom-call | flops 1024 | bytes 1024 | tf_op jit(solution)/shard_map/final/pallas_call | solution.py:164
  (5 shorter events, 0.0 us)
Async XLA Ops:
  3.1 8.9 %collective-permute-start.1 = (bf16[1024,512]{1,0:T(8,128)(2,1)S(1)}, bf16[1024,512]{1,0:T(8,128)(2,1)S(1)}, u32[]{:S(2)}, u32[]{:S(2)}) collective-permute-start(bf16[1024,512]{1,0:T(8,128)(2,1)S(1)} %get-tuple-element.30.refs_2_), channel_id=1, source_target_pairs={{0,1},{1,0},{2,3},{3,2},{4,5},{5,4},{6,7},{7,6},{8,9},{9,8},{10,11... | collective-permute-start | bytes 3145736 | tf_op jit(solution)/shard_map/ppermute | solution.py:184
  3.7 0.7 %copy-start = (s32[1,1,3,8,2]{3,4,2,1,0:T(2,128)S(1)}, s32[1,1,3,8,2]{3,4,2,1,0:T(2,128)}, u32[]{:S(2)}) copy-start(s32[1,1,3,8,2]{3,4,2,1,0:T(2,128)} %param.8) | copy-start | bytes 580
  3.7 0.7 %copy-start.1 = (s32[1,1,3]{2,1,0:T(1,128)S(1)}, s32[1,1,3]{2,1,0:T(1,128)}, u32[]{:S(2)}) copy-start(s32[1,1,3]{2,1,0:T(1,128)} %counts.5) | copy-start | bytes 40
  5.3 6.8 %collective-permute-start.2 = (bf16[1024,256]{1,0:T(8,128)(2,1)S(1)}, bf16[1024,256]{1,0:T(8,128)(2,1)S(1)}, u32[]{:S(2)}, u32[]{:S(2)}) collective-permute-start(bf16[1024,256]{1,0:T(8,128)(2,1)S(1)} %get-tuple-element.34), channel_id=1, source_target_pairs={{0,1},{1,0},{2,3},{3,2},{4,5},{5,4},{6,7},{7,6},{8,9},{9,8},{10,11... | collective-permute-start | bytes 1572872 | tf_op jit(solution)/shard_map/ppermute | solution.py:184
  5.3 6.7 %collective-permute-start = (bf16[128,512]{1,0:T(8,128)(2,1)S(1)}, bf16[128,512]{1,0:T(8,128)(2,1)S(1)}, u32[]{:S(2)}, u32[]{:S(2)}) collective-permute-start(bf16[128,512]{1,0:T(8,128)(2,1)S(1)} %convert_element_type.3.refs_0_), channel_id=1, source_target_pairs={{0,2},{1,3},{2,0},{3,1},{4,6},{5,7},{6,4},{7,5},{8,10},{9,11},{10,... | collective-permute-start | bytes 393224 | tf_op jit(solution)/shard_map/ppermute | solution.py:184
  14.0 6.3 %collective-permute-start.6 = (bf16[1024,256]{1,0:T(8,128)(2,1)S(1)}, bf16[1024,256]{1,0:T(8,128)(2,1)S(1)}, u32[]{:S(2)}, u32[]{:S(2)}) collective-permute-start(bf16[1024,256]{1,0:T(8,128)(2,1)S(1)} %get-tuple-element.39.refs_6_), channel_id=1, source_target_pairs={{0,1},{1,0},{2,3},{3,2},{4,5},{5,4},{6,7},{7,6},{8,9},{9,8},{10,11... | collective-permute-start | bytes 1572872 | tf_op jit(solution)/shard_map/ppermute | solution.py:184
  14.1 2.8 %collective-permute-start.5 = (bf16[256,512]{1,0:T(8,128)(2,1)S(1)}, bf16[256,512]{1,0:T(8,128)(2,1)S(1)}, u32[]{:S(2)}, u32[]{:S(2)}) collective-permute-start(bf16[256,512]{1,0:T(8,128)(2,1)S(1)} %get-tuple-element.37.refs_0_), channel_id=1, source_target_pairs={{0,1},{1,0},{2,3},{3,2},{4,5},{5,4},{6,7},{7,6},{8,9},{9,8},{10,11... | collective-permute-start | bytes 786440 | tf_op jit(solution)/shard_map/ppermute | solution.py:184
  14.6 5.8 %collective-permute-start.7 = (bf16[1024,256]{1,0:T(8,128)(2,1)S(1)}, bf16[1024,256]{1,0:T(8,128)(2,1)S(1)}, u32[]{:S(2)}, u32[]{:S(2)}) collective-permute-start(bf16[1024,256]{1,0:T(8,128)(2,1)S(1)} %get-tuple-element.38.refs_3_), channel_id=1, source_target_pairs={{0,1},{1,0},{2,3},{3,2},{4,5},{5,4},{6,7},{7,6},{8,9},{9,8},{10,11... | collective-permute-start | bytes 1572872 | tf_op jit(solution)/shard_map/ppermute | solution.py:184
  14.6 7.2 %collective-permute-start.8 = (bf16[1024,256]{1,0:T(8,128)(2,1)S(1)}, bf16[1024,256]{1,0:T(8,128)(2,1)S(1)}, u32[]{:S(2)}, u32[]{:S(2)}) collective-permute-start(bf16[1024,256]{1,0:T(8,128)(2,1)S(1)} %get-tuple-element.43), channel_id=1, source_target_pairs={{0,1},{1,0},{2,3},{3,2},{4,5},{5,4},{6,7},{7,6},{8,9},{9,8},{10,11... | collective-permute-start | bytes 1572872 | tf_op jit(solution)/shard_map/ppermute | solution.py:184
  15.1 12.0 %collective-permute-start.3 = (bf16[256,512]{1,0:T(8,128)(2,1)S(1)}, bf16[256,512]{1,0:T(8,128)(2,1)S(1)}, u32[]{:S(2)}, u32[]{:S(2)}) collective-permute-start(bf16[256,512]{1,0:T(8,128)(2,1)S(1)} %get-tuple-element.35), channel_id=1, source_target_pairs={{0,4},{1,5},{2,6},{3,7},{4,8},{5,9},{6,10},{7,11},{8,12},{9,13},{1... | collective-permute-start | bytes 786440 | tf_op jit(solution)/shard_map/ppermute | solution.py:184
  16.9 16.1 %collective-permute-start.4 = (bf16[256,512]{1,0:T(8,128)(2,1)S(1)}, bf16[256,512]{1,0:T(8,128)(2,1)S(1)}, u32[]{:S(2)}, u32[]{:S(2)}) collective-permute-start(bf16[256,512]{1,0:T(8,128)(2,1)S(1)} %get-tuple-element.36), channel_id=1, source_target_pairs={{0,6},{1,7},{2,4},{3,5},{4,10},{5,11},{6,8},{7,9},{8,14},{9,15},{1... | collective-permute-start | bytes 786440 | tf_op jit(solution)/shard_map/ppermute | solution.py:184
  20.3 19.2 %collective-permute-start.14 = (bf16[1024,256]{1,0:T(8,128)(2,1)S(1)}, bf16[1024,256]{1,0:T(8,128)(2,1)S(1)}, u32[]{:S(2)}, u32[]{:S(2)}) collective-permute-start(bf16[1024,256]{1,0:T(8,128)(2,1)S(1)} %get-tuple-element.52), channel_id=1, source_target_pairs={{0,1},{1,0},{2,3},{3,2},{4,5},{5,4},{6,7},{7,6},{8,9},{9,8},{10,11... | collective-permute-start | bytes 1572872 | tf_op jit(solution)/shard_map/ppermute | solution.py:184
  35.0 3.1 %collective-permute-start.12 = (bf16[1024,256]{1,0:T(8,128)(2,1)S(1)}, bf16[1024,256]{1,0:T(8,128)(2,1)S(1)}, u32[]{:S(2)}, u32[]{:S(2)}) collective-permute-start(bf16[1024,256]{1,0:T(8,128)(2,1)S(1)} %get-tuple-element.48.refs_6_), channel_id=1, source_target_pairs={{0,1},{1,0},{2,3},{3,2},{4,5},{5,4},{6,7},{7,6},{8,9},{9,8},{10,11... | collective-permute-start | bytes 1572872 | tf_op jit(solution)/shard_map/ppermute | solution.py:184
  35.0 3.0 %collective-permute-start.13 = (bf16[1024,256]{1,0:T(8,128)(2,1)S(1)}, bf16[1024,256]{1,0:T(8,128)(2,1)S(1)}, u32[]{:S(2)}, u32[]{:S(2)}) collective-permute-start(bf16[1024,256]{1,0:T(8,128)(2,1)S(1)} %get-tuple-element.47.refs_3_), channel_id=1, source_target_pairs={{0,1},{1,0},{2,3},{3,2},{4,5},{5,4},{6,7},{7,6},{8,9},{9,8},{10,11... | collective-permute-start | bytes 1572872 | tf_op jit(solution)/shard_map/ppermute | solution.py:184
  35.5 2.5 %collective-permute-start.11 = (bf16[256,512]{1,0:T(8,128)(2,1)S(1)}, bf16[256,512]{1,0:T(8,128)(2,1)S(1)}, u32[]{:S(2)}, u32[]{:S(2)}) collective-permute-start(bf16[256,512]{1,0:T(8,128)(2,1)S(1)} %get-tuple-element.46.refs_0_), channel_id=1, source_target_pairs={{0,1},{1,0},{2,3},{3,2},{4,5},{5,4},{6,7},{7,6},{8,9},{9,8},{10,11... | collective-permute-start | bytes 786440 | tf_op jit(solution)/shard_map/ppermute | solution.py:184
  35.6 11.8 %collective-permute-start.9 = (bf16[256,512]{1,0:T(8,128)(2,1)S(1)}, bf16[256,512]{1,0:T(8,128)(2,1)S(1)}, u32[]{:S(2)}, u32[]{:S(2)}) collective-permute-start(bf16[256,512]{1,0:T(8,128)(2,1)S(1)} %get-tuple-element.44), channel_id=1, source_target_pairs={{0,4},{1,5},{2,6},{3,7},{4,8},{5,9},{6,10},{7,11},{8,12},{9,13},{1... | collective-permute-start | bytes 786440 | tf_op jit(solution)/shard_map/ppermute | solution.py:184
  38.1 14.5 %collective-permute-start.10 = (bf16[256,512]{1,0:T(8,128)(2,1)S(1)}, bf16[256,512]{1,0:T(8,128)(2,1)S(1)}, u32[]{:S(2)}, u32[]{:S(2)}) collective-permute-start(bf16[256,512]{1,0:T(8,128)(2,1)S(1)} %get-tuple-element.45), channel_id=1, source_target_pairs={{0,6},{1,7},{2,4},{3,5},{4,10},{5,11},{6,8},{7,9},{8,14},{9,15},{1... | collective-permute-start | bytes 786440 | tf_op jit(solution)/shard_map/ppermute | solution.py:184
  54.5 2.4 %collective-permute-start.16 = (bf16[1024,256]{1,0:T(8,128)(2,1)S(1)}, bf16[1024,256]{1,0:T(8,128)(2,1)S(1)}, u32[]{:S(2)}, u32[]{:S(2)}) collective-permute-start(bf16[1024,256]{1,0:T(8,128)(2,1)S(1)} %get-tuple-element.55), channel_id=1, source_target_pairs={{0,1},{1,0},{2,3},{3,2},{4,5},{5,4},{6,7},{7,6},{8,9},{9,8},{10,11... | collective-permute-start | bytes 1572872 | tf_op jit(solution)/shard_map/ppermute | solution.py:184
  54.6 2.3 %collective-permute-start.15 = (bf16[256,512]{1,0:T(8,128)(2,1)S(1)}, bf16[256,512]{1,0:T(8,128)(2,1)S(1)}, u32[]{:S(2)}, u32[]{:S(2)}) collective-permute-start(bf16[256,512]{1,0:T(8,128)(2,1)S(1)} %get-tuple-element.53.refs_0_), channel_id=1, source_target_pairs={{0,1},{1,0},{2,3},{3,2},{4,5},{5,4},{6,7},{7,6},{8,9},{9,8},{10,11... | collective-permute-start | bytes 786440 | tf_op jit(solution)/shard_map/ppermute | solution.py:184
  55.1 5.5 %collective-permute-start.17 = (bf16[128,512]{1,0:T(8,128)(2,1)S(1)}, bf16[128,512]{1,0:T(8,128)(2,1)S(1)}, u32[]{:S(2)}, u32[]{:S(2)}) collective-permute-start(bf16[128,512]{1,0:T(8,128)(2,1)S(1)} %get-tuple-element.57), channel_id=1, source_target_pairs={{0,2},{1,3},{2,0},{3,1},{4,6},{5,7},{6,4},{7,5},{8,10},{9,11},{10,... | collective-permute-start | bytes 393224 | tf_op jit(solution)/shard_map/ppermute | solution.py:184

commit v3 on v2

--- a/solution.py
+++ b/solution.py
@@ -16,6 +16,8 @@
 HB = pl.BlockSpec(memory_space=pltpu.HBM)
 CORES = 2
 CHUNK = 512
+MARK = 1 << 32
+LEAD = 0
 
 
 def place_of(close, chip, core, rows):
@@ -36,29 +38,17 @@
     return jnp.concatenate(parts, 0) != 0
 
 
-def round_kernel(panel, out):
-    out[...] = panel[...].astype(out.dtype)
-
-
-def stage_kernel(*refs):
-    count, sem = (len(refs) - 2) // 2, refs[-1]
-    copies = [
-        pltpu.make_async_copy(refs[1 + i], refs[1 + count + i], sem.at[i]) for i in range(count)
-    ]
-    for copy in copies:
-        copy.start()
-    for copy in copies:
-        copy.wait()
-
-
-def prepare_kernel(visit, rows, close, place, blocks, counts, rates, words, keep, send):
+def prepare_kernel(visit, rows, close, place, *refs):
+    for i in range(CORES):
+        lay_out(visit, rows, close, place[0], *refs[4 * i : 4 * i + 4], refs[4 * CORES + i])
+
+
+def lay_out(visit, rows, close, core, blocks, counts, rates, words, keep):
     side = rates.shape[-1]
-    core = place[0]
     nothing = jnp.full((side, side), jnp.nan, keep.dtype)
     for at in range(0, keep.shape[0], side):
         for lane in range(0, keep.shape[1], side):
             keep[at : at + side, lane : lane + side] = nothing
-            send[at : at + side, lane : lane + side] = nothing
 
     def tile(k, carry):
         users = pl.ds(pl.multiple_of(blocks[0, 0, visit, 0, k] * side, side), side)
@@ -74,64 +64,72 @@
             @pl.when(lax.rem(piece, CORES) == core)
             def _():
                 keep[users, at] = known
-
-            @pl.when(lax.rem(piece, CORES) != core)
-            def _():
-                send[users, at] = known
         else:
             at = pl.ds(pl.multiple_of(first, side), side)
             piece = lax.div(first + lax.broadcasted_iota(jnp.int32, known.shape, 1), rows)
             mine = lax.rem(piece, CORES) == core
             keep[users, at] = jnp.where(mine, known, jnp.nan).astype(keep.dtype)
-            send[users, at] = jnp.where(mine, jnp.nan, known).astype(keep.dtype)
         return carry
 
     lax.fori_loop(0, counts[0, 0, visit], tile, 0)
 
 
-def tiles_kernel(first, last, chips, close, place, *refs):
+def tiles_kernel(first, last, chips, group, groups, close, place, *refs):
     arrived, refs = refs[:chips], refs[chips:]
     (users, peers, rates, peer_rates), refs = refs[:4], refs[4:]
-    (low, errors, peer_errors), refs = refs[:3], refs[3:]
-    outs, (panel, total) = refs[:-2], refs[-2:]
+    panel, total = refs[-2:]
+    span = chips // groups
+    before = 0 if group == 0 else 3 + (chips if last else 0)
+    (low, errors, peer_errors), outs = refs[before : before + 3], refs[before + 3 : -2]
     core, chip = place[0], place[1]
-    rows = panel.shape[0] // chips
+    rows = panel.shape[0] // span
+    held = total.shape[0]
+    mine = slice(group * held, (group + 1) * held)
     if first:
         for k in range(chips):
             origin = lax.rem(chip + chips - k, chips)
-            at = pl.multiple_of(origin * rows, rows)
-            panel[pl.ds(at, rows), :] = arrived[k][...].astype(jnp.float32)
+
+            @pl.when(lax.div(origin, span) == group)
+            def _():
+                at = pl.multiple_of((origin - group * span) * rows, rows)
+                panel[pl.ds(at, rows), :] = arrived[k][...].astype(jnp.float32)
+
     else:
         now = arrived[0][...].astype(jnp.float32)
         for other in arrived[1:]:
             now = now + step_item * other[...].astype(jnp.float32)
         panel[...] = now
     if close:
-        low[...] = panel[...].astype(low.dtype)
+        low[mine, :] = panel[...].astype(low.dtype)
     else:
-        low[...] = jnp.zeros_like(low)
-        for j in range(chips):
-            low[pl.ds(place_of(close, j, core, rows), rows), :] = panel[
+        low[mine, :] = jnp.zeros((held, low.shape[1]), low.dtype)
+        for j in range(span):
+            low[pl.ds(group * held + place_of(close, j, core, rows), rows), :] = panel[
                 j * rows : (j + 1) * rows, :
             ].astype(low.dtype)
     for who, known, error in ((users, rates, errors), (peers, peer_rates, peer_errors)):
         for at in range(0, who.shape[0], CHUNK):
             cut = slice(at, at + CHUNK)
-            predicted = multiply(who[cut, :], low[...], 1, 1)
-            rating = known[cut, :].astype(jnp.float32)
-            error[cut, :] = jnp.where(rating == rating, rating - predicted, 0.0).astype(error.dtype)
-    total[...] = multiply(errors[...], users[...], 0, 0)
-    total[...] += multiply(peer_errors[...], peers[...], 0, 0)
+            predicted = multiply(who[cut, :], low[mine, :], 1, 1)
+            rating = known[cut, mine].astype(jnp.float32)
+            error[cut, mine] = jnp.where(rating == rating, rating - predicted, 0.0).astype(error.dtype)
+    total[...] = multiply(errors[:, mine], users[...], 0, 0)
+    total[...] += multiply(peer_errors[:, mine], peers[...], 0, 0)
     if last:
         for k in range(chips):
             owner = lax.rem(chip + k, chips)
-            term = total[pl.ds(place_of(close, owner, core, rows), rows), :]
-            if k == 0:
-                old = panel[pl.ds(pl.multiple_of(owner * rows, rows), rows), :]
-                term = old + step_item * (term - shrinkage * old)
-            outs[k][...] = term.astype(outs[k].dtype)
+
+            @pl.when(lax.div(owner, span) == group)
+            def _():
+                local = owner - group * span
+                term = total[pl.ds(place_of(close, local, core, rows), rows), :]
+                if k == 0:
+                    old = panel[pl.ds(pl.multiple_of(local * rows, rows), rows), :]
+                    term = old + step_item * (term - shrinkage * old)
+                outs[k][...] = term.astype(outs[k].dtype)
+
     else:
-        for j in range(chips):
+        for j in range(span):
             cut = slice(j * rows, (j + 1) * rows)
             term = total[pl.ds(place_of(close, j, core, rows), rows), :]
             old = panel[cut, :]
@@ -140,7 +138,7 @@
 
 
 def users_kernel(count, *refs):
-    (low, other_low), refs = refs[:2], refs[2:]
+    (_, low, other_low), refs = refs[:3], refs[3:]
     for i in range(count):
         users, errors, other_errors = refs[3 * i : 3 * i + 3]
         out = refs[3 * count + i]
@@ -160,7 +158,7 @@
     refs[count][...] = total
 
 
-def kernel_call(body, name, ins, outs, flops, scratch=(), extra=()):
+def kernel_call(body, name, ins, outs, flops, scratch=(), extra=(), aliases=()):
     return pl.pallas_call(
         body,
         name=name,
@@ -168,9 +166,26 @@
         in_specs=[SM if x.dtype == jnp.int32 and x.ndim != 6 else VM for x in ins] + [HB] * len(extra),
         out_specs=(VM,) * len(outs),
         scratch_shapes=list(scratch),
+        input_output_aliases=dict(aliases),
         compiler_params=pltpu.CompilerParams(vmem_limit_bytes=16 << 20),
         cost_estimate=pl.CostEstimate(flops=flops, bytes_accessed=1024, transcendentals=0),
     )(*ins, *[pltpu.with_memory_space_constraint(x, pltpu.HBM) for x in extra])
+
+
+def mark_kernel(*refs):
+    refs[-1][...] = jnp.zeros_like(refs[-1])
+
+
+def marked(*arrays):
+    return pl.pallas_call(
+        mark_kernel,
+        name="mark",
+        out_shape=pltpu.VMEM((8, 128), jnp.float32),
+        in_specs=[VM] * len(arrays),
+        out_specs=VM,
+        compiler_params=pltpu.CompilerParams(vmem_limit_bytes=16 << 20),
+        cost_estimate=pl.CostEstimate(flops=MARK, bytes_accessed=1024, transcendentals=0),
+    )(*arrays)
 
 
 def moved(x, by_strata, by_chip, flip, *, strata, peers):
@@ -202,48 +217,50 @@
     blocks = jnp.swapaxes(tile_blocks, 3, 4)
 
     def prepared(visit):
-        keep, send = kernel_call(
+        return kernel_call(
             functools.partial(prepare_kernel, visit, rows, close),
             "prepare",
-            [place, blocks, tile_counts, rates, words],
-            [pltpu.VMEM((count, held), low_type)] * 2,
+            [place, *tiles, *other_tiles],
+            [pltpu.VMEM((count, held), low_type)] * CORES,
             1024,
         )
-        return keep, swap(send)
 
     panel_low = item_factors.astype(low_type)
-    users, rates, words = kernel_call(
-        stage_kernel,
-        "stage",
-        [panel_low],
-        [pltpu.VMEM(x.shape, x.dtype) for x in (user_factors, ratings, mask_words)],
-        1024,
-        [pltpu.SemaphoreType.DMA((3,))],
-        [user_factors, ratings, mask_words],
-    )
     arrived = [panel_low] + [move(panel_low, 0, k, False) for k in range(1, chips)]
-    other_users = swap(users)
+    users, other_users = user_factors, swap(user_factors)
+    tiles = [blocks, tile_counts, ratings, mask_words]
+    other_tiles = [swap(x) for x in tiles]
+    groups = 2 if chips % 2 == 0 else 1
+    share, part = held // groups, part // groups
+    arrived = [arrived] * groups
     for visit in range(visits):
         last = visit + 1 == visits
-        known, other_known = prepared(visit)
+        known = prepared(visit)
+        shared = [pltpu.VMEM((held, width), low_type)] + [pltpu.VMEM((count, held), low_type)] * 2
         if last:
-            sent = [pltpu.VMEM((rows, width), full_type)]
-            sent += [pltpu.VMEM((rows, width), low_type)] * (chips - 1)
-        else:
-            sent = [pltpu.VMEM((part, width), low_type)] * 2
-        low, errors, other_errors, *sent = kernel_call(
-            functools.partial(tiles_kernel, visit == 0, last, chips, close),
-            "tiles",
-            [place, *arrived, users, other_users, known, other_known],
-            [pltpu.VMEM((held, width), low_type)] + [pltpu.VMEM((count, held), low_type)] * 2 + sent,
-            1024,
-            [pltpu.VMEM((part, width), full_type), pltpu.VMEM((held, width), full_type)],
-        )
+            shared += [pltpu.VMEM((rows, width), full_type)]
+            shared += [pltpu.VMEM((rows, width), low_type)] * (chips - 1)
+        made, sent = [], []
+        for group in range(groups):
+            ins = [place, *arrived[group], users, other_users, *known]
+            *outs, = kernel_call(
+                functools.partial(tiles_kernel, visit == 0, last, chips, group, groups, close),
+                "tiles",
+                [*ins, *made],
+                shared + ([] if last else [pltpu.VMEM((part, width), low_type)] * 2),
+                1024,
+                [pltpu.VMEM((part, width), full_type), pltpu.VMEM((share, width), full_type)],
+                aliases=[(len(ins) + i, i) for i in range(len(made))],
+            )
+            made, messages = outs[: len(shared)], outs[len(shared) :]
+            if not last:
+                sent.append([move(messages[min(k, 1)], 1, k, False) for k in range(chips)])
+        low, errors, other_errors, *ends = made
         if last:
-            arrived = sent[:1] + [move(sent[k], 0, k, False) for k in range(1, chips)]
-        else:
-            arrived = [move(sent[min(k, 1)], 1, k, False) for k in range(chips)]
-        sets = [low, swap(low), users, errors, swap(other_errors)]
+            sent = ends[:1] + [move(ends[k], 0, k, False) for k in range(1, chips)]
+        arrived = sent
+        mark = marked(*sent[LEAD]) if not last else place
+        sets = [mark, low, swap(low), users, errors, swap(other_errors)]
         if not last:
             sets += [other_users, other_errors, swap(errors)]
         kind = jax.ShapeDtypeStruct if last else pltpu.VMEM

time: 61.5 us -> 54.2 us (0.88)
  waiting for transfers between devices: 31.8 us -> 13.8 us
  starting transfers between devices: 11.7 us -> 18 us
  Pallas kernels: 15.3 us -> 19.2 us
    ppermute x18 -> x23, waiting for transfers between devices: 31.8 us -> 13.8 us  [moved(): return lax.ppermute(x, ('strata', 'shard'), pairs)]
    ppermute x18 -> x23, starting transfers between devices: 11.7 us -> 18 us  [moved(): return lax.ppermute(x, ('strata', 'shard'), pairs)]
    pallas_call x11 -> x13, Pallas kernels: 15.3 us -> 19.2 us  [kernel_call(): pl.pallas_call(body, name=name, out_shape=tuple(outs), in_specs=[SM if x....]
  transfers between devices with their start and end apart: 18 -> 23, of which waited for: 8 -> 11; matrix products, arithmetic and copies ran while one was open for 0% -> 2% of each run, Pallas kernels for 15% -> 28%
where the time goes in v3:
time: 54.2 us; the launch traced here: 54 us
  Pallas kernels  19.2 us (35%)
  starting transfers between devices  18 us (33%)
  waiting for transfers between devices  13.8 us (25%)
  local copies, waits for them, and re-layouts  1.15 us (2%)
  other arithmetic  1.06 us (2%)
  between operations  0.84 us (2%)
    pallas_call x13, Pallas kernels, kernel_call(): pl.pallas_call(body, name=name, out_shape=tuple(outs), in_specs=[SM if x....  19.2 us
    ppermute x23, starting transfers between devices, moved(): return lax.ppermute(x, ('strata', 'shard'), pairs)  18 us
    ppermute x23, waiting for transfers between devices, moved(): return lax.ppermute(x, ('strata', 'shard'), pairs)  13.8 us
    unnamed x12, local copies, waits for them, and re-layouts  1.15 us
  transfers between devices with their start and end apart: 23, of which 11 were waited for; matrix products, arithmetic and copies ran while one was open for 2% of the time, Pallas kernels for 28%

profile of v3, /device:TPU:0, one launch (start us, length us, event | category | flops | bytes accessed | tf_op | source)
XLA Modules:
  0.0 54.0 jit_solution(15963735867167609615)
XLA Ops:
  0.7 0.5 collective-permute-start.1
  1.2 0.1 collective-permute-start.4
  1.2 0.4 collective-permute-start.5
  1.7 1.0 %convert_element_type.3.refs_0_ = bf16[128,512]{1,0:T(8,128)(2,1)S(1)} convert(f32[128,512]{1,0:T(8,128)} %param.7) | non-fusion elementwise | flops 65536 | bytes 393216 | tf_op jit(solution)/shard_map/convert_element_type | solution.py:228
  2.7 2.7 %collective-permute-start = (bf16[128,512]{1,0:T(8,128)(2,1)S(1)}, bf16[128,512]{1,0:T(8,128)(2,1)S(1)}, u32[]{:S(2)}, u32[]{:S(2)}) collective-permute-start(bf16[128,512]{1,0:T(8,128)(2,1)S(1)} %convert_element_type.3.refs_0_), channel_id=1, source_target_pairs={{0,2},{1,3},{2,0},{3,1},{4,6},{5,7},{6,4},{7,5},{8,10},{9,11},{10,... | collective-permute-start | bytes 393224 | tf_op jit(solution)/shard_map/ppermute | solution.py:199
  5.3 0.2 collective-permute-start.3
  5.5 1.0 %collective-permute-done.3.refs_5_ = s32[1,1,3]{2,1,0:T(1,128)S(1)} collective-permute-done((s32[1,1,3]{2,1,0:T(1,128)S(1)}, s32[1,1,3]{2,1,0:T(1,128)S(1)}, u32[]{:S(2)}, u32[]{:S(2)}) %collective-permute-start.3) | collective-permute-done | bytes 44 | tf_op jit(solution)/shard_map/ppermute | solution.py:199
  6.5 0.2 collective-permute-start.2
  6.7 0.1 pad_add_fusion.place.refs_0_
  6.8 0.9 %collective-permute-done.2.refs_4_ = s32[1,1,3,2,8]{4,3,2,1,0:T(2,128)S(1)} collective-permute-done((s32[1,1,3,2,8]{4,3,2,1,0:T(2,128)S(1)}, s32[1,1,3,2,8]{4,3,2,1,0:T(2,128)S(1)}, u32[]{:S(2)}, u32[]{:S(2)}) %collective-permute-start.2) | collective-permute-done | bytes 224 | tf_op jit(solution)/shard_map/ppermute | solution.py:199
  7.6 0.0 copy-start.1
  7.7 1.1 %copy-done.1 = bf16[1,1,3,8,128,128]{5,4,3,2,1,0:T(8,128)(2,1)S(1)} copy-done((bf16[1,1,3,8,128,128]{5,4,3,2,1,0:T(8,128)(2,1)S(1)}, bf16[1,1,3,8,128,128]{5,4,3,2,1,0:T(8,128)(2,1)}, u32[]{:S(2)}) %copy-start.1) | copy-done | bytes 786456
  8.8 0.9 %prepare.3 = (bf16[1024,256]{1,0:T(8,128)(2,1)S(1)}, bf16[1024,256]{1,0:T(8,128)(2,1)S(1)}) custom-call(s32[2]{0:T(128)S(1)} %pad_add_fusion.place.refs_0_, s32[1,1,3,2,8]{4,3,2,1,0:T(2,128)S(1)} %bitcast.4, s32[1,1,3]{2,1,0:T(1,128)S(1)} %copy-done.5, bf16[1,1,3,8,128,128]{5,4,3,2,1,0:T(8,128)(2,1)S(1)} %copy-done.1, ...), custom_call_target="tpu_custom_call" | custom-call | flops 1024 | bytes 1024 | tf_op jit(solution)/shard_map/prepare/pallas_call | solution.py:162
  9.8 1.7 %tiles.6 = (bf16[256,512]{1,0:T(8,128)(2,1)S(1)}, bf16[1024,256]{1,0:T(8,128)(2,1)S(1)}, bf16[1024,256]{1,0:T(8,128)(2,1)S(1)}, bf16[128,512]{1,0:T(8,128)(2,1)S(1)}, bf16[128,512]{1,0:T(8,128)(2,1)S(1)}) custom-call(s32[2]{0:T(128)S(1)} %pad_add_fusion.place.refs_0_, bf16[128,512]{1,0:T(8,128)(2,1)S(1)} %convert_element_type.3.refs_0_, ...), custom_call_target="tpu_custom_call" | custom-call | flops 1024 | bytes 1024 | tf_op jit(solution)/shard_map/tiles/pallas_call | solution.py:162
  11.5 1.6 %collective-permute-start.8 = (bf16[128,512]{1,0:T(8,128)(2,1)S(1)}, bf16[128,512]{1,0:T(8,128)(2,1)S(1)}, u32[]{:S(2)}, u32[]{:S(2)}) collective-permute-start(bf16[128,512]{1,0:T(8,128)(2,1)S(1)} %get-tuple-element.49), channel_id=1, source_target_pairs={{0,4},{1,5},{2,6},{3,7},{4,8},{5,9},{6,10},{7,11},{8,12},{9,13},{1... | collective-permute-start | bytes 393224 | tf_op jit(solution)/shard_map/ppermute | solution.py:199
  13.1 2.3 %collective-permute-start.9 = (bf16[128,512]{1,0:T(8,128)(2,1)S(1)}, bf16[128,512]{1,0:T(8,128)(2,1)S(1)}, u32[]{:S(2)}, u32[]{:S(2)}) collective-permute-start(bf16[128,512]{1,0:T(8,128)(2,1)S(1)} %get-tuple-element.50), channel_id=1, source_target_pairs={{0,6},{1,7},{2,4},{3,5},{4,10},{5,11},{6,8},{7,9},{8,14},{9,15},{1... | collective-permute-start | bytes 393224 | tf_op jit(solution)/shard_map/ppermute | solution.py:199
  15.4 1.7 %tiles.7 = (bf16[256,512]{1,0:T(8,128)(2,1)S(1)}, bf16[1024,256]{1,0:T(8,128)(2,1)S(1)}, bf16[1024,256]{1,0:T(8,128)(2,1)S(1)}, bf16[128,512]{1,0:T(8,128)(2,1)S(1)}, bf16[128,512]{1,0:T(8,128)(2,1)S(1)}) custom-call(s32[2]{0:T(128)S(1)} %pad_add_fusion.place.refs_0_, ...), custom_call_target="tpu_custom_call", output_to_operand_aliasing={{0}: (7, {}), {1}: (8, {}), {2}: (9, {})} | custom-call | flops 1024 | bytes 1024 | tf_op jit(solution)/shard_map/tiles/pallas_call | solution.py:162
  17.1 0.1 collective-permute-start.11
  17.2 0.5 collective-permute-start.12
  17.7 1.0 %prepare.4 = (bf16[1024,256]{1,0:T(8,128)(2,1)S(1)}, bf16[1024,256]{1,0:T(8,128)(2,1)S(1)}) custom-call(s32[2]{0:T(128)S(1)} %pad_add_fusion.place.refs_0_, s32[1,1,3,2,8]{4,3,2,1,0:T(2,128)S(1)} %bitcast.5, s32[1,1,3]{2,1,0:T(1,128)S(1)} %copy-done.5, bf16[1,1,3,8,128,128]{5,4,3,2,1,0:T(8,128)(2,1)S(1)} %copy-done.2, ...), custom_call_target="tpu_custom_call" | custom-call | flops 1024 | bytes 1024 | tf_op jit(solution)/shard_map/prepare/pallas_call | solution.py:162
  18.7 1.6 %collective-permute-start.6 = (bf16[128,512]{1,0:T(8,128)(2,1)S(1)}, bf16[128,512]{1,0:T(8,128)(2,1)S(1)}, u32[]{:S(2)}, u32[]{:S(2)}) collective-permute-start(bf16[128,512]{1,0:T(8,128)(2,1)S(1)} %get-tuple-element.47), channel_id=1, source_target_pairs={{0,4},{1,5},{2,6},{3,7},{4,8},{5,9},{6,10},{7,11},{8,12},{9,13},{1... | collective-permute-start | bytes 393224 | tf_op jit(solution)/shard_map/ppermute | solution.py:199
  20.3 0.2 collective-permute-done.8.refs_0_
  20.5 1.4 %collective-permute-start.7 = (bf16[128,512]{1,0:T(8,128)(2,1)S(1)}, bf16[128,512]{1,0:T(8,128)(2,1)S(1)}, u32[]{:S(2)}, u32[]{:S(2)}) collective-permute-start(bf16[128,512]{1,0:T(8,128)(2,1)S(1)} %get-tuple-element.48), channel_id=1, source_target_pairs={{0,6},{1,7},{2,4},{3,5},{4,10},{5,11},{6,8},{7,9},{8,14},{9,15},{1... | collective-permute-start | bytes 393224 | tf_op jit(solution)/shard_map/ppermute | solution.py:199
  21.9 1.3 %collective-permute-done.9.refs_1_ = bf16[128,512]{1,0:T(8,128)(2,1)S(1)} collective-permute-done((bf16[128,512]{1,0:T(8,128)(2,1)S(1)}, bf16[128,512]{1,0:T(8,128)(2,1)S(1)}, u32[]{:S(2)}, u32[]{:S(2)}) %collective-permute-start.9) | collective-permute-done | bytes 131104 | tf_op jit(solution)/shard_map/ppermute | solution.py:199
  23.2 1.5 %collective-permute-done.10.refs_2_ = bf16[256,512]{1,0:T(8,128)(2,1)S(1)} collective-permute-done((bf16[256,512]{1,0:T(8,128)(2,1)S(1)}, bf16[256,512]{1,0:T(8,128)(2,1)S(1)}, u32[]{:S(2)}, u32[]{:S(2)}) %collective-permute-start.10) | collective-permute-done | bytes 262176 | tf_op jit(solution)/shard_map/ppermute | solution.py:199
  24.8 1.5 %users.3 = (bf16[1024,512]{1,0:T(8,128)(2,1)S(1)}, bf16[1024,512]{1,0:T(8,128)(2,1)S(1)}) custom-call(f32[8,128]{1,0:T(8,128)S(1)} %mark.2.refs_0_, bf16[256,512]{1,0:T(8,128)(2,1)S(1)} %get-tuple-element.51.refs_1_, bf16[256,512]{1,0:T(8,128)(2,1)S(1)} %collective-permute-done.10.refs_2_, bf16[1024,512]{1,0:T(8,128)(2,1)S(1)} %copy-done, ...), custom_call_target="tpu_custom_call" | custom-call | flops 1024 | bytes 1024 | tf_op jit(solution)/shard_map/users/pallas_call | solution.py:162
  26.2 1.7 %tiles.8 = (bf16[256,512]{1,0:T(8,128)(2,1)S(1)}, bf16[1024,256]{1,0:T(8,128)(2,1)S(1)}, bf16[1024,256]{1,0:T(8,128)(2,1)S(1)}, bf16[128,512]{1,0:T(8,128)(2,1)S(1)}, bf16[128,512]{1,0:T(8,128)(2,1)S(1)}) custom-call(s32[2]{0:T(128)S(1)} %pad_add_fusion.place.refs_0_, bf16[128,512]{1,0:T(8,128)(2,1)S(1)} %collective-permute-done.8.refs_0_, ...), custom_call_target="tpu_custom_call" | custom-call | flops 1024 | bytes 1024 | tf_op jit(solution)/shard_map/tiles/pallas_call | solution.py:162
  27.9 0.4 collective-permute-start.15
  28.3 2.2 %collective-permute-start.16 = (bf16[128,512]{1,0:T(8,128)(2,1)S(1)}, bf16[128,512]{1,0:T(8,128)(2,1)S(1)}, u32[]{:S(2)}, u32[]{:S(2)}) collective-permute-start(bf16[128,512]{1,0:T(8,128)(2,1)S(1)} %get-tuple-element.64), channel_id=1, source_target_pairs={{0,6},{1,7},{2,4},{3,5},{4,10},{5,11},{6,8},{7,9},{8,14},{9,15},{1... | collective-permute-start | bytes 393224 | tf_op jit(solution)/shard_map/ppermute | solution.py:199
  30.5 1.7 %tiles.9 = (bf16[256,512]{1,0:T(8,128)(2,1)S(1)}, bf16[1024,256]{1,0:T(8,128)(2,1)S(1)}, bf16[1024,256]{1,0:T(8,128)(2,1)S(1)}, bf16[128,512]{1,0:T(8,128)(2,1)S(1)}, bf16[128,512]{1,0:T(8,128)(2,1)S(1)}) custom-call(s32[2]{0:T(128)S(1)} %pad_add_fusion.place.refs_0_, ...), custom_call_target="tpu_custom_call", output_to_operand_aliasing={{0}: (7, {}), {1}: (8, {}), {2}: (9, {})} | custom-call | flops 1024 | bytes 1024 | tf_op jit(solution)/shard_map/tiles/pallas_call | solution.py:162
  32.2 0.1 collective-permute-start.18
  32.2 0.5 collective-permute-start.19
  32.7 1.1 %prepare.5 = (bf16[1024,256]{1,0:T(8,128)(2,1)S(1)}, bf16[1024,256]{1,0:T(8,128)(2,1)S(1)}) custom-call(s32[2]{0:T(128)S(1)} %pad_add_fusion.place.refs_0_, s32[1,1,3,2,8]{4,3,2,1,0:T(2,128)S(1)} %bitcast.6, s32[1,1,3]{2,1,0:T(1,128)S(1)} %copy-done.5, bf16[1,1,3,8,128,128]{5,4,3,2,1,0:T(8,128)(2,1)S(1)} %copy-done.2, ...), custom_call_target="tpu_custom_call" | custom-call | flops 1024 | bytes 1024 | tf_op jit(solution)/shard_map/prepare/pallas_call | solution.py:162
  33.8 1.6 %collective-permute-start.13 = (bf16[128,512]{1,0:T(8,128)(2,1)S(1)}, bf16[128,512]{1,0:T(8,128)(2,1)S(1)}, u32[]{:S(2)}, u32[]{:S(2)}) collective-permute-start(bf16[128,512]{1,0:T(8,128)(2,1)S(1)} %get-tuple-element.61), channel_id=1, source_target_pairs={{0,4},{1,5},{2,6},{3,7},{4,8},{5,9},{6,10},{7,11},{8,12},{9,13},{1... | collective-permute-start | bytes 393224 | tf_op jit(solution)/shard_map/ppermute | solution.py:199
  35.5 1.5 %collective-permute-done.15.refs_0_ = bf16[128,512]{1,0:T(8,128)(2,1)S(1)} collective-permute-done((bf16[128,512]{1,0:T(8,128)(2,1)S(1)}, bf16[128,512]{1,0:T(8,128)(2,1)S(1)}, u32[]{:S(2)}, u32[]{:S(2)}) %collective-permute-start.15) | collective-permute-done | bytes 131104 | tf_op jit(solution)/shard_map/ppermute | solution.py:199
  37.0 2.6 %collective-permute-done.16.refs_1_ = bf16[128,512]{1,0:T(8,128)(2,1)S(1)} collective-permute-done((bf16[128,512]{1,0:T(8,128)(2,1)S(1)}, bf16[128,512]{1,0:T(8,128)(2,1)S(1)}, u32[]{:S(2)}, u32[]{:S(2)}) %collective-permute-start.16) | collective-permute-done | bytes 131104 | tf_op jit(solution)/shard_map/ppermute | solution.py:199
  39.6 1.5 %collective-permute-done.17.refs_2_ = bf16[256,512]{1,0:T(8,128)(2,1)S(1)} collective-permute-done((bf16[256,512]{1,0:T(8,128)(2,1)S(1)}, bf16[256,512]{1,0:T(8,128)(2,1)S(1)}, u32[]{:S(2)}, u32[]{:S(2)}) %collective-permute-start.17) | collective-permute-done | bytes 262176 | tf_op jit(solution)/shard_map/ppermute | solution.py:199
  41.2 1.5 %users.4 = (bf16[1024,512]{1,0:T(8,128)(2,1)S(1)}, bf16[1024,512]{1,0:T(8,128)(2,1)S(1)}) custom-call(f32[8,128]{1,0:T(8,128)S(1)} %mark.3.refs_0_, bf16[256,512]{1,0:T(8,128)(2,1)S(1)} %get-tuple-element.65.refs_1_, bf16[256,512]{1,0:T(8,128)(2,1)S(1)} %collective-permute-done.17.refs_2_, bf16[1024,512]{1,0:T(8,128)(2,1)S(1)} %get-tuple-element.54.refs_2_.refs_3_, ...), custom_call_target="tpu_custom_call" | custom-call | flops 1024 | bytes 1024 | tf_op jit(solution)/shard_map/users/pallas_call | solution.py:162
  42.6 1.7 %tiles.10 = (bf16[256,512]{1,0:T(8,128)(2,1)S(1)}, bf16[1024,256]{1,0:T(8,128)(2,1)S(1)}, bf16[1024,256]{1,0:T(8,128)(2,1)S(1)}, f32[128,512]{1,0:T(8,128)S(1)}, bf16[128,512]{1,0:T(8,128)(2,1)S(1)}) custom-call(s32[2]{0:T(128)S(1)} %pad_add_fusion.place.refs_0_, bf16[128,512]{1,0:T(8,128)(2,1)S(1)} %collective-permute-done.15.refs_0_, ...), custom_call_target="tpu_custom_call" | custom-call | flops 1024 | bytes 1024 | tf_op jit(solution)/shard_map/tiles/pallas_call | solution.py:162
  44.3 1.2 %collective-permute-done.14.refs_1_ = bf16[128,512]{1,0:T(8,128)(2,1)S(1)} collective-permute-done((bf16[128,512]{1,0:T(8,128)(2,1)S(1)}, bf16[128,512]{1,0:T(8,128)(2,1)S(1)}, u32[]{:S(2)}, u32[]{:S(2)}) %collective-permute-start.14) | collective-permute-done | bytes 131104 | tf_op jit(solution)/shard_map/ppermute | solution.py:199
  45.6 1.7 %tiles.11 = (bf16[256,512]{1,0:T(8,128)(2,1)S(1)}, bf16[1024,256]{1,0:T(8,128)(2,1)S(1)}, bf16[1024,256]{1,0:T(8,128)(2,1)S(1)}, f32[128,512]{1,0:T(8,128)S(1)}, bf16[128,512]{1,0:T(8,128)(2,1)S(1)}) custom-call(s32[2]{0:T(128)S(1)} %pad_add_fusion.place.refs_0_, ...), custom_call_target="tpu_custom_call", output_to_operand_aliasing={{0}: (7, {}), {1}: (8, {}), {2}: (9, {}), {3}: (10, {}), {4... | custom-call | flops 1024 | bytes 1024 | tf_op jit(solution)/shard_map/tiles/pallas_call | solution.py:162
  47.3 0.1 collective-permute-start.21
  47.3 0.5 collective-permute-start.20
  47.8 1.2 %collective-permute-start.22 = (bf16[128,512]{1,0:T(8,128)(2,1)S(1)}, bf16[128,512]{1,0:T(8,128)(2,1)S(1)}, u32[]{:S(2)}, u32[]{:S(2)}) collective-permute-start(bf16[128,512]{1,0:T(8,128)(2,1)S(1)} %get-tuple-element.81), channel_id=1, source_target_pairs={{0,2},{1,3},{2,0},{3,1},{4,6},{5,7},{6,4},{7,5},{8,10},{9,11},{10,... | collective-permute-start | bytes 393224 | tf_op jit(solution)/shard_map/ppermute | solution.py:199
  49.0 0.6 %collective-permute-done.20.refs_2_ = bf16[256,512]{1,0:T(8,128)(2,1)S(1)} collective-permute-done((bf16[256,512]{1,0:T(8,128)(2,1)S(1)}, bf16[256,512]{1,0:T(8,128)(2,1)S(1)}, u32[]{:S(2)}, u32[]{:S(2)}) %collective-permute-start.20) | collective-permute-done | bytes 262176 | tf_op jit(solution)/shard_map/ppermute | solution.py:199
  49.6 2.3 %users.5.refs_2_ = bf16[1024,512]{1,0:T(8,128)(2,1)} custom-call(s32[2]{0:T(128)S(1)} %pad_add_fusion.place.refs_0_, bf16[256,512]{1,0:T(8,128)(2,1)S(1)} %get-tuple-element.77.refs_1_, bf16[256,512]{1,0:T(8,128)(2,1)S(1)} %collective-permute-done.20.refs_2_, bf16[1024,512]{1,0:T(8,128)(2,1)S(1)} %get-tuple-element.68.refs_2_.refs_3_, ...), custom_call_target="tpu_custom_call" | custom-call | flops 1024 | bytes 1024 | tf_op jit(solution)/shard_map/users/pallas_call | solution.py:162
  51.9 1.4 %collective-permute-done.22.refs_1_ = bf16[128,512]{1,0:T(8,128)(2,1)S(1)} collective-permute-done((bf16[128,512]{1,0:T(8,128)(2,1)S(1)}, bf16[128,512]{1,0:T(8,128)(2,1)S(1)}, u32[]{:S(2)}, u32[]{:S(2)}) %collective-permute-start.22) | collective-permute-done | bytes 131104 | tf_op jit(solution)/shard_map/ppermute | solution.py:199
  53.3 0.7 %final.1 = f32[128,512]{1,0:T(8,128)} custom-call(f32[128,512]{1,0:T(8,128)S(1)} %get-tuple-element.80.refs_0_, bf16[128,512]{1,0:T(8,128)(2,1)S(1)} %collective-permute-done.22.refs_1_, bf16[1024,512]{1,0:T(8,128)(2,1)} %users.5.refs_2_), custom_call_target="tpu_custom_call" | custom-call | flops 1024 | bytes 1024 | tf_op jit(solution)/shard_map/final/pallas_call | solution.py:162
  (27 shorter events, 0.1 us)
Async XLA Ops:
  0.6 7.0 %copy-start.3 = (s32[1,1,3,8,16,128]{5,4,3,2,1,0:T(8,128)S(1)}, s32[1,1,3,8,16,128]{5,4,3,2,1,0:T(8,128)}, u32[]{:S(2)}) copy-start(s32[1,1,3,8,16,128]{5,4,3,2,1,0:T(8,128)} %refs_3_.7) | copy-start | bytes 589828
  0.6 4.7 %copy-start.5 = (s32[1,1,3]{2,1,0:T(1,128)S(1)}, s32[1,1,3]{2,1,0:T(1,128)}, u32[]{:S(2)}) copy-start(s32[1,1,3]{2,1,0:T(1,128)} %refs_1_.5) | copy-start | bytes 40
  0.7 9.1 %collective-permute-start.1 = (bf16[1024,512]{1,0:T(8,128)(2,1)}, bf16[1024,512]{1,0:T(8,128)(2,1)S(1)}, u32[]{:S(2)}, u32[]{:S(2)}) collective-permute-start(bf16[1024,512]{1,0:T(8,128)(2,1)} %refs_3_.5), channel_id=1, source_target_pairs={{0,1},{1,0},{2,3},{3,2},{4,5},{5,4},{6,7},{7,6},{8,9},{9,8},{10,11... | collective-permute-start | bytes 3145736 | tf_op jit(solution)/shard_map/ppermute | solution.py:199
  1.2 6.5 %collective-permute-start.4 = (bf16[1,1,3,8,128,128]{5,4,3,2,1,0:T(8,128)(2,1)}, bf16[1,1,3,8,128,128]{5,4,3,2,1,0:T(8,128)(2,1)S(1)}, u32[]{:S(2)}, u32[]{:S(2)}) collective-permute-start(bf16[1,1,3,8,128,128]{5,4,3,2,1,0:T(8,128)(2,1)} %refs_2_.9), channel_id=1, source_target_pairs={{0,1},{1,0},{2,3},{3,2},{4,5},{5,4},{6,7},{7,6},{8,9},{9,8},{10,11... | collective-permute-start | bytes 2359304 | tf_op jit(solution)/shard_map/ppermute | solution.py:199
  1.2 6.4 %collective-permute-start.5 = (s32[1,1,3,8,16,128]{5,4,3,2,1,0:T(8,128)}, s32[1,1,3,8,16,128]{5,4,3,2,1,0:T(8,128)S(1)}, u32[]{:S(2)}, u32[]{:S(2)}) collective-permute-start(s32[1,1,3,8,16,128]{5,4,3,2,1,0:T(8,128)} %refs_3_.7), channel_id=1, source_target_pairs={{0,1},{1,0},{2,3},{3,2},{4,5},{5,4},{6,7},{7,6},{8,9},{9,8},{10,11... | collective-permute-start | bytes 589832 | tf_op jit(solution)/shard_map/ppermute | solution.py:199
  1.7 4.8 %copy-start.4 = (s32[1,1,3,8,2]{3,4,2,1,0:T(2,128)S(1)}, s32[1,1,3,8,2]{3,4,2,1,0:T(2,128)}, u32[]{:S(2)}) copy-start(s32[1,1,3,8,2]{3,4,2,1,0:T(2,128)} %param.8) | copy-start | bytes 580
  2.7 7.1 %copy-start = (bf16[1024,512]{1,0:T(8,128)(2,1)S(1)}, bf16[1024,512]{1,0:T(8,128)(2,1)}, u32[]{:S(2)}) copy-start(bf16[1024,512]{1,0:T(8,128)(2,1)} %refs_3_.5) | copy-start | bytes 3145732
  2.7 7.1 %collective-permute-start = (bf16[128,512]{1,0:T(8,128)(2,1)S(1)}, bf16[128,512]{1,0:T(8,128)(2,1)S(1)}, u32[]{:S(2)}, u32[]{:S(2)}) collective-permute-start(bf16[128,512]{1,0:T(8,128)(2,1)S(1)} %convert_element_type.3.refs_0_), channel_id=1, source_target_pairs={{0,2},{1,3},{2,0},{3,1},{4,6},{5,7},{6,4},{7,5},{8,10},{9,11},{10,... | collective-permute-start | bytes 393224 | tf_op jit(solution)/shard_map/ppermute | solution.py:199
  5.3 1.1 %collective-permute-start.3 = (s32[1,1,3]{2,1,0:T(1,128)S(1)}, s32[1,1,3]{2,1,0:T(1,128)S(1)}, u32[]{:S(2)}, u32[]{:S(2)}) collective-permute-start(s32[1,1,3]{2,1,0:T(1,128)S(1)} %copy-done.5), channel_id=1, source_target_pairs={{0,1},{1,0},{2,3},{3,2},{4,5},{5,4},{6,7},{7,6},{8,9},{9,8},{10,11... | collective-permute-start | bytes 44 | tf_op jit(solution)/shard_map/ppermute | solution.py:199
  6.5 1.2 %collective-permute-start.2 = (s32[1,1,3,2,8]{4,3,2,1,0:T(2,128)S(1)}, s32[1,1,3,2,8]{4,3,2,1,0:T(2,128)S(1)}, u32[]{:S(2)}, u32[]{:S(2)}) collective-permute-start(s32[1,1,3,2,8]{4,3,2,1,0:T(2,128)S(1)} %bitcast.3), channel_id=1, source_target_pairs={{0,1},{1,0},{2,3},{3,2},{4,5},{5,4},{6,7},{7,6},{8,9},{9,8},{10,11... | collective-permute-start | bytes 584 | tf_op jit(solution)/shard_map/ppermute | solution.py:199
  7.6 1.1 %copy-start.1 = (bf16[1,1,3,8,128,128]{5,4,3,2,1,0:T(8,128)(2,1)S(1)}, bf16[1,1,3,8,128,128]{5,4,3,2,1,0:T(8,128)(2,1)}, u32[]{:S(2)}) copy-start(bf16[1,1,3,8,128,128]{5,4,3,2,1,0:T(8,128)(2,1)} %refs_2_.9) | copy-start | bytes 2359300
  11.5 9.0 %collective-permute-start.8 = (bf16[128,512]{1,0:T(8,128)(2,1)S(1)}, bf16[128,512]{1,0:T(8,128)(2,1)S(1)}, u32[]{:S(2)}, u32[]{:S(2)}) collective-permute-start(bf16[128,512]{1,0:T(8,128)(2,1)S(1)} %get-tuple-element.49), channel_id=1, source_target_pairs={{0,4},{1,5},{2,6},{3,7},{4,8},{5,9},{6,10},{7,11},{8,12},{9,13},{1... | collective-permute-start | bytes 393224 | tf_op jit(solution)/shard_map/ppermute | solution.py:199
  13.1 10.1 %collective-permute-start.9 = (bf16[128,512]{1,0:T(8,128)(2,1)S(1)}, bf16[128,512]{1,0:T(8,128)(2,1)S(1)}, u32[]{:S(2)}, u32[]{:S(2)}) collective-permute-start(bf16[128,512]{1,0:T(8,128)(2,1)S(1)} %get-tuple-element.50), channel_id=1, source_target_pairs={{0,6},{1,7},{2,4},{3,5},{4,10},{5,11},{6,8},{7,9},{8,14},{9,15},{1... | collective-permute-start | bytes 393224 | tf_op jit(solution)/shard_map/ppermute | solution.py:199
  15.4 2.3 %copy-start.2 = (bf16[1,1,3,8,128,128]{5,4,3,2,1,0:T(8,128)(2,1)S(1)}, bf16[1,1,3,8,128,128]{5,4,3,2,1,0:T(8,128)(2,1)}, u32[]{:S(2)}) copy-start(bf16[1,1,3,8,128,128]{5,4,3,2,1,0:T(8,128)(2,1)} %refs_2_.9) | copy-start | bytes 2359300
  17.1 7.6 %collective-permute-start.11 = (bf16[1024,256]{1,0:T(8,128)(2,1)S(1)}, bf16[1024,256]{1,0:T(8,128)(2,1)S(1)}, u32[]{:S(2)}, u32[]{:S(2)}) collective-permute-start(bf16[1024,256]{1,0:T(8,128)(2,1)S(1)} %get-tuple-element.53.refs_7_), channel_id=1, source_target_pairs={{0,1},{1,0},{2,3},{3,2},{4,5},{5,4},{6,7},{7,6},{8,9},{9,8},{10,11... | collective-permute-start | bytes 1572872 | tf_op jit(solution)/shard_map/ppermute | solution.py:199
  17.2 7.5 %collective-permute-start.12 = (bf16[1024,256]{1,0:T(8,128)(2,1)S(1)}, bf16[1024,256]{1,0:T(8,128)(2,1)S(1)}, u32[]{:S(2)}, u32[]{:S(2)}) collective-permute-start(bf16[1024,256]{1,0:T(8,128)(2,1)S(1)} %get-tuple-element.52.refs_4_), channel_id=1, source_target_pairs={{0,1},{1,0},{2,3},{3,2},{4,5},{5,4},{6,7},{7,6},{8,9},{9,8},{10,11... | collective-permute-start | bytes 1572872 | tf_op jit(solution)/shard_map/ppermute | solution.py:199
  18.7 11.7 %collective-permute-start.6 = (bf16[128,512]{1,0:T(8,128)(2,1)S(1)}, bf16[128,512]{1,0:T(8,128)(2,1)S(1)}, u32[]{:S(2)}, u32[]{:S(2)}) collective-permute-start(bf16[128,512]{1,0:T(8,128)(2,1)S(1)} %get-tuple-element.47), channel_id=1, source_target_pairs={{0,4},{1,5},{2,6},{3,7},{4,8},{5,9},{6,10},{7,11},{8,12},{9,13},{1... | collective-permute-start | bytes 393224 | tf_op jit(solution)/shard_map/ppermute | solution.py:199
  20.5 9.9 %collective-permute-start.7 = (bf16[128,512]{1,0:T(8,128)(2,1)S(1)}, bf16[128,512]{1,0:T(8,128)(2,1)S(1)}, u32[]{:S(2)}, u32[]{:S(2)}) collective-permute-start(bf16[128,512]{1,0:T(8,128)(2,1)S(1)} %get-tuple-element.48), channel_id=1, source_target_pairs={{0,6},{1,7},{2,4},{3,5},{4,10},{5,11},{6,8},{7,9},{8,14},{9,15},{1... | collective-permute-start | bytes 393224 | tf_op jit(solution)/shard_map/ppermute | solution.py:199
  23.2 1.5 %collective-permute-start.10 = (bf16[256,512]{1,0:T(8,128)(2,1)S(1)}, bf16[256,512]{1,0:T(8,128)(2,1)S(1)}, u32[]{:S(2)}, u32[]{:S(2)}) collective-permute-start(bf16[256,512]{1,0:T(8,128)(2,1)S(1)} %get-tuple-element.51.refs_1_), channel_id=1, source_target_pairs={{0,1},{1,0},{2,3},{3,2},{4,5},{5,4},{6,7},{7,6},{8,9},{9,8},{10,11... | collective-permute-start | bytes 786440 | tf_op jit(solution)/shard_map/ppermute | solution.py:199
  27.9 9.1 %collective-permute-start.15 = (bf16[128,512]{1,0:T(8,128)(2,1)S(1)}, bf16[128,512]{1,0:T(8,128)(2,1)S(1)}, u32[]{:S(2)}, u32[]{:S(2)}) collective-permute-start(bf16[128,512]{1,0:T(8,128)(2,1)S(1)} %get-tuple-element.63), channel_id=1, source_target_pairs={{0,4},{1,5},{2,6},{3,7},{4,8},{5,9},{6,10},{7,11},{8,12},{9,13},{1... | collective-permute-start | bytes 393224 | tf_op jit(solution)/shard_map/ppermute | solution.py:199
  28.3 11.3 %collective-permute-start.16 = (bf16[128,512]{1,0:T(8,128)(2,1)S(1)}, bf16[128,512]{1,0:T(8,128)(2,1)S(1)}, u32[]{:S(2)}, u32[]{:S(2)}) collective-permute-start(bf16[128,512]{1,0:T(8,128)(2,1)S(1)} %get-tuple-element.64), channel_id=1, source_target_pairs={{0,6},{1,7},{2,4},{3,5},{4,10},{5,11},{6,8},{7,9},{8,14},{9,15},{1... | collective-permute-start | bytes 393224 | tf_op jit(solution)/shard_map/ppermute | solution.py:199
  32.2 9.0 %collective-permute-start.18 = (bf16[1024,256]{1,0:T(8,128)(2,1)S(1)}, bf16[1024,256]{1,0:T(8,128)(2,1)S(1)}, u32[]{:S(2)}, u32[]{:S(2)}) collective-permute-start(bf16[1024,256]{1,0:T(8,128)(2,1)S(1)} %get-tuple-element.67.refs_7_), channel_id=1, source_target_pairs={{0,1},{1,0},{2,3},{3,2},{4,5},{5,4},{6,7},{7,6},{8,9},{9,8},{10,11... | collective-permute-start | bytes 1572872 | tf_op jit(solution)/shard_map/ppermute | solution.py:199
  32.2 8.9 %collective-permute-start.19 = (bf16[1024,256]{1,0:T(8,128)(2,1)S(1)}, bf16[1024,256]{1,0:T(8,128)(2,1)S(1)}, u32[]{:S(2)}, u32[]{:S(2)}) collective-permute-start(bf16[1024,256]{1,0:T(8,128)(2,1)S(1)} %get-tuple-element.66.refs_4_), channel_id=1, source_target_pairs={{0,1},{1,0},{2,3},{3,2},{4,5},{5,4},{6,7},{7,6},{8,9},{9,8},{10,11... | collective-permute-start | bytes 1572872 | tf_op jit(solution)/shard_map/ppermute | solution.py:199
  33.8 10.5 %collective-permute-start.13 = (bf16[128,512]{1,0:T(8,128)(2,1)S(1)}, bf16[128,512]{1,0:T(8,128)(2,1)S(1)}, u32[]{:S(2)}, u32[]{:S(2)}) collective-permute-start(bf16[128,512]{1,0:T(8,128)(2,1)S(1)} %get-tuple-element.61), channel_id=1, source_target_pairs={{0,4},{1,5},{2,6},{3,7},{4,8},{5,9},{6,10},{7,11},{8,12},{9,13},{1... | collective-permute-start | bytes 393224 | tf_op jit(solution)/shard_map/ppermute | solution.py:199
  37.0 8.6 %collective-permute-start.14 = (bf16[128,512]{1,0:T(8,128)(2,1)S(1)}, bf16[128,512]{1,0:T(8,128)(2,1)S(1)}, u32[]{:S(2)}, u32[]{:S(2)}) collective-permute-start(bf16[128,512]{1,0:T(8,128)(2,1)S(1)} %get-tuple-element.62), channel_id=1, source_target_pairs={{0,6},{1,7},{2,4},{3,5},{4,10},{5,11},{6,8},{7,9},{8,14},{9,15},{1... | collective-permute-start | bytes 393224 | tf_op jit(solution)/shard_map/ppermute | solution.py:199
  39.6 1.5 %collective-permute-start.17 = (bf16[256,512]{1,0:T(8,128)(2,1)S(1)}, bf16[256,512]{1,0:T(8,128)(2,1)S(1)}, u32[]{:S(2)}, u32[]{:S(2)}) collective-permute-start(bf16[256,512]{1,0:T(8,128)(2,1)S(1)} %get-tuple-element.65.refs_1_), channel_id=1, source_target_pairs={{0,1},{1,0},{2,3},{3,2},{4,5},{5,4},{6,7},{7,6},{8,9},{9,8},{10,11... | collective-permute-start | bytes 786440 | tf_op jit(solution)/shard_map/ppermute | solution.py:199
  47.3 2.4 %collective-permute-start.21 = (bf16[1024,256]{1,0:T(8,128)(2,1)S(1)}, bf16[1024,256]{1,0:T(8,128)(2,1)S(1)}, u32[]{:S(2)}, u32[]{:S(2)}) collective-permute-start(bf16[1024,256]{1,0:T(8,128)(2,1)S(1)} %get-tuple-element.79), channel_id=1, source_target_pairs={{0,1},{1,0},{2,3},{3,2},{4,5},{5,4},{6,7},{7,6},{8,9},{9,8},{10,11... | collective-permute-start | bytes 1572872 | tf_op jit(solution)/shard_map/ppermute | solution.py:199
  47.3 2.3 %collective-permute-start.20 = (bf16[256,512]{1,0:T(8,128)(2,1)S(1)}, bf16[256,512]{1,0:T(8,128)(2,1)S(1)}, u32[]{:S(2)}, u32[]{:S(2)}) collective-permute-start(bf16[256,512]{1,0:T(8,128)(2,1)S(1)} %get-tuple-element.77.refs_1_), channel_id=1, source_target_pairs={{0,1},{1,0},{2,3},{3,2},{4,5},{5,4},{6,7},{7,6},{8,9},{9,8},{10,11... | collective-permute-start | bytes 786440 | tf_op jit(solution)/shard_map/ppermute | solution.py:199
  47.8 5.5 %collective-permute-start.22 = (bf16[128,512]{1,0:T(8,128)(2,1)S(1)}, bf16[128,512]{1,0:T(8,128)(2,1)S(1)}, u32[]{:S(2)}, u32[]{:S(2)}) collective-permute-start(bf16[128,512]{1,0:T(8,128)(2,1)S(1)} %get-tuple-element.81), channel_id=1, source_target_pairs={{0,2},{1,3},{2,0},{3,1},{4,6},{5,7},{6,4},{7,5},{8,10},{9,11},{10,... | collective-permute-start | bytes 393224 | tf_op jit(solution)/shard_map/ppermute | solution.py:199

commit v4 on v2

v4 whole, which is shorter than its diff:
```python
import functools

import jax
import jax.numpy as jnp
from jax import lax
from jax.experimental import pallas as pl
from jax.experimental.pallas import tpu as pltpu
from jax.sharding import PartitionSpec as P

step_user = 0.05
step_item = 0.004
shrinkage = 0.05

VM = pl.BlockSpec(memory_space=pltpu.VMEM)
SM = pl.BlockSpec(memory_space=pltpu.SMEM)
HB = pl.BlockSpec(memory_space=pltpu.HBM)
CORES = 2
CHUNK = 512


def place_of(close, chip, core, rows):
    return pl.multiple_of((chip if close else CORES * chip + core) * rows, rows)


def multiply(a, b, across, over):
    return lax.dot_general(a, b, (((across,), (over,)), ((), ())), preferred_element_type=jnp.float32)


def observed(words):
    count, lanes = words.shape
    shift = lax.broadcasted_iota(jnp.int32, (8, lanes), 0)
    parts = [
        jnp.bitwise_and(jnp.right_shift(jnp.broadcast_to(words[i : i + 1], (8, lanes)), shift), 1)
        for i in range(count)
    ]
    return jnp.concatenate(parts, 0) != 0


def prepare_kernel(visit, rows, close, place, *refs):
    sets = len(refs) // 5
    for i in range(sets):
        lay_out(visit, rows, close, place[0], *refs[4 * i : 4 * i + 4], refs[4 * sets + i])


def lay_out(visit, rows, close, core, blocks, counts, rates, words, keep):
    side = rates.shape[-1]
    nothing = jnp.full((side, side), jnp.nan, keep.dtype)
    for at in range(0, keep.shape[0], side):
        for lane in range(0, keep.shape[1], side):
            keep[at : at + side, lane : lane + side] = nothing

    def tile(k, carry):
        users = pl.ds(pl.multiple_of(blocks[0, 0, visit, 0, k] * side, side), side)
        first = blocks[0, 0, visit, 1, k] * side
        seen = observed(words[0, 0, visit, k])
        known = jnp.where(seen, rates[0, 0, visit, k].astype(jnp.float32), jnp.nan)
        if close:
            piece = lax.div(first, rows)
            at = lax.div(piece, CORES) * rows + lax.rem(first, rows)
            at = pl.ds(pl.multiple_of(at, side), side)
            known = known.astype(keep.dtype)

            @pl.when(lax.rem(piece, CORES) == core)
            def _():
                keep[users, at] = known
        else:
            at = pl.ds(pl.multiple_of(first, side), side)
            piece = lax.div(first + lax.broadcasted_iota(jnp.int32, known.shape, 1), rows)
            mine = lax.rem(piece, CORES) == core
            keep[users, at] = jnp.where(mine, known, jnp.nan).astype(keep.dtype)
        return carry

    lax.fori_loop(0, counts[0, 0, visit], tile, 0)


def tiles_kernel(first, last, chips, groups, close, place, *refs):
    count = chips if first else chips + groups - 1
    arrived, refs = refs[:count], refs[count:]
    (users, peers, rates, peer_rates), refs = refs[:4], refs[4:]
    (low, errors, peer_errors), outs, (panel, total) = refs[:3], refs[3:-2], refs[-2:]
    span = chips // groups
    core, chip = place[0], place[1]
    rows = panel.shape[0] // chips
    if first:
        for k in range(chips):
            origin = lax.rem(chip + chips - k, chips)
            at = pl.multiple_of(origin * rows, rows)
            panel[pl.ds(at, rows), :] = arrived[k][...].astype(jnp.float32)
    else:
        now = arrived[0][...].astype(jnp.float32)
        for other in arrived[1:chips]:
            now = now + step_item * other[...].astype(jnp.float32)
        panel[: span * rows, :] = now
        if groups > 1:
            panel[span * rows :, :] = arrived[chips][...].astype(jnp.float32)
    if close:
        low[...] = panel[...].astype(low.dtype)
    else:
        low[...] = jnp.zeros_like(low)
        for j in range(chips):
            low[pl.ds(place_of(close, j, core, rows), rows), :] = panel[
                j * rows : (j + 1) * rows, :
            ].astype(low.dtype)
    held = low.shape[0]
    for i in range(low.shape[1] // held):
        below = peers.shape[0] + i * held
        peer_errors[below : below + held, :] = low[:, i * held : (i + 1) * held]
    for who, known, error in ((users, rates, errors), (peers, peer_rates, peer_errors)):
        for at in range(0, who.shape[0], CHUNK):
            cut = slice(at, at + CHUNK)
            predicted = multiply(who[cut, :], low[...], 1, 1)
            rating = known[cut, :].astype(jnp.float32)
            error[cut, :] = jnp.where(rating == rating, rating - predicted, 0.0).astype(error.dtype)
    total[...] = multiply(errors[...], users[...], 0, 0)
    total[...] += multiply(peer_errors[: peers.shape[0], :], peers[...], 0, 0)
    if last:
        for k in range(chips):
            owner = lax.rem(chip + k, chips)
            term = total[pl.ds(place_of(close, owner, core, rows), rows), :]
            if k == 0:
                old = panel[pl.ds(pl.multiple_of(owner * rows, rows), rows), :]
                term = old + step_item * (term - shrinkage * old)
            outs[k][...] = term.astype(outs[k].dtype)
    else:
        for j in range(chips):
            joined, plain = outs[2 * (j // span)], outs[2 * (j // span) + 1]
            at, to = slice(j * rows, (j + 1) * rows), slice(j % span * rows, (j % span + 1) * rows)
            term = total[pl.ds(place_of(close, j, core, rows), rows), :]
            old = panel[at, :]
            joined[to, :] = (old + step_item * (term - shrinkage * old)).astype(joined.dtype)
            plain[to, :] = term.astype(plain.dtype)


def users_kernel(last, _, low, *refs):
    if last:
        users, errors, other_errors, out = refs
        sets = [(users, errors, other_errors, out)]
        lows = other_errors
    else:
        users, peers, errors, peer_errors, from_errors, from_peer_errors, out, peer_out = refs
        sets = [(users, errors, from_peer_errors, out), (peers, peer_errors, from_errors, peer_out)]
        lows = from_peer_errors
    held, width = low.shape
    for users, errors, other_errors, out in sets:
        count = users.shape[0]
        for at in range(0, count, CHUNK):
            cut = slice(at, at + CHUNK)
            for lane in range(0, width, held):
                to = slice(lane, lane + held)
                below = pl.ds(count + lane, held)
                grad = multiply(errors[cut, :], low[:, to], 1, 0)
                grad = grad + multiply(other_errors[cut, :], lows[below, :], 1, 0)
                factor = users[cut, to].astype(jnp.float32)
                out[cut, to] = (factor + step_user * (grad - shrinkage * factor)).astype(out.dtype)


def final_kernel(count, *refs):
    refs = refs[:count] + refs[-1:]
    total = refs[0][...]
    for other in refs[1:count]:
        total = total + step_item * other[...].astype(jnp.float32)
    refs[count][...] = total.astype(refs[count].dtype)


def kernel_call(body, name, ins, outs, flops, scratch=(), extra=(), aliases=()):
    return pl.pallas_call(
        body,
        name=name,
        out_shape=tuple(outs),
        in_specs=[SM if x.dtype == jnp.int32 and x.ndim != 6 else VM for x in ins] + [HB] * len(extra),
        out_specs=(VM,) * len(outs),
        scratch_shapes=list(scratch),
        input_output_aliases=dict(aliases),
        compiler_params=pltpu.CompilerParams(vmem_limit_bytes=16 << 20),
        cost_estimate=pl.CostEstimate(flops=flops, bytes_accessed=1024, transcendentals=0),
    )(*ins, *[pltpu.with_memory_space_constraint(x, pltpu.HBM) for x in extra])


def moved(x, by_strata, by_chip, flip, *, strata, peers):
    pairs = []
    for s in range(strata):
        for h in range(peers):
            chip, core = divmod(h, CORES)
            chip = (chip + by_chip) % (peers // CORES)
            core = 1 - core if flip else core
            pairs.append((s * peers + h, (s + by_strata) % strata * peers + chip * CORES + core))
    return lax.ppermute(x, ("strata", "shard"), pairs)


def shards(user_factors, item_factors, tile_blocks, tile_counts, ratings, mask_words):
    low_type, full_type = jnp.bfloat16, jnp.float32
    strata, peers = lax.axis_size("strata"), lax.axis_size("shard")
    chips = peers // CORES
    move = functools.partial(moved, strata=strata, peers=peers)
    swap = lambda x: move(x, 0, 0, True)
    visits = tile_counts.shape[-1]
    side = ratings.shape[-1]
    rows, width = item_factors.shape
    count = user_factors.shape[0]
    close = rows % side == 0
    held = (chips if close else peers) * rows
    part = chips * rows
    me = lax.axis_index("shard")
    place = jnp.stack([lax.rem(me, CORES), lax.div(me, CORES)]).astype(jnp.int32)
    blocks = jnp.swapaxes(tile_blocks, 3, 4)

    def prepared(visit, *sets):
        return kernel_call(
            functools.partial(prepare_kernel, visit, rows, close),
            "prepare",
            [place, *(x for one in sets for x in one)],
            [pltpu.VMEM((count, held), low_type)] * len(sets),
            1024,
        )

    panel_low = item_factors.astype(low_type)
    arrived = [panel_low] + [move(panel_low, 0, k, False) for k in range(1, chips)]
    users, other_users = user_factors, swap(user_factors)
    tiles = [blocks, tile_counts, ratings, mask_words]
    other_tiles = [swap(x) for x in tiles]
    groups = 2 if chips % 2 == 0 else 1
    part = part // groups
    for visit in range(visits):
        last = visit + 1 == visits
        if visit == 0:
            known = [*prepared(visit, tiles), *prepared(visit, other_tiles)]
        else:
            known = prepared(visit, tiles, other_tiles)
        shared = [pltpu.VMEM((held, width), low_type)]
        shared += [pltpu.VMEM((count, held), low_type), pltpu.VMEM((count + width, held), low_type)]
        if last:
            shared += [pltpu.VMEM((rows, width), full_type)]
            shared += [pltpu.VMEM((rows, width), low_type)] * (chips - 1)
        if not last:
            for group in range(groups):
                shared += [pltpu.VMEM((part, width), full_type if group else low_type)]
                shared += [pltpu.VMEM((part, width), low_type)]
        low, errors, other_errors, *ends = kernel_call(
            functools.partial(tiles_kernel, visit == 0, last, chips, groups, close),
            "tiles",
            [place, *arrived, users, other_users, *known],
            shared,
            1024,
            [pltpu.VMEM((chips * rows, width), full_type), pltpu.VMEM((held, width), full_type)],
        )
        if last:
            arrived = ends[:1] + [move(ends[k], 0, k, False) for k in range(1, chips)]
            sets = [place, low, users, errors, swap(other_errors)]
        else:
            if groups > 1:
                others = [move(ends[3], 0, k, False) for k in range(1, chips)]
            arrived = [move(ends[min(k, 1)], 1, k, False) for k in range(chips)]
            if groups > 1:
                (summed,) = kernel_call(
                    functools.partial(final_kernel, chips),
                    "join",
                    [ends[2], *others],
                    [pltpu.VMEM((part, width), low_type)],
                    1024,
                )
                arrived += [move(summed, 1, 0, False)]
            sets = [place, low, users, other_users]
            sets += [errors, other_errors, swap(errors), swap(other_errors)]
        kind = jax.ShapeDtypeStruct if last else pltpu.VMEM
        users, *other_users = kernel_call(
            functools.partial(users_kernel, last),
            "users",
            sets,
            [kind((count, width), low_type)] * (1 if last else 2),
            1024,
        )
        if not last:
            other_users = other_users[0]
    (panel,) = kernel_call(
        functools.partial(final_kernel, chips),
        "final",
        arrived,
        [jax.ShapeDtypeStruct((rows, width), full_type)],
        1024,
        extra=[users],
    )
    return (users, panel)


def solution(mesh):
    placed = (
        P(("strata", "shard"), None),
        P(("strata", "shard"), None),
        P("strata", "shard", None, None, None),
        P("strata", "shard", None),
        P("strata", "shard", None, None, None, None),
        P("strata", "shard", None, None, None, None),
    )
    return jax.shard_map(
        shards,
        mesh=mesh,
        in_specs=placed,
        out_specs=(P(("strata", "shard"), None), P(("strata", "shard"), None)),
        check_vma=False,
    )
```

time: 61.5 us -> 53.2 us (0.87)
  waiting for transfers between devices: 31.8 us -> 17.9 us
  starting transfers between devices: 11.7 us -> 15.3 us
  Pallas kernels: 15.3 us -> 16.4 us
  local copies, waits for them, and re-layouts: 0.69 us -> 1.53 us
    ppermute x18 -> x20, waiting for transfers between devices: 31.8 us -> 17.9 us  [moved(): return lax.ppermute(x, ('strata', 'shard'), pairs)]
    ppermute x18 -> x20, starting transfers between devices: 11.7 us -> 15.3 us  [moved(): return lax.ppermute(x, ('strata', 'shard'), pairs)]
    pallas_call x11 -> x13, Pallas kernels: 15.3 us -> 16.4 us  [kernel_call(): pl.pallas_call(body, name=name, out_shape=tuple(outs), in_specs=[SM if x....]
    unnamed x4 -> x12, local copies, waits for them, and re-layouts: 0.69 us -> 1.53 us
  transfers between devices with their start and end apart: 18 -> 20, of which waited for: 8 -> 11; matrix products, arithmetic and copies ran while one was open for 0% -> 2% of each run, Pallas kernels for 15% -> 19%
where the time goes in v4:
time: 53.2 us; the launch traced here: 53 us
  waiting for transfers between devices  17.9 us (34%)
  Pallas kernels  16.4 us (31%)
  starting transfers between devices  15.3 us (29%)
  local copies, waits for them, and re-layouts  1.53 us (3%)
  other arithmetic  1.04 us (2%)
  between operations  0.84 us (2%)
    ppermute x20, waiting for transfers between devices, moved(): return lax.ppermute(x, ('strata', 'shard'), pairs)  17.9 us
    pallas_call x13, Pallas kernels, kernel_call(): pl.pallas_call(body, name=name, out_shape=tuple(outs), in_specs=[SM if x....  16.4 us
    ppermute x20, starting transfers between devices, moved(): return lax.ppermute(x, ('strata', 'shard'), pairs)  15.3 us
    unnamed x12, local copies, waits for them, and re-layouts  1.53 us
  transfers between devices with their start and end apart: 20, of which 11 were waited for; matrix products, arithmetic and copies ran while one was open for 2% of the time, Pallas kernels for 19%

profile of v4, /device:TPU:0, one launch (start us, length us, event | category | flops | bytes accessed | tf_op | source)
XLA Modules:
  0.0 53.0 jit_solution(12470080546490837503)
XLA Ops:
  0.7 0.5 collective-permute-start.1
  1.2 0.1 collective-permute-start.4
  1.2 0.4 collective-permute-start.5
  1.7 1.0 %convert_element_type.3.refs_0_ = bf16[128,512]{1,0:T(8,128)(2,1)S(1)} convert(f32[128,512]{1,0:T(8,128)} %param.7) | non-fusion elementwise | flops 65536 | bytes 393216 | tf_op jit(solution)/shard_map/convert_element_type | solution.py:216
  2.7 2.7 %collective-permute-start = (bf16[128,512]{1,0:T(8,128)(2,1)S(1)}, bf16[128,512]{1,0:T(8,128)(2,1)S(1)}, u32[]{:S(2)}, u32[]{:S(2)}) collective-permute-start(bf16[128,512]{1,0:T(8,128)(2,1)S(1)} %convert_element_type.3.refs_0_), channel_id=1, source_target_pairs={{0,2},{1,3},{2,0},{3,1},{4,6},{5,7},{6,4},{7,5},{8,10},{9,11},{10,... | collective-permute-start | bytes 393224 | tf_op jit(solution)/shard_map/ppermute | solution.py:187
  5.3 0.2 collective-permute-start.3
  5.5 1.0 %collective-permute-done.3.refs_1_.refs_5_ = s32[1,1,3]{2,1,0:T(1,128)S(1)} collective-permute-done((s32[1,1,3]{2,1,0:T(1,128)S(1)}, s32[1,1,3]{2,1,0:T(1,128)S(1)}, u32[]{:S(2)}, u32[]{:S(2)}) %collective-permute-start.3) | collective-permute-done | bytes 44 | tf_op jit(solution)/shard_map/ppermute | solution.py:187
  6.4 0.2 collective-permute-start.2
  6.6 0.1 pad_add_fusion.place._
  6.7 1.1 %copy-done = bf16[1,1,3,8,128,128]{5,4,3,2,1,0:T(8,128)(2,1)S(1)} copy-done((bf16[1,1,3,8,128,128]{5,4,3,2,1,0:T(8,128)(2,1)S(1)}, bf16[1,1,3,8,128,128]{5,4,3,2,1,0:T(8,128)(2,1)}, u32[]{:S(2)}) %copy-start) | copy-done | bytes 786456
  7.9 0.7 %prepare.4.refs_4_ = bf16[1024,256]{1,0:T(8,128)(2,1)S(1)} custom-call(s32[2]{0:T(128)S(1)} %pad_add_fusion.place._, s32[1,1,3,2,8]{4,3,2,1,0:T(2,128)S(1)} %bitcast.4, s32[1,1,3]{2,1,0:T(1,128)S(1)} %copy-done.5, bf16[1,1,3,8,128,128]{5,4,3,2,1,0:T(8,128)(2,1)S(1)} %copy-done, s32[1,1,3,8,16,128]{5,4,3,2,1,0:T(8,128)S(1)} %copy-done.3), custom_call_target="tpu_custom_call" | custom-call | flops 1024 | bytes 1024 | tf_op jit(solution)/shard_map/prepare/pallas_call | solution.py:166
  8.6 0.0 copy-start.2
  8.6 0.0 collective-permute-done.2.refs_0_.refs_4_
  8.6 0.0 collective-permute-done.4.refs_2_.refs_6_
  8.6 0.7 %prepare.5.refs_5_ = bf16[1024,256]{1,0:T(8,128)(2,1)S(1)} custom-call(s32[2]{0:T(128)S(1)} %pad_add_fusion.place._, s32[1,1,3,2,8]{4,3,2,1,0:T(2,128)S(1)} %collective-permute-done.2.refs_0_.refs_4_, s32[1,1,3]{2,1,0:T(1,128)S(1)} %collective-permute-done.3.refs_1_.refs_5_, bf16[1,1,3,8,128,128]{5,4,3,2,1,0:T(8,128)(2,1)S(1)} %collective-permute-done.4.refs_2_.refs_6_, ...), custom_call_target="tpu_custom_call" | custom-call | flops 1024 | bytes 1024 | tf_op jit(solution)/shard_map/prepare/pallas_call | solution.py:166
  9.3 0.1 collective-permute-done.refs_1_
  9.4 0.4 copy-done.2
  9.8 1.9 %tiles.3 = (bf16[256,512]{1,0:T(8,128)(2,1)S(1)}, bf16[1024,256]{1,0:T(8,128)(2,1)S(1)}, bf16[1536,256]{1,0:T(8,128)(2,1)S(1)}, bf16[128,512]{1,0:T(8,128)(2,1)S...) custom-call(s32[2]{0:T(128)S(1)} %pad_add_fusion.place._, ...), custom_call_target="tpu_custom_call" | custom-call | flops 1024 | bytes 1024 | tf_op jit(solution)/shard_map/tiles/pallas_call | solution.py:166
  11.7 0.4 collective-permute-start.11
  12.1 0.2 collective-permute-start.10
  12.3 1.4 %collective-permute-start.8 = (bf16[128,512]{1,0:T(8,128)(2,1)S(1)}, bf16[128,512]{1,0:T(8,128)(2,1)S(1)}, u32[]{:S(2)}, u32[]{:S(2)}) collective-permute-start(bf16[128,512]{1,0:T(8,128)(2,1)S(1)} %get-tuple-element.32), channel_id=1, source_target_pairs={{0,2},{1,3},{2,0},{3,1},{4,6},{5,7},{6,4},{7,5},{8,10},{9,11},{10,... | collective-permute-start | bytes 393224 | tf_op jit(solution)/shard_map/ppermute | solution.py:187
  13.7 1.5 %collective-permute-start.6 = (bf16[128,512]{1,0:T(8,128)(2,1)S(1)}, bf16[128,512]{1,0:T(8,128)(2,1)S(1)}, u32[]{:S(2)}, u32[]{:S(2)}) collective-permute-start(bf16[128,512]{1,0:T(8,128)(2,1)S(1)} %get-tuple-element.29), channel_id=1, source_target_pairs={{0,4},{1,5},{2,6},{3,7},{4,8},{5,9},{6,10},{7,11},{8,12},{9,13},{1... | collective-permute-start | bytes 393224 | tf_op jit(solution)/shard_map/ppermute | solution.py:187
  15.2 1.7 %collective-permute-start.7 = (bf16[128,512]{1,0:T(8,128)(2,1)S(1)}, bf16[128,512]{1,0:T(8,128)(2,1)S(1)}, u32[]{:S(2)}, u32[]{:S(2)}) collective-permute-start(bf16[128,512]{1,0:T(8,128)(2,1)S(1)} %get-tuple-element.30), channel_id=1, source_target_pairs={{0,6},{1,7},{2,4},{3,5},{4,10},{5,11},{6,8},{7,9},{8,14},{9,15},{1... | collective-permute-start | bytes 393224 | tf_op jit(solution)/shard_map/ppermute | solution.py:187
  16.9 1.2 %collective-permute-done.8.refs_1_ = bf16[128,512]{1,0:T(8,128)(2,1)S(1)} collective-permute-done((bf16[128,512]{1,0:T(8,128)(2,1)S(1)}, bf16[128,512]{1,0:T(8,128)(2,1)S(1)}, u32[]{:S(2)}, u32[]{:S(2)}) %collective-permute-start.8) | collective-permute-done | bytes 131104 | tf_op jit(solution)/shard_map/ppermute | solution.py:187
  18.1 1.6 %collective-permute-start.9 = (bf16[128,512]{1,0:T(8,128)(2,1)S(1)}, bf16[128,512]{1,0:T(8,128)(2,1)S(1)}, u32[]{:S(2)}, u32[]{:S(2)}) collective-permute-start(bf16[128,512]{1,0:T(8,128)(2,1)S(1)} %join.2), channel_id=1, source_target_pairs={{0,4},{1,5},{2,6},{3,7},{4,8},{5,9},{6,10},{7,11},{8,12},{9,13},{1... | collective-permute-start | bytes 393224 | tf_op jit(solution)/shard_map/ppermute | solution.py:187
  19.7 1.0 %prepare.6 = (bf16[1024,256]{1,0:T(8,128)(2,1)S(1)}, bf16[1024,256]{1,0:T(8,128)(2,1)S(1)}) custom-call(s32[2]{0:T(128)S(1)} %pad_add_fusion.place._, s32[1,1,3,2,8]{4,3,2,1,0:T(2,128)S(1)} %bitcast.5, s32[1,1,3]{2,1,0:T(1,128)S(1)} %copy-done.5, bf16[1,1,3,8,128,128]{5,4,3,2,1,0:T(8,128)(2,1)S(1)} %copy-done.1, s32[1,1,3,8,16,128]{5,4,3,2,1,0:T(8,128)S(1)} %copy-done.3, ...), custom_call_target="tpu_custom_call" | custom-call | flops 1024 | bytes 1024 | tf_op jit(solution)/shard_map/prepare/pallas_call | solution.py:166
  20.8 2.0 %users.3 = (bf16[1024,512]{1,0:T(8,128)(2,1)S(1)}, bf16[1024,512]{1,0:T(8,128)(2,1)S(1)}) custom-call(s32[2]{0:T(128)S(1)} %pad_add_fusion.place._, bf16[256,512]{1,0:T(8,128)(2,1)S(1)} %get-tuple-element.33.low, bf16[1024,512]{1,0:T(8,128)(2,1)S(1)} %copy-done.2, bf16[1024,512]{1,0:T(8,128)(2,1)S(1)} %collective-permute-done.1.refs_3_.refs_1_, ...), custom_call_target="tpu_custom_call" | custom-call | flops 1024 | bytes 1024 | tf_op jit(solution)/shard_map/users/pallas_call | solution.py:166
  22.8 2.8 %collective-permute-done.7.refs_1_ = bf16[128,512]{1,0:T(8,128)(2,1)S(1)} collective-permute-done((bf16[128,512]{1,0:T(8,128)(2,1)S(1)}, bf16[128,512]{1,0:T(8,128)(2,1)S(1)}, u32[]{:S(2)}, u32[]{:S(2)}) %collective-permute-start.7) | collective-permute-done | bytes 131104 | tf_op jit(solution)/shard_map/ppermute | solution.py:187
  25.6 1.7 %collective-permute-done.9.refs_2_ = bf16[128,512]{1,0:T(8,128)(2,1)S(1)} collective-permute-done((bf16[128,512]{1,0:T(8,128)(2,1)S(1)}, bf16[128,512]{1,0:T(8,128)(2,1)S(1)}, u32[]{:S(2)}, u32[]{:S(2)}) %collective-permute-start.9) | collective-permute-done | bytes 131104 | tf_op jit(solution)/shard_map/ppermute | solution.py:187
  27.3 1.9 %tiles.4 = (bf16[256,512]{1,0:T(8,128)(2,1)S(1)}, bf16[1024,256]{1,0:T(8,128)(2,1)S(1)}, bf16[1536,256]{1,0:T(8,128)(2,1)S(1)}, bf16[128,512]{1,0:T(8,128)(2,1)S...) custom-call(s32[2]{0:T(128)S(1)} %pad_add_fusion.place._, ...), custom_call_target="tpu_custom_call" | custom-call | flops 1024 | bytes 1024 | tf_op jit(solution)/shard_map/tiles/pallas_call | solution.py:166
  29.2 0.1 collective-permute-start.17
  29.3 0.5 collective-permute-start.16
  29.8 0.9 %collective-permute-start.14 = (bf16[128,512]{1,0:T(8,128)(2,1)S(1)}, bf16[128,512]{1,0:T(8,128)(2,1)S(1)}, u32[]{:S(2)}, u32[]{:S(2)}) collective-permute-start(bf16[128,512]{1,0:T(8,128)(2,1)S(1)} %get-tuple-element.43), channel_id=1, source_target_pairs={{0,2},{1,3},{2,0},{3,1},{4,6},{5,7},{6,4},{7,5},{8,10},{9,11},{10,... | collective-permute-start | bytes 393224 | tf_op jit(solution)/shard_map/ppermute | solution.py:187
  30.7 1.7 %collective-permute-start.13 = (bf16[128,512]{1,0:T(8,128)(2,1)S(1)}, bf16[128,512]{1,0:T(8,128)(2,1)S(1)}, u32[]{:S(2)}, u32[]{:S(2)}) collective-permute-start(bf16[128,512]{1,0:T(8,128)(2,1)S(1)} %get-tuple-element.41), channel_id=1, source_target_pairs={{0,6},{1,7},{2,4},{3,5},{4,10},{5,11},{6,8},{7,9},{8,14},{9,15},{1... | collective-permute-start | bytes 393224 | tf_op jit(solution)/shard_map/ppermute | solution.py:187
  32.4 2.9 %collective-permute-done.14.refs_1_ = bf16[128,512]{1,0:T(8,128)(2,1)S(1)} collective-permute-done((bf16[128,512]{1,0:T(8,128)(2,1)S(1)}, bf16[128,512]{1,0:T(8,128)(2,1)S(1)}, u32[]{:S(2)}, u32[]{:S(2)}) %collective-permute-start.14) | collective-permute-done | bytes 131104 | tf_op jit(solution)/shard_map/ppermute | solution.py:187
  35.3 0.1 collective-permute-start.15
  35.4 0.9 %prepare.7 = (bf16[1024,256]{1,0:T(8,128)(2,1)S(1)}, bf16[1024,256]{1,0:T(8,128)(2,1)S(1)}) custom-call(s32[2]{0:T(128)S(1)} %pad_add_fusion.place._, s32[1,1,3,2,8]{4,3,2,1,0:T(2,128)S(1)} %bitcast.6, s32[1,1,3]{2,1,0:T(1,128)S(1)} %copy-done.5, bf16[1,1,3,8,128,128]{5,4,3,2,1,0:T(8,128)(2,1)S(1)} %copy-done.1, s32[1,1,3,8,16,128]{5,4,3,2,1,0:T(8,128)S(1)} %copy-done.3, ...), custom_call_target="tpu_custom_call" | custom-call | flops 1024 | bytes 1024 | tf_op jit(solution)/shard_map/prepare/pallas_call | solution.py:166
  36.4 2.0 %users.4 = (bf16[1024,512]{1,0:T(8,128)(2,1)S(1)}, bf16[1024,512]{1,0:T(8,128)(2,1)S(1)}) custom-call(s32[2]{0:T(128)S(1)} %pad_add_fusion.place._, bf16[256,512]{1,0:T(8,128)(2,1)S(1)} %get-tuple-element.44.low, bf16[1024,512]{1,0:T(8,128)(2,1)S(1)} %get-tuple-element.36.refs_3_.refs_0_, bf16[1024,512]{1,0:T(8,128)(2,1)S(1)} %get-tuple-element.37.refs_4_.refs_1_, ...), custom_call_target="tpu_custom_call" | custom-call | flops 1024 | bytes 1024 | tf_op jit(solution)/shard_map/users/pallas_call | solution.py:166
  38.4 1.5 %collective-permute-done.12.refs_0_ = bf16[128,512]{1,0:T(8,128)(2,1)S(1)} collective-permute-done((bf16[128,512]{1,0:T(8,128)(2,1)S(1)}, bf16[128,512]{1,0:T(8,128)(2,1)S(1)}, u32[]{:S(2)}, u32[]{:S(2)}) %collective-permute-start.12) | collective-permute-done | bytes 131104 | tf_op jit(solution)/shard_map/ppermute | solution.py:187
  39.8 3.3 %collective-permute-done.13.refs_1_ = bf16[128,512]{1,0:T(8,128)(2,1)S(1)} collective-permute-done((bf16[128,512]{1,0:T(8,128)(2,1)S(1)}, bf16[128,512]{1,0:T(8,128)(2,1)S(1)}, u32[]{:S(2)}, u32[]{:S(2)}) %collective-permute-start.13) | collective-permute-done | bytes 131104 | tf_op jit(solution)/shard_map/ppermute | solution.py:187
  43.2 1.1 %collective-permute-done.15.refs_2_ = bf16[128,512]{1,0:T(8,128)(2,1)S(1)} collective-permute-done((bf16[128,512]{1,0:T(8,128)(2,1)S(1)}, bf16[128,512]{1,0:T(8,128)(2,1)S(1)}, u32[]{:S(2)}, u32[]{:S(2)}) %collective-permute-start.15) | collective-permute-done | bytes 131104 | tf_op jit(solution)/shard_map/ppermute | solution.py:187
  44.3 2.0 %tiles.5 = (bf16[256,512]{1,0:T(8,128)(2,1)S(1)}, bf16[1024,256]{1,0:T(8,128)(2,1)S(1)}, bf16[1536,256]{1,0:T(8,128)(2,1)S(1)}, f32[128,512]{1,0:T(8,128)S(1)}, bf16[128,512]{1,0:T(8,128)(2,1)S(1)}) custom-call(s32[2]{0:T(128)S(1)} %pad_add_fusion.place._, bf16[128,512]{1,0:T(8,128)(2,1)S(1)} %collective-permute-done.12.refs_0_, ...), custom_call_target="tpu_custom_call" | custom-call | flops 1024 | bytes 1024 | tf_op jit(solution)/shard_map/tiles/pallas_call | solution.py:166
  46.2 0.1 collective-permute-start.18
  46.3 1.1 %collective-permute-start.19 = (bf16[128,512]{1,0:T(8,128)(2,1)S(1)}, bf16[128,512]{1,0:T(8,128)(2,1)S(1)}, u32[]{:S(2)}, u32[]{:S(2)}) collective-permute-start(bf16[128,512]{1,0:T(8,128)(2,1)S(1)} %get-tuple-element.55), channel_id=1, source_target_pairs={{0,2},{1,3},{2,0},{3,1},{4,6},{5,7},{6,4},{7,5},{8,10},{9,11},{10,... | collective-permute-start | bytes 393224 | tf_op jit(solution)/shard_map/ppermute | solution.py:187
  47.5 1.1 %collective-permute-done.18.refs_2_ = bf16[1536,256]{1,0:T(8,128)(2,1)S(1)} collective-permute-done((bf16[1536,256]{1,0:T(8,128)(2,1)S(1)}, bf16[1536,256]{1,0:T(8,128)(2,1)S(1)}, u32[]{:S(2)}, u32[]{:S(2)}) %collective-permute-start.18) | collective-permute-done | bytes 786464 | tf_op jit(solution)/shard_map/ppermute | solution.py:187
  48.6 2.3 %users.5.refs_2_ = bf16[1024,512]{1,0:T(8,128)(2,1)} custom-call(s32[2]{0:T(128)S(1)} %pad_add_fusion.place._, bf16[256,512]{1,0:T(8,128)(2,1)S(1)} %get-tuple-element.51.low, bf16[1024,512]{1,0:T(8,128)(2,1)S(1)} %get-tuple-element.47.refs_3_.refs_0_, bf16[1024,256]{1,0:T(8,128)(2,1)S(1)} %get-tuple-element.52.refs_1_, ...), custom_call_target="tpu_custom_call" | custom-call | flops 1024 | bytes 1024 | tf_op jit(solution)/shard_map/users/pallas_call | solution.py:166
  50.9 1.3 %collective-permute-done.19.refs_1_ = bf16[128,512]{1,0:T(8,128)(2,1)S(1)} collective-permute-done((bf16[128,512]{1,0:T(8,128)(2,1)S(1)}, bf16[128,512]{1,0:T(8,128)(2,1)S(1)}, u32[]{:S(2)}, u32[]{:S(2)}) %collective-permute-start.19) | collective-permute-done | bytes 131104 | tf_op jit(solution)/shard_map/ppermute | solution.py:187
  52.2 0.7 %final.1 = f32[128,512]{1,0:T(8,128)} custom-call(f32[128,512]{1,0:T(8,128)S(1)} %get-tuple-element.54.refs_0_, bf16[128,512]{1,0:T(8,128)(2,1)S(1)} %collective-permute-done.19.refs_1_, bf16[1024,512]{1,0:T(8,128)(2,1)} %users.5.refs_2_), custom_call_target="tpu_custom_call" | custom-call | flops 1024 | bytes 1024 | tf_op jit(solution)/shard_map/final/pallas_call | solution.py:166
  (19 shorter events, 0.1 us)
Async XLA Ops:
  0.6 6.1 %copy-start.3 = (s32[1,1,3,8,16,128]{5,4,3,2,1,0:T(8,128)S(1)}, s32[1,1,3,8,16,128]{5,4,3,2,1,0:T(8,128)}, u32[]{:S(2)}) copy-start(s32[1,1,3,8,16,128]{5,4,3,2,1,0:T(8,128)} %refs_3_.5) | copy-start | bytes 589828
  0.6 4.7 %copy-start.5 = (s32[1,1,3]{2,1,0:T(1,128)S(1)}, s32[1,1,3]{2,1,0:T(1,128)}, u32[]{:S(2)}) copy-start(s32[1,1,3]{2,1,0:T(1,128)} %refs_1_.5) | copy-start | bytes 40
  0.7 8.8 %collective-permute-start.1 = (bf16[1024,512]{1,0:T(8,128)(2,1)}, bf16[1024,512]{1,0:T(8,128)(2,1)S(1)}, u32[]{:S(2)}, u32[]{:S(2)}) collective-permute-start(bf16[1024,512]{1,0:T(8,128)(2,1)} %refs_0_.1), channel_id=1, source_target_pairs={{0,1},{1,0},{2,3},{3,2},{4,5},{5,4},{6,7},{7,6},{8,9},{9,8},{10,11... | collective-permute-start | bytes 3145736 | tf_op jit(solution)/shard_map/ppermute | solution.py:187
  1.2 7.4 %collective-permute-start.4 = (bf16[1,1,3,8,128,128]{5,4,3,2,1,0:T(8,128)(2,1)}, bf16[1,1,3,8,128,128]{5,4,3,2,1,0:T(8,128)(2,1)S(1)}, u32[]{:S(2)}, u32[]{:S(2)}) collective-permute-start(bf16[1,1,3,8,128,128]{5,4,3,2,1,0:T(8,128)(2,1)} %refs_2_.7), channel_id=1, source_target_pairs={{0,1},{1,0},{2,3},{3,2},{4,5},{5,4},{6,7},{7,6},{8,9},{9,8},{10,11... | collective-permute-start | bytes 2359304 | tf_op jit(solution)/shard_map/ppermute | solution.py:187
  1.2 7.3 %collective-permute-start.5 = (s32[1,1,3,8,16,128]{5,4,3,2,1,0:T(8,128)}, s32[1,1,3,8,16,128]{5,4,3,2,1,0:T(8,128)S(1)}, u32[]{:S(2)}, u32[]{:S(2)}) collective-permute-start(s32[1,1,3,8,16,128]{5,4,3,2,1,0:T(8,128)} %refs_3_.5), channel_id=1, source_target_pairs={{0,1},{1,0},{2,3},{3,2},{4,5},{5,4},{6,7},{7,6},{8,9},{9,8},{10,11... | collective-permute-start | bytes 589832 | tf_op jit(solution)/shard_map/ppermute | solution.py:187
  2.7 6.8 %collective-permute-start = (bf16[128,512]{1,0:T(8,128)(2,1)S(1)}, bf16[128,512]{1,0:T(8,128)(2,1)S(1)}, u32[]{:S(2)}, u32[]{:S(2)}) collective-permute-start(bf16[128,512]{1,0:T(8,128)(2,1)S(1)} %convert_element_type.3.refs_0_), channel_id=1, source_target_pairs={{0,2},{1,3},{2,0},{3,1},{4,6},{5,7},{6,4},{7,5},{8,10},{9,11},{10,... | collective-permute-start | bytes 393224 | tf_op jit(solution)/shard_map/ppermute | solution.py:187
  5.3 1.1 %collective-permute-start.3 = (s32[1,1,3]{2,1,0:T(1,128)S(1)}, s32[1,1,3]{2,1,0:T(1,128)S(1)}, u32[]{:S(2)}, u32[]{:S(2)}) collective-permute-start(s32[1,1,3]{2,1,0:T(1,128)S(1)} %copy-done.5), channel_id=1, source_target_pairs={{0,1},{1,0},{2,3},{3,2},{4,5},{5,4},{6,7},{7,6},{8,9},{9,8},{10,11... | collective-permute-start | bytes 44 | tf_op jit(solution)/shard_map/ppermute | solution.py:187
  5.5 1.0 %copy-start.4 = (s32[1,1,3,8,2]{3,4,2,1,0:T(2,128)S(1)}, s32[1,1,3,8,2]{3,4,2,1,0:T(2,128)}, u32[]{:S(2)}) copy-start(s32[1,1,3,8,2]{3,4,2,1,0:T(2,128)} %param.8) | copy-start | bytes 580
  6.4 2.1 %collective-permute-start.2 = (s32[1,1,3,2,8]{4,3,2,1,0:T(2,128)S(1)}, s32[1,1,3,2,8]{4,3,2,1,0:T(2,128)S(1)}, u32[]{:S(2)}, u32[]{:S(2)}) collective-permute-start(s32[1,1,3,2,8]{4,3,2,1,0:T(2,128)S(1)} %bitcast.3), channel_id=1, source_target_pairs={{0,1},{1,0},{2,3},{3,2},{4,5},{5,4},{6,7},{7,6},{8,9},{9,8},{10,11... | collective-permute-start | bytes 584 | tf_op jit(solution)/shard_map/ppermute | solution.py:187
  6.7 1.1 %copy-start = (bf16[1,1,3,8,128,128]{5,4,3,2,1,0:T(8,128)(2,1)S(1)}, bf16[1,1,3,8,128,128]{5,4,3,2,1,0:T(8,128)(2,1)}, u32[]{:S(2)}) copy-start(bf16[1,1,3,8,128,128]{5,4,3,2,1,0:T(8,128)(2,1)} %refs_2_.7) | copy-start | bytes 2359300
  8.6 1.2 %copy-start.2 = (bf16[1024,512]{1,0:T(8,128)(2,1)S(1)}, bf16[1024,512]{1,0:T(8,128)(2,1)}, u32[]{:S(2)}) copy-start(bf16[1024,512]{1,0:T(8,128)(2,1)} %refs_0_.1) | copy-start | bytes 3145732
  9.8 9.9 %copy-start.1 = (bf16[1,1,3,8,128,128]{5,4,3,2,1,0:T(8,128)(2,1)S(1)}, bf16[1,1,3,8,128,128]{5,4,3,2,1,0:T(8,128)(2,1)}, u32[]{:S(2)}) copy-start(bf16[1,1,3,8,128,128]{5,4,3,2,1,0:T(8,128)(2,1)} %refs_2_.7) | copy-start | bytes 2359300
  11.7 9.0 %collective-permute-start.11 = (bf16[1536,256]{1,0:T(8,128)(2,1)S(1)}, bf16[1536,256]{1,0:T(8,128)(2,1)S(1)}, u32[]{:S(2)}, u32[]{:S(2)}) collective-permute-start(bf16[1536,256]{1,0:T(8,128)(2,1)S(1)} %get-tuple-element.35.refs_3_), channel_id=1, source_target_pairs={{0,1},{1,0},{2,3},{3,2},{4,5},{5,4},{6,7},{7,6},{8,9},{9,8},{10,11... | collective-permute-start | bytes 2359304 | tf_op jit(solution)/shard_map/ppermute | solution.py:187
  12.1 8.6 %collective-permute-start.10 = (bf16[1024,256]{1,0:T(8,128)(2,1)S(1)}, bf16[1024,256]{1,0:T(8,128)(2,1)S(1)}, u32[]{:S(2)}, u32[]{:S(2)}) collective-permute-start(bf16[1024,256]{1,0:T(8,128)(2,1)S(1)} %get-tuple-element.34.refs_2_), channel_id=1, source_target_pairs={{0,1},{1,0},{2,3},{3,2},{4,5},{5,4},{6,7},{7,6},{8,9},{9,8},{10,11... | collective-permute-start | bytes 1572872 | tf_op jit(solution)/shard_map/ppermute | solution.py:187
  12.3 5.7 %collective-permute-start.8 = (bf16[128,512]{1,0:T(8,128)(2,1)S(1)}, bf16[128,512]{1,0:T(8,128)(2,1)S(1)}, u32[]{:S(2)}, u32[]{:S(2)}) collective-permute-start(bf16[128,512]{1,0:T(8,128)(2,1)S(1)} %get-tuple-element.32), channel_id=1, source_target_pairs={{0,2},{1,3},{2,0},{3,1},{4,6},{5,7},{6,4},{7,5},{8,10},{9,11},{10,... | collective-permute-start | bytes 393224 | tf_op jit(solution)/shard_map/ppermute | solution.py:187
  13.7 9.1 %collective-permute-start.6 = (bf16[128,512]{1,0:T(8,128)(2,1)S(1)}, bf16[128,512]{1,0:T(8,128)(2,1)S(1)}, u32[]{:S(2)}, u32[]{:S(2)}) collective-permute-start(bf16[128,512]{1,0:T(8,128)(2,1)S(1)} %get-tuple-element.29), channel_id=1, source_target_pairs={{0,4},{1,5},{2,6},{3,7},{4,8},{5,9},{6,10},{7,11},{8,12},{9,13},{1... | collective-permute-start | bytes 393224 | tf_op jit(solution)/shard_map/ppermute | solution.py:187
  15.2 10.4 %collective-permute-start.7 = (bf16[128,512]{1,0:T(8,128)(2,1)S(1)}, bf16[128,512]{1,0:T(8,128)(2,1)S(1)}, u32[]{:S(2)}, u32[]{:S(2)}) collective-permute-start(bf16[128,512]{1,0:T(8,128)(2,1)S(1)} %get-tuple-element.30), channel_id=1, source_target_pairs={{0,6},{1,7},{2,4},{3,5},{4,10},{5,11},{6,8},{7,9},{8,14},{9,15},{1... | collective-permute-start | bytes 393224 | tf_op jit(solution)/shard_map/ppermute | solution.py:187
  18.1 9.2 %collective-permute-start.9 = (bf16[128,512]{1,0:T(8,128)(2,1)S(1)}, bf16[128,512]{1,0:T(8,128)(2,1)S(1)}, u32[]{:S(2)}, u32[]{:S(2)}) collective-permute-start(bf16[128,512]{1,0:T(8,128)(2,1)S(1)} %join.2), channel_id=1, source_target_pairs={{0,4},{1,5},{2,6},{3,7},{4,8},{5,9},{6,10},{7,11},{8,12},{9,13},{1... | collective-permute-start | bytes 393224 | tf_op jit(solution)/shard_map/ppermute | solution.py:187
  29.2 7.1 %collective-permute-start.17 = (bf16[1536,256]{1,0:T(8,128)(2,1)S(1)}, bf16[1536,256]{1,0:T(8,128)(2,1)S(1)}, u32[]{:S(2)}, u32[]{:S(2)}) collective-permute-start(bf16[1536,256]{1,0:T(8,128)(2,1)S(1)} %get-tuple-element.46.refs_3_), channel_id=1, source_target_pairs={{0,1},{1,0},{2,3},{3,2},{4,5},{5,4},{6,7},{7,6},{8,9},{9,8},{10,11... | collective-permute-start | bytes 2359304 | tf_op jit(solution)/shard_map/ppermute | solution.py:187
  29.3 7.0 %collective-permute-start.16 = (bf16[1024,256]{1,0:T(8,128)(2,1)S(1)}, bf16[1024,256]{1,0:T(8,128)(2,1)S(1)}, u32[]{:S(2)}, u32[]{:S(2)}) collective-permute-start(bf16[1024,256]{1,0:T(8,128)(2,1)S(1)} %get-tuple-element.45.refs_2_), channel_id=1, source_target_pairs={{0,1},{1,0},{2,3},{3,2},{4,5},{5,4},{6,7},{7,6},{8,9},{9,8},{10,11... | collective-permute-start | bytes 1572872 | tf_op jit(solution)/shard_map/ppermute | solution.py:187
  29.8 5.5 %collective-permute-start.14 = (bf16[128,512]{1,0:T(8,128)(2,1)S(1)}, bf16[128,512]{1,0:T(8,128)(2,1)S(1)}, u32[]{:S(2)}, u32[]{:S(2)}) collective-permute-start(bf16[128,512]{1,0:T(8,128)(2,1)S(1)} %get-tuple-element.43), channel_id=1, source_target_pairs={{0,2},{1,3},{2,0},{3,1},{4,6},{5,7},{6,4},{7,5},{8,10},{9,11},{10,... | collective-permute-start | bytes 393224 | tf_op jit(solution)/shard_map/ppermute | solution.py:187
  30.7 9.1 %collective-permute-start.12 = (bf16[128,512]{1,0:T(8,128)(2,1)S(1)}, bf16[128,512]{1,0:T(8,128)(2,1)S(1)}, u32[]{:S(2)}, u32[]{:S(2)}) collective-permute-start(bf16[128,512]{1,0:T(8,128)(2,1)S(1)} %get-tuple-element.40), channel_id=1, source_target_pairs={{0,4},{1,5},{2,6},{3,7},{4,8},{5,9},{6,10},{7,11},{8,12},{9,13},{1... | collective-permute-start | bytes 393224 | tf_op jit(solution)/shard_map/ppermute | solution.py:187
  30.7 12.4 %collective-permute-start.13 = (bf16[128,512]{1,0:T(8,128)(2,1)S(1)}, bf16[128,512]{1,0:T(8,128)(2,1)S(1)}, u32[]{:S(2)}, u32[]{:S(2)}) collective-permute-start(bf16[128,512]{1,0:T(8,128)(2,1)S(1)} %get-tuple-element.41), channel_id=1, source_target_pairs={{0,6},{1,7},{2,4},{3,5},{4,10},{5,11},{6,8},{7,9},{8,14},{9,15},{1... | collective-permute-start | bytes 393224 | tf_op jit(solution)/shard_map/ppermute | solution.py:187
  35.3 8.9 %collective-permute-start.15 = (bf16[128,512]{1,0:T(8,128)(2,1)S(1)}, bf16[128,512]{1,0:T(8,128)(2,1)S(1)}, u32[]{:S(2)}, u32[]{:S(2)}) collective-permute-start(bf16[128,512]{1,0:T(8,128)(2,1)S(1)} %join.3), channel_id=1, source_target_pairs={{0,4},{1,5},{2,6},{3,7},{4,8},{5,9},{6,10},{7,11},{8,12},{9,13},{1... | collective-permute-start | bytes 393224 | tf_op jit(solution)/shard_map/ppermute | solution.py:187
  46.2 2.4 %collective-permute-start.18 = (bf16[1536,256]{1,0:T(8,128)(2,1)S(1)}, bf16[1536,256]{1,0:T(8,128)(2,1)S(1)}, u32[]{:S(2)}, u32[]{:S(2)}) collective-permute-start(bf16[1536,256]{1,0:T(8,128)(2,1)S(1)} %get-tuple-element.53), channel_id=1, source_target_pairs={{0,1},{1,0},{2,3},{3,2},{4,5},{5,4},{6,7},{7,6},{8,9},{9,8},{10,11... | collective-permute-start | bytes 2359304 | tf_op jit(solution)/shard_map/ppermute | solution.py:187
  46.3 5.9 %collective-permute-start.19 = (bf16[128,512]{1,0:T(8,128)(2,1)S(1)}, bf16[128,512]{1,0:T(8,128)(2,1)S(1)}, u32[]{:S(2)}, u32[]{:S(2)}) collective-permute-start(bf16[128,512]{1,0:T(8,128)(2,1)S(1)} %get-tuple-element.55), channel_id=1, source_target_pairs={{0,2},{1,3},{2,0},{3,1},{4,6},{5,7},{6,4},{7,5},{8,10},{9,11},{10,... | collective-permute-start | bytes 393224 | tf_op jit(solution)/shard_map/ppermute | solution.py:187

commit v5 on v4

--- a/solution.py
+++ b/solution.py
@@ -16,6 +16,7 @@
 HB = pl.BlockSpec(memory_space=pltpu.HBM)
 CORES = 2
 CHUNK = 512
+MARK = 1 << 34
 
 
 def place_of(close, chip, core, rows):
@@ -154,15 +155,25 @@
                 out[cut, to] = (factor + step_user * (grad - shrinkage * factor)).astype(out.dtype)
 
 
+def joined(parts):
+    total = parts[0][...]
+    for other in parts[1:]:
+        total = total + step_item * other[...].astype(jnp.float32)
+    return total
+
+
+def join_kernel(count, *refs):
+    held, (out, *copies) = refs[count : count + 2], refs[count + 2 :]
+    out[...] = joined(refs[:count]).astype(out.dtype)
+    for source, copy in zip(held, copies):
+        copy[...] = source[...]
+
+
 def final_kernel(count, *refs):
-    refs = refs[:count] + refs[-1:]
-    total = refs[0][...]
-    for other in refs[1:count]:
-        total = total + step_item * other[...].astype(jnp.float32)
-    refs[count][...] = total.astype(refs[count].dtype)
-
-
-def kernel_call(body, name, ins, outs, flops, scratch=(), extra=(), aliases=()):
+    refs[-1][...] = joined(refs[:count])
+
+
+def kernel_call(body, name, ins, outs, flops, scratch=(), extra=()):
     return pl.pallas_call(
         body,
         name=name,
@@ -170,10 +181,25 @@
         in_specs=[SM if x.dtype == jnp.int32 and x.ndim != 6 else VM for x in ins] + [HB] * len(extra),
         out_specs=(VM,) * len(outs),
         scratch_shapes=list(scratch),
-        input_output_aliases=dict(aliases),
         compiler_params=pltpu.CompilerParams(vmem_limit_bytes=16 << 20),
         cost_estimate=pl.CostEstimate(flops=flops, bytes_accessed=1024, transcendentals=0),
     )(*ins, *[pltpu.with_memory_space_constraint(x, pltpu.HBM) for x in extra])
+
+
+def mark_kernel(*refs):
+    refs[-1][...] = jnp.zeros_like(refs[-1])
+
+
+def marked(*arrays):
+    return pl.pallas_call(
+        mark_kernel,
+        name="mark",
+        out_shape=pltpu.VMEM((8, 128), jnp.float32),
+        in_specs=[VM] * len(arrays),
+        out_specs=VM,
+        compiler_params=pltpu.CompilerParams(vmem_limit_bytes=16 << 20),
+        cost_estimate=pl.CostEstimate(flops=MARK, bytes_accessed=1024, transcendentals=0),
+    )(*arrays)
 
 
 def moved(x, by_strata, by_chip, flip, *, strata, peers):
@@ -251,15 +277,15 @@
                 others = [move(ends[3], 0, k, False) for k in range(1, chips)]
             arrived = [move(ends[min(k, 1)], 1, k, False) for k in range(chips)]
             if groups > 1:
-                (summed,) = kernel_call(
-                    functools.partial(final_kernel, chips),
+                summed, errors, other_errors = kernel_call(
+                    functools.partial(join_kernel, chips),
                     "join",
-                    [ends[2], *others],
-                    [pltpu.VMEM((part, width), low_type)],
+                    [ends[2], *others, errors, other_errors],
+                    [pltpu.VMEM(x.shape, low_type) for x in (ends[2], errors, other_errors)],
                     1024,
                 )
                 arrived += [move(summed, 1, 0, False)]
-            sets = [place, low, users, other_users]
+            sets = [marked(arrived[0]), low, users, other_users]
             sets += [errors, other_errors, swap(errors), swap(other_errors)]
         kind = jax.ShapeDtypeStruct if last else pltpu.VMEM
         users, *other_users = kernel_call(

time: 53.2 us -> 51.2 us (0.962)
  Pallas kernels: 16.4 us -> 15.4 us
  waiting for transfers between devices: 17.9 us -> 17.1 us
    pallas_call x13, Pallas kernels: 16.4 us -> 15.4 us  [kernel_call(): pl.pallas_call(body, name=name, out_shape=tuple(outs), in_specs=[SM if x....]
    ppermute x20, waiting for transfers between devices: 17.9 us -> 17.1 us  [moved(): return lax.ppermute(x, ('strata', 'shard'), pairs)]
  transfers between devices with their start and end apart: 20 -> 20, of which waited for: 11 -> 11; matrix products, arithmetic and copies ran while one was open for 2% -> 2% of each run, Pallas kernels for 19% -> 17%
where the time goes in v5:
time: 51.2 us; the launch traced here: 51.1 us
  waiting for transfers between devices  17.1 us (33%)
  Pallas kernels  15.4 us (30%)
  starting transfers between devices  15.3 us (30%)
  local copies, waits for them, and re-layouts  1.56 us (3%)
  other arithmetic  1.04 us (2%)
  between operations  0.82 us (2%)
    ppermute x20, waiting for transfers between devices, moved(): return lax.ppermute(x, ('strata', 'shard'), pairs)  17.1 us
    pallas_call x13, Pallas kernels, kernel_call(): pl.pallas_call(body, name=name, out_shape=tuple(outs), in_specs=[SM if x....  15.4 us
    ppermute x20, starting transfers between devices, moved(): return lax.ppermute(x, ('strata', 'shard'), pairs)  15.3 us
    unnamed x12, local copies, waits for them, and re-layouts  1.56 us
  transfers between devices with their start and end apart: 20, of which 11 were waited for; matrix products, arithmetic and copies ran while one was open for 2% of the time, Pallas kernels for 17%

profile of v5, /device:TPU:0, one launch (start us, length us, event | category | flops | bytes accessed | tf_op | source)
XLA Modules:
  0.0 51.1 jit_solution(3212498426708158018)
XLA Ops:
  0.7 0.5 %collective-permute-start.1 = (bf16[1024,512]{1,0:T(8,128)(2,1)}, bf16[1024,512]{1,0:T(8,128)(2,1)S(1)}, u32[]{:S(2)}, u32[]{:S(2)}) collective-permute-start(bf16[1024,512]{1,0:T(8,128)(2,1)} %refs_0_.1), channel_id=1, source_target_pairs={{0,1},{1,0},{2,3},{3,2},{4,5},{5,4},{6,7},{7,6},{8,9},{9,8},{10,11... | collective-permute-start | bytes 3145736 | tf_op jit(solution)/shard_map/ppermute | solution.py:213
  1.2 0.1 collective-permute-start.4
  1.2 0.4 collective-permute-start.5
  1.7 1.0 %convert_element_type.3.refs_0_ = bf16[128,512]{1,0:T(8,128)(2,1)S(1)} convert(f32[128,512]{1,0:T(8,128)} %param.7) | non-fusion elementwise | flops 65536 | bytes 393216 | tf_op jit(solution)/shard_map/convert_element_type | solution.py:242
  2.7 2.7 %collective-permute-start = (bf16[128,512]{1,0:T(8,128)(2,1)S(1)}, bf16[128,512]{1,0:T(8,128)(2,1)S(1)}, u32[]{:S(2)}, u32[]{:S(2)}) collective-permute-start(bf16[128,512]{1,0:T(8,128)(2,1)S(1)} %convert_element_type.3.refs_0_), channel_id=1, source_target_pairs={{0,2},{1,3},{2,0},{3,1},{4,6},{5,7},{6,4},{7,5},{8,10},{9,11},{10,... | collective-permute-start | bytes 393224 | tf_op jit(solution)/shard_map/ppermute | solution.py:213
  5.3 0.2 collective-permute-start.3
  5.5 1.0 %collective-permute-done.3.refs_1_.refs_5_ = s32[1,1,3]{2,1,0:T(1,128)S(1)} collective-permute-done((s32[1,1,3]{2,1,0:T(1,128)S(1)}, s32[1,1,3]{2,1,0:T(1,128)S(1)}, u32[]{:S(2)}, u32[]{:S(2)}) %collective-permute-start.3) | collective-permute-done | bytes 44 | tf_op jit(solution)/shard_map/ppermute | solution.py:213
  6.4 0.2 collective-permute-start.2
  6.6 0.1 pad_add_fusion.place._
  6.7 1.1 %copy-done = bf16[1,1,3,8,128,128]{5,4,3,2,1,0:T(8,128)(2,1)S(1)} copy-done((bf16[1,1,3,8,128,128]{5,4,3,2,1,0:T(8,128)(2,1)S(1)}, bf16[1,1,3,8,128,128]{5,4,3,2,1,0:T(8,128)(2,1)}, u32[]{:S(2)}) %copy-start) | copy-done | bytes 786456
  7.9 0.7 %prepare.4.refs_4_ = bf16[1024,256]{1,0:T(8,128)(2,1)S(1)} custom-call(s32[2]{0:T(128)S(1)} %pad_add_fusion.place._, s32[1,1,3,2,8]{4,3,2,1,0:T(2,128)S(1)} %bitcast.4, s32[1,1,3]{2,1,0:T(1,128)S(1)} %copy-done.5, bf16[1,1,3,8,128,128]{5,4,3,2,1,0:T(8,128)(2,1)S(1)} %copy-done, s32[1,1,3,8,16,128]{5,4,3,2,1,0:T(8,128)S(1)} %copy-done.3), custom_call_target="tpu_custom_call" | custom-call | flops 1024 | bytes 1024 | tf_op jit(solution)/shard_map/prepare/pallas_call | solution.py:177
  8.6 0.7 %prepare.5.refs_5_ = bf16[1024,256]{1,0:T(8,128)(2,1)S(1)} custom-call(s32[2]{0:T(128)S(1)} %pad_add_fusion.place._, s32[1,1,3,2,8]{4,3,2,1,0:T(2,128)S(1)} %collective-permute-done.2.refs_0_.refs_4_, s32[1,1,3]{2,1,0:T(1,128)S(1)} %collective-permute-done.3.refs_1_.refs_5_, bf16[1,1,3,8,128,128]{5,4,3,2,1,0:T(8,128)(2,1)S(1)} %collective-permute-done.4.refs_2_.refs_6_, ...), custom_call_target="tpu_custom_call" | custom-call | flops 1024 | bytes 1024 | tf_op jit(solution)/shard_map/prepare/pallas_call | solution.py:177
  9.4 0.0 collective-permute-done.refs_1_
  9.4 0.4 copy-done.2
  9.8 1.9 %tiles.3 = (bf16[256,512]{1,0:T(8,128)(2,1)S(1)}, bf16[1024,256]{1,0:T(8,128)(2,1)S(1)}, bf16[1536,256]{1,0:T(8,128)(2,1)S(1)}, bf16[128,512]{1,0:T(8,128)(2,1)S...) custom-call(s32[2]{0:T(128)S(1)} %pad_add_fusion.place._, ...), custom_call_target="tpu_custom_call" | custom-call | flops 1024 | bytes 1024 | tf_op jit(solution)/shard_map/tiles/pallas_call | solution.py:177
  11.8 1.4 %collective-permute-start.8 = (bf16[128,512]{1,0:T(8,128)(2,1)S(1)}, bf16[128,512]{1,0:T(8,128)(2,1)S(1)}, u32[]{:S(2)}, u32[]{:S(2)}) collective-permute-start(bf16[128,512]{1,0:T(8,128)(2,1)S(1)} %get-tuple-element.38), channel_id=1, source_target_pairs={{0,2},{1,3},{2,0},{3,1},{4,6},{5,7},{6,4},{7,5},{8,10},{9,11},{10,... | collective-permute-start | bytes 393224 | tf_op jit(solution)/shard_map/ppermute | solution.py:213
  13.2 1.5 %collective-permute-start.6 = (bf16[128,512]{1,0:T(8,128)(2,1)S(1)}, bf16[128,512]{1,0:T(8,128)(2,1)S(1)}, u32[]{:S(2)}, u32[]{:S(2)}) collective-permute-start(bf16[128,512]{1,0:T(8,128)(2,1)S(1)} %get-tuple-element.35), channel_id=1, source_target_pairs={{0,4},{1,5},{2,6},{3,7},{4,8},{5,9},{6,10},{7,11},{8,12},{9,13},{1... | collective-permute-start | bytes 393224 | tf_op jit(solution)/shard_map/ppermute | solution.py:213
  14.7 1.1 %prepare.6 = (bf16[1024,256]{1,0:T(8,128)(2,1)S(1)}, bf16[1024,256]{1,0:T(8,128)(2,1)S(1)}) custom-call(s32[2]{0:T(128)S(1)} %pad_add_fusion.place._, s32[1,1,3,2,8]{4,3,2,1,0:T(2,128)S(1)} %bitcast.5, s32[1,1,3]{2,1,0:T(1,128)S(1)} %copy-done.5, bf16[1,1,3,8,128,128]{5,4,3,2,1,0:T(8,128)(2,1)S(1)} %copy-done.1, s32[1,1,3,8,16,128]{5,4,3,2,1,0:T(8,128)S(1)} %copy-done.3, ...), custom_call_target="tpu_custom_call" | custom-call | flops 1024 | bytes 1024 | tf_op jit(solution)/shard_map/prepare/pallas_call | solution.py:177
  15.8 1.7 %collective-permute-start.7 = (bf16[128,512]{1,0:T(8,128)(2,1)S(1)}, bf16[128,512]{1,0:T(8,128)(2,1)S(1)}, u32[]{:S(2)}, u32[]{:S(2)}) collective-permute-start(bf16[128,512]{1,0:T(8,128)(2,1)S(1)} %get-tuple-element.36), channel_id=1, source_target_pairs={{0,6},{1,7},{2,4},{3,5},{4,10},{5,11},{6,8},{7,9},{8,14},{9,15},{1... | collective-permute-start | bytes 393224 | tf_op jit(solution)/shard_map/ppermute | solution.py:213
  17.5 0.0 collective-permute-done.8.refs_1_
  17.5 0.1 join.2
  17.6 1.6 %collective-permute-start.9 = (bf16[128,512]{1,0:T(8,128)(2,1)S(1)}, bf16[128,512]{1,0:T(8,128)(2,1)S(1)}, u32[]{:S(2)}, u32[]{:S(2)}) collective-permute-start(bf16[128,512]{1,0:T(8,128)(2,1)S(1)} %get-tuple-element.41), channel_id=1, source_target_pairs={{0,4},{1,5},{2,6},{3,7},{4,8},{5,9},{6,10},{7,11},{8,12},{9,13},{1... | collective-permute-start | bytes 393224 | tf_op jit(solution)/shard_map/ppermute | solution.py:213
  19.3 0.5 collective-permute-start.11
  19.8 1.5 %collective-permute-done.6.refs_0_ = bf16[128,512]{1,0:T(8,128)(2,1)S(1)} collective-permute-done((bf16[128,512]{1,0:T(8,128)(2,1)S(1)}, bf16[128,512]{1,0:T(8,128)(2,1)S(1)}, u32[]{:S(2)}, u32[]{:S(2)}) %collective-permute-start.6) | collective-permute-done | bytes 131104 | tf_op jit(solution)/shard_map/ppermute | solution.py:213
  21.3 1.0 %collective-permute-done.11.refs_5_ = bf16[1536,256]{1,0:T(8,128)(2,1)S(1)} collective-permute-done((bf16[1536,256]{1,0:T(8,128)(2,1)S(1)}, bf16[1536,256]{1,0:T(8,128)(2,1)S(1)}, u32[]{:S(2)}, u32[]{:S(2)}) %collective-permute-start.11) | collective-permute-done | bytes 786464 | tf_op jit(solution)/shard_map/ppermute | solution.py:213
  22.3 1.4 %users.3 = (bf16[1024,512]{1,0:T(8,128)(2,1)S(1)}, bf16[1024,512]{1,0:T(8,128)(2,1)S(1)}) custom-call(f32[8,128]{1,0:T(8,128)S(1)} %mark.2._, bf16[256,512]{1,0:T(8,128)(2,1)S(1)} %get-tuple-element.42.low, bf16[1024,512]{1,0:T(8,128)(2,1)S(1)} %copy-done.2, bf16[1024,512]{1,0:T(8,128)(2,1)S(1)} %collective-permute-done.1.refs_3_.refs_1_, ...), custom_call_target="tpu_custom_call" | custom-call | flops 1024 | bytes 1024 | tf_op jit(solution)/shard_map/users/pallas_call | solution.py:177
  23.7 2.0 %collective-permute-done.7.refs_1_ = bf16[128,512]{1,0:T(8,128)(2,1)S(1)} collective-permute-done((bf16[128,512]{1,0:T(8,128)(2,1)S(1)}, bf16[128,512]{1,0:T(8,128)(2,1)S(1)}, u32[]{:S(2)}, u32[]{:S(2)}) %collective-permute-start.7) | collective-permute-done | bytes 131104 | tf_op jit(solution)/shard_map/ppermute | solution.py:213
  25.7 1.1 %collective-permute-done.9.refs_2_ = bf16[128,512]{1,0:T(8,128)(2,1)S(1)} collective-permute-done((bf16[128,512]{1,0:T(8,128)(2,1)S(1)}, bf16[128,512]{1,0:T(8,128)(2,1)S(1)}, u32[]{:S(2)}, u32[]{:S(2)}) %collective-permute-start.9) | collective-permute-done | bytes 131104 | tf_op jit(solution)/shard_map/ppermute | solution.py:213
  26.8 1.9 %tiles.4 = (bf16[256,512]{1,0:T(8,128)(2,1)S(1)}, bf16[1024,256]{1,0:T(8,128)(2,1)S(1)}, bf16[1536,256]{1,0:T(8,128)(2,1)S(1)}, bf16[128,512]{1,0:T(8,128)(2,1)S...) custom-call(s32[2]{0:T(128)S(1)} %pad_add_fusion.place._, ...), custom_call_target="tpu_custom_call" | custom-call | flops 1024 | bytes 1024 | tf_op jit(solution)/shard_map/tiles/pallas_call | solution.py:177
  28.7 1.0 %collective-permute-start.14 = (bf16[128,512]{1,0:T(8,128)(2,1)S(1)}, bf16[128,512]{1,0:T(8,128)(2,1)S(1)}, u32[]{:S(2)}, u32[]{:S(2)}) collective-permute-start(bf16[128,512]{1,0:T(8,128)(2,1)S(1)} %get-tuple-element.52), channel_id=1, source_target_pairs={{0,2},{1,3},{2,0},{3,1},{4,6},{5,7},{6,4},{7,5},{8,10},{9,11},{10,... | collective-permute-start | bytes 393224 | tf_op jit(solution)/shard_map/ppermute | solution.py:213
  29.7 0.9 %prepare.7 = (bf16[1024,256]{1,0:T(8,128)(2,1)S(1)}, bf16[1024,256]{1,0:T(8,128)(2,1)S(1)}) custom-call(s32[2]{0:T(128)S(1)} %pad_add_fusion.place._, s32[1,1,3,2,8]{4,3,2,1,0:T(2,128)S(1)} %bitcast.6, s32[1,1,3]{2,1,0:T(1,128)S(1)} %copy-done.5, bf16[1,1,3,8,128,128]{5,4,3,2,1,0:T(8,128)(2,1)S(1)} %copy-done.1, s32[1,1,3,8,16,128]{5,4,3,2,1,0:T(8,128)S(1)} %copy-done.3, ...), custom_call_target="tpu_custom_call" | custom-call | flops 1024 | bytes 1024 | tf_op jit(solution)/shard_map/prepare/pallas_call | solution.py:177
  30.6 1.8 %collective-permute-start.13 = (bf16[128,512]{1,0:T(8,128)(2,1)S(1)}, bf16[128,512]{1,0:T(8,128)(2,1)S(1)}, u32[]{:S(2)}, u32[]{:S(2)}) collective-permute-start(bf16[128,512]{1,0:T(8,128)(2,1)S(1)} %get-tuple-element.50), channel_id=1, source_target_pairs={{0,6},{1,7},{2,4},{3,5},{4,10},{5,11},{6,8},{7,9},{8,14},{9,15},{1... | collective-permute-start | bytes 393224 | tf_op jit(solution)/shard_map/ppermute | solution.py:213
  32.4 1.3 %collective-permute-done.14.refs_1_ = bf16[128,512]{1,0:T(8,128)(2,1)S(1)} collective-permute-done((bf16[128,512]{1,0:T(8,128)(2,1)S(1)}, bf16[128,512]{1,0:T(8,128)(2,1)S(1)}, u32[]{:S(2)}, u32[]{:S(2)}) %collective-permute-start.14) | collective-permute-done | bytes 131104 | tf_op jit(solution)/shard_map/ppermute | solution.py:213
  33.7 0.1 join.3
  33.9 0.1 collective-permute-start.15
  33.9 0.1 collective-permute-start.16
  34.0 0.5 collective-permute-start.17
  34.5 4.2 %collective-permute-done.12.refs_0_ = bf16[128,512]{1,0:T(8,128)(2,1)S(1)} collective-permute-done((bf16[128,512]{1,0:T(8,128)(2,1)S(1)}, bf16[128,512]{1,0:T(8,128)(2,1)S(1)}, u32[]{:S(2)}, u32[]{:S(2)}) %collective-permute-start.12) | collective-permute-done | bytes 131104 | tf_op jit(solution)/shard_map/ppermute | solution.py:213
  38.7 1.4 %users.4 = (bf16[1024,512]{1,0:T(8,128)(2,1)S(1)}, bf16[1024,512]{1,0:T(8,128)(2,1)S(1)}) custom-call(f32[8,128]{1,0:T(8,128)S(1)} %mark.3._, bf16[256,512]{1,0:T(8,128)(2,1)S(1)} %get-tuple-element.56.low, bf16[1024,512]{1,0:T(8,128)(2,1)S(1)} %get-tuple-element.45.refs_3_.refs_0_, bf16[1024,512]{1,0:T(8,128)(2,1)S(1)} %get-tuple-element.46.refs_4_.refs_1_, ...), custom_call_target="tpu_custom_call" | custom-call | flops 1024 | bytes 1024 | tf_op jit(solution)/shard_map/users/pallas_call | solution.py:177
  40.1 1.2 %collective-permute-done.13.refs_1_ = bf16[128,512]{1,0:T(8,128)(2,1)S(1)} collective-permute-done((bf16[128,512]{1,0:T(8,128)(2,1)S(1)}, bf16[128,512]{1,0:T(8,128)(2,1)S(1)}, u32[]{:S(2)}, u32[]{:S(2)}) %collective-permute-start.13) | collective-permute-done | bytes 131104 | tf_op jit(solution)/shard_map/ppermute | solution.py:213
  41.3 1.1 %collective-permute-done.15.refs_2_ = bf16[128,512]{1,0:T(8,128)(2,1)S(1)} collective-permute-done((bf16[128,512]{1,0:T(8,128)(2,1)S(1)}, bf16[128,512]{1,0:T(8,128)(2,1)S(1)}, u32[]{:S(2)}, u32[]{:S(2)}) %collective-permute-start.15) | collective-permute-done | bytes 131104 | tf_op jit(solution)/shard_map/ppermute | solution.py:213
  42.4 2.0 %tiles.5 = (bf16[256,512]{1,0:T(8,128)(2,1)S(1)}, bf16[1024,256]{1,0:T(8,128)(2,1)S(1)}, bf16[1536,256]{1,0:T(8,128)(2,1)S(1)}, f32[128,512]{1,0:T(8,128)S(1)}, bf16[128,512]{1,0:T(8,128)(2,1)S(1)}) custom-call(s32[2]{0:T(128)S(1)} %pad_add_fusion.place._, bf16[128,512]{1,0:T(8,128)(2,1)S(1)} %collective-permute-done.12.refs_0_, ...), custom_call_target="tpu_custom_call" | custom-call | flops 1024 | bytes 1024 | tf_op jit(solution)/shard_map/tiles/pallas_call | solution.py:177
  44.4 0.1 collective-permute-start.18
  44.5 0.9 %collective-permute-start.19 = (bf16[128,512]{1,0:T(8,128)(2,1)S(1)}, bf16[128,512]{1,0:T(8,128)(2,1)S(1)}, u32[]{:S(2)}, u32[]{:S(2)}) collective-permute-start(bf16[128,512]{1,0:T(8,128)(2,1)S(1)} %get-tuple-element.67), channel_id=1, source_target_pairs={{0,2},{1,3},{2,0},{3,1},{4,6},{5,7},{6,4},{7,5},{8,10},{9,11},{10,... | collective-permute-start | bytes 393224 | tf_op jit(solution)/shard_map/ppermute | solution.py:213
  45.4 1.3 %collective-permute-done.18.refs_2_ = bf16[1536,256]{1,0:T(8,128)(2,1)S(1)} collective-permute-done((bf16[1536,256]{1,0:T(8,128)(2,1)S(1)}, bf16[1536,256]{1,0:T(8,128)(2,1)S(1)}, u32[]{:S(2)}, u32[]{:S(2)}) %collective-permute-start.18) | collective-permute-done | bytes 786464 | tf_op jit(solution)/shard_map/ppermute | solution.py:213
  46.8 2.3 %users.5.refs_2_ = bf16[1024,512]{1,0:T(8,128)(2,1)} custom-call(s32[2]{0:T(128)S(1)} %pad_add_fusion.place._, bf16[256,512]{1,0:T(8,128)(2,1)S(1)} %get-tuple-element.63.low, bf16[1024,512]{1,0:T(8,128)(2,1)S(1)} %get-tuple-element.59.refs_3_.refs_0_, bf16[1024,256]{1,0:T(8,128)(2,1)S(1)} %get-tuple-element.64.refs_1_, ...), custom_call_target="tpu_custom_call" | custom-call | flops 1024 | bytes 1024 | tf_op jit(solution)/shard_map/users/pallas_call | solution.py:177
  49.1 1.3 %collective-permute-done.19.refs_1_ = bf16[128,512]{1,0:T(8,128)(2,1)S(1)} collective-permute-done((bf16[128,512]{1,0:T(8,128)(2,1)S(1)}, bf16[128,512]{1,0:T(8,128)(2,1)S(1)}, u32[]{:S(2)}, u32[]{:S(2)}) %collective-permute-start.19) | collective-permute-done | bytes 131104 | tf_op jit(solution)/shard_map/ppermute | solution.py:213
  50.4 0.7 %final.1 = f32[128,512]{1,0:T(8,128)} custom-call(f32[128,512]{1,0:T(8,128)S(1)} %get-tuple-element.66.refs_0_, bf16[128,512]{1,0:T(8,128)(2,1)S(1)} %collective-permute-done.19.refs_1_, bf16[1024,512]{1,0:T(8,128)(2,1)} %users.5.refs_2_), custom_call_target="tpu_custom_call" | custom-call | flops 1024 | bytes 1024 | tf_op jit(solution)/shard_map/final/pallas_call | solution.py:177
  (21 shorter events, 0.1 us)
Async XLA Ops:
  0.6 6.1 %copy-start.3 = (s32[1,1,3,8,16,128]{5,4,3,2,1,0:T(8,128)S(1)}, s32[1,1,3,8,16,128]{5,4,3,2,1,0:T(8,128)}, u32[]{:S(2)}) copy-start(s32[1,1,3,8,16,128]{5,4,3,2,1,0:T(8,128)} %refs_3_.5) | copy-start | bytes 589828
  0.6 4.7 %copy-start.5 = (s32[1,1,3]{2,1,0:T(1,128)S(1)}, s32[1,1,3]{2,1,0:T(1,128)}, u32[]{:S(2)}) copy-start(s32[1,1,3]{2,1,0:T(1,128)} %refs_1_.5) | copy-start | bytes 40
  0.7 8.8 %collective-permute-start.1 = (bf16[1024,512]{1,0:T(8,128)(2,1)}, bf16[1024,512]{1,0:T(8,128)(2,1)S(1)}, u32[]{:S(2)}, u32[]{:S(2)}) collective-permute-start(bf16[1024,512]{1,0:T(8,128)(2,1)} %refs_0_.1), channel_id=1, source_target_pairs={{0,1},{1,0},{2,3},{3,2},{4,5},{5,4},{6,7},{7,6},{8,9},{9,8},{10,11... | collective-permute-start | bytes 3145736 | tf_op jit(solution)/shard_map/ppermute | solution.py:213
  1.2 7.4 %collective-permute-start.4 = (bf16[1,1,3,8,128,128]{5,4,3,2,1,0:T(8,128)(2,1)}, bf16[1,1,3,8,128,128]{5,4,3,2,1,0:T(8,128)(2,1)S(1)}, u32[]{:S(2)}, u32[]{:S(2)}) collective-permute-start(bf16[1,1,3,8,128,128]{5,4,3,2,1,0:T(8,128)(2,1)} %refs_2_.7), channel_id=1, source_target_pairs={{0,1},{1,0},{2,3},{3,2},{4,5},{5,4},{6,7},{7,6},{8,9},{9,8},{10,11... | collective-permute-start | bytes 2359304 | tf_op jit(solution)/shard_map/ppermute | solution.py:213
  1.2 7.4 %collective-permute-start.5 = (s32[1,1,3,8,16,128]{5,4,3,2,1,0:T(8,128)}, s32[1,1,3,8,16,128]{5,4,3,2,1,0:T(8,128)S(1)}, u32[]{:S(2)}, u32[]{:S(2)}) collective-permute-start(s32[1,1,3,8,16,128]{5,4,3,2,1,0:T(8,128)} %refs_3_.5), channel_id=1, source_target_pairs={{0,1},{1,0},{2,3},{3,2},{4,5},{5,4},{6,7},{7,6},{8,9},{9,8},{10,11... | collective-permute-start | bytes 589832 | tf_op jit(solution)/shard_map/ppermute | solution.py:213
  2.7 6.8 %collective-permute-start = (bf16[128,512]{1,0:T(8,128)(2,1)S(1)}, bf16[128,512]{1,0:T(8,128)(2,1)S(1)}, u32[]{:S(2)}, u32[]{:S(2)}) collective-permute-start(bf16[128,512]{1,0:T(8,128)(2,1)S(1)} %convert_element_type.3.refs_0_), channel_id=1, source_target_pairs={{0,2},{1,3},{2,0},{3,1},{4,6},{5,7},{6,4},{7,5},{8,10},{9,11},{10,... | collective-permute-start | bytes 393224 | tf_op jit(solution)/shard_map/ppermute | solution.py:213
  5.3 1.1 %collective-permute-start.3 = (s32[1,1,3]{2,1,0:T(1,128)S(1)}, s32[1,1,3]{2,1,0:T(1,128)S(1)}, u32[]{:S(2)}, u32[]{:S(2)}) collective-permute-start(s32[1,1,3]{2,1,0:T(1,128)S(1)} %copy-done.5), channel_id=1, source_target_pairs={{0,1},{1,0},{2,3},{3,2},{4,5},{5,4},{6,7},{7,6},{8,9},{9,8},{10,11... | collective-permute-start | bytes 44 | tf_op jit(solution)/shard_map/ppermute | solution.py:213
  5.5 1.0 %copy-start.4 = (s32[1,1,3,8,2]{3,4,2,1,0:T(2,128)S(1)}, s32[1,1,3,8,2]{3,4,2,1,0:T(2,128)}, u32[]{:S(2)}) copy-start(s32[1,1,3,8,2]{3,4,2,1,0:T(2,128)} %param.8) | copy-start | bytes 580
  6.4 2.2 %collective-permute-start.2 = (s32[1,1,3,2,8]{4,3,2,1,0:T(2,128)S(1)}, s32[1,1,3,2,8]{4,3,2,1,0:T(2,128)S(1)}, u32[]{:S(2)}, u32[]{:S(2)}) collective-permute-start(s32[1,1,3,2,8]{4,3,2,1,0:T(2,128)S(1)} %bitcast.3), channel_id=1, source_target_pairs={{0,1},{1,0},{2,3},{3,2},{4,5},{5,4},{6,7},{7,6},{8,9},{9,8},{10,11... | collective-permute-start | bytes 584 | tf_op jit(solution)/shard_map/ppermute | solution.py:213
  6.7 1.1 %copy-start = (bf16[1,1,3,8,128,128]{5,4,3,2,1,0:T(8,128)(2,1)S(1)}, bf16[1,1,3,8,128,128]{5,4,3,2,1,0:T(8,128)(2,1)}, u32[]{:S(2)}) copy-start(bf16[1,1,3,8,128,128]{5,4,3,2,1,0:T(8,128)(2,1)} %refs_2_.7) | copy-start | bytes 2359300
  8.6 1.2 %copy-start.2 = (bf16[1024,512]{1,0:T(8,128)(2,1)S(1)}, bf16[1024,512]{1,0:T(8,128)(2,1)}, u32[]{:S(2)}) copy-start(bf16[1024,512]{1,0:T(8,128)(2,1)} %refs_0_.1) | copy-start | bytes 3145732
  9.3 5.3 %copy-start.1 = (bf16[1,1,3,8,128,128]{5,4,3,2,1,0:T(8,128)(2,1)S(1)}, bf16[1,1,3,8,128,128]{5,4,3,2,1,0:T(8,128)(2,1)}, u32[]{:S(2)}) copy-start(bf16[1,1,3,8,128,128]{5,4,3,2,1,0:T(8,128)(2,1)} %refs_2_.7) | copy-start | bytes 2359300
  11.8 5.8 %collective-permute-start.8 = (bf16[128,512]{1,0:T(8,128)(2,1)S(1)}, bf16[128,512]{1,0:T(8,128)(2,1)S(1)}, u32[]{:S(2)}, u32[]{:S(2)}) collective-permute-start(bf16[128,512]{1,0:T(8,128)(2,1)S(1)} %get-tuple-element.38), channel_id=1, source_target_pairs={{0,2},{1,3},{2,0},{3,1},{4,6},{5,7},{6,4},{7,5},{8,10},{9,11},{10,... | collective-permute-start | bytes 393224 | tf_op jit(solution)/shard_map/ppermute | solution.py:213
  13.2 8.1 %collective-permute-start.6 = (bf16[128,512]{1,0:T(8,128)(2,1)S(1)}, bf16[128,512]{1,0:T(8,128)(2,1)S(1)}, u32[]{:S(2)}, u32[]{:S(2)}) collective-permute-start(bf16[128,512]{1,0:T(8,128)(2,1)S(1)} %get-tuple-element.35), channel_id=1, source_target_pairs={{0,4},{1,5},{2,6},{3,7},{4,8},{5,9},{6,10},{7,11},{8,12},{9,13},{1... | collective-permute-start | bytes 393224 | tf_op jit(solution)/shard_map/ppermute | solution.py:213
  15.8 9.9 %collective-permute-start.7 = (bf16[128,512]{1,0:T(8,128)(2,1)S(1)}, bf16[128,512]{1,0:T(8,128)(2,1)S(1)}, u32[]{:S(2)}, u32[]{:S(2)}) collective-permute-start(bf16[128,512]{1,0:T(8,128)(2,1)S(1)} %get-tuple-element.36), channel_id=1, source_target_pairs={{0,6},{1,7},{2,4},{3,5},{4,10},{5,11},{6,8},{7,9},{8,14},{9,15},{1... | collective-permute-start | bytes 393224 | tf_op jit(solution)/shard_map/ppermute | solution.py:213
  17.6 9.2 %collective-permute-start.9 = (bf16[128,512]{1,0:T(8,128)(2,1)S(1)}, bf16[128,512]{1,0:T(8,128)(2,1)S(1)}, u32[]{:S(2)}, u32[]{:S(2)}) collective-permute-start(bf16[128,512]{1,0:T(8,128)(2,1)S(1)} %get-tuple-element.41), channel_id=1, source_target_pairs={{0,4},{1,5},{2,6},{3,7},{4,8},{5,9},{6,10},{7,11},{8,12},{9,13},{1... | collective-permute-start | bytes 393224 | tf_op jit(solution)/shard_map/ppermute | solution.py:213
  19.3 2.0 %collective-permute-start.10 = (bf16[1024,256]{1,0:T(8,128)(2,1)S(1)}, bf16[1024,256]{1,0:T(8,128)(2,1)S(1)}, u32[]{:S(2)}, u32[]{:S(2)}) collective-permute-start(bf16[1024,256]{1,0:T(8,128)(2,1)S(1)} %get-tuple-element.43.refs_2_), channel_id=1, source_target_pairs={{0,1},{1,0},{2,3},{3,2},{4,5},{5,4},{6,7},{7,6},{8,9},{9,8},{10,11... | collective-permute-start | bytes 1572872 | tf_op jit(solution)/shard_map/ppermute | solution.py:213
  19.3 3.0 %collective-permute-start.11 = (bf16[1536,256]{1,0:T(8,128)(2,1)S(1)}, bf16[1536,256]{1,0:T(8,128)(2,1)S(1)}, u32[]{:S(2)}, u32[]{:S(2)}) collective-permute-start(bf16[1536,256]{1,0:T(8,128)(2,1)S(1)} %get-tuple-element.44.refs_3_), channel_id=1, source_target_pairs={{0,1},{1,0},{2,3},{3,2},{4,5},{5,4},{6,7},{7,6},{8,9},{9,8},{10,11... | collective-permute-start | bytes 2359304 | tf_op jit(solution)/shard_map/ppermute | solution.py:213
  28.7 5.0 %collective-permute-start.14 = (bf16[128,512]{1,0:T(8,128)(2,1)S(1)}, bf16[128,512]{1,0:T(8,128)(2,1)S(1)}, u32[]{:S(2)}, u32[]{:S(2)}) collective-permute-start(bf16[128,512]{1,0:T(8,128)(2,1)S(1)} %get-tuple-element.52), channel_id=1, source_target_pairs={{0,2},{1,3},{2,0},{3,1},{4,6},{5,7},{6,4},{7,5},{8,10},{9,11},{10,... | collective-permute-start | bytes 393224 | tf_op jit(solution)/shard_map/ppermute | solution.py:213
  29.7 9.0 %collective-permute-start.12 = (bf16[128,512]{1,0:T(8,128)(2,1)S(1)}, bf16[128,512]{1,0:T(8,128)(2,1)S(1)}, u32[]{:S(2)}, u32[]{:S(2)}) collective-permute-start(bf16[128,512]{1,0:T(8,128)(2,1)S(1)} %get-tuple-element.49), channel_id=1, source_target_pairs={{0,4},{1,5},{2,6},{3,7},{4,8},{5,9},{6,10},{7,11},{8,12},{9,13},{1... | collective-permute-start | bytes 393224 | tf_op jit(solution)/shard_map/ppermute | solution.py:213
  30.6 10.7 %collective-permute-start.13 = (bf16[128,512]{1,0:T(8,128)(2,1)S(1)}, bf16[128,512]{1,0:T(8,128)(2,1)S(1)}, u32[]{:S(2)}, u32[]{:S(2)}) collective-permute-start(bf16[128,512]{1,0:T(8,128)(2,1)S(1)} %get-tuple-element.50), channel_id=1, source_target_pairs={{0,6},{1,7},{2,4},{3,5},{4,10},{5,11},{6,8},{7,9},{8,14},{9,15},{1... | collective-permute-start | bytes 393224 | tf_op jit(solution)/shard_map/ppermute | solution.py:213
  33.9 8.6 %collective-permute-start.15 = (bf16[128,512]{1,0:T(8,128)(2,1)S(1)}, bf16[128,512]{1,0:T(8,128)(2,1)S(1)}, u32[]{:S(2)}, u32[]{:S(2)}) collective-permute-start(bf16[128,512]{1,0:T(8,128)(2,1)S(1)} %get-tuple-element.55), channel_id=1, source_target_pairs={{0,4},{1,5},{2,6},{3,7},{4,8},{5,9},{6,10},{7,11},{8,12},{9,13},{1... | collective-permute-start | bytes 393224 | tf_op jit(solution)/shard_map/ppermute | solution.py:213
  33.9 4.8 %collective-permute-start.16 = (bf16[1024,256]{1,0:T(8,128)(2,1)S(1)}, bf16[1024,256]{1,0:T(8,128)(2,1)S(1)}, u32[]{:S(2)}, u32[]{:S(2)}) collective-permute-start(bf16[1024,256]{1,0:T(8,128)(2,1)S(1)} %get-tuple-element.57.refs_2_), channel_id=1, source_target_pairs={{0,1},{1,0},{2,3},{3,2},{4,5},{5,4},{6,7},{7,6},{8,9},{9,8},{10,11... | collective-permute-start | bytes 1572872 | tf_op jit(solution)/shard_map/ppermute | solution.py:213
  34.0 4.7 %collective-permute-start.17 = (bf16[1536,256]{1,0:T(8,128)(2,1)S(1)}, bf16[1536,256]{1,0:T(8,128)(2,1)S(1)}, u32[]{:S(2)}, u32[]{:S(2)}) collective-permute-start(bf16[1536,256]{1,0:T(8,128)(2,1)S(1)} %get-tuple-element.58.refs_3_), channel_id=1, source_target_pairs={{0,1},{1,0},{2,3},{3,2},{4,5},{5,4},{6,7},{7,6},{8,9},{9,8},{10,11... | collective-permute-start | bytes 2359304 | tf_op jit(solution)/shard_map/ppermute | solution.py:213
  44.4 2.4 %collective-permute-start.18 = (bf16[1536,256]{1,0:T(8,128)(2,1)S(1)}, bf16[1536,256]{1,0:T(8,128)(2,1)S(1)}, u32[]{:S(2)}, u32[]{:S(2)}) collective-permute-start(bf16[1536,256]{1,0:T(8,128)(2,1)S(1)} %get-tuple-element.65), channel_id=1, source_target_pairs={{0,1},{1,0},{2,3},{3,2},{4,5},{5,4},{6,7},{7,6},{8,9},{9,8},{10,11... | collective-permute-start | bytes 2359304 | tf_op jit(solution)/shard_map/ppermute | solution.py:213
  44.5 5.9 %collective-permute-start.19 = (bf16[128,512]{1,0:T(8,128)(2,1)S(1)}, bf16[128,512]{1,0:T(8,128)(2,1)S(1)}, u32[]{:S(2)}, u32[]{:S(2)}) collective-permute-start(bf16[128,512]{1,0:T(8,128)(2,1)S(1)} %get-tuple-element.67), channel_id=1, source_target_pairs={{0,2},{1,3},{2,0},{3,1},{4,6},{5,7},{6,4},{7,5},{8,10},{9,11},{10,... | collective-permute-start | bytes 393224 | tf_op jit(solution)/shard_map/ppermute | solution.py:213

commit v6 on v5

--- a/solution.py
+++ b/solution.py
@@ -16,6 +16,7 @@
 HB = pl.BlockSpec(memory_space=pltpu.HBM)
 CORES = 2
 CHUNK = 512
+DIRECT = 7
 MARK = 1 << 34
 
 
@@ -74,12 +75,11 @@
     lax.fori_loop(0, counts[0, 0, visit], tile, 0)
 
 
-def tiles_kernel(first, last, chips, groups, close, place, *refs):
-    count = chips if first else chips + groups - 1
+def tiles_kernel(first, last, chips, direct, close, place, *refs):
+    count = chips if first else chips + 1
     arrived, refs = refs[:count], refs[count:]
     (users, peers, rates, peer_rates), refs = refs[:4], refs[4:]
     (low, errors, peer_errors), outs, (panel, total) = refs[:3], refs[3:-2], refs[-2:]
-    span = chips // groups
     core, chip = place[0], place[1]
     rows = panel.shape[0] // chips
     if first:
@@ -91,9 +91,8 @@
         now = arrived[0][...].astype(jnp.float32)
         for other in arrived[1:chips]:
             now = now + step_item * other[...].astype(jnp.float32)
-        panel[: span * rows, :] = now
-        if groups > 1:
-            panel[span * rows :, :] = arrived[chips][...].astype(jnp.float32)
+        panel[:direct, :] = now
+        panel[direct:, :] = arrived[chips][...].astype(jnp.float32)
     if close:
         low[...] = panel[...].astype(low.dtype)
     else:
@@ -124,12 +123,19 @@
             outs[k][...] = term.astype(outs[k].dtype)
     else:
         for j in range(chips):
-            joined, plain = outs[2 * (j // span)], outs[2 * (j // span) + 1]
-            at, to = slice(j * rows, (j + 1) * rows), slice(j % span * rows, (j % span + 1) * rows)
-            term = total[pl.ds(place_of(close, j, core, rows), rows), :]
-            old = panel[at, :]
-            joined[to, :] = (old + step_item * (term - shrinkage * old)).astype(joined.dtype)
-            plain[to, :] = term.astype(plain.dtype)
+            for (joined, plain), low_end, high_end in (
+                (outs[:2], 0, direct),
+                (outs[2:], direct, chips * rows),
+            ):
+                begin, end = max(j * rows, low_end), min((j + 1) * rows, high_end)
+                if begin >= end:
+                    continue
+                at = pl.multiple_of(place_of(close, j, core, rows) + begin - j * rows, 16)
+                term = total[pl.ds(at, end - begin), :]
+                old = panel[begin:end, :]
+                to = slice(begin - low_end, end - low_end)
+                joined[to, :] = (old + step_item * (term - shrinkage * old)).astype(joined.dtype)
+                plain[to, :] = term.astype(plain.dtype)
 
 
 def users_kernel(last, _, low, *refs):
@@ -244,8 +250,7 @@
     users, other_users = user_factors, swap(user_factors)
     tiles = [blocks, tile_counts, ratings, mask_words]
     other_tiles = [swap(x) for x in tiles]
-    groups = 2 if chips % 2 == 0 else 1
-    part = part // groups
+    direct = part * DIRECT // 256 * 16
     for visit in range(visits):
         last = visit + 1 == visits
         if visit == 0:
@@ -257,12 +262,11 @@
         if last:
             shared += [pltpu.VMEM((rows, width), full_type)]
             shared += [pltpu.VMEM((rows, width), low_type)] * (chips - 1)
-        if not last:
-            for group in range(groups):
-                shared += [pltpu.VMEM((part, width), full_type if group else low_type)]
-                shared += [pltpu.VMEM((part, width), low_type)]
+        else:
+            shared += [pltpu.VMEM((direct, width), low_type)] * 2
+            shared += [pltpu.VMEM((part - direct, width), kind) for kind in (full_type, low_type)]
         low, errors, other_errors, *ends = kernel_call(
-            functools.partial(tiles_kernel, visit == 0, last, chips, groups, close),
+            functools.partial(tiles_kernel, visit == 0, last, chips, direct, close),
             "tiles",
             [place, *arrived, users, other_users, *known],
             shared,
@@ -273,18 +277,16 @@
             arrived = ends[:1] + [move(ends[k], 0, k, False) for k in range(1, chips)]
             sets = [place, low, users, errors, swap(other_errors)]
         else:
-            if groups > 1:
-                others = [move(ends[3], 0, k, False) for k in range(1, chips)]
+            others = [move(ends[3], 0, k, False) for k in range(1, chips)]
             arrived = [move(ends[min(k, 1)], 1, k, False) for k in range(chips)]
-            if groups > 1:
-                summed, errors, other_errors = kernel_call(
-                    functools.partial(join_kernel, chips),
-                    "join",
-                    [ends[2], *others, errors, other_errors],
-                    [pltpu.VMEM(x.shape, low_type) for x in (ends[2], errors, other_errors)],
-                    1024,
-                )
-                arrived += [move(summed, 1, 0, False)]
+            summed, errors, other_errors = kernel_call(
+                functools.partial(join_kernel, chips),
+                "join",
+                [ends[2], *others, errors, other_errors],
+                [pltpu.VMEM(x.shape, low_type) for x in (ends[2], errors, other_errors)],
+                1024,
+            )
+            arrived += [move(summed, 1, 0, False)]
             sets = [marked(arrived[0]), low, users, other_users]
             sets += [errors, other_errors, swap(errors), swap(other_errors)]
         kind = jax.ShapeDtypeStruct if last else pltpu.VMEM

time: 51.2 us -> 51.1 us (level)
  transfers between devices with their start and end apart: 20 -> 20, of which waited for: 11 -> 13; matrix products, arithmetic and copies ran while one was open for 2% -> 2% of each run, Pallas kernels for 17% -> 17%
where the time goes in v6:
time: 51.1 us
  waiting for transfers between devices  16.9 us (33%)
  Pallas kernels  15.5 us (30%)
  starting transfers between devices  15.3 us (30%)
  local copies, waits for them, and re-layouts  1.49 us (3%)
  other arithmetic  1.04 us (2%)
  between operations  0.83 us (2%)
    ppermute x20, waiting for transfers between devices, moved(): return lax.ppermute(x, ('strata', 'shard'), pairs)  16.9 us
    pallas_call x13, Pallas kernels, kernel_call(): pl.pallas_call(body, name=name, out_shape=tuple(outs), in_specs=[SM if x....  15.5 us
    ppermute x20, starting transfers between devices, moved(): return lax.ppermute(x, ('strata', 'shard'), pairs)  15.3 us
    unnamed x12, local copies, waits for them, and re-layouts  1.49 us
  transfers between devices with their start and end apart: 20, of which 13 were waited for; matrix products, arithmetic and copies ran while one was open for 2% of the time, Pallas kernels for 17%

profile of v6, /device:TPU:0, one launch (start us, length us, event | category | flops | bytes accessed | tf_op | source)
XLA Modules:
  0.0 51.1 jit_solution(14456205718106447808)
XLA Ops:
  0.7 0.5 %collective-permute-start.1 = (bf16[1024,512]{1,0:T(8,128)(2,1)}, bf16[1024,512]{1,0:T(8,128)(2,1)S(1)}, u32[]{:S(2)}, u32[]{:S(2)}) collective-permute-start(bf16[1024,512]{1,0:T(8,128)(2,1)} %refs_0_.1), channel_id=1, source_target_pairs={{0,1},{1,0},{2,3},{3,2},{4,5},{5,4},{6,7},{7,6},{8,9},{9,8},{10,11... | collective-permute-start | bytes 3145736 | tf_op jit(solution)/shard_map/ppermute | solution.py:219
  1.2 0.1 collective-permute-start.4
  1.2 0.4 collective-permute-start.5
  1.7 1.0 %convert_element_type.3.refs_0_ = bf16[128,512]{1,0:T(8,128)(2,1)S(1)} convert(f32[128,512]{1,0:T(8,128)} %param.7) | non-fusion elementwise | flops 65536 | bytes 393216 | tf_op jit(solution)/shard_map/convert_element_type | solution.py:248
  2.7 2.7 %collective-permute-start = (bf16[128,512]{1,0:T(8,128)(2,1)S(1)}, bf16[128,512]{1,0:T(8,128)(2,1)S(1)}, u32[]{:S(2)}, u32[]{:S(2)}) collective-permute-start(bf16[128,512]{1,0:T(8,128)(2,1)S(1)} %convert_element_type.3.refs_0_), channel_id=1, source_target_pairs={{0,2},{1,3},{2,0},{3,1},{4,6},{5,7},{6,4},{7,5},{8,10},{9,11},{10,... | collective-permute-start | bytes 393224 | tf_op jit(solution)/shard_map/ppermute | solution.py:219
  5.3 0.2 collective-permute-start.3
  5.5 1.0 %collective-permute-done.3.refs_1_.refs_5_ = s32[1,1,3]{2,1,0:T(1,128)S(1)} collective-permute-done((s32[1,1,3]{2,1,0:T(1,128)S(1)}, s32[1,1,3]{2,1,0:T(1,128)S(1)}, u32[]{:S(2)}, u32[]{:S(2)}) %collective-permute-start.3) | collective-permute-done | bytes 44 | tf_op jit(solution)/shard_map/ppermute | solution.py:219
  6.4 0.2 collective-permute-start.2
  6.6 0.1 pad_add_fusion.place._
  6.7 1.1 %copy-done = bf16[1,1,3,8,128,128]{5,4,3,2,1,0:T(8,128)(2,1)S(1)} copy-done((bf16[1,1,3,8,128,128]{5,4,3,2,1,0:T(8,128)(2,1)S(1)}, bf16[1,1,3,8,128,128]{5,4,3,2,1,0:T(8,128)(2,1)}, u32[]{:S(2)}) %copy-start) | copy-done | bytes 786456
  7.9 0.7 %prepare.4.refs_4_ = bf16[1024,256]{1,0:T(8,128)(2,1)S(1)} custom-call(s32[2]{0:T(128)S(1)} %pad_add_fusion.place._, s32[1,1,3,2,8]{4,3,2,1,0:T(2,128)S(1)} %bitcast.4, s32[1,1,3]{2,1,0:T(1,128)S(1)} %copy-done.5, bf16[1,1,3,8,128,128]{5,4,3,2,1,0:T(8,128)(2,1)S(1)} %copy-done, s32[1,1,3,8,16,128]{5,4,3,2,1,0:T(8,128)S(1)} %copy-done.3), custom_call_target="tpu_custom_call" | custom-call | flops 1024 | bytes 1024 | tf_op jit(solution)/shard_map/prepare/pallas_call | solution.py:183
  8.6 0.8 %prepare.5.refs_5_ = bf16[1024,256]{1,0:T(8,128)(2,1)S(1)} custom-call(s32[2]{0:T(128)S(1)} %pad_add_fusion.place._, s32[1,1,3,2,8]{4,3,2,1,0:T(2,128)S(1)} %collective-permute-done.2.refs_0_.refs_4_, s32[1,1,3]{2,1,0:T(1,128)S(1)} %collective-permute-done.3.refs_1_.refs_5_, bf16[1,1,3,8,128,128]{5,4,3,2,1,0:T(8,128)(2,1)S(1)} %collective-permute-done.4.refs_2_.refs_6_, ...), custom_call_target="tpu_custom_call" | custom-call | flops 1024 | bytes 1024 | tf_op jit(solution)/shard_map/prepare/pallas_call | solution.py:183
  9.4 0.3 copy-done.2
  9.8 1.9 %tiles.3 = (bf16[256,512]{1,0:T(8,128)(2,1)S(1)}, bf16[1024,256]{1,0:T(8,128)(2,1)S(1)}, bf16[1536,256]{1,0:T(8,128)(2,1)S(1)}, bf16[112,512]{1,0:T(8,128)(2,1)S...) custom-call(s32[2]{0:T(128)S(1)} %pad_add_fusion.place._, ...), custom_call_target="tpu_custom_call" | custom-call | flops 1024 | bytes 1024 | tf_op jit(solution)/shard_map/tiles/pallas_call | solution.py:183
  11.7 1.5 %collective-permute-start.8 = (bf16[144,512]{1,0:T(8,128)(2,1)S(1)}, bf16[144,512]{1,0:T(8,128)(2,1)S(1)}, u32[]{:S(2)}, u32[]{:S(2)}) collective-permute-start(bf16[144,512]{1,0:T(8,128)(2,1)S(1)} %get-tuple-element.38), channel_id=1, source_target_pairs={{0,2},{1,3},{2,0},{3,1},{4,6},{5,7},{6,4},{7,5},{8,10},{9,11},{10,... | collective-permute-start | bytes 442376 | tf_op jit(solution)/shard_map/ppermute | solution.py:219
  13.2 1.5 %collective-permute-start.6 = (bf16[112,512]{1,0:T(8,128)(2,1)S(1)}, bf16[112,512]{1,0:T(8,128)(2,1)S(1)}, u32[]{:S(2)}, u32[]{:S(2)}) collective-permute-start(bf16[112,512]{1,0:T(8,128)(2,1)S(1)} %get-tuple-element.35), channel_id=1, source_target_pairs={{0,4},{1,5},{2,6},{3,7},{4,8},{5,9},{6,10},{7,11},{8,12},{9,13},{1... | collective-permute-start | bytes 344072 | tf_op jit(solution)/shard_map/ppermute | solution.py:219
  14.7 1.0 %prepare.6 = (bf16[1024,256]{1,0:T(8,128)(2,1)S(1)}, bf16[1024,256]{1,0:T(8,128)(2,1)S(1)}) custom-call(s32[2]{0:T(128)S(1)} %pad_add_fusion.place._, s32[1,1,3,2,8]{4,3,2,1,0:T(2,128)S(1)} %bitcast.5, s32[1,1,3]{2,1,0:T(1,128)S(1)} %copy-done.5, bf16[1,1,3,8,128,128]{5,4,3,2,1,0:T(8,128)(2,1)S(1)} %copy-done.1, s32[1,1,3,8,16,128]{5,4,3,2,1,0:T(8,128)S(1)} %copy-done.3, ...), custom_call_target="tpu_custom_call" | custom-call | flops 1024 | bytes 1024 | tf_op jit(solution)/shard_map/prepare/pallas_call | solution.py:183
  15.7 1.7 %collective-permute-start.7 = (bf16[112,512]{1,0:T(8,128)(2,1)S(1)}, bf16[112,512]{1,0:T(8,128)(2,1)S(1)}, u32[]{:S(2)}, u32[]{:S(2)}) collective-permute-start(bf16[112,512]{1,0:T(8,128)(2,1)S(1)} %get-tuple-element.36), channel_id=1, source_target_pairs={{0,6},{1,7},{2,4},{3,5},{4,10},{5,11},{6,8},{7,9},{8,14},{9,15},{1... | collective-permute-start | bytes 344072 | tf_op jit(solution)/shard_map/ppermute | solution.py:219
  17.4 0.6 %collective-permute-done.8.refs_1_ = bf16[144,512]{1,0:T(8,128)(2,1)S(1)} collective-permute-done((bf16[144,512]{1,0:T(8,128)(2,1)S(1)}, bf16[144,512]{1,0:T(8,128)(2,1)S(1)}, u32[]{:S(2)}, u32[]{:S(2)}) %collective-permute-start.8) | collective-permute-done | bytes 147488 | tf_op jit(solution)/shard_map/ppermute | solution.py:219
  18.0 0.1 join.2
  18.1 1.6 %collective-permute-start.9 = (bf16[144,512]{1,0:T(8,128)(2,1)S(1)}, bf16[144,512]{1,0:T(8,128)(2,1)S(1)}, u32[]{:S(2)}, u32[]{:S(2)}) collective-permute-start(bf16[144,512]{1,0:T(8,128)(2,1)S(1)} %get-tuple-element.41), channel_id=1, source_target_pairs={{0,4},{1,5},{2,6},{3,7},{4,8},{5,9},{6,10},{7,11},{8,12},{9,13},{1... | collective-permute-start | bytes 442376 | tf_op jit(solution)/shard_map/ppermute | solution.py:219
  19.7 0.5 collective-permute-start.11
  20.2 0.5 %collective-permute-done.6.refs_0_ = bf16[112,512]{1,0:T(8,128)(2,1)S(1)} collective-permute-done((bf16[112,512]{1,0:T(8,128)(2,1)S(1)}, bf16[112,512]{1,0:T(8,128)(2,1)S(1)}, u32[]{:S(2)}, u32[]{:S(2)}) %collective-permute-start.6) | collective-permute-done | bytes 114720 | tf_op jit(solution)/shard_map/ppermute | solution.py:219
  20.8 0.9 %collective-permute-done.10.refs_4_ = bf16[1024,256]{1,0:T(8,128)(2,1)S(1)} collective-permute-done((bf16[1024,256]{1,0:T(8,128)(2,1)S(1)}, bf16[1024,256]{1,0:T(8,128)(2,1)S(1)}, u32[]{:S(2)}, u32[]{:S(2)}) %collective-permute-start.10) | collective-permute-done | bytes 524320 | tf_op jit(solution)/shard_map/ppermute | solution.py:219
  21.6 1.1 %collective-permute-done.11.refs_5_ = bf16[1536,256]{1,0:T(8,128)(2,1)S(1)} collective-permute-done((bf16[1536,256]{1,0:T(8,128)(2,1)S(1)}, bf16[1536,256]{1,0:T(8,128)(2,1)S(1)}, u32[]{:S(2)}, u32[]{:S(2)}) %collective-permute-start.11) | collective-permute-done | bytes 786464 | tf_op jit(solution)/shard_map/ppermute | solution.py:219
  22.7 1.4 %users.3 = (bf16[1024,512]{1,0:T(8,128)(2,1)S(1)}, bf16[1024,512]{1,0:T(8,128)(2,1)S(1)}) custom-call(f32[8,128]{1,0:T(8,128)S(1)} %mark.2._, bf16[256,512]{1,0:T(8,128)(2,1)S(1)} %get-tuple-element.42.low, bf16[1024,512]{1,0:T(8,128)(2,1)S(1)} %copy-done.2, bf16[1024,512]{1,0:T(8,128)(2,1)S(1)} %collective-permute-done.1.refs_3_.refs_1_, ...), custom_call_target="tpu_custom_call" | custom-call | flops 1024 | bytes 1024 | tf_op jit(solution)/shard_map/users/pallas_call | solution.py:183
  24.1 1.0 %collective-permute-done.7.refs_1_ = bf16[112,512]{1,0:T(8,128)(2,1)S(1)} collective-permute-done((bf16[112,512]{1,0:T(8,128)(2,1)S(1)}, bf16[112,512]{1,0:T(8,128)(2,1)S(1)}, u32[]{:S(2)}, u32[]{:S(2)}) %collective-permute-start.7) | collective-permute-done | bytes 114720 | tf_op jit(solution)/shard_map/ppermute | solution.py:219
  25.2 1.6 %collective-permute-done.9.refs_2_ = bf16[144,512]{1,0:T(8,128)(2,1)S(1)} collective-permute-done((bf16[144,512]{1,0:T(8,128)(2,1)S(1)}, bf16[144,512]{1,0:T(8,128)(2,1)S(1)}, u32[]{:S(2)}, u32[]{:S(2)}) %collective-permute-start.9) | collective-permute-done | bytes 147488 | tf_op jit(solution)/shard_map/ppermute | solution.py:219
  26.8 1.9 %tiles.4 = (bf16[256,512]{1,0:T(8,128)(2,1)S(1)}, bf16[1024,256]{1,0:T(8,128)(2,1)S(1)}, bf16[1536,256]{1,0:T(8,128)(2,1)S(1)}, bf16[112,512]{1,0:T(8,128)(2,1)S...) custom-call(s32[2]{0:T(128)S(1)} %pad_add_fusion.place._, ...), custom_call_target="tpu_custom_call" | custom-call | flops 1024 | bytes 1024 | tf_op jit(solution)/shard_map/tiles/pallas_call | solution.py:183
  28.7 1.1 %collective-permute-start.14 = (bf16[144,512]{1,0:T(8,128)(2,1)S(1)}, bf16[144,512]{1,0:T(8,128)(2,1)S(1)}, u32[]{:S(2)}, u32[]{:S(2)}) collective-permute-start(bf16[144,512]{1,0:T(8,128)(2,1)S(1)} %get-tuple-element.52), channel_id=1, source_target_pairs={{0,2},{1,3},{2,0},{3,1},{4,6},{5,7},{6,4},{7,5},{8,10},{9,11},{10,... | collective-permute-start | bytes 442376 | tf_op jit(solution)/shard_map/ppermute | solution.py:219
  29.8 1.0 %prepare.7 = (bf16[1024,256]{1,0:T(8,128)(2,1)S(1)}, bf16[1024,256]{1,0:T(8,128)(2,1)S(1)}) custom-call(s32[2]{0:T(128)S(1)} %pad_add_fusion.place._, s32[1,1,3,2,8]{4,3,2,1,0:T(2,128)S(1)} %bitcast.6, s32[1,1,3]{2,1,0:T(1,128)S(1)} %copy-done.5, bf16[1,1,3,8,128,128]{5,4,3,2,1,0:T(8,128)(2,1)S(1)} %copy-done.1, s32[1,1,3,8,16,128]{5,4,3,2,1,0:T(8,128)S(1)} %copy-done.3, ...), custom_call_target="tpu_custom_call" | custom-call | flops 1024 | bytes 1024 | tf_op jit(solution)/shard_map/prepare/pallas_call | solution.py:183
  30.9 1.6 %collective-permute-start.13 = (bf16[112,512]{1,0:T(8,128)(2,1)S(1)}, bf16[112,512]{1,0:T(8,128)(2,1)S(1)}, u32[]{:S(2)}, u32[]{:S(2)}) collective-permute-start(bf16[112,512]{1,0:T(8,128)(2,1)S(1)} %get-tuple-element.50), channel_id=1, source_target_pairs={{0,6},{1,7},{2,4},{3,5},{4,10},{5,11},{6,8},{7,9},{8,14},{9,15},{1... | collective-permute-start | bytes 344072 | tf_op jit(solution)/shard_map/ppermute | solution.py:219
  32.5 1.5 %collective-permute-done.14.refs_1_ = bf16[144,512]{1,0:T(8,128)(2,1)S(1)} collective-permute-done((bf16[144,512]{1,0:T(8,128)(2,1)S(1)}, bf16[144,512]{1,0:T(8,128)(2,1)S(1)}, u32[]{:S(2)}, u32[]{:S(2)}) %collective-permute-start.14) | collective-permute-done | bytes 147488 | tf_op jit(solution)/shard_map/ppermute | solution.py:219
  33.9 0.1 join.3
  34.0 0.1 collective-permute-start.15
  34.1 0.1 collective-permute-start.16
  34.2 0.5 collective-permute-start.17
  34.7 3.8 %collective-permute-done.12.refs_0_ = bf16[112,512]{1,0:T(8,128)(2,1)S(1)} collective-permute-done((bf16[112,512]{1,0:T(8,128)(2,1)S(1)}, bf16[112,512]{1,0:T(8,128)(2,1)S(1)}, u32[]{:S(2)}, u32[]{:S(2)}) %collective-permute-start.12) | collective-permute-done | bytes 114720 | tf_op jit(solution)/shard_map/ppermute | solution.py:219
  38.5 1.4 %users.4 = (bf16[1024,512]{1,0:T(8,128)(2,1)S(1)}, bf16[1024,512]{1,0:T(8,128)(2,1)S(1)}) custom-call(f32[8,128]{1,0:T(8,128)S(1)} %mark.3._, bf16[256,512]{1,0:T(8,128)(2,1)S(1)} %get-tuple-element.56.low, bf16[1024,512]{1,0:T(8,128)(2,1)S(1)} %get-tuple-element.45.refs_3_.refs_0_, bf16[1024,512]{1,0:T(8,128)(2,1)S(1)} %get-tuple-element.46.refs_4_.refs_1_, ...), custom_call_target="tpu_custom_call" | custom-call | flops 1024 | bytes 1024 | tf_op jit(solution)/shard_map/users/pallas_call | solution.py:183
  39.9 1.3 %collective-permute-done.13.refs_1_ = bf16[112,512]{1,0:T(8,128)(2,1)S(1)} collective-permute-done((bf16[112,512]{1,0:T(8,128)(2,1)S(1)}, bf16[112,512]{1,0:T(8,128)(2,1)S(1)}, u32[]{:S(2)}, u32[]{:S(2)}) %collective-permute-start.13) | collective-permute-done | bytes 114720 | tf_op jit(solution)/shard_map/ppermute | solution.py:219
  41.2 1.2 %collective-permute-done.15.refs_2_ = bf16[144,512]{1,0:T(8,128)(2,1)S(1)} collective-permute-done((bf16[144,512]{1,0:T(8,128)(2,1)S(1)}, bf16[144,512]{1,0:T(8,128)(2,1)S(1)}, u32[]{:S(2)}, u32[]{:S(2)}) %collective-permute-start.15) | collective-permute-done | bytes 147488 | tf_op jit(solution)/shard_map/ppermute | solution.py:219
  42.4 2.0 %tiles.5 = (bf16[256,512]{1,0:T(8,128)(2,1)S(1)}, bf16[1024,256]{1,0:T(8,128)(2,1)S(1)}, bf16[1536,256]{1,0:T(8,128)(2,1)S(1)}, f32[128,512]{1,0:T(8,128)S(1)}, bf16[128,512]{1,0:T(8,128)(2,1)S(1)}) custom-call(s32[2]{0:T(128)S(1)} %pad_add_fusion.place._, bf16[112,512]{1,0:T(8,128)(2,1)S(1)} %collective-permute-done.12.refs_0_, ...), custom_call_target="tpu_custom_call" | custom-call | flops 1024 | bytes 1024 | tf_op jit(solution)/shard_map/tiles/pallas_call | solution.py:183
  44.3 0.1 collective-permute-start.18
  44.4 1.1 %collective-permute-start.19 = (bf16[128,512]{1,0:T(8,128)(2,1)S(1)}, bf16[128,512]{1,0:T(8,128)(2,1)S(1)}, u32[]{:S(2)}, u32[]{:S(2)}) collective-permute-start(bf16[128,512]{1,0:T(8,128)(2,1)S(1)} %get-tuple-element.67), channel_id=1, source_target_pairs={{0,2},{1,3},{2,0},{3,1},{4,6},{5,7},{6,4},{7,5},{8,10},{9,11},{10,... | collective-permute-start | bytes 393224 | tf_op jit(solution)/shard_map/ppermute | solution.py:219
  45.5 1.2 %collective-permute-done.18.refs_2_ = bf16[1536,256]{1,0:T(8,128)(2,1)S(1)} collective-permute-done((bf16[1536,256]{1,0:T(8,128)(2,1)S(1)}, bf16[1536,256]{1,0:T(8,128)(2,1)S(1)}, u32[]{:S(2)}, u32[]{:S(2)}) %collective-permute-start.18) | collective-permute-done | bytes 786464 | tf_op jit(solution)/shard_map/ppermute | solution.py:219
  46.7 2.3 %users.5.refs_2_ = bf16[1024,512]{1,0:T(8,128)(2,1)} custom-call(s32[2]{0:T(128)S(1)} %pad_add_fusion.place._, bf16[256,512]{1,0:T(8,128)(2,1)S(1)} %get-tuple-element.63.low, bf16[1024,512]{1,0:T(8,128)(2,1)S(1)} %get-tuple-element.59.refs_3_.refs_0_, bf16[1024,256]{1,0:T(8,128)(2,1)S(1)} %get-tuple-element.64.refs_1_, ...), custom_call_target="tpu_custom_call" | custom-call | flops 1024 | bytes 1024 | tf_op jit(solution)/shard_map/users/pallas_call | solution.py:183
  49.0 1.3 %collective-permute-done.19.refs_1_ = bf16[128,512]{1,0:T(8,128)(2,1)S(1)} collective-permute-done((bf16[128,512]{1,0:T(8,128)(2,1)S(1)}, bf16[128,512]{1,0:T(8,128)(2,1)S(1)}, u32[]{:S(2)}, u32[]{:S(2)}) %collective-permute-start.19) | collective-permute-done | bytes 131104 | tf_op jit(solution)/shard_map/ppermute | solution.py:219
  50.3 0.7 %final.1 = f32[128,512]{1,0:T(8,128)} custom-call(f32[128,512]{1,0:T(8,128)S(1)} %get-tuple-element.66.refs_0_, bf16[128,512]{1,0:T(8,128)(2,1)S(1)} %collective-permute-done.19.refs_1_, bf16[1024,512]{1,0:T(8,128)(2,1)} %users.5.refs_2_), custom_call_target="tpu_custom_call" | custom-call | flops 1024 | bytes 1024 | tf_op jit(solution)/shard_map/final/pallas_call | solution.py:183
  (21 shorter events, 0.1 us)
Async XLA Ops:
  0.6 6.1 %copy-start.3 = (s32[1,1,3,8,16,128]{5,4,3,2,1,0:T(8,128)S(1)}, s32[1,1,3,8,16,128]{5,4,3,2,1,0:T(8,128)}, u32[]{:S(2)}) copy-start(s32[1,1,3,8,16,128]{5,4,3,2,1,0:T(8,128)} %refs_3_.5) | copy-start | bytes 589828
  0.6 4.7 %copy-start.5 = (s32[1,1,3]{2,1,0:T(1,128)S(1)}, s32[1,1,3]{2,1,0:T(1,128)}, u32[]{:S(2)}) copy-start(s32[1,1,3]{2,1,0:T(1,128)} %refs_1_.5) | copy-start | bytes 40
  0.7 8.8 %collective-permute-start.1 = (bf16[1024,512]{1,0:T(8,128)(2,1)}, bf16[1024,512]{1,0:T(8,128)(2,1)S(1)}, u32[]{:S(2)}, u32[]{:S(2)}) collective-permute-start(bf16[1024,512]{1,0:T(8,128)(2,1)} %refs_0_.1), channel_id=1, source_target_pairs={{0,1},{1,0},{2,3},{3,2},{4,5},{5,4},{6,7},{7,6},{8,9},{9,8},{10,11... | collective-permute-start | bytes 3145736 | tf_op jit(solution)/shard_map/ppermute | solution.py:219
  1.2 7.4 %collective-permute-start.4 = (bf16[1,1,3,8,128,128]{5,4,3,2,1,0:T(8,128)(2,1)}, bf16[1,1,3,8,128,128]{5,4,3,2,1,0:T(8,128)(2,1)S(1)}, u32[]{:S(2)}, u32[]{:S(2)}) collective-permute-start(bf16[1,1,3,8,128,128]{5,4,3,2,1,0:T(8,128)(2,1)} %refs_2_.7), channel_id=1, source_target_pairs={{0,1},{1,0},{2,3},{3,2},{4,5},{5,4},{6,7},{7,6},{8,9},{9,8},{10,11... | collective-permute-start | bytes 2359304 | tf_op jit(solution)/shard_map/ppermute | solution.py:219
  1.2 7.3 %collective-permute-start.5 = (s32[1,1,3,8,16,128]{5,4,3,2,1,0:T(8,128)}, s32[1,1,3,8,16,128]{5,4,3,2,1,0:T(8,128)S(1)}, u32[]{:S(2)}, u32[]{:S(2)}) collective-permute-start(s32[1,1,3,8,16,128]{5,4,3,2,1,0:T(8,128)} %refs_3_.5), channel_id=1, source_target_pairs={{0,1},{1,0},{2,3},{3,2},{4,5},{5,4},{6,7},{7,6},{8,9},{9,8},{10,11... | collective-permute-start | bytes 589832 | tf_op jit(solution)/shard_map/ppermute | solution.py:219
  2.7 6.8 %collective-permute-start = (bf16[128,512]{1,0:T(8,128)(2,1)S(1)}, bf16[128,512]{1,0:T(8,128)(2,1)S(1)}, u32[]{:S(2)}, u32[]{:S(2)}) collective-permute-start(bf16[128,512]{1,0:T(8,128)(2,1)S(1)} %convert_element_type.3.refs_0_), channel_id=1, source_target_pairs={{0,2},{1,3},{2,0},{3,1},{4,6},{5,7},{6,4},{7,5},{8,10},{9,11},{10,... | collective-permute-start | bytes 393224 | tf_op jit(solution)/shard_map/ppermute | solution.py:219
  5.3 1.1 %collective-permute-start.3 = (s32[1,1,3]{2,1,0:T(1,128)S(1)}, s32[1,1,3]{2,1,0:T(1,128)S(1)}, u32[]{:S(2)}, u32[]{:S(2)}) collective-permute-start(s32[1,1,3]{2,1,0:T(1,128)S(1)} %copy-done.5), channel_id=1, source_target_pairs={{0,1},{1,0},{2,3},{3,2},{4,5},{5,4},{6,7},{7,6},{8,9},{9,8},{10,11... | collective-permute-start | bytes 44 | tf_op jit(solution)/shard_map/ppermute | solution.py:219
  5.5 1.0 %copy-start.4 = (s32[1,1,3,8,2]{3,4,2,1,0:T(2,128)S(1)}, s32[1,1,3,8,2]{3,4,2,1,0:T(2,128)}, u32[]{:S(2)}) copy-start(s32[1,1,3,8,2]{3,4,2,1,0:T(2,128)} %param.8) | copy-start | bytes 580
  6.4 2.1 %collective-permute-start.2 = (s32[1,1,3,2,8]{4,3,2,1,0:T(2,128)S(1)}, s32[1,1,3,2,8]{4,3,2,1,0:T(2,128)S(1)}, u32[]{:S(2)}, u32[]{:S(2)}) collective-permute-start(s32[1,1,3,2,8]{4,3,2,1,0:T(2,128)S(1)} %bitcast.3), channel_id=1, source_target_pairs={{0,1},{1,0},{2,3},{3,2},{4,5},{5,4},{6,7},{7,6},{8,9},{9,8},{10,11... | collective-permute-start | bytes 584 | tf_op jit(solution)/shard_map/ppermute | solution.py:219
  6.7 1.1 %copy-start = (bf16[1,1,3,8,128,128]{5,4,3,2,1,0:T(8,128)(2,1)S(1)}, bf16[1,1,3,8,128,128]{5,4,3,2,1,0:T(8,128)(2,1)}, u32[]{:S(2)}) copy-start(bf16[1,1,3,8,128,128]{5,4,3,2,1,0:T(8,128)(2,1)} %refs_2_.7) | copy-start | bytes 2359300
  8.5 1.2 %copy-start.2 = (bf16[1024,512]{1,0:T(8,128)(2,1)S(1)}, bf16[1024,512]{1,0:T(8,128)(2,1)}, u32[]{:S(2)}) copy-start(bf16[1024,512]{1,0:T(8,128)(2,1)} %refs_0_.1) | copy-start | bytes 3145732
  9.4 5.3 %copy-start.1 = (bf16[1,1,3,8,128,128]{5,4,3,2,1,0:T(8,128)(2,1)S(1)}, bf16[1,1,3,8,128,128]{5,4,3,2,1,0:T(8,128)(2,1)}, u32[]{:S(2)}) copy-start(bf16[1,1,3,8,128,128]{5,4,3,2,1,0:T(8,128)(2,1)} %refs_2_.7) | copy-start | bytes 2359300
  11.7 6.3 %collective-permute-start.8 = (bf16[144,512]{1,0:T(8,128)(2,1)S(1)}, bf16[144,512]{1,0:T(8,128)(2,1)S(1)}, u32[]{:S(2)}, u32[]{:S(2)}) collective-permute-start(bf16[144,512]{1,0:T(8,128)(2,1)S(1)} %get-tuple-element.38), channel_id=1, source_target_pairs={{0,2},{1,3},{2,0},{3,1},{4,6},{5,7},{6,4},{7,5},{8,10},{9,11},{10,... | collective-permute-start | bytes 442376 | tf_op jit(solution)/shard_map/ppermute | solution.py:219
  13.2 7.6 %collective-permute-start.6 = (bf16[112,512]{1,0:T(8,128)(2,1)S(1)}, bf16[112,512]{1,0:T(8,128)(2,1)S(1)}, u32[]{:S(2)}, u32[]{:S(2)}) collective-permute-start(bf16[112,512]{1,0:T(8,128)(2,1)S(1)} %get-tuple-element.35), channel_id=1, source_target_pairs={{0,4},{1,5},{2,6},{3,7},{4,8},{5,9},{6,10},{7,11},{8,12},{9,13},{1... | collective-permute-start | bytes 344072 | tf_op jit(solution)/shard_map/ppermute | solution.py:219
  15.7 9.5 %collective-permute-start.7 = (bf16[112,512]{1,0:T(8,128)(2,1)S(1)}, bf16[112,512]{1,0:T(8,128)(2,1)S(1)}, u32[]{:S(2)}, u32[]{:S(2)}) collective-permute-start(bf16[112,512]{1,0:T(8,128)(2,1)S(1)} %get-tuple-element.36), channel_id=1, source_target_pairs={{0,6},{1,7},{2,4},{3,5},{4,10},{5,11},{6,8},{7,9},{8,14},{9,15},{1... | collective-permute-start | bytes 344072 | tf_op jit(solution)/shard_map/ppermute | solution.py:219
  18.1 8.7 %collective-permute-start.9 = (bf16[144,512]{1,0:T(8,128)(2,1)S(1)}, bf16[144,512]{1,0:T(8,128)(2,1)S(1)}, u32[]{:S(2)}, u32[]{:S(2)}) collective-permute-start(bf16[144,512]{1,0:T(8,128)(2,1)S(1)} %get-tuple-element.41), channel_id=1, source_target_pairs={{0,4},{1,5},{2,6},{3,7},{4,8},{5,9},{6,10},{7,11},{8,12},{9,13},{1... | collective-permute-start | bytes 442376 | tf_op jit(solution)/shard_map/ppermute | solution.py:219
  19.7 1.9 %collective-permute-start.10 = (bf16[1024,256]{1,0:T(8,128)(2,1)S(1)}, bf16[1024,256]{1,0:T(8,128)(2,1)S(1)}, u32[]{:S(2)}, u32[]{:S(2)}) collective-permute-start(bf16[1024,256]{1,0:T(8,128)(2,1)S(1)} %get-tuple-element.43.refs_2_), channel_id=1, source_target_pairs={{0,1},{1,0},{2,3},{3,2},{4,5},{5,4},{6,7},{7,6},{8,9},{9,8},{10,11... | collective-permute-start | bytes 1572872 | tf_op jit(solution)/shard_map/ppermute | solution.py:219
  19.7 3.0 %collective-permute-start.11 = (bf16[1536,256]{1,0:T(8,128)(2,1)S(1)}, bf16[1536,256]{1,0:T(8,128)(2,1)S(1)}, u32[]{:S(2)}, u32[]{:S(2)}) collective-permute-start(bf16[1536,256]{1,0:T(8,128)(2,1)S(1)} %get-tuple-element.44.refs_3_), channel_id=1, source_target_pairs={{0,1},{1,0},{2,3},{3,2},{4,5},{5,4},{6,7},{7,6},{8,9},{9,8},{10,11... | collective-permute-start | bytes 2359304 | tf_op jit(solution)/shard_map/ppermute | solution.py:219
  28.7 5.2 %collective-permute-start.14 = (bf16[144,512]{1,0:T(8,128)(2,1)S(1)}, bf16[144,512]{1,0:T(8,128)(2,1)S(1)}, u32[]{:S(2)}, u32[]{:S(2)}) collective-permute-start(bf16[144,512]{1,0:T(8,128)(2,1)S(1)} %get-tuple-element.52), channel_id=1, source_target_pairs={{0,2},{1,3},{2,0},{3,1},{4,6},{5,7},{6,4},{7,5},{8,10},{9,11},{10,... | collective-permute-start | bytes 442376 | tf_op jit(solution)/shard_map/ppermute | solution.py:219
  29.8 8.7 %collective-permute-start.12 = (bf16[112,512]{1,0:T(8,128)(2,1)S(1)}, bf16[112,512]{1,0:T(8,128)(2,1)S(1)}, u32[]{:S(2)}, u32[]{:S(2)}) collective-permute-start(bf16[112,512]{1,0:T(8,128)(2,1)S(1)} %get-tuple-element.49), channel_id=1, source_target_pairs={{0,4},{1,5},{2,6},{3,7},{4,8},{5,9},{6,10},{7,11},{8,12},{9,13},{1... | collective-permute-start | bytes 344072 | tf_op jit(solution)/shard_map/ppermute | solution.py:219
  30.9 10.3 %collective-permute-start.13 = (bf16[112,512]{1,0:T(8,128)(2,1)S(1)}, bf16[112,512]{1,0:T(8,128)(2,1)S(1)}, u32[]{:S(2)}, u32[]{:S(2)}) collective-permute-start(bf16[112,512]{1,0:T(8,128)(2,1)S(1)} %get-tuple-element.50), channel_id=1, source_target_pairs={{0,6},{1,7},{2,4},{3,5},{4,10},{5,11},{6,8},{7,9},{8,14},{9,15},{1... | collective-permute-start | bytes 344072 | tf_op jit(solution)/shard_map/ppermute | solution.py:219
  34.0 8.3 %collective-permute-start.15 = (bf16[144,512]{1,0:T(8,128)(2,1)S(1)}, bf16[144,512]{1,0:T(8,128)(2,1)S(1)}, u32[]{:S(2)}, u32[]{:S(2)}) collective-permute-start(bf16[144,512]{1,0:T(8,128)(2,1)S(1)} %get-tuple-element.55), channel_id=1, source_target_pairs={{0,4},{1,5},{2,6},{3,7},{4,8},{5,9},{6,10},{7,11},{8,12},{9,13},{1... | collective-permute-start | bytes 442376 | tf_op jit(solution)/shard_map/ppermute | solution.py:219
  34.1 4.4 %collective-permute-start.16 = (bf16[1024,256]{1,0:T(8,128)(2,1)S(1)}, bf16[1024,256]{1,0:T(8,128)(2,1)S(1)}, u32[]{:S(2)}, u32[]{:S(2)}) collective-permute-start(bf16[1024,256]{1,0:T(8,128)(2,1)S(1)} %get-tuple-element.57.refs_2_), channel_id=1, source_target_pairs={{0,1},{1,0},{2,3},{3,2},{4,5},{5,4},{6,7},{7,6},{8,9},{9,8},{10,11... | collective-permute-start | bytes 1572872 | tf_op jit(solution)/shard_map/ppermute | solution.py:219
  34.2 4.3 %collective-permute-start.17 = (bf16[1536,256]{1,0:T(8,128)(2,1)S(1)}, bf16[1536,256]{1,0:T(8,128)(2,1)S(1)}, u32[]{:S(2)}, u32[]{:S(2)}) collective-permute-start(bf16[1536,256]{1,0:T(8,128)(2,1)S(1)} %get-tuple-element.58.refs_3_), channel_id=1, source_target_pairs={{0,1},{1,0},{2,3},{3,2},{4,5},{5,4},{6,7},{7,6},{8,9},{9,8},{10,11... | collective-permute-start | bytes 2359304 | tf_op jit(solution)/shard_map/ppermute | solution.py:219
  44.3 2.4 %collective-permute-start.18 = (bf16[1536,256]{1,0:T(8,128)(2,1)S(1)}, bf16[1536,256]{1,0:T(8,128)(2,1)S(1)}, u32[]{:S(2)}, u32[]{:S(2)}) collective-permute-start(bf16[1536,256]{1,0:T(8,128)(2,1)S(1)} %get-tuple-element.65), channel_id=1, source_target_pairs={{0,1},{1,0},{2,3},{3,2},{4,5},{5,4},{6,7},{7,6},{8,9},{9,8},{10,11... | collective-permute-start | bytes 2359304 | tf_op jit(solution)/shard_map/ppermute | solution.py:219
  44.4 5.9 %collective-permute-start.19 = (bf16[128,512]{1,0:T(8,128)(2,1)S(1)}, bf16[128,512]{1,0:T(8,128)(2,1)S(1)}, u32[]{:S(2)}, u32[]{:S(2)}) collective-permute-start(bf16[128,512]{1,0:T(8,128)(2,1)S(1)} %get-tuple-element.67), channel_id=1, source_target_pairs={{0,2},{1,3},{2,0},{3,1},{4,6},{5,7},{6,4},{7,5},{8,10},{9,11},{10,... | collective-permute-start | bytes 393224 | tf_op jit(solution)/shard_map/ppermute | solution.py:219

commit v7 on v6

--- a/solution.py
+++ b/solution.py
@@ -16,7 +16,8 @@
 HB = pl.BlockSpec(memory_space=pltpu.HBM)
 CORES = 2
 CHUNK = 512
-DIRECT = 7
+PASS = 1 << 34
+DIRECT = (7, 7)
 MARK = 1 << 34
 
 
@@ -38,33 +39,66 @@
     return jnp.concatenate(parts, 0) != 0
 
 
+def tables_kernel(blocks, counts, out):
+    visits, slots = counts.shape[-1], blocks.shape[-1]
+    row = lax.broadcasted_iota(jnp.int32, out.shape, 0)
+    lane = lax.broadcasted_iota(jnp.int32, out.shape, 1)
+    table = jnp.zeros(out.shape, jnp.int32)
+    for t in range(visits):
+        entries = [counts[0, 0, t]]
+        entries += [blocks[0, 0, t, i, k] for i in range(2) for k in range(slots)]
+        for at, entry in enumerate(entries):
+            table = jnp.where(jnp.logical_and(row == t, lane == at), entry, table)
+    out[...] = table
+
+
 def prepare_kernel(visit, rows, close, place, *refs):
-    sets = len(refs) // 5
+    sets = len(refs) // 4
     for i in range(sets):
-        lay_out(visit, rows, close, place[0], *refs[4 * i : 4 * i + 4], refs[4 * sets + i])
-
-
-def lay_out(visit, rows, close, core, blocks, counts, rates, words, keep):
-    side = rates.shape[-1]
+        table, rates, words = refs[3 * i : 3 * i + 3]
+        clear(rates.shape[-1], refs[3 * sets + i])
+        lay_out(visit, rows, close, place[0], table, rates.at[0, 0, visit], words.at[0, 0, visit], refs[3 * sets + i])
+
+
+def prepare_first_kernel(rows, close, place, table, rates, words, users, keep, users_here, rates_here, words_here, sem):
+    copies = [
+        pltpu.make_async_copy(rates.at[0, 0, 0], rates_here, sem.at[0]),
+        pltpu.make_async_copy(words.at[0, 0, 0], words_here, sem.at[1]),
+        pltpu.make_async_copy(users, users_here, sem.at[2]),
+    ]
+    for copy in copies:
+        copy.start()
+    clear(rates.shape[-1], keep)
+    for copy in copies[:2]:
+        copy.wait()
+    lay_out(0, rows, close, place[0], table, rates_here, words_here, keep)
+    copies[2].wait()
+
+
+def clear(side, keep):
     nothing = jnp.full((side, side), jnp.nan, keep.dtype)
     for at in range(0, keep.shape[0], side):
         for lane in range(0, keep.shape[1], side):
             keep[at : at + side, lane : lane + side] = nothing
 
+
+def lay_out(visit, rows, close, core, table, rates, words, keep):
+    slots, side = rates.shape[0], rates.shape[-1]
+
     def tile(k, carry):
-        users = pl.ds(pl.multiple_of(blocks[0, 0, visit, 0, k] * side, side), side)
-        first = blocks[0, 0, visit, 1, k] * side
-        seen = observed(words[0, 0, visit, k])
-        known = jnp.where(seen, rates[0, 0, visit, k].astype(jnp.float32), jnp.nan)
+        users = pl.ds(pl.multiple_of(table[visit, 1 + k] * side, side), side)
+        first = table[visit, 1 + slots + k] * side
+        seen = observed(words[k])
+        known = jnp.where(seen, rates[k].astype(jnp.float32), jnp.nan)
         if close:
             piece = lax.div(first, rows)
             at = lax.div(piece, CORES) * rows + lax.rem(first, rows)
             at = pl.ds(pl.multiple_of(at, side), side)
-            known = known.astype(keep.dtype)
 
             @pl.when(lax.rem(piece, CORES) == core)
             def _():
-                keep[users, at] = known
+                keep[users, at] = known.astype(keep.dtype)
+
         else:
             at = pl.ds(pl.multiple_of(first, side), side)
             piece = lax.div(first + lax.broadcasted_iota(jnp.int32, known.shape, 1), rows)
@@ -72,10 +106,10 @@
             keep[users, at] = jnp.where(mine, known, jnp.nan).astype(keep.dtype)
         return carry
 
-    lax.fori_loop(0, counts[0, 0, visit], tile, 0)
-
-
-def tiles_kernel(first, last, chips, direct, close, place, *refs):
+    lax.fori_loop(0, table[visit, 0], tile, 0)
+
+
+def tiles_kernel(first, last, chips, came, direct, close, place, *refs):
     count = chips if first else chips + 1
     arrived, refs = refs[:count], refs[count:]
     (users, peers, rates, peer_rates), refs = refs[:4], refs[4:]
@@ -91,8 +125,8 @@
         now = arrived[0][...].astype(jnp.float32)
         for other in arrived[1:chips]:
             now = now + step_item * other[...].astype(jnp.float32)
-        panel[:direct, :] = now
-        panel[direct:, :] = arrived[chips][...].astype(jnp.float32)
+        panel[:came, :] = now
+        panel[came:, :] = arrived[chips][...].astype(jnp.float32)
     if close:
         low[...] = panel[...].astype(low.dtype)
     else:
@@ -196,6 +230,22 @@
     refs[-1][...] = jnp.zeros_like(refs[-1])
 
 
+def pass_kernel(source, _, out):
+    out[...] = source[...]
+
+
+def passed(x, *after):
+    return pl.pallas_call(
+        pass_kernel,
+        name="pass",
+        out_shape=pltpu.VMEM(x.shape, x.dtype),
+        in_specs=[VM] * 2,
+        out_specs=VM,
+        compiler_params=pltpu.CompilerParams(vmem_limit_bytes=16 << 20),
+        cost_estimate=pl.CostEstimate(flops=PASS, bytes_accessed=1024, transcendentals=0),
+    )(x, *after)
+
+
 def marked(*arrays):
     return pl.pallas_call(
         mark_kernel,
@@ -248,13 +298,40 @@
     panel_low = item_factors.astype(low_type)
     arrived = [panel_low] + [move(panel_low, 0, k, False) for k in range(1, chips)]
     users, other_users = user_factors, swap(user_factors)
-    tiles = [blocks, tile_counts, ratings, mask_words]
+    (table,) = kernel_call(
+        tables_kernel,
+        "tables",
+        [blocks, tile_counts],
+        [pltpu.VMEM((8 * -(-visits // 8), 128), jnp.int32)],
+        1024,
+    )
+    tiles = [table, ratings, mask_words]
     other_tiles = [swap(x) for x in tiles]
-    direct = part * DIRECT // 256 * 16
+    direct = 0
     for visit in range(visits):
         last = visit + 1 == visits
+        came, direct = direct, part * DIRECT[min(visit, 1)] // 256 * 16
         if visit == 0:
-            known = [*prepared(visit, tiles), *prepared(visit, other_tiles)]
+            known, users = pl.pallas_call(
+                functools.partial(prepare_first_kernel, rows, close),
+                name="prepare",
+                out_shape=(pltpu.VMEM((count, held), low_type), pltpu.VMEM(users.shape, users.dtype)),
+                in_specs=[SM] * 2 + [HB] * 3,
+                out_specs=(VM,) * 2,
+                scratch_shapes=[
+                    pltpu.VMEM(ratings.shape[3:], ratings.dtype),
+                    pltpu.VMEM(mask_words.shape[3:], mask_words.dtype),
+                    pltpu.SemaphoreType.DMA((3,)),
+                ],
+                compiler_params=pltpu.CompilerParams(vmem_limit_bytes=16 << 20),
+                cost_estimate=pl.CostEstimate(flops=1024, bytes_accessed=1024, transcendentals=0),
+            )(
+                place,
+                table,
+                *[pltpu.with_memory_space_constraint(x, pltpu.HBM) for x in (*tiles[1:], users)],
+            )
+            known = [known, *prepared(visit, other_tiles)]
+            arrived = arrived[:1] + [passed(x, known[1]) for x in arrived[1:]]
         else:
             known = prepared(visit, tiles, other_tiles)
         shared = [pltpu.VMEM((held, width), low_type)]
@@ -266,7 +343,7 @@
             shared += [pltpu.VMEM((direct, width), low_type)] * 2
             shared += [pltpu.VMEM((part - direct, width), kind) for kind in (full_type, low_type)]
         low, errors, other_errors, *ends = kernel_call(
-            functools.partial(tiles_kernel, visit == 0, last, chips, direct, close),
+            functools.partial(tiles_kernel, visit == 0, last, chips, came, direct, close),
             "tiles",
             [place, *arrived, users, other_users, *known],
             shared,

time: 51.1 us -> 50.4 us (0.986)
  Pallas kernels: 15.5 us -> 17.5 us
  local copies, waits for them, and re-layouts: 1.49 us -> 0.02 us
  waiting for transfers between devices: 16.9 us -> 15.6 us
    pallas_call x0 -> x2, Pallas kernels: none -> 1.99 us  [the longest x1 1.98 us: shards(): pl.pallas_call(functools.partial(prepare_first_kernel, rows, close), name...]
    unnamed x12 -> x8, local copies, waits for them, and re-layouts: 1.49 us -> 0.02 us
    ppermute x20 -> x19, waiting for transfers between devices: 16.9 us -> 15.6 us  [moved(): return lax.ppermute(x, ('strata', 'shard'), pairs)]
    ppermute x20 -> x19, starting transfers between devices: 15.3 us -> 15.1 us  [moved(): return lax.ppermute(x, ('strata', 'shard'), pairs)]
  transfers between devices with their start and end apart: 20 -> 19, of which waited for: 13 -> 12; matrix products, arithmetic and copies ran while one was open for 2% -> 2% of each run, Pallas kernels for 17% -> 22%
where the time goes in v7:
time: 50.4 us; the launch traced here: 50.1 us
  Pallas kernels  17.5 us (35%)
  waiting for transfers between devices  15.6 us (31%)
  starting transfers between devices  15.1 us (30%)
  other arithmetic  1.06 us (2%)
  between operations  0.85 us (2%)
    ppermute x19, waiting for transfers between devices, moved(): return lax.ppermute(x, ('strata', 'shard'), pairs)  15.6 us
    pallas_call x13, Pallas kernels, kernel_call(): pl.pallas_call(body, name=name, out_shape=tuple(outs), in_specs=[SM if x....  15.5 us
    ppermute x19, starting transfers between devices, moved(): return lax.ppermute(x, ('strata', 'shard'), pairs)  15.1 us
    pallas_call x1, Pallas kernels, shards(): pl.pallas_call(functools.partial(prepare_first_kernel, rows, close), name...  1.98 us
  transfers between devices with their start and end apart: 19, of which 12 were waited for; matrix products, arithmetic and copies ran while one was open for 2% of the time, Pallas kernels for 22%

profile of v7, /device:TPU:0, one launch (start us, length us, event | category | flops | bytes accessed | tf_op | source)
XLA Modules:
  0.0 50.1 jit_solution(3809703842508430252)
XLA Ops:
  0.6 0.5 %collective-permute-start.2 = (bf16[1,1,3,8,128,128]{5,4,3,2,1,0:T(8,128)(2,1)}, bf16[1,1,3,8,128,128]{5,4,3,2,1,0:T(8,128)(2,1)S(1)}, u32[]{:S(2)}, u32[]{:S(2)}) collective-permute-start(bf16[1,1,3,8,128,128]{5,4,3,2,1,0:T(8,128)(2,1)} %refs_1_.3), channel_id=1, source_target_pairs={{0,1},{1,0},{2,3},{3,2},{4,5},{5,4},{6,7},{7,6},{8,9},{9,8},{10,11... | collective-permute-start | bytes 2359304 | tf_op jit(solution)/shard_map/ppermute | solution.py:269
  1.1 0.1 collective-permute-start.3
  1.2 1.0 %convert_element_type.3.refs_0_ = bf16[128,512]{1,0:T(8,128)(2,1)S(1)} convert(f32[128,512]{1,0:T(8,128)} %param.7) | non-fusion elementwise | flops 65536 | bytes 393216 | tf_op jit(solution)/shard_map/convert_element_type | solution.py:298
  2.2 0.0 copy-start.3
  2.2 3.0 %collective-permute-start = (bf16[128,512]{1,0:T(8,128)(2,1)S(1)}, bf16[128,512]{1,0:T(8,128)(2,1)S(1)}, u32[]{:S(2)}, u32[]{:S(2)}) collective-permute-start(bf16[128,512]{1,0:T(8,128)(2,1)S(1)} %convert_element_type.3.refs_0_), channel_id=1, source_target_pairs={{0,2},{1,3},{2,0},{3,1},{4,6},{5,7},{6,4},{7,5},{8,10},{9,11},{10,... | collective-permute-start | bytes 393224 | tf_op jit(solution)/shard_map/ppermute | solution.py:269
  5.2 0.6 %tables.1.table.refs_0_ = s32[8,128]{1,0:T(8,128)S(1)} custom-call(s32[1,1,3,2,8]{4,3,2,1,0:T(2,128)S(1)} %bitcast.3, s32[1,1,3]{2,1,0:T(1,128)S(1)} %copy-done.3), custom_call_target="tpu_custom_call" | custom-call | flops 1024 | bytes 1024 | tf_op jit(solution)/shard_map/tables/pallas_call | solution.py:217
  5.9 0.1 collective-permute-start.1
  6.0 0.1 pad_add_fusion.place._
  6.1 0.5 collective-permute-start.4
  6.5 2.0 %prepare.5 = (bf16[1024,256]{1,0:T(8,128)(2,1)S(1)}, bf16[1024,512]{1,0:T(8,128)(2,1)S(1)}) custom-call(s32[2]{0:T(128)S(1)} %pad_add_fusion.place._, s32[8,128]{1,0:T(8,128)S(1)} %tables.1.table.refs_0_, bf16[1,1,3,8,128,128]{5,4,3,2,1,0:T(8,128)(2,1)} %refs_1_.3, s32[1,1,3,8,16,128]{5,4,3,2,1,0:T(8,128)} %refs_2_.3, bf16[1024,512]{1,0:T(8,128)(2,1)} %users.4), custom_call_target="tpu_custom_call" | custom-call | flops 1024 | bytes 1024 | tf_op jit(solution)/shard_map/prepare/pallas_call | solution.py:315
  8.6 0.9 %prepare.4._.refs_5_ = bf16[1024,256]{1,0:T(8,128)(2,1)S(1)} custom-call(s32[2]{0:T(128)S(1)} %pad_add_fusion.place._, s32[8,128]{1,0:T(8,128)S(1)} %collective-permute-done.1.refs_0_.refs_3_, bf16[1,1,3,8,128,128]{5,4,3,2,1,0:T(8,128)(2,1)S(1)} %collective-permute-done.2.refs_1_.refs_4_, s32[1,1,3,8,16,128]{5,4,3,2,1,0:T(8,128)S(1)} %collective-permute-done.3.refs_2_.refs_5_), custom_call_target="tpu_custom_call" | custom-call | flops 1024 | bytes 1024 | tf_op jit(solution)/shard_map/prepare/pallas_call | solution.py:217
  9.5 0.0 copy-start
  9.5 0.0 copy-start.1
  9.5 1.9 %tiles.3 = (bf16[256,512]{1,0:T(8,128)(2,1)S(1)}, bf16[1024,256]{1,0:T(8,128)(2,1)S(1)}, bf16[1536,256]{1,0:T(8,128)(2,1)S(1)}, bf16[112,512]{1,0:T(8,128)(2,1)S...) custom-call(s32[2]{0:T(128)S(1)} %pad_add_fusion.place._, ...), custom_call_target="tpu_custom_call" | custom-call | flops 1024 | bytes 1024 | tf_op jit(solution)/shard_map/tiles/pallas_call | solution.py:217
  11.4 1.3 %collective-permute-start.7 = (bf16[144,512]{1,0:T(8,128)(2,1)S(1)}, bf16[144,512]{1,0:T(8,128)(2,1)S(1)}, u32[]{:S(2)}, u32[]{:S(2)}) collective-permute-start(bf16[144,512]{1,0:T(8,128)(2,1)S(1)} %get-tuple-element.42), channel_id=1, source_target_pairs={{0,2},{1,3},{2,0},{3,1},{4,6},{5,7},{6,4},{7,5},{8,10},{9,11},{10,... | collective-permute-start | bytes 442376 | tf_op jit(solution)/shard_map/ppermute | solution.py:269
  12.8 1.5 %collective-permute-start.5 = (bf16[112,512]{1,0:T(8,128)(2,1)S(1)}, bf16[112,512]{1,0:T(8,128)(2,1)S(1)}, u32[]{:S(2)}, u32[]{:S(2)}) collective-permute-start(bf16[112,512]{1,0:T(8,128)(2,1)S(1)} %get-tuple-element.39), channel_id=1, source_target_pairs={{0,4},{1,5},{2,6},{3,7},{4,8},{5,9},{6,10},{7,11},{8,12},{9,13},{1... | collective-permute-start | bytes 344072 | tf_op jit(solution)/shard_map/ppermute | solution.py:269
  14.3 0.9 %prepare.6 = (bf16[1024,256]{1,0:T(8,128)(2,1)S(1)}, bf16[1024,256]{1,0:T(8,128)(2,1)S(1)}) custom-call(s32[2]{0:T(128)S(1)} %pad_add_fusion.place._, s32[8,128]{1,0:T(8,128)S(1)} %tables.1.table.refs_0_, bf16[1,1,3,8,128,128]{5,4,3,2,1,0:T(8,128)(2,1)S(1)} %copy-done, s32[1,1,3,8,16,128]{5,4,3,2,1,0:T(8,128)S(1)} %copy-done.1, ...), custom_call_target="tpu_custom_call" | custom-call | flops 1024 | bytes 1024 | tf_op jit(solution)/shard_map/prepare/pallas_call | solution.py:217
  15.2 1.9 %collective-permute-start.6 = (bf16[112,512]{1,0:T(8,128)(2,1)S(1)}, bf16[112,512]{1,0:T(8,128)(2,1)S(1)}, u32[]{:S(2)}, u32[]{:S(2)}) collective-permute-start(bf16[112,512]{1,0:T(8,128)(2,1)S(1)} %get-tuple-element.40), channel_id=1, source_target_pairs={{0,6},{1,7},{2,4},{3,5},{4,10},{5,11},{6,8},{7,9},{8,14},{9,15},{1... | collective-permute-start | bytes 344072 | tf_op jit(solution)/shard_map/ppermute | solution.py:269
  17.1 0.1 collective-permute-done.7.refs_1_
  17.2 0.1 join.2
  17.3 1.5 %collective-permute-start.8 = (bf16[144,512]{1,0:T(8,128)(2,1)S(1)}, bf16[144,512]{1,0:T(8,128)(2,1)S(1)}, u32[]{:S(2)}, u32[]{:S(2)}) collective-permute-start(bf16[144,512]{1,0:T(8,128)(2,1)S(1)} %get-tuple-element.45), channel_id=1, source_target_pairs={{0,4},{1,5},{2,6},{3,7},{4,8},{5,9},{6,10},{7,11},{8,12},{9,13},{1... | collective-permute-start | bytes 442376 | tf_op jit(solution)/shard_map/ppermute | solution.py:269
  18.8 0.5 %collective-permute-start.10 = (bf16[1536,256]{1,0:T(8,128)(2,1)S(1)}, bf16[1536,256]{1,0:T(8,128)(2,1)S(1)}, u32[]{:S(2)}, u32[]{:S(2)}) collective-permute-start(bf16[1536,256]{1,0:T(8,128)(2,1)S(1)} %get-tuple-element.48.refs_3_), channel_id=1, source_target_pairs={{0,1},{1,0},{2,3},{3,2},{4,5},{5,4},{6,7},{7,6},{8,9},{9,8},{10,11... | collective-permute-start | bytes 2359304 | tf_op jit(solution)/shard_map/ppermute | solution.py:269
  19.3 1.0 %collective-permute-done.5.refs_0_ = bf16[112,512]{1,0:T(8,128)(2,1)S(1)} collective-permute-done((bf16[112,512]{1,0:T(8,128)(2,1)S(1)}, bf16[112,512]{1,0:T(8,128)(2,1)S(1)}, u32[]{:S(2)}, u32[]{:S(2)}) %collective-permute-start.5) | collective-permute-done | bytes 114720 | tf_op jit(solution)/shard_map/ppermute | solution.py:269
  20.3 0.4 collective-permute-done.9.refs_4_
  20.7 1.1 %collective-permute-done.10.refs_5_ = bf16[1536,256]{1,0:T(8,128)(2,1)S(1)} collective-permute-done((bf16[1536,256]{1,0:T(8,128)(2,1)S(1)}, bf16[1536,256]{1,0:T(8,128)(2,1)S(1)}, u32[]{:S(2)}, u32[]{:S(2)}) %collective-permute-start.10) | collective-permute-done | bytes 786464 | tf_op jit(solution)/shard_map/ppermute | solution.py:269
  21.9 1.4 %users.5 = (bf16[1024,512]{1,0:T(8,128)(2,1)S(1)}, bf16[1024,512]{1,0:T(8,128)(2,1)S(1)}) custom-call(f32[8,128]{1,0:T(8,128)S(1)} %mark.2._, bf16[256,512]{1,0:T(8,128)(2,1)S(1)} %get-tuple-element.46.low, bf16[1024,512]{1,0:T(8,128)(2,1)S(1)} %get-tuple-element.37.refs_2_.refs_0_, bf16[1024,512]{1,0:T(8,128)(2,1)S(1)} %collective-permute-done.4.refs_3_.refs_1_, ...), custom_call_target="tpu_custom_call" | custom-call | flops 1024 | bytes 1024 | tf_op jit(solution)/shard_map/users/pallas_call | solution.py:217
  23.3 1.3 %collective-permute-done.6.refs_1_ = bf16[112,512]{1,0:T(8,128)(2,1)S(1)} collective-permute-done((bf16[112,512]{1,0:T(8,128)(2,1)S(1)}, bf16[112,512]{1,0:T(8,128)(2,1)S(1)}, u32[]{:S(2)}, u32[]{:S(2)}) %collective-permute-start.6) | collective-permute-done | bytes 114720 | tf_op jit(solution)/shard_map/ppermute | solution.py:269
  24.6 1.6 %collective-permute-done.8.refs_2_ = bf16[144,512]{1,0:T(8,128)(2,1)S(1)} collective-permute-done((bf16[144,512]{1,0:T(8,128)(2,1)S(1)}, bf16[144,512]{1,0:T(8,128)(2,1)S(1)}, u32[]{:S(2)}, u32[]{:S(2)}) %collective-permute-start.8) | collective-permute-done | bytes 147488 | tf_op jit(solution)/shard_map/ppermute | solution.py:269
  26.2 1.9 %tiles.4 = (bf16[256,512]{1,0:T(8,128)(2,1)S(1)}, bf16[1024,256]{1,0:T(8,128)(2,1)S(1)}, bf16[1536,256]{1,0:T(8,128)(2,1)S(1)}, bf16[112,512]{1,0:T(8,128)(2,1)S...) custom-call(s32[2]{0:T(128)S(1)} %pad_add_fusion.place._, ...), custom_call_target="tpu_custom_call" | custom-call | flops 1024 | bytes 1024 | tf_op jit(solution)/shard_map/tiles/pallas_call | solution.py:217
  28.1 0.6 %collective-permute-start.13 = (bf16[144,512]{1,0:T(8,128)(2,1)S(1)}, bf16[144,512]{1,0:T(8,128)(2,1)S(1)}, u32[]{:S(2)}, u32[]{:S(2)}) collective-permute-start(bf16[144,512]{1,0:T(8,128)(2,1)S(1)} %get-tuple-element.56), channel_id=1, source_target_pairs={{0,2},{1,3},{2,0},{3,1},{4,6},{5,7},{6,4},{7,5},{8,10},{9,11},{10,... | collective-permute-start | bytes 442376 | tf_op jit(solution)/shard_map/ppermute | solution.py:269
  28.7 1.0 %prepare.7 = (bf16[1024,256]{1,0:T(8,128)(2,1)S(1)}, bf16[1024,256]{1,0:T(8,128)(2,1)S(1)}) custom-call(s32[2]{0:T(128)S(1)} %pad_add_fusion.place._, s32[8,128]{1,0:T(8,128)S(1)} %tables.1.table.refs_0_, bf16[1,1,3,8,128,128]{5,4,3,2,1,0:T(8,128)(2,1)S(1)} %copy-done, s32[1,1,3,8,16,128]{5,4,3,2,1,0:T(8,128)S(1)} %copy-done.1, ...), custom_call_target="tpu_custom_call" | custom-call | flops 1024 | bytes 1024 | tf_op jit(solution)/shard_map/prepare/pallas_call | solution.py:217
  29.7 1.9 %collective-permute-start.12 = (bf16[112,512]{1,0:T(8,128)(2,1)S(1)}, bf16[112,512]{1,0:T(8,128)(2,1)S(1)}, u32[]{:S(2)}, u32[]{:S(2)}) collective-permute-start(bf16[112,512]{1,0:T(8,128)(2,1)S(1)} %get-tuple-element.54), channel_id=1, source_target_pairs={{0,6},{1,7},{2,4},{3,5},{4,10},{5,11},{6,8},{7,9},{8,14},{9,15},{1... | collective-permute-start | bytes 344072 | tf_op jit(solution)/shard_map/ppermute | solution.py:269
  31.6 1.7 %collective-permute-done.13.refs_1_ = bf16[144,512]{1,0:T(8,128)(2,1)S(1)} collective-permute-done((bf16[144,512]{1,0:T(8,128)(2,1)S(1)}, bf16[144,512]{1,0:T(8,128)(2,1)S(1)}, u32[]{:S(2)}, u32[]{:S(2)}) %collective-permute-start.13) | collective-permute-done | bytes 147488 | tf_op jit(solution)/shard_map/ppermute | solution.py:269
  33.3 0.1 join.3
  33.4 0.1 collective-permute-start.14
  33.5 0.1 collective-permute-start.15
  33.6 0.5 collective-permute-start.16
  34.1 3.2 %collective-permute-done.11.refs_0_ = bf16[112,512]{1,0:T(8,128)(2,1)S(1)} collective-permute-done((bf16[112,512]{1,0:T(8,128)(2,1)S(1)}, bf16[112,512]{1,0:T(8,128)(2,1)S(1)}, u32[]{:S(2)}, u32[]{:S(2)}) %collective-permute-start.11) | collective-permute-done | bytes 114720 | tf_op jit(solution)/shard_map/ppermute | solution.py:269
  37.3 1.5 %users.6 = (bf16[1024,512]{1,0:T(8,128)(2,1)S(1)}, bf16[1024,512]{1,0:T(8,128)(2,1)S(1)}) custom-call(f32[8,128]{1,0:T(8,128)S(1)} %mark.3._, bf16[256,512]{1,0:T(8,128)(2,1)S(1)} %get-tuple-element.60.low, bf16[1024,512]{1,0:T(8,128)(2,1)S(1)} %get-tuple-element.49.refs_3_.refs_0_, bf16[1024,512]{1,0:T(8,128)(2,1)S(1)} %get-tuple-element.50.refs_4_.refs_1_, ...), custom_call_target="tpu_custom_call" | custom-call | flops 1024 | bytes 1024 | tf_op jit(solution)/shard_map/users/pallas_call | solution.py:217
  38.8 1.4 %collective-permute-done.12.refs_1_ = bf16[112,512]{1,0:T(8,128)(2,1)S(1)} collective-permute-done((bf16[112,512]{1,0:T(8,128)(2,1)S(1)}, bf16[112,512]{1,0:T(8,128)(2,1)S(1)}, u32[]{:S(2)}, u32[]{:S(2)}) %collective-permute-start.12) | collective-permute-done | bytes 114720 | tf_op jit(solution)/shard_map/ppermute | solution.py:269
  40.2 1.2 %collective-permute-done.14.refs_2_ = bf16[144,512]{1,0:T(8,128)(2,1)S(1)} collective-permute-done((bf16[144,512]{1,0:T(8,128)(2,1)S(1)}, bf16[144,512]{1,0:T(8,128)(2,1)S(1)}, u32[]{:S(2)}, u32[]{:S(2)}) %collective-permute-start.14) | collective-permute-done | bytes 147488 | tf_op jit(solution)/shard_map/ppermute | solution.py:269
  41.4 2.0 %tiles.5 = (bf16[256,512]{1,0:T(8,128)(2,1)S(1)}, bf16[1024,256]{1,0:T(8,128)(2,1)S(1)}, bf16[1536,256]{1,0:T(8,128)(2,1)S(1)}, f32[128,512]{1,0:T(8,128)S(1)}, bf16[128,512]{1,0:T(8,128)(2,1)S(1)}) custom-call(s32[2]{0:T(128)S(1)} %pad_add_fusion.place._, bf16[112,512]{1,0:T(8,128)(2,1)S(1)} %collective-permute-done.11.refs_0_, ...), custom_call_target="tpu_custom_call" | custom-call | flops 1024 | bytes 1024 | tf_op jit(solution)/shard_map/tiles/pallas_call | solution.py:217
  43.4 0.1 collective-permute-start.17
  43.4 1.0 %collective-permute-start.18 = (bf16[128,512]{1,0:T(8,128)(2,1)S(1)}, bf16[128,512]{1,0:T(8,128)(2,1)S(1)}, u32[]{:S(2)}, u32[]{:S(2)}) collective-permute-start(bf16[128,512]{1,0:T(8,128)(2,1)S(1)} %get-tuple-element.71), channel_id=1, source_target_pairs={{0,2},{1,3},{2,0},{3,1},{4,6},{5,7},{6,4},{7,5},{8,10},{9,11},{10,... | collective-permute-start | bytes 393224 | tf_op jit(solution)/shard_map/ppermute | solution.py:269
  44.4 1.3 %collective-permute-done.17.refs_2_ = bf16[1536,256]{1,0:T(8,128)(2,1)S(1)} collective-permute-done((bf16[1536,256]{1,0:T(8,128)(2,1)S(1)}, bf16[1536,256]{1,0:T(8,128)(2,1)S(1)}, u32[]{:S(2)}, u32[]{:S(2)}) %collective-permute-start.17) | collective-permute-done | bytes 786464 | tf_op jit(solution)/shard_map/ppermute | solution.py:269
  45.7 2.3 %users.7.refs_2_ = bf16[1024,512]{1,0:T(8,128)(2,1)} custom-call(s32[2]{0:T(128)S(1)} %pad_add_fusion.place._, bf16[256,512]{1,0:T(8,128)(2,1)S(1)} %get-tuple-element.67.low, bf16[1024,512]{1,0:T(8,128)(2,1)S(1)} %get-tuple-element.63.refs_3_.refs_0_, bf16[1024,256]{1,0:T(8,128)(2,1)S(1)} %get-tuple-element.68.refs_1_, ...), custom_call_target="tpu_custom_call" | custom-call | flops 1024 | bytes 1024 | tf_op jit(solution)/shard_map/users/pallas_call | solution.py:217
  48.0 1.3 %collective-permute-done.18.refs_1_ = bf16[128,512]{1,0:T(8,128)(2,1)S(1)} collective-permute-done((bf16[128,512]{1,0:T(8,128)(2,1)S(1)}, bf16[128,512]{1,0:T(8,128)(2,1)S(1)}, u32[]{:S(2)}, u32[]{:S(2)}) %collective-permute-start.18) | collective-permute-done | bytes 131104 | tf_op jit(solution)/shard_map/ppermute | solution.py:269
  49.3 0.7 %final.1 = f32[128,512]{1,0:T(8,128)} custom-call(f32[128,512]{1,0:T(8,128)S(1)} %get-tuple-element.70.refs_0_, bf16[128,512]{1,0:T(8,128)(2,1)S(1)} %collective-permute-done.18.refs_1_, bf16[1024,512]{1,0:T(8,128)(2,1)} %users.7.refs_2_), custom_call_target="tpu_custom_call" | custom-call | flops 1024 | bytes 1024 | tf_op jit(solution)/shard_map/final/pallas_call | solution.py:217
  (17 shorter events, 0.0 us)
Async XLA Ops:
  0.6 7.9 %collective-permute-start.2 = (bf16[1,1,3,8,128,128]{5,4,3,2,1,0:T(8,128)(2,1)}, bf16[1,1,3,8,128,128]{5,4,3,2,1,0:T(8,128)(2,1)S(1)}, u32[]{:S(2)}, u32[]{:S(2)}) collective-permute-start(bf16[1,1,3,8,128,128]{5,4,3,2,1,0:T(8,128)(2,1)} %refs_1_.3), channel_id=1, source_target_pairs={{0,1},{1,0},{2,3},{3,2},{4,5},{5,4},{6,7},{7,6},{8,9},{9,8},{10,11... | collective-permute-start | bytes 2359304 | tf_op jit(solution)/shard_map/ppermute | solution.py:269
  1.1 7.4 %collective-permute-start.3 = (s32[1,1,3,8,16,128]{5,4,3,2,1,0:T(8,128)}, s32[1,1,3,8,16,128]{5,4,3,2,1,0:T(8,128)S(1)}, u32[]{:S(2)}, u32[]{:S(2)}) collective-permute-start(s32[1,1,3,8,16,128]{5,4,3,2,1,0:T(8,128)} %refs_2_.3), channel_id=1, source_target_pairs={{0,1},{1,0},{2,3},{3,2},{4,5},{5,4},{6,7},{7,6},{8,9},{9,8},{10,11... | collective-permute-start | bytes 589832 | tf_op jit(solution)/shard_map/ppermute | solution.py:269
  1.2 4.0 %copy-start.2 = (s32[1,1,3,8,2]{3,4,2,1,0:T(2,128)S(1)}, s32[1,1,3,8,2]{3,4,2,1,0:T(2,128)}, u32[]{:S(2)}) copy-start(s32[1,1,3,8,2]{3,4,2,1,0:T(2,128)} %param.8) | copy-start | bytes 580
  2.2 3.0 %copy-start.3 = (s32[1,1,3]{2,1,0:T(1,128)S(1)}, s32[1,1,3]{2,1,0:T(1,128)}, u32[]{:S(2)}) copy-start(s32[1,1,3]{2,1,0:T(1,128)} %counts.1) | copy-start | bytes 40
  2.2 7.2 %collective-permute-start = (bf16[128,512]{1,0:T(8,128)(2,1)S(1)}, bf16[128,512]{1,0:T(8,128)(2,1)S(1)}, u32[]{:S(2)}, u32[]{:S(2)}) collective-permute-start(bf16[128,512]{1,0:T(8,128)(2,1)S(1)} %convert_element_type.3.refs_0_), channel_id=1, source_target_pairs={{0,2},{1,3},{2,0},{3,1},{4,6},{5,7},{6,4},{7,5},{8,10},{9,11},{10,... | collective-permute-start | bytes 393224 | tf_op jit(solution)/shard_map/ppermute | solution.py:269
  5.9 2.6 %collective-permute-start.1 = (s32[8,128]{1,0:T(8,128)S(1)}, s32[8,128]{1,0:T(8,128)S(1)}, u32[]{:S(2)}, u32[]{:S(2)}) collective-permute-start(s32[8,128]{1,0:T(8,128)S(1)} %tables.1.table.refs_0_), channel_id=1, source_target_pairs={{0,1},{1,0},{2,3},{3,2},{4,5},{5,4},{6,7},{7,6},{8,9},{9,8},{10,11... | collective-permute-start | bytes 12296 | tf_op jit(solution)/shard_map/ppermute | solution.py:269
  6.1 3.4 %collective-permute-start.4 = (bf16[1024,512]{1,0:T(8,128)(2,1)}, bf16[1024,512]{1,0:T(8,128)(2,1)S(1)}, u32[]{:S(2)}, u32[]{:S(2)}) collective-permute-start(bf16[1024,512]{1,0:T(8,128)(2,1)} %users.4), channel_id=1, source_target_pairs={{0,1},{1,0},{2,3},{3,2},{4,5},{5,4},{6,7},{7,6},{8,9},{9,8},{10,11... | collective-permute-start | bytes 3145736 | tf_op jit(solution)/shard_map/ppermute | solution.py:269
  9.5 4.8 %copy-start = (bf16[1,1,3,8,128,128]{5,4,3,2,1,0:T(8,128)(2,1)S(1)}, bf16[1,1,3,8,128,128]{5,4,3,2,1,0:T(8,128)(2,1)}, u32[]{:S(2)}) copy-start(bf16[1,1,3,8,128,128]{5,4,3,2,1,0:T(8,128)(2,1)} %refs_1_.3) | copy-start | bytes 2359300
  9.5 4.8 %copy-start.1 = (s32[1,1,3,8,16,128]{5,4,3,2,1,0:T(8,128)S(1)}, s32[1,1,3,8,16,128]{5,4,3,2,1,0:T(8,128)}, u32[]{:S(2)}) copy-start(s32[1,1,3,8,16,128]{5,4,3,2,1,0:T(8,128)} %refs_2_.3) | copy-start | bytes 589828
  11.4 5.7 %collective-permute-start.7 = (bf16[144,512]{1,0:T(8,128)(2,1)S(1)}, bf16[144,512]{1,0:T(8,128)(2,1)S(1)}, u32[]{:S(2)}, u32[]{:S(2)}) collective-permute-start(bf16[144,512]{1,0:T(8,128)(2,1)S(1)} %get-tuple-element.42), channel_id=1, source_target_pairs={{0,2},{1,3},{2,0},{3,1},{4,6},{5,7},{6,4},{7,5},{8,10},{9,11},{10,... | collective-permute-start | bytes 442376 | tf_op jit(solution)/shard_map/ppermute | solution.py:269
  12.8 7.5 %collective-permute-start.5 = (bf16[112,512]{1,0:T(8,128)(2,1)S(1)}, bf16[112,512]{1,0:T(8,128)(2,1)S(1)}, u32[]{:S(2)}, u32[]{:S(2)}) collective-permute-start(bf16[112,512]{1,0:T(8,128)(2,1)S(1)} %get-tuple-element.39), channel_id=1, source_target_pairs={{0,4},{1,5},{2,6},{3,7},{4,8},{5,9},{6,10},{7,11},{8,12},{9,13},{1... | collective-permute-start | bytes 344072 | tf_op jit(solution)/shard_map/ppermute | solution.py:269
  15.2 9.3 %collective-permute-start.6 = (bf16[112,512]{1,0:T(8,128)(2,1)S(1)}, bf16[112,512]{1,0:T(8,128)(2,1)S(1)}, u32[]{:S(2)}, u32[]{:S(2)}) collective-permute-start(bf16[112,512]{1,0:T(8,128)(2,1)S(1)} %get-tuple-element.40), channel_id=1, source_target_pairs={{0,6},{1,7},{2,4},{3,5},{4,10},{5,11},{6,8},{7,9},{8,14},{9,15},{1... | collective-permute-start | bytes 344072 | tf_op jit(solution)/shard_map/ppermute | solution.py:269
  17.3 8.9 %collective-permute-start.8 = (bf16[144,512]{1,0:T(8,128)(2,1)S(1)}, bf16[144,512]{1,0:T(8,128)(2,1)S(1)}, u32[]{:S(2)}, u32[]{:S(2)}) collective-permute-start(bf16[144,512]{1,0:T(8,128)(2,1)S(1)} %get-tuple-element.45), channel_id=1, source_target_pairs={{0,4},{1,5},{2,6},{3,7},{4,8},{5,9},{6,10},{7,11},{8,12},{9,13},{1... | collective-permute-start | bytes 442376 | tf_op jit(solution)/shard_map/ppermute | solution.py:269
  18.8 1.9 %collective-permute-start.9 = (bf16[1024,256]{1,0:T(8,128)(2,1)S(1)}, bf16[1024,256]{1,0:T(8,128)(2,1)S(1)}, u32[]{:S(2)}, u32[]{:S(2)}) collective-permute-start(bf16[1024,256]{1,0:T(8,128)(2,1)S(1)} %get-tuple-element.47.refs_2_), channel_id=1, source_target_pairs={{0,1},{1,0},{2,3},{3,2},{4,5},{5,4},{6,7},{7,6},{8,9},{9,8},{10,11... | collective-permute-start | bytes 1572872 | tf_op jit(solution)/shard_map/ppermute | solution.py:269
  18.8 3.0 %collective-permute-start.10 = (bf16[1536,256]{1,0:T(8,128)(2,1)S(1)}, bf16[1536,256]{1,0:T(8,128)(2,1)S(1)}, u32[]{:S(2)}, u32[]{:S(2)}) collective-permute-start(bf16[1536,256]{1,0:T(8,128)(2,1)S(1)} %get-tuple-element.48.refs_3_), channel_id=1, source_target_pairs={{0,1},{1,0},{2,3},{3,2},{4,5},{5,4},{6,7},{7,6},{8,9},{9,8},{10,11... | collective-permute-start | bytes 2359304 | tf_op jit(solution)/shard_map/ppermute | solution.py:269
  28.1 5.2 %collective-permute-start.13 = (bf16[144,512]{1,0:T(8,128)(2,1)S(1)}, bf16[144,512]{1,0:T(8,128)(2,1)S(1)}, u32[]{:S(2)}, u32[]{:S(2)}) collective-permute-start(bf16[144,512]{1,0:T(8,128)(2,1)S(1)} %get-tuple-element.56), channel_id=1, source_target_pairs={{0,2},{1,3},{2,0},{3,1},{4,6},{5,7},{6,4},{7,5},{8,10},{9,11},{10,... | collective-permute-start | bytes 442376 | tf_op jit(solution)/shard_map/ppermute | solution.py:269
  28.7 8.6 %collective-permute-start.11 = (bf16[112,512]{1,0:T(8,128)(2,1)S(1)}, bf16[112,512]{1,0:T(8,128)(2,1)S(1)}, u32[]{:S(2)}, u32[]{:S(2)}) collective-permute-start(bf16[112,512]{1,0:T(8,128)(2,1)S(1)} %get-tuple-element.53), channel_id=1, source_target_pairs={{0,4},{1,5},{2,6},{3,7},{4,8},{5,9},{6,10},{7,11},{8,12},{9,13},{1... | collective-permute-start | bytes 344072 | tf_op jit(solution)/shard_map/ppermute | solution.py:269
  29.7 10.5 %collective-permute-start.12 = (bf16[112,512]{1,0:T(8,128)(2,1)S(1)}, bf16[112,512]{1,0:T(8,128)(2,1)S(1)}, u32[]{:S(2)}, u32[]{:S(2)}) collective-permute-start(bf16[112,512]{1,0:T(8,128)(2,1)S(1)} %get-tuple-element.54), channel_id=1, source_target_pairs={{0,6},{1,7},{2,4},{3,5},{4,10},{5,11},{6,8},{7,9},{8,14},{9,15},{1... | collective-permute-start | bytes 344072 | tf_op jit(solution)/shard_map/ppermute | solution.py:269
  33.4 7.9 %collective-permute-start.14 = (bf16[144,512]{1,0:T(8,128)(2,1)S(1)}, bf16[144,512]{1,0:T(8,128)(2,1)S(1)}, u32[]{:S(2)}, u32[]{:S(2)}) collective-permute-start(bf16[144,512]{1,0:T(8,128)(2,1)S(1)} %get-tuple-element.59), channel_id=1, source_target_pairs={{0,4},{1,5},{2,6},{3,7},{4,8},{5,9},{6,10},{7,11},{8,12},{9,13},{1... | collective-permute-start | bytes 442376 | tf_op jit(solution)/shard_map/ppermute | solution.py:269
  33.5 3.8 %collective-permute-start.15 = (bf16[1024,256]{1,0:T(8,128)(2,1)S(1)}, bf16[1024,256]{1,0:T(8,128)(2,1)S(1)}, u32[]{:S(2)}, u32[]{:S(2)}) collective-permute-start(bf16[1024,256]{1,0:T(8,128)(2,1)S(1)} %get-tuple-element.61.refs_2_), channel_id=1, source_target_pairs={{0,1},{1,0},{2,3},{3,2},{4,5},{5,4},{6,7},{7,6},{8,9},{9,8},{10,11... | collective-permute-start | bytes 1572872 | tf_op jit(solution)/shard_map/ppermute | solution.py:269
  33.6 3.7 %collective-permute-start.16 = (bf16[1536,256]{1,0:T(8,128)(2,1)S(1)}, bf16[1536,256]{1,0:T(8,128)(2,1)S(1)}, u32[]{:S(2)}, u32[]{:S(2)}) collective-permute-start(bf16[1536,256]{1,0:T(8,128)(2,1)S(1)} %get-tuple-element.62.refs_3_), channel_id=1, source_target_pairs={{0,1},{1,0},{2,3},{3,2},{4,5},{5,4},{6,7},{7,6},{8,9},{9,8},{10,11... | collective-permute-start | bytes 2359304 | tf_op jit(solution)/shard_map/ppermute | solution.py:269
  43.4 2.4 %collective-permute-start.17 = (bf16[1536,256]{1,0:T(8,128)(2,1)S(1)}, bf16[1536,256]{1,0:T(8,128)(2,1)S(1)}, u32[]{:S(2)}, u32[]{:S(2)}) collective-permute-start(bf16[1536,256]{1,0:T(8,128)(2,1)S(1)} %get-tuple-element.69), channel_id=1, source_target_pairs={{0,1},{1,0},{2,3},{3,2},{4,5},{5,4},{6,7},{7,6},{8,9},{9,8},{10,11... | collective-permute-start | bytes 2359304 | tf_op jit(solution)/shard_map/ppermute | solution.py:269
  43.4 5.9 %collective-permute-start.18 = (bf16[128,512]{1,0:T(8,128)(2,1)S(1)}, bf16[128,512]{1,0:T(8,128)(2,1)S(1)}, u32[]{:S(2)}, u32[]{:S(2)}) collective-permute-start(bf16[128,512]{1,0:T(8,128)(2,1)S(1)} %get-tuple-element.71), channel_id=1, source_target_pairs={{0,2},{1,3},{2,0},{3,1},{4,6},{5,7},{6,4},{7,5},{8,10},{9,11},{10,... | collective-permute-start | bytes 393224 | tf_op jit(solution)/shard_map/ppermute | solution.py:269

commit v8 on v7

--- a/solution.py
+++ b/solution.py
@@ -145,6 +145,17 @@
             predicted = multiply(who[cut, :], low[...], 1, 1)
             rating = known[cut, :].astype(jnp.float32)
             error[cut, :] = jnp.where(rating == rating, rating - predicted, 0.0).astype(error.dtype)
+    if last and close:
+        for k in range(chips):
+            owner = lax.rem(chip + k, chips)
+            at = pl.ds(pl.multiple_of(owner * rows, rows), rows)
+            if k == 0:
+                outs[k][...] = panel[at, :]
+            else:
+                term = multiply(errors[:, at], users[...], 0, 0)
+                term = term + multiply(peer_errors[: peers.shape[0], at], peers[...], 0, 0)
+                outs[k][...] = term.astype(outs[k].dtype)
+        return
     total[...] = multiply(errors[...], users[...], 0, 0)
     total[...] += multiply(peer_errors[: peers.shape[0], :], peers[...], 0, 0)
     if last:
@@ -170,6 +181,14 @@
                 to = slice(begin - low_end, end - low_end)
                 joined[to, :] = (old + step_item * (term - shrinkage * old)).astype(joined.dtype)
                 plain[to, :] = term.astype(plain.dtype)
+
+
+def own_kernel(place, old, errors, peer_errors, users, peers, out):
+    rows = old.shape[0]
+    at = pl.ds(pl.multiple_of(place[1] * rows, rows), rows)
+    term = multiply(errors[:, at], users[...], 0, 0)
+    term = term + multiply(peer_errors[: peers.shape[0], at], peers[...], 0, 0)
+    out[...] = old[...] + step_item * (term - shrinkage * old[...])
 
 
 def users_kernel(last, _, low, *refs):
@@ -352,6 +371,14 @@
         )
         if last:
             arrived = ends[:1] + [move(ends[k], 0, k, False) for k in range(1, chips)]
+            if close:
+                arrived[:1] = kernel_call(
+                    own_kernel,
+                    "own",
+                    [place, ends[0], errors, other_errors, users, other_users],
+                    [pltpu.VMEM((rows, width), full_type)],
+                    1024,
+                )
             sets = [place, low, users, errors, swap(other_errors)]
         else:
             others = [move(ends[3], 0, k, False) for k in range(1, chips)]

time: 50.4 us -> 50.3 us (level)
  waiting for transfers between devices: 15.6 us -> 13.9 us
  Pallas kernels: 17.5 us -> 18.4 us
    ppermute x19, waiting for transfers between devices: 15.6 us -> 13.9 us  [moved(): return lax.ppermute(x, ('strata', 'shard'), pairs)]
    pallas_call x13 -> x14, Pallas kernels: 15.5 us -> 16.4 us  [kernel_call(): pl.pallas_call(body, name=name, out_shape=tuple(outs), in_specs=[SM if x....]
  transfers between devices with their start and end apart: 19 -> 19, of which waited for: 12 -> 11; matrix products, arithmetic and copies ran while one was open for 2% -> 2% of each run, Pallas kernels for 22% -> 24%
where the time goes in v8:
time: 50.3 us; the launch traced here: 49.8 us
  Pallas kernels  18.4 us (37%)
  starting transfers between devices  15.6 us (31%)
  waiting for transfers between devices  13.9 us (28%)
  other arithmetic  1.06 us (2%)
  between operations  0.86 us (2%)
    pallas_call x14, Pallas kernels, kernel_call(): pl.pallas_call(body, name=name, out_shape=tuple(outs), in_specs=[SM if x....  16.4 us
    ppermute x19, starting transfers between devices, moved(): return lax.ppermute(x, ('strata', 'shard'), pairs)  15.6 us
    ppermute x19, waiting for transfers between devices, moved(): return lax.ppermute(x, ('strata', 'shard'), pairs)  13.9 us
    pallas_call x1, Pallas kernels, shards(): pl.pallas_call(functools.partial(prepare_first_kernel, rows, close), name...  1.98 us
  transfers between devices with their start and end apart: 19, of which 11 were waited for; matrix products, arithmetic and copies ran while one was open for 2% of the time, Pallas kernels for 24%

profile of v8, /device:TPU:0, one launch (start us, length us, event | category | flops | bytes accessed | tf_op | source)
XLA Modules:
  0.0 49.8 jit_solution(14172171968452960740)
XLA Ops:
  0.6 0.5 %collective-permute-start.2 = (bf16[1,1,3,8,128,128]{5,4,3,2,1,0:T(8,128)(2,1)}, bf16[1,1,3,8,128,128]{5,4,3,2,1,0:T(8,128)(2,1)S(1)}, u32[]{:S(2)}, u32[]{:S(2)}) collective-permute-start(bf16[1,1,3,8,128,128]{5,4,3,2,1,0:T(8,128)(2,1)} %refs_1_.3), channel_id=1, source_target_pairs={{0,1},{1,0},{2,3},{3,2},{4,5},{5,4},{6,7},{7,6},{8,9},{9,8},{10,11... | collective-permute-start | bytes 2359304 | tf_op jit(solution)/shard_map/ppermute | solution.py:288
  1.1 0.1 collective-permute-start.3
  1.2 1.0 %convert_element_type.3.refs_0_ = bf16[128,512]{1,0:T(8,128)(2,1)S(1)} convert(f32[128,512]{1,0:T(8,128)} %param.7) | non-fusion elementwise | flops 65536 | bytes 393216 | tf_op jit(solution)/shard_map/convert_element_type | solution.py:317
  2.2 0.0 copy-start.3
  2.2 3.0 %collective-permute-start = (bf16[128,512]{1,0:T(8,128)(2,1)S(1)}, bf16[128,512]{1,0:T(8,128)(2,1)S(1)}, u32[]{:S(2)}, u32[]{:S(2)}) collective-permute-start(bf16[128,512]{1,0:T(8,128)(2,1)S(1)} %convert_element_type.3.refs_0_), channel_id=1, source_target_pairs={{0,2},{1,3},{2,0},{3,1},{4,6},{5,7},{6,4},{7,5},{8,10},{9,11},{10,... | collective-permute-start | bytes 393224 | tf_op jit(solution)/shard_map/ppermute | solution.py:288
  5.2 0.6 %tables.1.table.refs_0_ = s32[8,128]{1,0:T(8,128)S(1)} custom-call(s32[1,1,3,2,8]{4,3,2,1,0:T(2,128)S(1)} %bitcast.3, s32[1,1,3]{2,1,0:T(1,128)S(1)} %copy-done.3), custom_call_target="tpu_custom_call" | custom-call | flops 1024 | bytes 1024 | tf_op jit(solution)/shard_map/tables/pallas_call | solution.py:236
  5.9 0.1 collective-permute-start.1
  6.0 0.1 pad_add_fusion.place._
  6.1 0.5 collective-permute-start.4
  6.5 2.0 %prepare.5 = (bf16[1024,256]{1,0:T(8,128)(2,1)S(1)}, bf16[1024,512]{1,0:T(8,128)(2,1)S(1)}) custom-call(s32[2]{0:T(128)S(1)} %pad_add_fusion.place._, s32[8,128]{1,0:T(8,128)S(1)} %tables.1.table.refs_0_, bf16[1,1,3,8,128,128]{5,4,3,2,1,0:T(8,128)(2,1)} %refs_1_.3, s32[1,1,3,8,16,128]{5,4,3,2,1,0:T(8,128)} %refs_2_.3, bf16[1024,512]{1,0:T(8,128)(2,1)} %users.4), custom_call_target="tpu_custom_call" | custom-call | flops 1024 | bytes 1024 | tf_op jit(solution)/shard_map/prepare/pallas_call | solution.py:334
  8.6 0.7 %prepare.4._.refs_5_ = bf16[1024,256]{1,0:T(8,128)(2,1)S(1)} custom-call(s32[2]{0:T(128)S(1)} %pad_add_fusion.place._, s32[8,128]{1,0:T(8,128)S(1)} %collective-permute-done.1.refs_0_.refs_3_, bf16[1,1,3,8,128,128]{5,4,3,2,1,0:T(8,128)(2,1)S(1)} %collective-permute-done.2.refs_1_.refs_4_, s32[1,1,3,8,16,128]{5,4,3,2,1,0:T(8,128)S(1)} %collective-permute-done.3.refs_2_.refs_5_), custom_call_target="tpu_custom_call" | custom-call | flops 1024 | bytes 1024 | tf_op jit(solution)/shard_map/prepare/pallas_call | solution.py:236
  9.3 0.0 copy-start
  9.4 1.9 %tiles.3 = (bf16[256,512]{1,0:T(8,128)(2,1)S(1)}, bf16[1024,256]{1,0:T(8,128)(2,1)S(1)}, bf16[1536,256]{1,0:T(8,128)(2,1)S(1)}, bf16[112,512]{1,0:T(8,128)(2,1)S...) custom-call(s32[2]{0:T(128)S(1)} %pad_add_fusion.place._, ...), custom_call_target="tpu_custom_call" | custom-call | flops 1024 | bytes 1024 | tf_op jit(solution)/shard_map/tiles/pallas_call | solution.py:236
  11.3 1.5 %collective-permute-start.7 = (bf16[144,512]{1,0:T(8,128)(2,1)S(1)}, bf16[144,512]{1,0:T(8,128)(2,1)S(1)}, u32[]{:S(2)}, u32[]{:S(2)}) collective-permute-start(bf16[144,512]{1,0:T(8,128)(2,1)S(1)} %get-tuple-element.42), channel_id=1, source_target_pairs={{0,2},{1,3},{2,0},{3,1},{4,6},{5,7},{6,4},{7,5},{8,10},{9,11},{10,... | collective-permute-start | bytes 442376 | tf_op jit(solution)/shard_map/ppermute | solution.py:288
  12.8 1.5 %collective-permute-start.5 = (bf16[112,512]{1,0:T(8,128)(2,1)S(1)}, bf16[112,512]{1,0:T(8,128)(2,1)S(1)}, u32[]{:S(2)}, u32[]{:S(2)}) collective-permute-start(bf16[112,512]{1,0:T(8,128)(2,1)S(1)} %get-tuple-element.39), channel_id=1, source_target_pairs={{0,4},{1,5},{2,6},{3,7},{4,8},{5,9},{6,10},{7,11},{8,12},{9,13},{1... | collective-permute-start | bytes 344072 | tf_op jit(solution)/shard_map/ppermute | solution.py:288
  14.3 1.1 %prepare.6 = (bf16[1024,256]{1,0:T(8,128)(2,1)S(1)}, bf16[1024,256]{1,0:T(8,128)(2,1)S(1)}) custom-call(s32[2]{0:T(128)S(1)} %pad_add_fusion.place._, s32[8,128]{1,0:T(8,128)S(1)} %tables.1.table.refs_0_, bf16[1,1,3,8,128,128]{5,4,3,2,1,0:T(8,128)(2,1)S(1)} %copy-done, s32[1,1,3,8,16,128]{5,4,3,2,1,0:T(8,128)S(1)} %copy-done.1, ...), custom_call_target="tpu_custom_call" | custom-call | flops 1024 | bytes 1024 | tf_op jit(solution)/shard_map/prepare/pallas_call | solution.py:236
  15.3 1.6 %collective-permute-start.6 = (bf16[112,512]{1,0:T(8,128)(2,1)S(1)}, bf16[112,512]{1,0:T(8,128)(2,1)S(1)}, u32[]{:S(2)}, u32[]{:S(2)}) collective-permute-start(bf16[112,512]{1,0:T(8,128)(2,1)S(1)} %get-tuple-element.40), channel_id=1, source_target_pairs={{0,6},{1,7},{2,4},{3,5},{4,10},{5,11},{6,8},{7,9},{8,14},{9,15},{1... | collective-permute-start | bytes 344072 | tf_op jit(solution)/shard_map/ppermute | solution.py:288
  17.0 0.3 collective-permute-done.7.refs_1_
  17.3 0.1 join.2
  17.4 1.4 %collective-permute-start.8 = (bf16[144,512]{1,0:T(8,128)(2,1)S(1)}, bf16[144,512]{1,0:T(8,128)(2,1)S(1)}, u32[]{:S(2)}, u32[]{:S(2)}) collective-permute-start(bf16[144,512]{1,0:T(8,128)(2,1)S(1)} %get-tuple-element.45), channel_id=1, source_target_pairs={{0,4},{1,5},{2,6},{3,7},{4,8},{5,9},{6,10},{7,11},{8,12},{9,13},{1... | collective-permute-start | bytes 442376 | tf_op jit(solution)/shard_map/ppermute | solution.py:288
  18.8 0.5 %collective-permute-start.10 = (bf16[1536,256]{1,0:T(8,128)(2,1)S(1)}, bf16[1536,256]{1,0:T(8,128)(2,1)S(1)}, u32[]{:S(2)}, u32[]{:S(2)}) collective-permute-start(bf16[1536,256]{1,0:T(8,128)(2,1)S(1)} %get-tuple-element.48.refs_3_), channel_id=1, source_target_pairs={{0,1},{1,0},{2,3},{3,2},{4,5},{5,4},{6,7},{7,6},{8,9},{9,8},{10,11... | collective-permute-start | bytes 2359304 | tf_op jit(solution)/shard_map/ppermute | solution.py:288
  19.3 1.0 %collective-permute-done.5.refs_0_ = bf16[112,512]{1,0:T(8,128)(2,1)S(1)} collective-permute-done((bf16[112,512]{1,0:T(8,128)(2,1)S(1)}, bf16[112,512]{1,0:T(8,128)(2,1)S(1)}, u32[]{:S(2)}, u32[]{:S(2)}) %collective-permute-start.5) | collective-permute-done | bytes 114720 | tf_op jit(solution)/shard_map/ppermute | solution.py:288
  20.4 0.4 collective-permute-done.9.refs_4_
  20.7 1.1 %collective-permute-done.10.refs_5_ = bf16[1536,256]{1,0:T(8,128)(2,1)S(1)} collective-permute-done((bf16[1536,256]{1,0:T(8,128)(2,1)S(1)}, bf16[1536,256]{1,0:T(8,128)(2,1)S(1)}, u32[]{:S(2)}, u32[]{:S(2)}) %collective-permute-start.10) | collective-permute-done | bytes 786464 | tf_op jit(solution)/shard_map/ppermute | solution.py:288
  21.9 1.4 %users.5 = (bf16[1024,512]{1,0:T(8,128)(2,1)S(1)}, bf16[1024,512]{1,0:T(8,128)(2,1)S(1)}) custom-call(f32[8,128]{1,0:T(8,128)S(1)} %mark.2._, bf16[256,512]{1,0:T(8,128)(2,1)S(1)} %get-tuple-element.46.low, bf16[1024,512]{1,0:T(8,128)(2,1)S(1)} %get-tuple-element.37.refs_2_.refs_0_, bf16[1024,512]{1,0:T(8,128)(2,1)S(1)} %collective-permute-done.4.refs_3_.refs_1_, ...), custom_call_target="tpu_custom_call" | custom-call | flops 1024 | bytes 1024 | tf_op jit(solution)/shard_map/users/pallas_call | solution.py:236
  23.3 1.2 %collective-permute-done.6.refs_1_ = bf16[112,512]{1,0:T(8,128)(2,1)S(1)} collective-permute-done((bf16[112,512]{1,0:T(8,128)(2,1)S(1)}, bf16[112,512]{1,0:T(8,128)(2,1)S(1)}, u32[]{:S(2)}, u32[]{:S(2)}) %collective-permute-start.6) | collective-permute-done | bytes 114720 | tf_op jit(solution)/shard_map/ppermute | solution.py:288
  24.5 1.5 %collective-permute-done.8.refs_2_ = bf16[144,512]{1,0:T(8,128)(2,1)S(1)} collective-permute-done((bf16[144,512]{1,0:T(8,128)(2,1)S(1)}, bf16[144,512]{1,0:T(8,128)(2,1)S(1)}, u32[]{:S(2)}, u32[]{:S(2)}) %collective-permute-start.8) | collective-permute-done | bytes 147488 | tf_op jit(solution)/shard_map/ppermute | solution.py:288
  26.0 1.9 %tiles.4 = (bf16[256,512]{1,0:T(8,128)(2,1)S(1)}, bf16[1024,256]{1,0:T(8,128)(2,1)S(1)}, bf16[1536,256]{1,0:T(8,128)(2,1)S(1)}, bf16[112,512]{1,0:T(8,128)(2,1)S...) custom-call(s32[2]{0:T(128)S(1)} %pad_add_fusion.place._, ...), custom_call_target="tpu_custom_call" | custom-call | flops 1024 | bytes 1024 | tf_op jit(solution)/shard_map/tiles/pallas_call | solution.py:236
  27.9 0.7 %collective-permute-start.13 = (bf16[144,512]{1,0:T(8,128)(2,1)S(1)}, bf16[144,512]{1,0:T(8,128)(2,1)S(1)}, u32[]{:S(2)}, u32[]{:S(2)}) collective-permute-start(bf16[144,512]{1,0:T(8,128)(2,1)S(1)} %get-tuple-element.56), channel_id=1, source_target_pairs={{0,2},{1,3},{2,0},{3,1},{4,6},{5,7},{6,4},{7,5},{8,10},{9,11},{10,... | collective-permute-start | bytes 442376 | tf_op jit(solution)/shard_map/ppermute | solution.py:288
  28.6 1.1 %prepare.7 = (bf16[1024,256]{1,0:T(8,128)(2,1)S(1)}, bf16[1024,256]{1,0:T(8,128)(2,1)S(1)}) custom-call(s32[2]{0:T(128)S(1)} %pad_add_fusion.place._, s32[8,128]{1,0:T(8,128)S(1)} %tables.1.table.refs_0_, bf16[1,1,3,8,128,128]{5,4,3,2,1,0:T(8,128)(2,1)S(1)} %copy-done, s32[1,1,3,8,16,128]{5,4,3,2,1,0:T(8,128)S(1)} %copy-done.1, ...), custom_call_target="tpu_custom_call" | custom-call | flops 1024 | bytes 1024 | tf_op jit(solution)/shard_map/prepare/pallas_call | solution.py:236
  29.8 2.3 %collective-permute-start.12 = (bf16[112,512]{1,0:T(8,128)(2,1)S(1)}, bf16[112,512]{1,0:T(8,128)(2,1)S(1)}, u32[]{:S(2)}, u32[]{:S(2)}) collective-permute-start(bf16[112,512]{1,0:T(8,128)(2,1)S(1)} %get-tuple-element.54), channel_id=1, source_target_pairs={{0,6},{1,7},{2,4},{3,5},{4,10},{5,11},{6,8},{7,9},{8,14},{9,15},{1... | collective-permute-start | bytes 344072 | tf_op jit(solution)/shard_map/ppermute | solution.py:288
  32.0 1.1 %collective-permute-done.13.refs_1_ = bf16[144,512]{1,0:T(8,128)(2,1)S(1)} collective-permute-done((bf16[144,512]{1,0:T(8,128)(2,1)S(1)}, bf16[144,512]{1,0:T(8,128)(2,1)S(1)}, u32[]{:S(2)}, u32[]{:S(2)}) %collective-permute-start.13) | collective-permute-done | bytes 147488 | tf_op jit(solution)/shard_map/ppermute | solution.py:288
  33.2 0.1 join.3
  33.3 0.1 collective-permute-start.14
  33.3 0.1 collective-permute-start.15
  33.4 0.5 collective-permute-start.16
  33.9 3.4 %collective-permute-done.11.refs_0_ = bf16[112,512]{1,0:T(8,128)(2,1)S(1)} collective-permute-done((bf16[112,512]{1,0:T(8,128)(2,1)S(1)}, bf16[112,512]{1,0:T(8,128)(2,1)S(1)}, u32[]{:S(2)}, u32[]{:S(2)}) %collective-permute-start.11) | collective-permute-done | bytes 114720 | tf_op jit(solution)/shard_map/ppermute | solution.py:288
  37.3 1.5 %users.6 = (bf16[1024,512]{1,0:T(8,128)(2,1)S(1)}, bf16[1024,512]{1,0:T(8,128)(2,1)S(1)}) custom-call(f32[8,128]{1,0:T(8,128)S(1)} %mark.3._, bf16[256,512]{1,0:T(8,128)(2,1)S(1)} %get-tuple-element.60.low, bf16[1024,512]{1,0:T(8,128)(2,1)S(1)} %get-tuple-element.49.refs_3_.refs_0_, bf16[1024,512]{1,0:T(8,128)(2,1)S(1)} %get-tuple-element.50.refs_4_.refs_1_, ...), custom_call_target="tpu_custom_call" | custom-call | flops 1024 | bytes 1024 | tf_op jit(solution)/shard_map/users/pallas_call | solution.py:236
  38.8 1.5 %collective-permute-done.12.refs_1_ = bf16[112,512]{1,0:T(8,128)(2,1)S(1)} collective-permute-done((bf16[112,512]{1,0:T(8,128)(2,1)S(1)}, bf16[112,512]{1,0:T(8,128)(2,1)S(1)}, u32[]{:S(2)}, u32[]{:S(2)}) %collective-permute-start.12) | collective-permute-done | bytes 114720 | tf_op jit(solution)/shard_map/ppermute | solution.py:288
  40.3 1.0 %collective-permute-done.14.refs_2_ = bf16[144,512]{1,0:T(8,128)(2,1)S(1)} collective-permute-done((bf16[144,512]{1,0:T(8,128)(2,1)S(1)}, bf16[144,512]{1,0:T(8,128)(2,1)S(1)}, u32[]{:S(2)}, u32[]{:S(2)}) %collective-permute-start.14) | collective-permute-done | bytes 147488 | tf_op jit(solution)/shard_map/ppermute | solution.py:288
  41.3 1.8 %tiles.5 = (bf16[256,512]{1,0:T(8,128)(2,1)S(1)}, bf16[1024,256]{1,0:T(8,128)(2,1)S(1)}, bf16[1536,256]{1,0:T(8,128)(2,1)S(1)}, f32[128,512]{1,0:T(8,128)S(1)}, bf16[128,512]{1,0:T(8,128)(2,1)S(1)}) custom-call(s32[2]{0:T(128)S(1)} %pad_add_fusion.place._, bf16[112,512]{1,0:T(8,128)(2,1)S(1)} %collective-permute-done.11.refs_0_, ...), custom_call_target="tpu_custom_call" | custom-call | flops 1024 | bytes 1024 | tf_op jit(solution)/shard_map/tiles/pallas_call | solution.py:236
  43.1 0.1 collective-permute-start.17
  43.2 1.2 %collective-permute-start.18 = (bf16[128,512]{1,0:T(8,128)(2,1)S(1)}, bf16[128,512]{1,0:T(8,128)(2,1)S(1)}, u32[]{:S(2)}, u32[]{:S(2)}) collective-permute-start(bf16[128,512]{1,0:T(8,128)(2,1)S(1)} %get-tuple-element.71), channel_id=1, source_target_pairs={{0,2},{1,3},{2,0},{3,1},{4,6},{5,7},{6,4},{7,5},{8,10},{9,11},{10,... | collective-permute-start | bytes 393224 | tf_op jit(solution)/shard_map/ppermute | solution.py:288
  44.4 1.0 %own.1.refs_0_ = f32[128,512]{1,0:T(8,128)S(1)} custom-call(s32[2]{0:T(128)S(1)} %pad_add_fusion.place._, f32[128,512]{1,0:T(8,128)S(1)} %get-tuple-element.70.old, bf16[1024,256]{1,0:T(8,128)(2,1)S(1)} %get-tuple-element.68.refs_1_.errors, bf16[1536,256]{1,0:T(8,128)(2,1)S(1)} %get-tuple-element.69.peer_errors, ...), custom_call_target="tpu_custom_call" | custom-call | flops 1024 | bytes 1024 | tf_op jit(solution)/shard_map/own/pallas_call | solution.py:236
  45.4 0.0 collective-permute-done.17.refs_2_
  45.5 2.3 %users.7.refs_2_ = bf16[1024,512]{1,0:T(8,128)(2,1)} custom-call(s32[2]{0:T(128)S(1)} %pad_add_fusion.place._, bf16[256,512]{1,0:T(8,128)(2,1)S(1)} %get-tuple-element.67.low, bf16[1024,512]{1,0:T(8,128)(2,1)S(1)} %get-tuple-element.63.refs_3_.refs_0_.users, bf16[1024,256]{1,0:T(8,128)(2,1)S(1)} %get-tuple-element.68.refs_1_.errors, ...), custom_call_target="tpu_custom_call" | custom-call | flops 1024 | bytes 1024 | tf_op jit(solution)/shard_map/users/pallas_call | solution.py:236
  47.8 1.3 %collective-permute-done.18.refs_1_ = bf16[128,512]{1,0:T(8,128)(2,1)S(1)} collective-permute-done((bf16[128,512]{1,0:T(8,128)(2,1)S(1)}, bf16[128,512]{1,0:T(8,128)(2,1)S(1)}, u32[]{:S(2)}, u32[]{:S(2)}) %collective-permute-start.18) | collective-permute-done | bytes 131104 | tf_op jit(solution)/shard_map/ppermute | solution.py:288
  49.1 0.7 %final.1 = f32[128,512]{1,0:T(8,128)} custom-call(f32[128,512]{1,0:T(8,128)S(1)} %own.1.refs_0_, bf16[128,512]{1,0:T(8,128)(2,1)S(1)} %collective-permute-done.18.refs_1_, bf16[1024,512]{1,0:T(8,128)(2,1)} %users.7.refs_2_), custom_call_target="tpu_custom_call" | custom-call | flops 1024 | bytes 1024 | tf_op jit(solution)/shard_map/final/pallas_call | solution.py:236
  (18 shorter events, 0.1 us)
Async XLA Ops:
  0.6 7.9 %collective-permute-start.2 = (bf16[1,1,3,8,128,128]{5,4,3,2,1,0:T(8,128)(2,1)}, bf16[1,1,3,8,128,128]{5,4,3,2,1,0:T(8,128)(2,1)S(1)}, u32[]{:S(2)}, u32[]{:S(2)}) collective-permute-start(bf16[1,1,3,8,128,128]{5,4,3,2,1,0:T(8,128)(2,1)} %refs_1_.3), channel_id=1, source_target_pairs={{0,1},{1,0},{2,3},{3,2},{4,5},{5,4},{6,7},{7,6},{8,9},{9,8},{10,11... | collective-permute-start | bytes 2359304 | tf_op jit(solution)/shard_map/ppermute | solution.py:288
  1.1 7.4 %collective-permute-start.3 = (s32[1,1,3,8,16,128]{5,4,3,2,1,0:T(8,128)}, s32[1,1,3,8,16,128]{5,4,3,2,1,0:T(8,128)S(1)}, u32[]{:S(2)}, u32[]{:S(2)}) collective-permute-start(s32[1,1,3,8,16,128]{5,4,3,2,1,0:T(8,128)} %refs_2_.3), channel_id=1, source_target_pairs={{0,1},{1,0},{2,3},{3,2},{4,5},{5,4},{6,7},{7,6},{8,9},{9,8},{10,11... | collective-permute-start | bytes 589832 | tf_op jit(solution)/shard_map/ppermute | solution.py:288
  1.2 4.0 %copy-start.2 = (s32[1,1,3,8,2]{3,4,2,1,0:T(2,128)S(1)}, s32[1,1,3,8,2]{3,4,2,1,0:T(2,128)}, u32[]{:S(2)}) copy-start(s32[1,1,3,8,2]{3,4,2,1,0:T(2,128)} %param.8) | copy-start | bytes 580
  2.2 3.0 %copy-start.3 = (s32[1,1,3]{2,1,0:T(1,128)S(1)}, s32[1,1,3]{2,1,0:T(1,128)}, u32[]{:S(2)}) copy-start(s32[1,1,3]{2,1,0:T(1,128)} %counts.1) | copy-start | bytes 40
  2.2 7.1 %collective-permute-start = (bf16[128,512]{1,0:T(8,128)(2,1)S(1)}, bf16[128,512]{1,0:T(8,128)(2,1)S(1)}, u32[]{:S(2)}, u32[]{:S(2)}) collective-permute-start(bf16[128,512]{1,0:T(8,128)(2,1)S(1)} %convert_element_type.3.refs_0_), channel_id=1, source_target_pairs={{0,2},{1,3},{2,0},{3,1},{4,6},{5,7},{6,4},{7,5},{8,10},{9,11},{10,... | collective-permute-start | bytes 393224 | tf_op jit(solution)/shard_map/ppermute | solution.py:288
  5.9 2.6 %collective-permute-start.1 = (s32[8,128]{1,0:T(8,128)S(1)}, s32[8,128]{1,0:T(8,128)S(1)}, u32[]{:S(2)}, u32[]{:S(2)}) collective-permute-start(s32[8,128]{1,0:T(8,128)S(1)} %tables.1.table.refs_0_), channel_id=1, source_target_pairs={{0,1},{1,0},{2,3},{3,2},{4,5},{5,4},{6,7},{7,6},{8,9},{9,8},{10,11... | collective-permute-start | bytes 12296 | tf_op jit(solution)/shard_map/ppermute | solution.py:288
  6.1 3.3 %collective-permute-start.4 = (bf16[1024,512]{1,0:T(8,128)(2,1)}, bf16[1024,512]{1,0:T(8,128)(2,1)S(1)}, u32[]{:S(2)}, u32[]{:S(2)}) collective-permute-start(bf16[1024,512]{1,0:T(8,128)(2,1)} %users.4), channel_id=1, source_target_pairs={{0,1},{1,0},{2,3},{3,2},{4,5},{5,4},{6,7},{7,6},{8,9},{9,8},{10,11... | collective-permute-start | bytes 3145736 | tf_op jit(solution)/shard_map/ppermute | solution.py:288
  9.3 4.9 %copy-start = (bf16[1,1,3,8,128,128]{5,4,3,2,1,0:T(8,128)(2,1)S(1)}, bf16[1,1,3,8,128,128]{5,4,3,2,1,0:T(8,128)(2,1)}, u32[]{:S(2)}) copy-start(bf16[1,1,3,8,128,128]{5,4,3,2,1,0:T(8,128)(2,1)} %refs_1_.3) | copy-start | bytes 2359300
  9.3 4.9 %copy-start.1 = (s32[1,1,3,8,16,128]{5,4,3,2,1,0:T(8,128)S(1)}, s32[1,1,3,8,16,128]{5,4,3,2,1,0:T(8,128)}, u32[]{:S(2)}) copy-start(s32[1,1,3,8,16,128]{5,4,3,2,1,0:T(8,128)} %refs_2_.3) | copy-start | bytes 589828
  11.3 6.0 %collective-permute-start.7 = (bf16[144,512]{1,0:T(8,128)(2,1)S(1)}, bf16[144,512]{1,0:T(8,128)(2,1)S(1)}, u32[]{:S(2)}, u32[]{:S(2)}) collective-permute-start(bf16[144,512]{1,0:T(8,128)(2,1)S(1)} %get-tuple-element.42), channel_id=1, source_target_pairs={{0,2},{1,3},{2,0},{3,1},{4,6},{5,7},{6,4},{7,5},{8,10},{9,11},{10,... | collective-permute-start | bytes 442376 | tf_op jit(solution)/shard_map/ppermute | solution.py:288
  12.8 7.6 %collective-permute-start.5 = (bf16[112,512]{1,0:T(8,128)(2,1)S(1)}, bf16[112,512]{1,0:T(8,128)(2,1)S(1)}, u32[]{:S(2)}, u32[]{:S(2)}) collective-permute-start(bf16[112,512]{1,0:T(8,128)(2,1)S(1)} %get-tuple-element.39), channel_id=1, source_target_pairs={{0,4},{1,5},{2,6},{3,7},{4,8},{5,9},{6,10},{7,11},{8,12},{9,13},{1... | collective-permute-start | bytes 344072 | tf_op jit(solution)/shard_map/ppermute | solution.py:288
  15.3 9.2 %collective-permute-start.6 = (bf16[112,512]{1,0:T(8,128)(2,1)S(1)}, bf16[112,512]{1,0:T(8,128)(2,1)S(1)}, u32[]{:S(2)}, u32[]{:S(2)}) collective-permute-start(bf16[112,512]{1,0:T(8,128)(2,1)S(1)} %get-tuple-element.40), channel_id=1, source_target_pairs={{0,6},{1,7},{2,4},{3,5},{4,10},{5,11},{6,8},{7,9},{8,14},{9,15},{1... | collective-permute-start | bytes 344072 | tf_op jit(solution)/shard_map/ppermute | solution.py:288
  17.4 8.6 %collective-permute-start.8 = (bf16[144,512]{1,0:T(8,128)(2,1)S(1)}, bf16[144,512]{1,0:T(8,128)(2,1)S(1)}, u32[]{:S(2)}, u32[]{:S(2)}) collective-permute-start(bf16[144,512]{1,0:T(8,128)(2,1)S(1)} %get-tuple-element.45), channel_id=1, source_target_pairs={{0,4},{1,5},{2,6},{3,7},{4,8},{5,9},{6,10},{7,11},{8,12},{9,13},{1... | collective-permute-start | bytes 442376 | tf_op jit(solution)/shard_map/ppermute | solution.py:288
  18.8 1.9 %collective-permute-start.9 = (bf16[1024,256]{1,0:T(8,128)(2,1)S(1)}, bf16[1024,256]{1,0:T(8,128)(2,1)S(1)}, u32[]{:S(2)}, u32[]{:S(2)}) collective-permute-start(bf16[1024,256]{1,0:T(8,128)(2,1)S(1)} %get-tuple-element.47.refs_2_), channel_id=1, source_target_pairs={{0,1},{1,0},{2,3},{3,2},{4,5},{5,4},{6,7},{7,6},{8,9},{9,8},{10,11... | collective-permute-start | bytes 1572872 | tf_op jit(solution)/shard_map/ppermute | solution.py:288
  18.8 3.0 %collective-permute-start.10 = (bf16[1536,256]{1,0:T(8,128)(2,1)S(1)}, bf16[1536,256]{1,0:T(8,128)(2,1)S(1)}, u32[]{:S(2)}, u32[]{:S(2)}) collective-permute-start(bf16[1536,256]{1,0:T(8,128)(2,1)S(1)} %get-tuple-element.48.refs_3_), channel_id=1, source_target_pairs={{0,1},{1,0},{2,3},{3,2},{4,5},{5,4},{6,7},{7,6},{8,9},{9,8},{10,11... | collective-permute-start | bytes 2359304 | tf_op jit(solution)/shard_map/ppermute | solution.py:288
  27.9 5.2 %collective-permute-start.13 = (bf16[144,512]{1,0:T(8,128)(2,1)S(1)}, bf16[144,512]{1,0:T(8,128)(2,1)S(1)}, u32[]{:S(2)}, u32[]{:S(2)}) collective-permute-start(bf16[144,512]{1,0:T(8,128)(2,1)S(1)} %get-tuple-element.56), channel_id=1, source_target_pairs={{0,2},{1,3},{2,0},{3,1},{4,6},{5,7},{6,4},{7,5},{8,10},{9,11},{10,... | collective-permute-start | bytes 442376 | tf_op jit(solution)/shard_map/ppermute | solution.py:288
  28.6 8.6 %collective-permute-start.11 = (bf16[112,512]{1,0:T(8,128)(2,1)S(1)}, bf16[112,512]{1,0:T(8,128)(2,1)S(1)}, u32[]{:S(2)}, u32[]{:S(2)}) collective-permute-start(bf16[112,512]{1,0:T(8,128)(2,1)S(1)} %get-tuple-element.53), channel_id=1, source_target_pairs={{0,4},{1,5},{2,6},{3,7},{4,8},{5,9},{6,10},{7,11},{8,12},{9,13},{1... | collective-permute-start | bytes 344072 | tf_op jit(solution)/shard_map/ppermute | solution.py:288
  29.8 10.5 %collective-permute-start.12 = (bf16[112,512]{1,0:T(8,128)(2,1)S(1)}, bf16[112,512]{1,0:T(8,128)(2,1)S(1)}, u32[]{:S(2)}, u32[]{:S(2)}) collective-permute-start(bf16[112,512]{1,0:T(8,128)(2,1)S(1)} %get-tuple-element.54), channel_id=1, source_target_pairs={{0,6},{1,7},{2,4},{3,5},{4,10},{5,11},{6,8},{7,9},{8,14},{9,15},{1... | collective-permute-start | bytes 344072 | tf_op jit(solution)/shard_map/ppermute | solution.py:288
  33.3 8.0 %collective-permute-start.14 = (bf16[144,512]{1,0:T(8,128)(2,1)S(1)}, bf16[144,512]{1,0:T(8,128)(2,1)S(1)}, u32[]{:S(2)}, u32[]{:S(2)}) collective-permute-start(bf16[144,512]{1,0:T(8,128)(2,1)S(1)} %get-tuple-element.59), channel_id=1, source_target_pairs={{0,4},{1,5},{2,6},{3,7},{4,8},{5,9},{6,10},{7,11},{8,12},{9,13},{1... | collective-permute-start | bytes 442376 | tf_op jit(solution)/shard_map/ppermute | solution.py:288
  33.3 3.9 %collective-permute-start.15 = (bf16[1024,256]{1,0:T(8,128)(2,1)S(1)}, bf16[1024,256]{1,0:T(8,128)(2,1)S(1)}, u32[]{:S(2)}, u32[]{:S(2)}) collective-permute-start(bf16[1024,256]{1,0:T(8,128)(2,1)S(1)} %get-tuple-element.61.refs_2_), channel_id=1, source_target_pairs={{0,1},{1,0},{2,3},{3,2},{4,5},{5,4},{6,7},{7,6},{8,9},{9,8},{10,11... | collective-permute-start | bytes 1572872 | tf_op jit(solution)/shard_map/ppermute | solution.py:288
  33.4 3.9 %collective-permute-start.16 = (bf16[1536,256]{1,0:T(8,128)(2,1)S(1)}, bf16[1536,256]{1,0:T(8,128)(2,1)S(1)}, u32[]{:S(2)}, u32[]{:S(2)}) collective-permute-start(bf16[1536,256]{1,0:T(8,128)(2,1)S(1)} %get-tuple-element.62.refs_3_), channel_id=1, source_target_pairs={{0,1},{1,0},{2,3},{3,2},{4,5},{5,4},{6,7},{7,6},{8,9},{9,8},{10,11... | collective-permute-start | bytes 2359304 | tf_op jit(solution)/shard_map/ppermute | solution.py:288
  43.1 2.4 %collective-permute-start.17 = (bf16[1536,256]{1,0:T(8,128)(2,1)S(1)}, bf16[1536,256]{1,0:T(8,128)(2,1)S(1)}, u32[]{:S(2)}, u32[]{:S(2)}) collective-permute-start(bf16[1536,256]{1,0:T(8,128)(2,1)S(1)} %get-tuple-element.69.peer_errors), channel_id=1, source_target_pairs={{0,1},{1,0},{2,3},{3,2},{4,5},{5,4},{6,7},{7,6},{8,9},{9,8},{10,11... | collective-permute-start | bytes 2359304 | tf_op jit(solution)/shard_map/ppermute | solution.py:288
  43.2 5.9 %collective-permute-start.18 = (bf16[128,512]{1,0:T(8,128)(2,1)S(1)}, bf16[128,512]{1,0:T(8,128)(2,1)S(1)}, u32[]{:S(2)}, u32[]{:S(2)}) collective-permute-start(bf16[128,512]{1,0:T(8,128)(2,1)S(1)} %get-tuple-element.71), channel_id=1, source_target_pairs={{0,2},{1,3},{2,0},{3,1},{4,6},{5,7},{6,4},{7,5},{8,10},{9,11},{10,... | collective-permute-start | bytes 393224 | tf_op jit(solution)/shard_map/ppermute | solution.py:288

commit v9 on v8

--- a/solution.py
+++ b/solution.py
@@ -391,7 +391,7 @@
                 1024,
             )
             arrived += [move(summed, 1, 0, False)]
-            sets = [marked(arrived[0]), low, users, other_users]
+            sets = [marked(*arrived[:2]), low, users, other_users]
             sets += [errors, other_errors, swap(errors), swap(other_errors)]
         kind = jax.ShapeDtypeStruct if last else pltpu.VMEM
         users, *other_users = kernel_call(

time: 50.3 us -> 49.8 us (0.990)
  waiting for transfers between devices: 13.9 us -> 13.3 us
    ppermute x19, waiting for transfers between devices: 13.9 us -> 13.3 us  [moved(): return lax.ppermute(x, ('strata', 'shard'), pairs)]
  transfers between devices with their start and end apart: 19 -> 19, of which waited for: 11 -> 9; matrix products, arithmetic and copies ran while one was open for 2% -> 2% of each run, Pallas kernels for 24% -> 24%
where the time goes in v9:
time: 49.8 us; the launch traced here: 49.7 us
  Pallas kernels  18.5 us (37%)
  starting transfers between devices  16 us (32%)
  waiting for transfers between devices  13.3 us (27%)
  other arithmetic  1.06 us (2%)
  between operations  0.85 us (2%)
    pallas_call x14, Pallas kernels, kernel_call(): pl.pallas_call(body, name=name, out_shape=tuple(outs), in_specs=[SM if x....  16.5 us
    ppermute x19, starting transfers between devices, moved(): return lax.ppermute(x, ('strata', 'shard'), pairs)  16 us
    ppermute x19, waiting for transfers between devices, moved(): return lax.ppermute(x, ('strata', 'shard'), pairs)  13.3 us
    pallas_call x1, Pallas kernels, shards(): pl.pallas_call(functools.partial(prepare_first_kernel, rows, close), name...  1.98 us
  transfers between devices with their start and end apart: 19, of which 9 were waited for; matrix products, arithmetic and copies ran while one was open for 2% of the time, Pallas kernels for 24%

profile of v9, /device:TPU:0, one launch (start us, length us, event | category | flops | bytes accessed | tf_op | source)
XLA Modules:
  0.0 49.7 jit_solution(13754228223160236067)
XLA Ops:
  0.6 0.5 %collective-permute-start.2 = (bf16[1,1,3,8,128,128]{5,4,3,2,1,0:T(8,128)(2,1)}, bf16[1,1,3,8,128,128]{5,4,3,2,1,0:T(8,128)(2,1)S(1)}, u32[]{:S(2)}, u32[]{:S(2)}) collective-permute-start(bf16[1,1,3,8,128,128]{5,4,3,2,1,0:T(8,128)(2,1)} %refs_1_.3), channel_id=1, source_target_pairs={{0,1},{1,0},{2,3},{3,2},{4,5},{5,4},{6,7},{7,6},{8,9},{9,8},{10,11... | collective-permute-start | bytes 2359304 | tf_op jit(solution)/shard_map/ppermute | solution.py:288
  1.1 0.1 collective-permute-start.3
  1.2 1.0 %convert_element_type.3.refs_0_ = bf16[128,512]{1,0:T(8,128)(2,1)S(1)} convert(f32[128,512]{1,0:T(8,128)} %param.7) | non-fusion elementwise | flops 65536 | bytes 393216 | tf_op jit(solution)/shard_map/convert_element_type | solution.py:317
  2.2 0.0 copy-start.3
  2.2 3.0 %collective-permute-start = (bf16[128,512]{1,0:T(8,128)(2,1)S(1)}, bf16[128,512]{1,0:T(8,128)(2,1)S(1)}, u32[]{:S(2)}, u32[]{:S(2)}) collective-permute-start(bf16[128,512]{1,0:T(8,128)(2,1)S(1)} %convert_element_type.3.refs_0_), channel_id=1, source_target_pairs={{0,2},{1,3},{2,0},{3,1},{4,6},{5,7},{6,4},{7,5},{8,10},{9,11},{10,... | collective-permute-start | bytes 393224 | tf_op jit(solution)/shard_map/ppermute | solution.py:288
  5.2 0.6 %tables.1.table.refs_0_ = s32[8,128]{1,0:T(8,128)S(1)} custom-call(s32[1,1,3,2,8]{4,3,2,1,0:T(2,128)S(1)} %bitcast.3, s32[1,1,3]{2,1,0:T(1,128)S(1)} %copy-done.3), custom_call_target="tpu_custom_call" | custom-call | flops 1024 | bytes 1024 | tf_op jit(solution)/shard_map/tables/pallas_call | solution.py:236
  5.9 0.1 collective-permute-start.1
  6.0 0.1 pad_add_fusion.place._
  6.1 0.5 collective-permute-start.4
  6.5 2.0 %prepare.5 = (bf16[1024,256]{1,0:T(8,128)(2,1)S(1)}, bf16[1024,512]{1,0:T(8,128)(2,1)S(1)}) custom-call(s32[2]{0:T(128)S(1)} %pad_add_fusion.place._, s32[8,128]{1,0:T(8,128)S(1)} %tables.1.table.refs_0_, bf16[1,1,3,8,128,128]{5,4,3,2,1,0:T(8,128)(2,1)} %refs_1_.3, s32[1,1,3,8,16,128]{5,4,3,2,1,0:T(8,128)} %refs_2_.3, bf16[1024,512]{1,0:T(8,128)(2,1)} %users.4), custom_call_target="tpu_custom_call" | custom-call | flops 1024 | bytes 1024 | tf_op jit(solution)/shard_map/prepare/pallas_call | solution.py:334
  8.5 0.0 collective-permute-done.1.refs_0_.refs_3_
  8.5 0.0 collective-permute-done.3.refs_2_.refs_5_
  8.6 0.8 %prepare.4._.refs_5_ = bf16[1024,256]{1,0:T(8,128)(2,1)S(1)} custom-call(s32[2]{0:T(128)S(1)} %pad_add_fusion.place._, s32[8,128]{1,0:T(8,128)S(1)} %collective-permute-done.1.refs_0_.refs_3_, bf16[1,1,3,8,128,128]{5,4,3,2,1,0:T(8,128)(2,1)S(1)} %collective-permute-done.2.refs_1_.refs_4_, s32[1,1,3,8,16,128]{5,4,3,2,1,0:T(8,128)S(1)} %collective-permute-done.3.refs_2_.refs_5_), custom_call_target="tpu_custom_call" | custom-call | flops 1024 | bytes 1024 | tf_op jit(solution)/shard_map/prepare/pallas_call | solution.py:236
  9.4 0.0 collective-permute-done.source
  9.4 0.0 copy-start
  9.4 0.0 copy-start.1
  9.4 1.9 %tiles.3 = (bf16[256,512]{1,0:T(8,128)(2,1)S(1)}, bf16[1024,256]{1,0:T(8,128)(2,1)S(1)}, bf16[1536,256]{1,0:T(8,128)(2,1)S(1)}, bf16[112,512]{1,0:T(8,128)(2,1)S...) custom-call(s32[2]{0:T(128)S(1)} %pad_add_fusion.place._, ...), custom_call_target="tpu_custom_call" | custom-call | flops 1024 | bytes 1024 | tf_op jit(solution)/shard_map/tiles/pallas_call | solution.py:236
  11.4 1.4 %collective-permute-start.7 = (bf16[144,512]{1,0:T(8,128)(2,1)S(1)}, bf16[144,512]{1,0:T(8,128)(2,1)S(1)}, u32[]{:S(2)}, u32[]{:S(2)}) collective-permute-start(bf16[144,512]{1,0:T(8,128)(2,1)S(1)} %get-tuple-element.42), channel_id=1, source_target_pairs={{0,2},{1,3},{2,0},{3,1},{4,6},{5,7},{6,4},{7,5},{8,10},{9,11},{10,... | collective-permute-start | bytes 442376 | tf_op jit(solution)/shard_map/ppermute | solution.py:288
  12.8 1.5 %collective-permute-start.5 = (bf16[112,512]{1,0:T(8,128)(2,1)S(1)}, bf16[112,512]{1,0:T(8,128)(2,1)S(1)}, u32[]{:S(2)}, u32[]{:S(2)}) collective-permute-start(bf16[112,512]{1,0:T(8,128)(2,1)S(1)} %get-tuple-element.39), channel_id=1, source_target_pairs={{0,4},{1,5},{2,6},{3,7},{4,8},{5,9},{6,10},{7,11},{8,12},{9,13},{1... | collective-permute-start | bytes 344072 | tf_op jit(solution)/shard_map/ppermute | solution.py:288
  14.3 1.6 %collective-permute-start.6 = (bf16[112,512]{1,0:T(8,128)(2,1)S(1)}, bf16[112,512]{1,0:T(8,128)(2,1)S(1)}, u32[]{:S(2)}, u32[]{:S(2)}) collective-permute-start(bf16[112,512]{1,0:T(8,128)(2,1)S(1)} %get-tuple-element.40), channel_id=1, source_target_pairs={{0,6},{1,7},{2,4},{3,5},{4,10},{5,11},{6,8},{7,9},{8,14},{9,15},{1... | collective-permute-start | bytes 344072 | tf_op jit(solution)/shard_map/ppermute | solution.py:288
  15.9 1.0 %prepare.6 = (bf16[1024,256]{1,0:T(8,128)(2,1)S(1)}, bf16[1024,256]{1,0:T(8,128)(2,1)S(1)}) custom-call(s32[2]{0:T(128)S(1)} %pad_add_fusion.place._, s32[8,128]{1,0:T(8,128)S(1)} %tables.1.table.refs_0_, bf16[1,1,3,8,128,128]{5,4,3,2,1,0:T(8,128)(2,1)S(1)} %copy-done, s32[1,1,3,8,16,128]{5,4,3,2,1,0:T(8,128)S(1)} %copy-done.1, ...), custom_call_target="tpu_custom_call" | custom-call | flops 1024 | bytes 1024 | tf_op jit(solution)/shard_map/prepare/pallas_call | solution.py:236
  16.9 0.4 collective-permute-done.7.refs_1_
  17.3 0.1 join.2
  17.4 2.0 %collective-permute-start.8 = (bf16[144,512]{1,0:T(8,128)(2,1)S(1)}, bf16[144,512]{1,0:T(8,128)(2,1)S(1)}, u32[]{:S(2)}, u32[]{:S(2)}) collective-permute-start(bf16[144,512]{1,0:T(8,128)(2,1)S(1)} %get-tuple-element.45), channel_id=1, source_target_pairs={{0,4},{1,5},{2,6},{3,7},{4,8},{5,9},{6,10},{7,11},{8,12},{9,13},{1... | collective-permute-start | bytes 442376 | tf_op jit(solution)/shard_map/ppermute | solution.py:288
  19.4 0.5 %collective-permute-start.10 = (bf16[1536,256]{1,0:T(8,128)(2,1)S(1)}, bf16[1536,256]{1,0:T(8,128)(2,1)S(1)}, u32[]{:S(2)}, u32[]{:S(2)}) collective-permute-start(bf16[1536,256]{1,0:T(8,128)(2,1)S(1)} %get-tuple-element.48.refs_3_), channel_id=1, source_target_pairs={{0,1},{1,0},{2,3},{3,2},{4,5},{5,4},{6,7},{7,6},{8,9},{9,8},{10,11... | collective-permute-start | bytes 2359304 | tf_op jit(solution)/shard_map/ppermute | solution.py:288
  19.9 1.6 %collective-permute-done.5.refs_0_ = bf16[112,512]{1,0:T(8,128)(2,1)S(1)} collective-permute-done((bf16[112,512]{1,0:T(8,128)(2,1)S(1)}, bf16[112,512]{1,0:T(8,128)(2,1)S(1)}, u32[]{:S(2)}, u32[]{:S(2)}) %collective-permute-start.5) | collective-permute-done | bytes 114720 | tf_op jit(solution)/shard_map/ppermute | solution.py:288
  21.4 2.7 %collective-permute-done.6.refs_1_ = bf16[112,512]{1,0:T(8,128)(2,1)S(1)} collective-permute-done((bf16[112,512]{1,0:T(8,128)(2,1)S(1)}, bf16[112,512]{1,0:T(8,128)(2,1)S(1)}, u32[]{:S(2)}, u32[]{:S(2)}) %collective-permute-start.6) | collective-permute-done | bytes 114720 | tf_op jit(solution)/shard_map/ppermute | solution.py:288
  24.1 1.4 %users.5 = (bf16[1024,512]{1,0:T(8,128)(2,1)S(1)}, bf16[1024,512]{1,0:T(8,128)(2,1)S(1)}) custom-call(f32[8,128]{1,0:T(8,128)S(1)} %mark.2._, bf16[256,512]{1,0:T(8,128)(2,1)S(1)} %get-tuple-element.46.low, bf16[1024,512]{1,0:T(8,128)(2,1)S(1)} %get-tuple-element.37.refs_2_.refs_0_, bf16[1024,512]{1,0:T(8,128)(2,1)S(1)} %collective-permute-done.4.refs_3_.refs_1_, ...), custom_call_target="tpu_custom_call" | custom-call | flops 1024 | bytes 1024 | tf_op jit(solution)/shard_map/users/pallas_call | solution.py:236
  25.5 0.3 collective-permute-done.8.refs_2_
  25.9 1.9 %tiles.4 = (bf16[256,512]{1,0:T(8,128)(2,1)S(1)}, bf16[1024,256]{1,0:T(8,128)(2,1)S(1)}, bf16[1536,256]{1,0:T(8,128)(2,1)S(1)}, bf16[112,512]{1,0:T(8,128)(2,1)S...) custom-call(s32[2]{0:T(128)S(1)} %pad_add_fusion.place._, ...), custom_call_target="tpu_custom_call" | custom-call | flops 1024 | bytes 1024 | tf_op jit(solution)/shard_map/tiles/pallas_call | solution.py:236
  27.8 1.2 %collective-permute-start.13 = (bf16[144,512]{1,0:T(8,128)(2,1)S(1)}, bf16[144,512]{1,0:T(8,128)(2,1)S(1)}, u32[]{:S(2)}, u32[]{:S(2)}) collective-permute-start(bf16[144,512]{1,0:T(8,128)(2,1)S(1)} %get-tuple-element.56), channel_id=1, source_target_pairs={{0,2},{1,3},{2,0},{3,1},{4,6},{5,7},{6,4},{7,5},{8,10},{9,11},{10,... | collective-permute-start | bytes 442376 | tf_op jit(solution)/shard_map/ppermute | solution.py:288
  29.0 1.6 %collective-permute-start.12 = (bf16[112,512]{1,0:T(8,128)(2,1)S(1)}, bf16[112,512]{1,0:T(8,128)(2,1)S(1)}, u32[]{:S(2)}, u32[]{:S(2)}) collective-permute-start(bf16[112,512]{1,0:T(8,128)(2,1)S(1)} %get-tuple-element.54), channel_id=1, source_target_pairs={{0,6},{1,7},{2,4},{3,5},{4,10},{5,11},{6,8},{7,9},{8,14},{9,15},{1... | collective-permute-start | bytes 344072 | tf_op jit(solution)/shard_map/ppermute | solution.py:288
  30.6 1.2 %prepare.7 = (bf16[1024,256]{1,0:T(8,128)(2,1)S(1)}, bf16[1024,256]{1,0:T(8,128)(2,1)S(1)}) custom-call(s32[2]{0:T(128)S(1)} %pad_add_fusion.place._, s32[8,128]{1,0:T(8,128)S(1)} %tables.1.table.refs_0_, bf16[1,1,3,8,128,128]{5,4,3,2,1,0:T(8,128)(2,1)S(1)} %copy-done, s32[1,1,3,8,16,128]{5,4,3,2,1,0:T(8,128)S(1)} %copy-done.1, ...), custom_call_target="tpu_custom_call" | custom-call | flops 1024 | bytes 1024 | tf_op jit(solution)/shard_map/prepare/pallas_call | solution.py:236
  31.8 1.2 %collective-permute-done.13.refs_1_ = bf16[144,512]{1,0:T(8,128)(2,1)S(1)} collective-permute-done((bf16[144,512]{1,0:T(8,128)(2,1)S(1)}, bf16[144,512]{1,0:T(8,128)(2,1)S(1)}, u32[]{:S(2)}, u32[]{:S(2)}) %collective-permute-start.13) | collective-permute-done | bytes 147488 | tf_op jit(solution)/shard_map/ppermute | solution.py:288
  33.0 0.1 join.3
  33.1 0.4 collective-permute-start.14
  33.5 0.5 %collective-permute-start.16 = (bf16[1536,256]{1,0:T(8,128)(2,1)S(1)}, bf16[1536,256]{1,0:T(8,128)(2,1)S(1)}, u32[]{:S(2)}, u32[]{:S(2)}) collective-permute-start(bf16[1536,256]{1,0:T(8,128)(2,1)S(1)} %get-tuple-element.62.refs_3_), channel_id=1, source_target_pairs={{0,1},{1,0},{2,3},{3,2},{4,5},{5,4},{6,7},{7,6},{8,9},{9,8},{10,11... | collective-permute-start | bytes 2359304 | tf_op jit(solution)/shard_map/ppermute | solution.py:288
  34.1 2.4 %collective-permute-done.11.refs_0_ = bf16[112,512]{1,0:T(8,128)(2,1)S(1)} collective-permute-done((bf16[112,512]{1,0:T(8,128)(2,1)S(1)}, bf16[112,512]{1,0:T(8,128)(2,1)S(1)}, u32[]{:S(2)}, u32[]{:S(2)}) %collective-permute-start.11) | collective-permute-done | bytes 114720 | tf_op jit(solution)/shard_map/ppermute | solution.py:288
  36.4 3.2 %collective-permute-done.12.refs_1_ = bf16[112,512]{1,0:T(8,128)(2,1)S(1)} collective-permute-done((bf16[112,512]{1,0:T(8,128)(2,1)S(1)}, bf16[112,512]{1,0:T(8,128)(2,1)S(1)}, u32[]{:S(2)}, u32[]{:S(2)}) %collective-permute-start.12) | collective-permute-done | bytes 114720 | tf_op jit(solution)/shard_map/ppermute | solution.py:288
  39.6 1.5 %users.6 = (bf16[1024,512]{1,0:T(8,128)(2,1)S(1)}, bf16[1024,512]{1,0:T(8,128)(2,1)S(1)}) custom-call(f32[8,128]{1,0:T(8,128)S(1)} %mark.3._, bf16[256,512]{1,0:T(8,128)(2,1)S(1)} %get-tuple-element.60.low, bf16[1024,512]{1,0:T(8,128)(2,1)S(1)} %get-tuple-element.49.refs_3_.refs_0_, bf16[1024,512]{1,0:T(8,128)(2,1)S(1)} %get-tuple-element.50.refs_4_.refs_1_, ...), custom_call_target="tpu_custom_call" | custom-call | flops 1024 | bytes 1024 | tf_op jit(solution)/shard_map/users/pallas_call | solution.py:236
  41.1 1.8 %tiles.5 = (bf16[256,512]{1,0:T(8,128)(2,1)S(1)}, bf16[1024,256]{1,0:T(8,128)(2,1)S(1)}, bf16[1536,256]{1,0:T(8,128)(2,1)S(1)}, f32[128,512]{1,0:T(8,128)S(1)}, bf16[128,512]{1,0:T(8,128)(2,1)S(1)}) custom-call(s32[2]{0:T(128)S(1)} %pad_add_fusion.place._, bf16[112,512]{1,0:T(8,128)(2,1)S(1)} %collective-permute-done.11.refs_0_, ...), custom_call_target="tpu_custom_call" | custom-call | flops 1024 | bytes 1024 | tf_op jit(solution)/shard_map/tiles/pallas_call | solution.py:236
  43.0 0.1 collective-permute-start.17
  43.0 1.0 %collective-permute-start.18 = (bf16[128,512]{1,0:T(8,128)(2,1)S(1)}, bf16[128,512]{1,0:T(8,128)(2,1)S(1)}, u32[]{:S(2)}, u32[]{:S(2)}) collective-permute-start(bf16[128,512]{1,0:T(8,128)(2,1)S(1)} %get-tuple-element.71), channel_id=1, source_target_pairs={{0,2},{1,3},{2,0},{3,1},{4,6},{5,7},{6,4},{7,5},{8,10},{9,11},{10,... | collective-permute-start | bytes 393224 | tf_op jit(solution)/shard_map/ppermute | solution.py:288
  44.1 1.0 %own.1.refs_0_ = f32[128,512]{1,0:T(8,128)S(1)} custom-call(s32[2]{0:T(128)S(1)} %pad_add_fusion.place._, f32[128,512]{1,0:T(8,128)S(1)} %get-tuple-element.70.old, bf16[1024,256]{1,0:T(8,128)(2,1)S(1)} %get-tuple-element.68.refs_1_.errors, bf16[1536,256]{1,0:T(8,128)(2,1)S(1)} %get-tuple-element.69.peer_errors, ...), custom_call_target="tpu_custom_call" | custom-call | flops 1024 | bytes 1024 | tf_op jit(solution)/shard_map/own/pallas_call | solution.py:236
  45.1 0.2 collective-permute-done.17.refs_2_
  45.3 2.3 %users.7.refs_2_ = bf16[1024,512]{1,0:T(8,128)(2,1)} custom-call(s32[2]{0:T(128)S(1)} %pad_add_fusion.place._, bf16[256,512]{1,0:T(8,128)(2,1)S(1)} %get-tuple-element.67.low, bf16[1024,512]{1,0:T(8,128)(2,1)S(1)} %get-tuple-element.63.refs_3_.refs_0_.users, bf16[1024,256]{1,0:T(8,128)(2,1)S(1)} %get-tuple-element.68.refs_1_.errors, ...), custom_call_target="tpu_custom_call" | custom-call | flops 1024 | bytes 1024 | tf_op jit(solution)/shard_map/users/pallas_call | solution.py:236
  47.6 1.3 %collective-permute-done.18.refs_1_ = bf16[128,512]{1,0:T(8,128)(2,1)S(1)} collective-permute-done((bf16[128,512]{1,0:T(8,128)(2,1)S(1)}, bf16[128,512]{1,0:T(8,128)(2,1)S(1)}, u32[]{:S(2)}, u32[]{:S(2)}) %collective-permute-start.18) | collective-permute-done | bytes 131104 | tf_op jit(solution)/shard_map/ppermute | solution.py:288
  48.9 0.7 %final.1 = f32[128,512]{1,0:T(8,128)} custom-call(f32[128,512]{1,0:T(8,128)S(1)} %own.1.refs_0_, bf16[128,512]{1,0:T(8,128)(2,1)S(1)} %collective-permute-done.18.refs_1_, bf16[1024,512]{1,0:T(8,128)(2,1)} %users.7.refs_2_), custom_call_target="tpu_custom_call" | custom-call | flops 1024 | bytes 1024 | tf_op jit(solution)/shard_map/final/pallas_call | solution.py:236
  (18 shorter events, 0.1 us)
Async XLA Ops:
  0.6 7.9 %collective-permute-start.2 = (bf16[1,1,3,8,128,128]{5,4,3,2,1,0:T(8,128)(2,1)}, bf16[1,1,3,8,128,128]{5,4,3,2,1,0:T(8,128)(2,1)S(1)}, u32[]{:S(2)}, u32[]{:S(2)}) collective-permute-start(bf16[1,1,3,8,128,128]{5,4,3,2,1,0:T(8,128)(2,1)} %refs_1_.3), channel_id=1, source_target_pairs={{0,1},{1,0},{2,3},{3,2},{4,5},{5,4},{6,7},{7,6},{8,9},{9,8},{10,11... | collective-permute-start | bytes 2359304 | tf_op jit(solution)/shard_map/ppermute | solution.py:288
  1.1 7.4 %collective-permute-start.3 = (s32[1,1,3,8,16,128]{5,4,3,2,1,0:T(8,128)}, s32[1,1,3,8,16,128]{5,4,3,2,1,0:T(8,128)S(1)}, u32[]{:S(2)}, u32[]{:S(2)}) collective-permute-start(s32[1,1,3,8,16,128]{5,4,3,2,1,0:T(8,128)} %refs_2_.3), channel_id=1, source_target_pairs={{0,1},{1,0},{2,3},{3,2},{4,5},{5,4},{6,7},{7,6},{8,9},{9,8},{10,11... | collective-permute-start | bytes 589832 | tf_op jit(solution)/shard_map/ppermute | solution.py:288
  1.2 4.0 %copy-start.2 = (s32[1,1,3,8,2]{3,4,2,1,0:T(2,128)S(1)}, s32[1,1,3,8,2]{3,4,2,1,0:T(2,128)}, u32[]{:S(2)}) copy-start(s32[1,1,3,8,2]{3,4,2,1,0:T(2,128)} %param.8) | copy-start | bytes 580
  2.2 3.0 %copy-start.3 = (s32[1,1,3]{2,1,0:T(1,128)S(1)}, s32[1,1,3]{2,1,0:T(1,128)}, u32[]{:S(2)}) copy-start(s32[1,1,3]{2,1,0:T(1,128)} %counts.1) | copy-start | bytes 40
  2.2 7.2 %collective-permute-start = (bf16[128,512]{1,0:T(8,128)(2,1)S(1)}, bf16[128,512]{1,0:T(8,128)(2,1)S(1)}, u32[]{:S(2)}, u32[]{:S(2)}) collective-permute-start(bf16[128,512]{1,0:T(8,128)(2,1)S(1)} %convert_element_type.3.refs_0_), channel_id=1, source_target_pairs={{0,2},{1,3},{2,0},{3,1},{4,6},{5,7},{6,4},{7,5},{8,10},{9,11},{10,... | collective-permute-start | bytes 393224 | tf_op jit(solution)/shard_map/ppermute | solution.py:288
  5.9 2.6 %collective-permute-start.1 = (s32[8,128]{1,0:T(8,128)S(1)}, s32[8,128]{1,0:T(8,128)S(1)}, u32[]{:S(2)}, u32[]{:S(2)}) collective-permute-start(s32[8,128]{1,0:T(8,128)S(1)} %tables.1.table.refs_0_), channel_id=1, source_target_pairs={{0,1},{1,0},{2,3},{3,2},{4,5},{5,4},{6,7},{7,6},{8,9},{9,8},{10,11... | collective-permute-start | bytes 12296 | tf_op jit(solution)/shard_map/ppermute | solution.py:288
  6.1 3.4 %collective-permute-start.4 = (bf16[1024,512]{1,0:T(8,128)(2,1)}, bf16[1024,512]{1,0:T(8,128)(2,1)S(1)}, u32[]{:S(2)}, u32[]{:S(2)}) collective-permute-start(bf16[1024,512]{1,0:T(8,128)(2,1)} %users.4), channel_id=1, source_target_pairs={{0,1},{1,0},{2,3},{3,2},{4,5},{5,4},{6,7},{7,6},{8,9},{9,8},{10,11... | collective-permute-start | bytes 3145736 | tf_op jit(solution)/shard_map/ppermute | solution.py:288
  9.4 6.5 %copy-start = (bf16[1,1,3,8,128,128]{5,4,3,2,1,0:T(8,128)(2,1)S(1)}, bf16[1,1,3,8,128,128]{5,4,3,2,1,0:T(8,128)(2,1)}, u32[]{:S(2)}) copy-start(bf16[1,1,3,8,128,128]{5,4,3,2,1,0:T(8,128)(2,1)} %refs_1_.3) | copy-start | bytes 2359300
  9.4 6.5 %copy-start.1 = (s32[1,1,3,8,16,128]{5,4,3,2,1,0:T(8,128)S(1)}, s32[1,1,3,8,16,128]{5,4,3,2,1,0:T(8,128)}, u32[]{:S(2)}) copy-start(s32[1,1,3,8,16,128]{5,4,3,2,1,0:T(8,128)} %refs_2_.3) | copy-start | bytes 589828
  11.4 5.9 %collective-permute-start.7 = (bf16[144,512]{1,0:T(8,128)(2,1)S(1)}, bf16[144,512]{1,0:T(8,128)(2,1)S(1)}, u32[]{:S(2)}, u32[]{:S(2)}) collective-permute-start(bf16[144,512]{1,0:T(8,128)(2,1)S(1)} %get-tuple-element.42), channel_id=1, source_target_pairs={{0,2},{1,3},{2,0},{3,1},{4,6},{5,7},{6,4},{7,5},{8,10},{9,11},{10,... | collective-permute-start | bytes 442376 | tf_op jit(solution)/shard_map/ppermute | solution.py:288
  12.8 8.6 %collective-permute-start.5 = (bf16[112,512]{1,0:T(8,128)(2,1)S(1)}, bf16[112,512]{1,0:T(8,128)(2,1)S(1)}, u32[]{:S(2)}, u32[]{:S(2)}) collective-permute-start(bf16[112,512]{1,0:T(8,128)(2,1)S(1)} %get-tuple-element.39), channel_id=1, source_target_pairs={{0,4},{1,5},{2,6},{3,7},{4,8},{5,9},{6,10},{7,11},{8,12},{9,13},{1... | collective-permute-start | bytes 344072 | tf_op jit(solution)/shard_map/ppermute | solution.py:288
  14.3 9.8 %collective-permute-start.6 = (bf16[112,512]{1,0:T(8,128)(2,1)S(1)}, bf16[112,512]{1,0:T(8,128)(2,1)S(1)}, u32[]{:S(2)}, u32[]{:S(2)}) collective-permute-start(bf16[112,512]{1,0:T(8,128)(2,1)S(1)} %get-tuple-element.40), channel_id=1, source_target_pairs={{0,6},{1,7},{2,4},{3,5},{4,10},{5,11},{6,8},{7,9},{8,14},{9,15},{1... | collective-permute-start | bytes 344072 | tf_op jit(solution)/shard_map/ppermute | solution.py:288
  17.4 8.5 %collective-permute-start.8 = (bf16[144,512]{1,0:T(8,128)(2,1)S(1)}, bf16[144,512]{1,0:T(8,128)(2,1)S(1)}, u32[]{:S(2)}, u32[]{:S(2)}) collective-permute-start(bf16[144,512]{1,0:T(8,128)(2,1)S(1)} %get-tuple-element.45), channel_id=1, source_target_pairs={{0,4},{1,5},{2,6},{3,7},{4,8},{5,9},{6,10},{7,11},{8,12},{9,13},{1... | collective-permute-start | bytes 442376 | tf_op jit(solution)/shard_map/ppermute | solution.py:288
  19.4 4.8 %collective-permute-start.9 = (bf16[1024,256]{1,0:T(8,128)(2,1)S(1)}, bf16[1024,256]{1,0:T(8,128)(2,1)S(1)}, u32[]{:S(2)}, u32[]{:S(2)}) collective-permute-start(bf16[1024,256]{1,0:T(8,128)(2,1)S(1)} %get-tuple-element.47.refs_2_), channel_id=1, source_target_pairs={{0,1},{1,0},{2,3},{3,2},{4,5},{5,4},{6,7},{7,6},{8,9},{9,8},{10,11... | collective-permute-start | bytes 1572872 | tf_op jit(solution)/shard_map/ppermute | solution.py:288
  19.4 4.8 %collective-permute-start.10 = (bf16[1536,256]{1,0:T(8,128)(2,1)S(1)}, bf16[1536,256]{1,0:T(8,128)(2,1)S(1)}, u32[]{:S(2)}, u32[]{:S(2)}) collective-permute-start(bf16[1536,256]{1,0:T(8,128)(2,1)S(1)} %get-tuple-element.48.refs_3_), channel_id=1, source_target_pairs={{0,1},{1,0},{2,3},{3,2},{4,5},{5,4},{6,7},{7,6},{8,9},{9,8},{10,11... | collective-permute-start | bytes 2359304 | tf_op jit(solution)/shard_map/ppermute | solution.py:288
  27.8 5.2 %collective-permute-start.13 = (bf16[144,512]{1,0:T(8,128)(2,1)S(1)}, bf16[144,512]{1,0:T(8,128)(2,1)S(1)}, u32[]{:S(2)}, u32[]{:S(2)}) collective-permute-start(bf16[144,512]{1,0:T(8,128)(2,1)S(1)} %get-tuple-element.56), channel_id=1, source_target_pairs={{0,2},{1,3},{2,0},{3,1},{4,6},{5,7},{6,4},{7,5},{8,10},{9,11},{10,... | collective-permute-start | bytes 442376 | tf_op jit(solution)/shard_map/ppermute | solution.py:288
  29.0 7.5 %collective-permute-start.11 = (bf16[112,512]{1,0:T(8,128)(2,1)S(1)}, bf16[112,512]{1,0:T(8,128)(2,1)S(1)}, u32[]{:S(2)}, u32[]{:S(2)}) collective-permute-start(bf16[112,512]{1,0:T(8,128)(2,1)S(1)} %get-tuple-element.53), channel_id=1, source_target_pairs={{0,4},{1,5},{2,6},{3,7},{4,8},{5,9},{6,10},{7,11},{8,12},{9,13},{1... | collective-permute-start | bytes 344072 | tf_op jit(solution)/shard_map/ppermute | solution.py:288
  29.0 10.7 %collective-permute-start.12 = (bf16[112,512]{1,0:T(8,128)(2,1)S(1)}, bf16[112,512]{1,0:T(8,128)(2,1)S(1)}, u32[]{:S(2)}, u32[]{:S(2)}) collective-permute-start(bf16[112,512]{1,0:T(8,128)(2,1)S(1)} %get-tuple-element.54), channel_id=1, source_target_pairs={{0,6},{1,7},{2,4},{3,5},{4,10},{5,11},{6,8},{7,9},{8,14},{9,15},{1... | collective-permute-start | bytes 344072 | tf_op jit(solution)/shard_map/ppermute | solution.py:288
  33.1 8.0 %collective-permute-start.14 = (bf16[144,512]{1,0:T(8,128)(2,1)S(1)}, bf16[144,512]{1,0:T(8,128)(2,1)S(1)}, u32[]{:S(2)}, u32[]{:S(2)}) collective-permute-start(bf16[144,512]{1,0:T(8,128)(2,1)S(1)} %get-tuple-element.59), channel_id=1, source_target_pairs={{0,4},{1,5},{2,6},{3,7},{4,8},{5,9},{6,10},{7,11},{8,12},{9,13},{1... | collective-permute-start | bytes 442376 | tf_op jit(solution)/shard_map/ppermute | solution.py:288
  33.5 6.1 %collective-permute-start.15 = (bf16[1024,256]{1,0:T(8,128)(2,1)S(1)}, bf16[1024,256]{1,0:T(8,128)(2,1)S(1)}, u32[]{:S(2)}, u32[]{:S(2)}) collective-permute-start(bf16[1024,256]{1,0:T(8,128)(2,1)S(1)} %get-tuple-element.61.refs_2_), channel_id=1, source_target_pairs={{0,1},{1,0},{2,3},{3,2},{4,5},{5,4},{6,7},{7,6},{8,9},{9,8},{10,11... | collective-permute-start | bytes 1572872 | tf_op jit(solution)/shard_map/ppermute | solution.py:288
  33.5 6.1 %collective-permute-start.16 = (bf16[1536,256]{1,0:T(8,128)(2,1)S(1)}, bf16[1536,256]{1,0:T(8,128)(2,1)S(1)}, u32[]{:S(2)}, u32[]{:S(2)}) collective-permute-start(bf16[1536,256]{1,0:T(8,128)(2,1)S(1)} %get-tuple-element.62.refs_3_), channel_id=1, source_target_pairs={{0,1},{1,0},{2,3},{3,2},{4,5},{5,4},{6,7},{7,6},{8,9},{9,8},{10,11... | collective-permute-start | bytes 2359304 | tf_op jit(solution)/shard_map/ppermute | solution.py:288
  43.0 2.4 %collective-permute-start.17 = (bf16[1536,256]{1,0:T(8,128)(2,1)S(1)}, bf16[1536,256]{1,0:T(8,128)(2,1)S(1)}, u32[]{:S(2)}, u32[]{:S(2)}) collective-permute-start(bf16[1536,256]{1,0:T(8,128)(2,1)S(1)} %get-tuple-element.69.peer_errors), channel_id=1, source_target_pairs={{0,1},{1,0},{2,3},{3,2},{4,5},{5,4},{6,7},{7,6},{8,9},{9,8},{10,11... | collective-permute-start | bytes 2359304 | tf_op jit(solution)/shard_map/ppermute | solution.py:288
  43.0 5.9 %collective-permute-start.18 = (bf16[128,512]{1,0:T(8,128)(2,1)S(1)}, bf16[128,512]{1,0:T(8,128)(2,1)S(1)}, u32[]{:S(2)}, u32[]{:S(2)}) collective-permute-start(bf16[128,512]{1,0:T(8,128)(2,1)S(1)} %get-tuple-element.71), channel_id=1, source_target_pairs={{0,2},{1,3},{2,0},{3,1},{4,6},{5,7},{6,4},{7,5},{8,10},{9,11},{10,... | collective-permute-start | bytes 393224 | tf_op jit(solution)/shard_map/ppermute | solution.py:288
